TPU v7x, 128 devices: a whole 4x4x4 slice. The times are simulated.
128 devices in a mesh: comp: 2 (over core), face: 8 (over z_lo, y), tile: 8 (over z_hi, x).
Axes of the slice: x: 4, y: 4, z: 4 (z_hi: 2, z_lo: 2; z = z_hi * 2 + z_lo), core: 2. Of those that a mesh axis runs over, the one named last changes fastest.
Arguments:
- tokens: bfloat16 [2, 512, 128, 512], P('comp', 'tile', 'face'), may hold values from -6 to 6
- norm_gains: bfloat16 [2, 3, 512], P('comp'), may hold values from 0.5 to 1.5
- qkv_weight: bfloat16 [2, 512, 1536], P('comp'), may hold values from -0.25 to 0.25
- out_weight: bfloat16 [2, 512, 512], P('comp'), may hold values from -0.25 to 0.25
- cross_query: bfloat16 [2, 512, 512], P('comp'), may hold values from -0.25 to 0.25
- cross_kv: bfloat16 [2, 512, 1024], P('comp'), may hold values from -0.25 to 0.25
- cross_out: bfloat16 [2, 512, 512], P('comp'), may hold values from -0.25 to 0.25
- up_weight: bfloat16 [2, 512, 2048], P('comp'), may hold values from -0.25 to 0.25
- down_weight: bfloat16 [2, 2048, 512], P('comp'), may hold values from -0.125 to 0.125
- intersection_list: int32 [2, 64, 8, 4], P(None, 'tile', 'face'), may hold values from 0 to 7, all different within a row
- land_bands: int32 [8, 8], replicated, may hold values from 0 to 7
Outputs:
- evolved: bfloat16 [2, 512, 128, 512], P('comp', 'tile', 'face')
Inputs may be any that keep to these rules, and one draw needn't show every extreme that they name: `intersection_list`: each band names 4 different bands of the other component's tile. `land_bands`: the land bands of an ocean tile are its first ones.
All inputs are finite; a program needn't handle non-finite values.
Results may differ from a plain program's by a relative error of at most 0.0045.
Values may be sent and summed in bfloat16 or wider, within the bound.
No kernel may reach another device: no remote copies, remote signals or barrier semaphores. Data moves between devices by JAX's collectives and lax.ppermute only.
A program may use at most 128 MiB of HBM per device.

v0:
```python
import jax
import jax.numpy as jnp
from jax import lax
from jax.sharding import PartitionSpec as P

D = 512
HEADS = 8
RX = 16
BR = 8
NB = 8
KC = 4


EPSILON = 1e-05


def padded(block, sides, width):
    for axis, dim in sides:
        count = lax.axis_size(axis)
        forward = [(i, i + 1) for i in range(count - 1)]
        forward.append((count - 1, 0))
        backward = [(target, source) for source, target in forward]
        low = lax.ppermute(
            lax.slice_in_dim(block, block.shape[dim] - width, None, axis=dim), axis, forward
        )
        high = lax.ppermute(lax.slice_in_dim(block, 0, width, axis=dim), axis, backward)
        block = jnp.concatenate([low, block, high], axis=dim)
    return block


def swapped(shard, axis, bit):
    return lax.ppermute(shard, axis, [(i, i ^ 1 << bit) for i in range(lax.axis_size(axis))])


def norm_round(values, gain):
    mean_square = jnp.mean(values * values, axis=-1, keepdims=True)
    return (values * lax.rsqrt(mean_square + EPSILON) * gain.astype(jnp.float32)).astype(
        jnp.bfloat16
    )


def attend(queries, key_rows, value_rows, usable):
    blocks, count_q, feat_width = queries.shape
    count_k = key_rows.shape[1]
    head_dim = feat_width // HEADS
    score_scale = head_dim ** (-0.5)
    q_heads = queries.reshape(blocks, count_q, HEADS, head_dim)
    k_heads = key_rows.reshape(blocks, count_k, HEADS, head_dim)
    v_heads = value_rows.reshape(blocks, count_k, HEADS, head_dim)
    scores = (
        jnp.einsum("bqhd,bkhd->bhqk", q_heads, k_heads, preferred_element_type=jnp.float32)
        * score_scale
    )
    scores = jnp.where(usable[:, None, None, :], scores, -1e30)
    highest = jnp.maximum(jnp.max(scores, axis=-1, keepdims=True), 0.0)
    exp_terms = jnp.exp(scores - highest)
    denominator = jnp.sum(exp_terms, axis=-1, keepdims=True) + jnp.exp(-highest)
    weights = (exp_terms / denominator).astype(jnp.bfloat16)
    blended = jnp.einsum("bhqk,bkhd->bqhd", weights, v_heads, preferred_element_type=jnp.float32)
    return blended.reshape(blocks, count_q, feat_width).astype(jnp.bfloat16)


def window_bands(array_in):
    grouped = array_in.reshape((NB + 2, BR) + array_in.shape[1:])
    joined = jnp.concatenate([grouped[0:NB], grouped[1 : NB + 1], grouped[2 : NB + 2]], axis=1)
    return joined.reshape((NB, -1) + array_in.shape[2:])


def per_device(
    tokens,
    norm_gains,
    qkv_weight,
    out_weight,
    cross_query,
    cross_kv,
    cross_out,
    up_weight,
    down_weight,
    intersection_list,
    land_bands,
):
    component = lax.axis_index("comp")
    tile_row = lax.axis_index("tile")
    tile_col = lax.axis_index("face")
    tiles_lat = lax.axis_size("tile")
    tiles_lon = lax.axis_size("face")
    rows_dev = NB * BR
    lat_total = rows_dev * tiles_lat
    lon_total = RX * tiles_lon
    is_ocean = component == 1
    residual_in = tokens[0].astype(jnp.float32).reshape(rows_dev * RX, D)
    gains_here = norm_gains[0]
    attn_input = norm_round(residual_in, gains_here[0])
    cross_input = norm_round(residual_in, gains_here[1])
    weights_qkv = qkv_weight[0]
    projected = jnp.dot(attn_input, weights_qkv, preferred_element_type=jnp.float32).astype(
        jnp.bfloat16
    )
    queries = projected[:, :D]
    pair_pad = padded(projected[:, D:].reshape(rows_dev, RX, 2 * D), (("face", 1), ("tile", 0)), BR)
    rows_pad = tile_row * rows_dev - BR + jnp.arange(rows_dev + 2 * BR, dtype=jnp.int32)
    lat_ok = (rows_pad >= 0) & (rows_pad < lat_total)
    rows_in = jnp.clip(rows_pad, 0, lat_total - 1)
    cols_pad = (tile_col * RX - BR + jnp.arange(RX + 2 * BR, dtype=jnp.int32)) % lon_total
    row_onehot = (
        (rows_in // rows_dev)[:, None] == jnp.arange(tiles_lat, dtype=jnp.int32)[None, :]
    ).astype(jnp.int32)
    col_onehot = (
        (cols_pad // RX)[:, None] == jnp.arange(tiles_lon, dtype=jnp.int32)[None, :]
    ).astype(jnp.int32)
    land_pad = jnp.dot(jnp.dot(row_onehot, land_bands), col_onehot.T)
    sea_ok = (rows_in % rows_dev // BR)[:, None] >= land_pad
    usable = lat_ok[:, None] & (jnp.logical_not(is_ocean) | sea_ok)
    pair_win = window_bands(pair_pad)
    window_out = attend(
        queries.reshape(NB, BR * RX, D),
        pair_win[:, :, :D],
        pair_win[:, :, D:],
        window_bands(usable),
    )
    here_mask = (jnp.arange(tiles_lat, dtype=jnp.int32)[:, None] == tile_row) & (
        jnp.arange(tiles_lon, dtype=jnp.int32)[None, :] == tile_col
    )
    own_land = jnp.sum(jnp.where(here_mask, land_bands, 0))
    cross_q = (
        jnp.dot(cross_input, cross_query[0], preferred_element_type=jnp.float32)
        .astype(jnp.bfloat16)
        .reshape(NB, BR * RX, D)
    )
    cross_pair = (
        jnp.dot(cross_input, cross_kv[0], preferred_element_type=jnp.float32)
        .astype(jnp.bfloat16)
        .reshape(NB, BR * RX, 2 * D)
    )
    air_links = intersection_list[0, :, 0, :]
    sea_links = intersection_list[1, :, 0, :]
    my_links = jnp.where(is_ocean, sea_links, air_links)
    partner_pair = swapped(cross_pair, "comp", 0)
    key_floor = jnp.where(is_ocean, 0, own_land)
    picked = jnp.take(partner_pair, my_links, axis=0).reshape(NB, KC * BR * RX, 2 * D)
    usable_keys = jnp.repeat(my_links >= key_floor, BR * RX, axis=1)
    cross_res = attend(cross_q, picked[:, :, :D], picked[:, :, D:], usable_keys)
    live_rows = jnp.logical_not(is_ocean) | (
        jnp.arange(rows_dev, dtype=jnp.int32) // BR >= own_land
    )
    live_mask = jnp.repeat(jnp.where(live_rows, jnp.float32(1.0), jnp.float32(0.0)), RX)[:, None]
    update = jnp.dot(window_out.reshape(-1, D), out_weight[0], preferred_element_type=jnp.float32)
    update = update + jnp.dot(
        cross_res.reshape(-1, D), cross_out[0], preferred_element_type=jnp.float32
    )
    middle = residual_in + live_mask * update
    mlp_input = norm_round(middle, gains_here[2])
    hidden = jax.nn.silu(
        jnp.dot(mlp_input, up_weight[0], preferred_element_type=jnp.float32)
    ).astype(jnp.bfloat16)
    result_rows = middle + live_mask * jnp.dot(
        hidden, down_weight[0], preferred_element_type=jnp.float32
    )
    return result_rows.astype(jnp.bfloat16).reshape(1, rows_dev, RX, D)


def solution(mesh):
    placed = (
        P("comp", "tile", "face", None),
        P("comp", None, None),
        P("comp", None, None),
        P("comp", None, None),
        P("comp", None, None),
        P("comp", None, None),
        P("comp", None, None),
        P("comp", None, None),
        P("comp", None, None),
        P(None, "tile", "face", None),
        P(),
    )
    return jax.shard_map(
        per_device,
        mesh=mesh,
        in_specs=placed,
        out_specs=P("comp", "tile", "face", None),
        check_vma=False,
    )
```

profile of v0, /device:TPU:30, one launch (start us, length us, event | category | flops | bytes accessed | tf_op | source)
XLA Modules:
  0.0 206.7 jit_solution(17911633333399519121)
XLA Ops:
  0.0 0.0 copy-start
  0.0 1.4 slice_convert_fusion
  1.5 1.5 multiply_reduce_fusion.1
  3.0 0.0 copy-start.12
  3.0 1.7 multiply_convert_fusion.3
  4.8 4.2 %convolution_convert_fusion.1 = bf16[1024,1024]{1,0:T(8,128)(2,1)} fusion(bf16[1024,512]{1,0:T(8,128)(2,1)S(1)} %bitcast.108, bf16[1,512,1024]{2,1,0:T(8,128)(2,1)} %param.16), kind=kOutput, calls=%fused_computation.38 | convolution fusion | flops 1074790400 | bytes 4194304 | tf_op jit(solution)/shard_map/dot_general | solution.py:131
  8.9 0.0 collective-permute-start.4
  8.9 0.0 copy-done.12
  9.0 1.8 convolution_convert_fusion
  10.8 0.0 copy-start.9
  10.8 0.0 copy-start.10
  10.8 0.3 slice.109
  11.1 0.0 copy-start.1
  11.1 1.6 copy-done.1
  12.7 1.5 fusion.62
  14.2 1.6 collective-permute-start
  15.8 0.5 collective-permute-start.1
  16.2 0.7 select_reduce_fusion
  17.6 3.1 %convolution_convert_fusion.2 = bf16[1024,512]{1,0:T(8,128)(2,1)} fusion(bf16[1024,512]{1,0:T(8,128)(2,1)} %bitcast.109, bf16[1,512,512]{2,1,0:T(8,128)(2,1)} %param.15), kind=kOutput, calls=%fused_computation.41 | convolution fusion | flops 537395200 | bytes 2621440 | tf_op jit(solution)/shard_map/dot_general | solution.py:126
  20.7 2.3 %slice.116 = bf16[1024,512]{1,0:T(8,128)(2,1)} slice(bf16[1024,1536]{1,0:T(8,128)(2,1)} %copy-done.5), slice={[0:1024], [0:512]} | slice | bytes 2097152 | tf_op jit(solution)/shard_map/slice | solution.py:99
  23.0 0.1 copy.26
  23.1 0.1 reshape.312
  23.2 3.9 %reshape.321 = bf16[8,128,8,64]{3,2,1,0:T(8,128)(2,1)} reshape(bf16[1024,512]{1,0:T(8,128)(2,1)} %convolution_convert_fusion.2) | data formatting | bytes 2097152 | tf_op jit(solution)/shard_map/reshape;reshape | solution.py:47
  27.1 0.4 fusion.34
  27.5 0.1 fusion.63
  27.6 0.1 copy.19
  27.7 0.1 copy.20
  27.8 0.1 copy.21
  27.9 0.1 broadcast_in_dim.82
  28.0 3.9 %reshape.320 = bf16[8,128,8,64]{3,2,1,0:T(8,128)(2,1)} reshape(bf16[1024,512]{1,0:T(8,128)(2,1)} %slice.116) | data formatting | bytes 2097152 | tf_op jit(solution)/shard_map/reshape;reshape | solution.py:47
  31.9 0.6 or_select_fusion
  32.5 0.1 broadcast_in_dim.81
  32.6 0.7 mul.96
  33.3 6.7 %collective-permute-done = bf16[64,8,1024]{2,1,0:T(8,128)(2,1)S(1)} collective-permute-done((bf16[64,8,1024]{2,1,0:T(8,128)(2,1)}, bf16[64,8,1024]{2,1,0:T(8,128)(2,1)S(1)}, u32[]{:S(2)}, u32[]{:S(2)}) %collective-permute-start) | collective-permute-done | bytes 1048608 | tf_op jit(solution)/shard_map/ppermute | solution.py:23
  40.0 3.5 %collective-permute-done.1 = bf16[64,8,1024]{2,1,0:T(8,128)(2,1)} collective-permute-done((bf16[64,8,1024]{2,1,0:T(8,128)(2,1)}, bf16[64,8,1024]{2,1,0:T(8,128)(2,1)}, u32[]{:S(2)}, u32[]{:S(2)}) %collective-permute-start.1) | collective-permute-done | bytes 1048608 | tf_op jit(solution)/shard_map/ppermute | solution.py:26
  43.5 1.2 pad_maximum_fusion.9
  44.8 3.6 %collective-permute-start.2 = (bf16[8,32,1024]{2,1,0:T(8,128)(2,1)S(1)}, bf16[8,32,1024]{2,1,0:T(8,128)(2,1)S(1)}, u32[]{:S(2)}, u32[]{:S(2)}) collective-permute-start(bf16[8,32,1024]{2,1,0:T(8,128)(2,1)S(1)} %get-tuple-element.13), channel_id=1, source_target_pairs={{0,1},{1,2},{2,3},{3,4},{4,5},{5,6},{6,7},{7,0},{8,9},{9,10},{10,1... | collective-permute-start | bytes 1572872 | tf_op jit(solution)/shard_map/ppermute | solution.py:23
  48.3 0.0 collective-permute-start.3
  48.3 0.1 broadcast_bitcast_fusion.1
  48.4 0.1 broadcast_bitcast_fusion
  48.5 10.6 %collective-permute-done.2 = bf16[8,32,1024]{2,1,0:T(8,128)(2,1)S(1)} collective-permute-done((bf16[8,32,1024]{2,1,0:T(8,128)(2,1)S(1)}, bf16[8,32,1024]{2,1,0:T(8,128)(2,1)S(1)}, u32[]{:S(2)}, u32[]{:S(2)}) %collective-permute-start.2) | collective-permute-done | bytes 524320 | tf_op jit(solution)/shard_map/ppermute | solution.py:23
  59.1 5.8 %collective-permute-done.3 = bf16[8,32,1024]{2,1,0:T(8,128)(2,1)S(1)} collective-permute-done((bf16[8,32,1024]{2,1,0:T(8,128)(2,1)S(1)}, bf16[8,32,1024]{2,1,0:T(8,128)(2,1)S(1)}, u32[]{:S(2)}, u32[]{:S(2)}) %collective-permute-start.3) | collective-permute-done | bytes 524320 | tf_op jit(solution)/shard_map/ppermute | solution.py:26
  64.9 3.1 %pad_maximum_fusion.4 = (bf16[64,32,1024]{2,1,0:T(8,128)(2,1)S(1)}, bf16[64,32,1024]{2,1,0:T(8,128)(2,1)S(1)}) fusion(bf16[8,32,1024]{2,1,0:T(8,128)(2,1)S(1)} %collective-permute-done.2, bf16[64,8,1024]{2,1,0:T(8,128)(2,1)} %collective-permute-done.1, bf16[64,16,1024]{2,1,0:T(8,128)(2,1)S(1)} %bitcast.95, bf16[64,8,1024]{2,1,0:T(8,128)(2,1)S(1)} %collective-permute-done, ...), kind=kLoop, calls=%fused_computation.19 | loop fusion | flops 33554432 | bytes 13631488 | tf_op jit(solution)/shard_map/concatenate | solution.py:27
  68.0 11.6 %pad_maximum_fusion = bf16[8,24,32,1024]{3,2,1,0:T(8,128)(2,1)S(1)} fusion(bf16[8,8,32,1024]{3,2,1,0:T(8,128)(2,1)S(1)} %bitcast.102, bf16[8,8,8,1024]{3,2,1,0:T(8,128)(2,1)} %bitcast.8, bf16[8,8,16,1024]{3,2,1,0:T(8,128)(2,1)S(1)} %bitcast.96, bf16[8,8,8,1024]{3,2,1,0:T(8,128)(2,1)S(1)} %bitcast.103, bf16[8,8,32,1024]{3,2,1,0:T(8,128)(2,1)S(1)} %bitcast.101), kind=kLoop, calls=%fused_computation.11 | loop fusion | flops 62914560 | bytes 25165824 | tf_op jit(solution)/shard_map/concatenate | solution.py:65
  79.6 5.0 %fusion.60 = (bf16[8,768,512]{2,1,0:T(8,128)(2,1)}, bf16[8,768,512]{2,1,0:T(8,128)(2,1)}) fusion(bf16[8,768,1024]{2,1,0:T(8,128)(2,1)S(1)} %bitcast.97), kind=kLoop, calls=%fused_computation.119 | loop fusion | bytes 25165824 | tf_op jit(solution)/shard_map/slice | solution.py:117
  84.6 8.7 %copy.36 = bf16[8,768,512]{1,2,0:T(8,128)(2,1)} copy(bf16[8,768,512]{2,1,0:T(8,128)(2,1)} %get-tuple-element.7) | data formatting | bytes 12582912
  93.3 12.9 %fusion = (f32[8,8,128]{2,1,0:T(8,128)S(1)}, f32[8,8,128,768]{3,2,1,0:T(8,128)}) fusion(pred[8,768]{1,0:T(8,128)(4,1)S(1)} %broadcast_in_dim.82, bf16[8,768,8,64]{1,3,2,0:T(8,128)(2,1)} %bitcast.99, bf16[8,128,8,64]{3,2,1,0:T(8,128)(2,1)} %reshape.320), kind=kOutput, calls=%fused_computation.4 | convolution fusion | flops 824172544 | bytes 32544768 | tf_op jit(solution)/shard_map/bqhd,bkhd->bhqk/dot_general | solution.py:51
  106.2 12.3 %fusion.1 = f32[8,8,128]{2,1,0:T(8,128)S(1)} fusion(f32[8,8,128,768]{3,2,1,0:T(8,128)} %get-tuple-element.26, f32[8,8,128]{2,1,0:T(8,128)S(1)} %broadcast_maximum_fusion.1, pred[8,768]{1,0:T(8,128)(4,1)S(1)} %broadcast_in_dim.82), kind=kLoop, calls=%fused_computation.5 | loop fusion | flops 25157632 | bytes 25237504 | tf_op jit(solution)/shard_map/reduce_sum | solution.py:57
  118.6 8.7 %copy.35 = bf16[8,768,512]{1,2,0:T(8,128)(2,1)} copy(bf16[8,768,512]{2,1,0:T(8,128)(2,1)} %get-tuple-element.8) | data formatting | bytes 12582912
  127.3 13.8 %fusion.24 = bf16[8,128,8,64]{1,3,2,0:T(8,128)(2,1)S(1)} fusion(bf16[8,768,8,64]{1,3,2,0:T(8,128)(2,1)} %bitcast.105, f32[8,8,128,768]{3,2,1,0:T(8,128)} %get-tuple-element.26, f32[8,8,128]{2,1,0:T(8,128)S(1)} %exponential_add_fusion.1, f32[8,8,128]{2,1,0:T(8,128)S(1)} %broadcast_maximum_fusion.1, pred[8,768]{1,0:T(8,128)(4,1)S(1)} %broadcast_in_dim.82), kind=kOutput, calls=%fused_computation.44 | convolution fusion | flops 837287936 | bytes 32577536 | tf_op jit(solution)/shard_map/bhqk,bkhd->bqhd/dot_general | solution.py:59
  141.0 0.7 copy.25
  141.8 2.1 %fusion.39 = f32[1024,512]{1,0:T(8,128)} fusion(bf16[64,8,8,128]{3,2,1,0:T(8,128)(2,1)S(1)} %bitcast.104, bf16[1,512,512]{2,1,0:T(8,128)(2,1)S(1)} %copy-done.7), kind=kOutput, calls=%fused_computation.52 | convolution fusion | flops 536870912 | bytes 3670016 | tf_op jit(solution)/shard_map/dot_general | solution.py:147
  143.8 0.0 collective-permute-done.4
  143.8 6.8 %gather_fusion = bf16[32,128,1024]{2,1,0:T(8,128)(2,1)} fusion(bf16[8,128,1024]{2,1,0:T(8,128)(2,1)} %collective-permute-done.4, s32[1024]{0:T(1024)S(1)} %pad_clamp_fusion), kind=kCustom, calls=%fused_computation | custom fusion | bytes 16777344 | tf_op jit(solution)/shard_map/jit(_take)/gather | solution.py:140
  150.6 11.4 %copy.27 = bf16[8,512,1024]{1,2,0:T(8,128)(2,1)} copy(bf16[8,512,1024]{2,1,0:T(8,128)(2,1)} %bitcast.98) | data formatting | bytes 16777216 | tf_op jit(solution)/shard_map/jit(_take)/gather | solution.py:140
  162.0 7.4 %broadcast_select_fusion = bf16[8,512,1024]{1,2,0:T(8,128)(2,1)} fusion(bf16[8,512,1024]{1,2,0:T(8,128)(2,1)} %copy.27, pred[8,512]{1,0:T(8,128)(4,1)S(1)} %broadcast_bitcast_fusion.1), kind=kLoop, calls=%fused_computation.14 | loop fusion | flops 4194304 | bytes 16781312 | tf_op jit(solution)/shard_map/jit(_take)/select_n | solution.py:140
  169.4 5.9 %fusion.61 = (bf16[8,512,512]{1,2,0:T(8,128)(2,1)}, bf16[8,512,512]{1,2,0:T(8,128)(2,1)}) fusion(bf16[8,512,1024]{1,2,0:T(8,128)(2,1)} %broadcast_select_fusion), kind=kLoop, calls=%fused_computation.120 | loop fusion | bytes 16777216 | tf_op jit(solution)/shard_map/slice | solution.py:142
  175.3 4.3 %fusion.2 = (f32[8,8,128]{2,1,0:T(8,128)S(1)}, f32[8,8,128,512]{3,2,1,0:T(8,128)S(1)}) fusion(pred[8,512]{1,0:T(8,128)(4,1)S(1)} %broadcast_bitcast_fusion, bf16[8,512,8,64]{1,3,2,0:T(8,128)(2,1)} %bitcast.100, bf16[8,128,8,64]{3,2,1,0:T(8,128)(2,1)S(1)} %copy-done.4), kind=kOutput, calls=%fused_computation.9 | convolution fusion | flops 549445632 | bytes 22056960 | tf_op jit(solution)/shard_map/bqhd,bkhd->bhqk/dot_general | solution.py:51
  179.5 4.4 %fusion.3 = f32[8,8,128]{2,1,0:T(8,128)S(1)} fusion(f32[8,8,128,512]{3,2,1,0:T(8,128)S(1)} %get-tuple-element.28, f32[8,8,128]{2,1,0:T(8,128)S(1)} %broadcast_maximum_fusion, pred[8,512]{1,0:T(8,128)(4,1)S(1)} %broadcast_bitcast_fusion), kind=kLoop, calls=%fused_computation.10 | loop fusion | flops 16769024 | bytes 16846848 | tf_op jit(solution)/shard_map/reduce_sum | solution.py:57
  183.9 0.6 exponential_add_fusion
  184.6 7.8 %fusion.23 = bf16[8,128,8,64]{1,3,2,0:T(8,128)(2,1)} fusion(bf16[8,512,8,64]{1,3,2,0:T(8,128)(2,1)} %bitcast.107, f32[8,8,128,512]{3,2,1,0:T(8,128)S(1)} %get-tuple-element.28, f32[8,8,128]{2,1,0:T(8,128)} %exponential_add_fusion, f32[8,8,128]{2,1,0:T(8,128)S(1)} %broadcast_maximum_fusion, pred[8,512]{1,0:T(8,128)(4,1)S(1)} %broadcast_bitcast_fusion), kind=kOutput, calls=%fused_computation.43 | convolution fusion | flops 558366720 | bytes 22089728 | tf_op jit(solution)/shard_map/bhqk,bkhd->bqhd/dot_general | solution.py:59
  192.4 1.9 copy.30
  194.3 3.7 %multiply_reduce_fusion = (f32[1024]{0:T(1024)S(1)}, f32[1024,512]{1,0:T(8,128)}) fusion(f32[1024,512]{1,0:T(8,128)S(1)} %copy-done.3, bf16[1,512,512]{2,1,0:T(8,128)(2,1)} %param.17, bf16[64,8,8,128]{3,2,1,0:T(8,128)(2,1)S(1)} %bitcast.106, f32[1024]{0:T(1024)S(1)} %copy-done.8, bf16[1,64,16,512]{3,2,1,0:T(8,128)(2,1)} %param.11), kind=kOutput, calls=%fused_computation.34 | convolution fusion | flops 540015616 | bytes 6823936 | tf_op jit(solution)/shard_map/dot_general | solution.py:148
  198.0 8.7 %add_convert_fusion = bf16[1024,512]{1,0:T(8,128)(2,1)} fusion(f32[1024,512]{1,0:T(8,128)} %get-tuple-element.30, bf16[1,2048,512]{2,1,0:T(8,128)(2,1)S(1)} %copy-done, bf16[1,512,2048]{2,1,0:T(8,128)(2,1)} %param.18, f32[512]{0:T(512)S(1)} %bitcast.116, f32[1024]{0:T(1024)S(1)} %add_rsqrt_fusion.1, f32[1024]{0:T(1024)S(1)} %copy-done.8), kind=kOutput, calls=%fused_computation.32 | convolution fusion | flops 4308598784 | bytes 7350272 | tf_op jit(solution)/shard_map/dot_general | solution.py:156
  (33 shorter events, 0.2 us)
Async XLA Ops:
  0.0 198.0 %copy-start = (bf16[1,2048,512]{2,1,0:T(8,128)(2,1)S(1)}, bf16[1,2048,512]{2,1,0:T(8,128)(2,1)}, u32[]{:S(2)}) copy-start(bf16[1,2048,512]{2,1,0:T(8,128)(2,1)} %param.19) | copy-start | bytes 6291460
  3.0 6.0 %copy-start.12 = (bf16[1,512,1536]{2,1,0:T(8,128)(2,1)S(1)}, bf16[1,512,1536]{2,1,0:T(8,128)(2,1)}, u32[]{:S(2)}) copy-start(bf16[1,512,1536]{2,1,0:T(8,128)(2,1)} %param.13) | copy-start | bytes 4718596
  4.7 4.2 %copy-start.6 = (bf16[1,64,16,512]{3,2,1,0:T(8,128)(2,1)}, bf16[1,64,16,512]{3,2,1,0:T(8,128)(2,1)S(1)}, u32[]{:S(2)}) copy-start(bf16[1,64,16,512]{3,2,1,0:T(8,128)(2,1)S(1)} %get-tuple-element.17) | copy-start | bytes 3145732
  8.9 134.9 %collective-permute-start.4 = (bf16[8,128,1024]{2,1,0:T(8,128)(2,1)}, bf16[8,128,1024]{2,1,0:T(8,128)(2,1)}, u32[]{:S(2)}, u32[]{:S(2)}) collective-permute-start(bf16[8,128,1024]{2,1,0:T(8,128)(2,1)} %bitcast.23), channel_id=1, source_target_pairs={{0,64},{64,0},{1,65},{65,1},{2,66},{66,2},{3,67},{67,3},{4,68},{68... | collective-permute-start | bytes 6291464 | tf_op jit(solution)/shard_map/ppermute | solution.py:32
  10.8 3.5 %copy-start.5 = (bf16[1024,1536]{1,0:T(8,128)(2,1)}, bf16[1024,1536]{1,0:T(8,128)(2,1)S(1)}, u32[]{:S(2)}) copy-start(bf16[1024,1536]{1,0:T(8,128)(2,1)S(1)} %convolution_convert_fusion) | copy-start | bytes 9437188
  10.8 5.5 %copy-start.9 = (s32[8,8]{1,0:T(8,128)S(1)}, s32[8,8]{1,0:T(8,128)}, u32[]{:S(2)}) copy-start(s32[8,8]{1,0:T(8,128)} %param.21) | copy-start | bytes 772
  10.8 6.7 %copy-start.10 = (s32[2,8,1,4]{1,3,2,0:T(4,128)S(1)}, s32[2,8,1,4]{1,3,2,0:T(4,128)}, u32[]{:S(2)}) copy-start(s32[2,8,1,4]{1,3,2,0:T(4,128)} %param.20) | copy-start | bytes 772
  11.1 1.6 copy-start.1
  14.2 25.8 %collective-permute-start = (bf16[64,8,1024]{2,1,0:T(8,128)(2,1)}, bf16[64,8,1024]{2,1,0:T(8,128)(2,1)S(1)}, u32[]{:S(2)}, u32[]{:S(2)}) collective-permute-start(bf16[64,8,1024]{2,1,0:T(8,128)(2,1)} %get-tuple-element.15), channel_id=1, source_target_pairs={{0,8},{8,16},{16,24},{24,32},{32,40},{40,48},{48,56},{56,0},{1,9},... | collective-permute-start | bytes 3145736 | tf_op jit(solution)/shard_map/ppermute | solution.py:23
  15.8 27.7 %collective-permute-start.1 = (bf16[64,8,1024]{2,1,0:T(8,128)(2,1)}, bf16[64,8,1024]{2,1,0:T(8,128)(2,1)}, u32[]{:S(2)}, u32[]{:S(2)}) collective-permute-start(bf16[64,8,1024]{2,1,0:T(8,128)(2,1)} %get-tuple-element.16), channel_id=1, source_target_pairs={{8,0},{16,8},{24,16},{32,24},{40,32},{48,40},{56,48},{0,56},{9,1},... | collective-permute-start | bytes 3145736 | tf_op jit(solution)/shard_map/ppermute | solution.py:26
  33.2 31.7 %copy-start.2 = (bf16[1024,1024]{1,0:T(8,128)(2,1)S(1)}, bf16[1024,1024]{1,0:T(8,128)(2,1)}, u32[]{:S(2)}) copy-start(bf16[1024,1024]{1,0:T(8,128)(2,1)} %copy-done.1) | copy-start | bytes 6291460
  44.8 14.3 %collective-permute-start.2 = (bf16[8,32,1024]{2,1,0:T(8,128)(2,1)S(1)}, bf16[8,32,1024]{2,1,0:T(8,128)(2,1)S(1)}, u32[]{:S(2)}, u32[]{:S(2)}) collective-permute-start(bf16[8,32,1024]{2,1,0:T(8,128)(2,1)S(1)} %get-tuple-element.13), channel_id=1, source_target_pairs={{0,1},{1,2},{2,3},{3,4},{4,5},{5,6},{6,7},{7,0},{8,9},{9,10},{10,1... | collective-permute-start | bytes 1572872 | tf_op jit(solution)/shard_map/ppermute | solution.py:23
  48.3 16.6 %collective-permute-start.3 = (bf16[8,32,1024]{2,1,0:T(8,128)(2,1)S(1)}, bf16[8,32,1024]{2,1,0:T(8,128)(2,1)S(1)}, u32[]{:S(2)}, u32[]{:S(2)}) collective-permute-start(bf16[8,32,1024]{2,1,0:T(8,128)(2,1)S(1)} %get-tuple-element.14), channel_id=1, source_target_pairs={{1,0},{2,1},{3,2},{4,3},{5,4},{6,5},{7,6},{0,7},{9,8},{10,9},{11,1... | collective-permute-start | bytes 1572872 | tf_op jit(solution)/shard_map/ppermute | solution.py:26
  127.3 14.5 %copy-start.7 = (bf16[1,512,512]{2,1,0:T(8,128)(2,1)S(1)}, bf16[1,512,512]{2,1,0:T(8,128)(2,1)}, u32[]{:S(2)}) copy-start(bf16[1,512,512]{2,1,0:T(8,128)(2,1)} %param.14) | copy-start | bytes 1572868
  169.4 5.9 %copy-start.4 = (bf16[8,128,8,64]{3,2,1,0:T(8,128)(2,1)S(1)}, bf16[8,128,8,64]{3,2,1,0:T(8,128)(2,1)}, u32[]{:S(2)}) copy-start(bf16[8,128,8,64]{3,2,1,0:T(8,128)(2,1)} %reshape.321) | copy-start | bytes 3145732
  184.5 9.7 %copy-start.3 = (f32[1024,512]{1,0:T(8,128)S(1)}, f32[1024,512]{1,0:T(8,128)}, u32[]{:S(2)}) copy-start(f32[1024,512]{1,0:T(8,128)} %fusion.39) | copy-start | bytes 6291460
  184.6 9.7 %copy-start.8 = (f32[1024]{0:T(1024)S(1)}, f32[1024]{0:T(1024)}, u32[]{:S(2)}) copy-start(f32[1024]{0:T(1024)} %mul.96) | copy-start | bytes 12292
  192.4 5.6 %copy-start.11 = (f32[1,1,512]{2,1,0:T(1,128)S(1)}, f32[1,1,512]{2,1,0:T(1,128)}, u32[]{:S(2)}) copy-start(f32[1,1,512]{2,1,0:T(1,128)} %get-tuple-element.19) | copy-start | bytes 6148
where the time goes:
time: 208 us; the launch traced here: 207 us
  local copies, waits for them, and re-layouts  64.2 us (31%)
  matrix products  62.6 us (30%)
  other arithmetic  46.7 us (22%)
  waiting for transfers between devices  26.7 us (13%)
  starting transfers between devices  5.6 us (3%)
    dot_general x2, matrix products, attend(): jnp.einsum('bhqk,bkhd->bqhd', weights, v_heads, preferred_element_type=jn...  21.6 us
    unnamed x28, local copies, waits for them, and re-layouts  19 us
    gather x2, local copies, waits for them, and re-layouts, per_device(): jnp.take(partner_pair, my_links, axis=0).reshape(NB, KC * BR * RX, 2 * D)  18.2 us
    ppermute x2, waiting for transfers between devices, padded(): lax.ppermute(lax.slice_in_dim(block, block.shape[dim] - width, None, axis...  17.3 us
    dot_general x2, matrix products, attend(): jnp.einsum('bqhd,bkhd->bhqk', q_heads, k_heads, preferred_element_type=jn...  17.2 us
    reduce_sum x2, other arithmetic, attend(): denominator = jnp.sum(exp_terms, axis=-1, keepdims=True) + jnp.exp(-highest)  16.7 us
    concatenate x2, other arithmetic, window_bands(): jnp.concatenate([grouped[0:NB], grouped[1:NB + 1], grouped[2:NB + 2]], ax...  11.6 us
    ppermute x2, waiting for transfers between devices, padded(): lax.ppermute(lax.slice_in_dim(block, 0, width, axis=dim), axis, backward)  9.33 us
  transfers between devices with their start and end apart: 5, of which 4 were waited for; matrix products, arithmetic and copies ran while one was open for 49% of the time, Pallas kernels for 0%

commit v1 on v0

v1 whole, which is shorter than its diff:
```python
import jax
import jax.numpy as jnp
from jax import lax
from jax.experimental import pallas as pl
from jax.experimental.pallas import tpu as pltpu
from jax.sharding import PartitionSpec as P

D = 512
FF = 2048
HEADS = 8
PAIRS = HEADS // 2
LANES = 128
RX = 16
BR = 8
NB = 8
KC = 4
CELLS = BR * RX
ROWS = NB * CELLS
SIDE = BR * BR
GROUP = CELLS + 2 * SIDE
WINDOW = 3 * GROUP

EPSILON = 1e-05
Q_SCALE = 1.4426950408889634 / 8.0
LIMIT = 2.0**100
BF = jnp.bfloat16
F32 = jnp.float32
MIB = 1 << 20


def norm_round(values, gain):
    mean_square = jnp.mean(values * values, axis=-1, keepdims=True)
    return (values * lax.rsqrt(mean_square + EPSILON) * gain.astype(F32)).astype(BF)


def mm(a, b):
    return jnp.dot(a, b, preferred_element_type=F32)


def mm_nt(a, b):
    return lax.dot_general(a, b, (((1,), (1,)), ((), ())), preferred_element_type=F32)


def low_half(rows):
    return lax.broadcasted_iota(jnp.int32, (rows, LANES), 1) < LANES // 2


def augment(values, flag, out_ref, row, rows):
    lo = low_half(rows)
    one = jnp.ones((rows, LANES), BF)
    keep = flag.astype(F32).astype(BF)
    for p in range(PAIRS):
        pair = values[:, p * LANES : (p + 1) * LANES]
        even = jnp.where(lo, pair, one) * keep
        odd = jnp.where(lo, one, pair) * keep
        out_ref[pl.ds(row, rows), pl.ds(2 * p * LANES, LANES)] = even
        out_ref[pl.ds(row, rows), pl.ds((2 * p + 1) * LANES, LANES)] = odd


def attend_pair(pair, keys, even_values, odd_values, mask=None):
    lo = low_half(CELLS)
    zero = jnp.zeros_like(pair)
    stacked = jnp.concatenate([jnp.where(lo, pair, zero), jnp.where(lo, zero, pair)], axis=0)
    scores = mm_nt(stacked, keys)
    if mask is None:
        extra = 1.0
    else:
        scores = jnp.where(mask > 0.5, scores, -1e30)
        highest = jnp.maximum(jnp.max(scores, axis=-1, keepdims=True), 0.0)
        scores = scores - highest
        extra = jnp.exp2(-highest)
        extra = jnp.where(lo, extra[:CELLS], extra[CELLS:])
    terms = jnp.exp2(scores).astype(BF)
    even = mm(terms[:CELLS], even_values)
    odd = mm(terms[CELLS:], odd_values)
    sums = jnp.where(lo, odd, even)
    below = pltpu.roll(sums, LANES // 2, 1) + extra
    return (jnp.where(lo, even, odd) / below).astype(BF), sums


def kernel_cross_kv(x_ref, gain_ref, weight_ref, out_ref):
    cross_input = norm_round(x_ref[...].astype(F32), gain_ref[1:2, :])
    out_ref[...] = mm(cross_input, weight_ref[...]).astype(BF)


def kernel_own(x_ref, gain_ref, qkv_ref, cq_ref, q_ref, k_ref, v_ref, c_ref):
    values = x_ref[...].astype(F32)
    mean_square = jnp.mean(values * values, axis=-1, keepdims=True)
    unit = values * lax.rsqrt(mean_square + EPSILON)
    attn_input = (unit * gain_ref[0:1, :].astype(F32)).astype(BF)
    cross_input = (unit * gain_ref[1:2, :].astype(F32)).astype(BF)
    q_ref[...] = (mm(attn_input, qkv_ref[:, :D]) * Q_SCALE).astype(BF)
    k_ref[...] = mm(attn_input, qkv_ref[:, D : 2 * D]).astype(BF)
    v_ref[...] = mm(attn_input, qkv_ref[:, 2 * D :]).astype(BF)
    c_ref[...] = (mm(cross_input, cq_ref[...]) * Q_SCALE).astype(BF)


def kernel_cross(links_ref, land_ref, q_ref, kv_ref, out_ref, va_ref, bad_ref):
    component = lax.axis_index("comp")
    own_land = land_ref[lax.axis_index("tile"), lax.axis_index("face")]
    floor = jnp.where(component == 1, 0, own_land)

    def prepare(j, carry):
        row = pl.multiple_of(j * CELLS, CELLS)
        augment(kv_ref[pl.ds(row, CELLS), D:], j >= floor, va_ref, row, CELLS)
        return carry

    lax.fori_loop(0, NB, prepare, 0)
    bad_ref[...] = jnp.zeros_like(bad_ref)

    def band(exact):
        def body(i, carry):
            row = pl.multiple_of(i * CELLS, CELLS)
            picks = [links_ref[component, i, 0, k] for k in range(KC)]
            rows = [pl.multiple_of(j * CELLS, CELLS) for j in picks]
            mask = None
            if exact:
                mask = jnp.concatenate(
                    [jnp.full((1, CELLS), (j >= floor).astype(F32)) for j in picks], axis=1
                )
            for p in range(PAIRS):
                pair = q_ref[pl.ds(row, CELLS), pl.ds(p * LANES, LANES)]
                keys = jnp.concatenate(
                    [kv_ref[pl.ds(r, CELLS), pl.ds(p * LANES, LANES)] for r in rows], axis=0
                )
                even, odd = [
                    jnp.concatenate(
                        [va_ref[pl.ds(r, CELLS), pl.ds((2 * p + h) * LANES, LANES)] for r in rows],
                        axis=0,
                    )
                    for h in range(2)
                ]
                result, sums = attend_pair(pair, keys, even, odd, mask)
                out_ref[pl.ds(row, CELLS), pl.ds(p * LANES, LANES)] = result
                if not exact:
                    bad_ref[...] += jnp.where(sums < LIMIT, 0.0, 1.0)
            return carry

        return body

    lax.fori_loop(0, NB, band(False), 0)

    @pl.when(jnp.sum(bad_ref[...]) > 0.0)
    def _():
        lax.fori_loop(0, NB, band(True), 0)


def kernel_window(
    land_ref,
    x_ref,
    north_ref,
    south_ref,
    west_ref,
    east_ref,
    gain_ref,
    qkv_ref,
    q_ref,
    k_ref,
    v_ref,
    cross_ref,
    out_w_ref,
    cross_w_ref,
    up_ref,
    down_ref,
    out_ref,
    keys_ref,
    va_ref,
    win_ref,
    bad_ref,
):
    is_air = lax.axis_index("comp") == 0
    tile_row = lax.axis_index("tile")
    tile_col = lax.axis_index("face")
    columns = (tile_col, (tile_col + 7) % 8, (tile_col + 1) % 8)

    def flags(r):
        inside_row = jnp.where(r == 0, tile_row - 1, jnp.where(r == NB + 1, tile_row + 1, tile_row))
        lat_ok = (inside_row >= 0) & (inside_row < 8)
        safe_row = jnp.clip(inside_row, 0, 7)
        index = jnp.where(r == 0, NB - 1, jnp.where(r == NB + 1, 0, r - 1))
        return [lat_ok & (is_air | (index >= land_ref[safe_row, c])) for c in columns]

    def project(rows_x, r, offset, parts):
        normed = norm_round(rows_x.astype(F32), gain_ref[0:1, :])
        start = pl.multiple_of(r * GROUP, GROUP) + offset
        keys_ref[pl.ds(start, rows_x.shape[0]), :] = mm(normed, qkv_ref[:, D : 2 * D]).astype(BF)
        values = mm(normed, qkv_ref[:, 2 * D :]).astype(BF)
        at = 0
        for rows, flag in parts:
            augment(values[at : at + rows], flag, va_ref, start + at, rows)
            at += rows

    def sides(r, carry):
        _, west_ok, east_ok = flags(r)
        at = pl.multiple_of(r * SIDE, SIDE)
        rows_x = jnp.concatenate([west_ref[pl.ds(at, SIDE), :], east_ref[pl.ds(at, SIDE), :]], axis=0)
        project(rows_x, r, CELLS, ((SIDE, west_ok), (SIDE, east_ok)))
        return carry

    lax.fori_loop(0, NB + 2, sides, 0)
    project(north_ref[...], 0, 0, ((CELLS, flags(0)[0]),))
    project(south_ref[...], NB + 1, 0, ((CELLS, flags(NB + 1)[0]),))

    def own(i, carry):
        row = pl.multiple_of(i * CELLS, CELLS)
        start = pl.multiple_of((i + 1) * GROUP, GROUP)
        keys_ref[pl.ds(start, CELLS), :] = k_ref[pl.ds(row, CELLS), :]
        augment(v_ref[pl.ds(row, CELLS), :], flags(i + 1)[0], va_ref, start, CELLS)
        return carry

    lax.fori_loop(0, NB, own, 0)
    bad_ref[...] = jnp.zeros_like(bad_ref)

    def band(exact):
        def body(i, carry):
            row = pl.multiple_of(i * CELLS, CELLS)
            start = pl.multiple_of(i * GROUP, GROUP)
            mask = None
            if exact:
                pieces = []
                for b in range(3):
                    for rows, flag in zip((CELLS, SIDE, SIDE), flags(i + b)):
                        pieces.append(jnp.full((1, rows), flag.astype(F32)))
                mask = jnp.concatenate(pieces, axis=1)
            for p in range(PAIRS):
                pair = q_ref[pl.ds(row, CELLS), pl.ds(p * LANES, LANES)]
                keys = keys_ref[pl.ds(start, WINDOW), pl.ds(p * LANES, LANES)]
                even = va_ref[pl.ds(start, WINDOW), pl.ds(2 * p * LANES, LANES)]
                odd = va_ref[pl.ds(start, WINDOW), pl.ds((2 * p + 1) * LANES, LANES)]
                result, sums = attend_pair(pair, keys, even, odd, mask)
                win_ref[pl.ds(row, CELLS), pl.ds(p * LANES, LANES)] = result
                if not exact:
                    bad_ref[...] += jnp.where(sums < LIMIT, 0.0, 1.0)
            return carry

        return body

    lax.fori_loop(0, NB, band(False), 0)

    @pl.when(jnp.sum(bad_ref[...]) > 0.0)
    def _():
        lax.fori_loop(0, NB, band(True), 0)

    chunk = 256
    own_land = land_ref[tile_row, tile_col]

    def feed(c, carry):
        row = pl.multiple_of(c * chunk, chunk)
        at = pl.ds(row, chunk)
        index = (row + lax.broadcasted_iota(jnp.int32, (chunk, 1), 0)) // CELLS
        live = jnp.where(is_air | (index >= own_land), 1.0, 0.0)
        update = mm(win_ref[at, :], out_w_ref[...]) + mm(cross_ref[at, :], cross_w_ref[...])
        middle = x_ref[at, :].astype(F32) + live * update
        mlp_input = norm_round(middle, gain_ref[2:3, :])
        half = 0.5 * mm(mlp_input, up_ref[...])
        hidden = (half + half * jnp.tanh(half)).astype(BF)
        out_ref[at, :] = (middle + live * mm(hidden, down_ref[...])).astype(BF)
        return carry

    lax.fori_loop(0, ROWS // chunk, feed, 0)


VMEM = pl.BlockSpec(memory_space=pltpu.VMEM)
SMEM = pl.BlockSpec(memory_space=pltpu.SMEM)


def array(*shape, dtype=BF):
    return jax.ShapeDtypeStruct(shape, dtype)


def cost(macs, size, exps=0):
    return pl.CostEstimate(flops=2 * macs, bytes_accessed=size, transcendentals=exps)


def per_device(
    tokens,
    norm_gains,
    qkv_weight,
    out_weight,
    cross_query,
    cross_kv,
    cross_out,
    up_weight,
    down_weight,
    intersection_list,
    land_bands,
):
    grid_x = tokens[0]
    x = grid_x.reshape(ROWS, D)
    gains = norm_gains[0]
    up_ring = [(i, i + 1) for i in range(7)]
    down_ring = [(i + 1, i) for i in range(7)]
    east_ring = [(i, (i + 1) % 8) for i in range(8)]
    west_ring = [((i + 1) % 8, i) for i in range(8)]

    north = lax.ppermute(grid_x[-BR:], "tile", up_ring)
    south = lax.ppermute(grid_x[:BR], "tile", down_ring)

    half = ROWS // 2
    pair_out = pl.pallas_call(
        kernel_cross_kv,
        grid=(2,),
        in_specs=[
            pl.BlockSpec((half, D), lambda i: (i, 0)),
            pl.BlockSpec((3, D), lambda i: (0, 0)),
            pl.BlockSpec((D, 2 * D), lambda i: (0, 0)),
        ],
        out_specs=pl.BlockSpec((half, 2 * D), lambda i: (i, 0)),
        out_shape=array(ROWS, 2 * D),
        cost_estimate=cost(ROWS * D * 2 * D, 4 * MIB),
        compiler_params=pltpu.CompilerParams(vmem_limit_bytes=24 * MIB),
        name="cross_kv",
    )(x, gains, cross_kv[0])
    partner = lax.ppermute(pair_out, "comp", [(0, 1), (1, 0)])

    tall = jnp.concatenate([north, grid_x, south], axis=0)
    west = lax.ppermute(tall[:, RX - BR :], "face", east_ring).reshape((NB + 2) * SIDE, D)
    east = lax.ppermute(tall[:, :BR], "face", west_ring).reshape((NB + 2) * SIDE, D)

    block = pl.BlockSpec((half, D), lambda i: (i, 0))
    q, k, v, cross_q = pl.pallas_call(
        kernel_own,
        grid=(2,),
        in_specs=[
            block,
            pl.BlockSpec((3, D), lambda i: (0, 0)),
            pl.BlockSpec((D, 3 * D), lambda i: (0, 0)),
            pl.BlockSpec((D, D), lambda i: (0, 0)),
        ],
        out_specs=[block] * 4,
        out_shape=[array(ROWS, D)] * 4,
        cost_estimate=cost(ROWS * D * 4 * D, 7 * MIB),
        compiler_params=pltpu.CompilerParams(vmem_limit_bytes=24 * MIB),
        name="own",
    )(x, gains, qkv_weight[0], cross_query[0])

    cross = pl.pallas_call(
        kernel_cross,
        in_specs=[SMEM, SMEM, VMEM, VMEM],
        out_specs=VMEM,
        out_shape=array(ROWS, D),
        scratch_shapes=[pltpu.VMEM((ROWS, HEADS * LANES), BF), pltpu.VMEM((CELLS, LANES), F32)],
        cost_estimate=cost(8 * ROWS * 512 * D, 4 * MIB, ROWS * HEADS * 512),
        compiler_params=pltpu.CompilerParams(vmem_limit_bytes=24 * MIB),
        name="cross",
    )(intersection_list, land_bands, cross_q, partner)

    padded_rows = (NB + 2) * GROUP
    result = pl.pallas_call(
        kernel_window,
        in_specs=[SMEM] + [VMEM] * 15,
        out_specs=VMEM,
        out_shape=array(ROWS, D),
        scratch_shapes=[
            pltpu.VMEM((padded_rows, D), BF),
            pltpu.VMEM((padded_rows, HEADS * LANES), BF),
            pltpu.VMEM((ROWS, D), BF),
            pltpu.VMEM((CELLS, LANES), F32),
        ],
        cost_estimate=cost(6 << 30, 12 * MIB, ROWS * HEADS * WINDOW),
        compiler_params=pltpu.CompilerParams(vmem_limit_bytes=40 * MIB),
        name="window",
    )(
        land_bands,
        x,
        north.reshape(CELLS, D),
        south.reshape(CELLS, D),
        west,
        east,
        gains,
        qkv_weight[0],
        q,
        k,
        v,
        cross,
        out_weight[0],
        cross_out[0],
        up_weight[0],
        down_weight[0],
    )
    return result.reshape(1, NB * BR, RX, D)


def solution(mesh):
    placed = (
        P("comp", "tile", "face", None),
        P("comp", None, None),
        P("comp", None, None),
        P("comp", None, None),
        P("comp", None, None),
        P("comp", None, None),
        P("comp", None, None),
        P("comp", None, None),
        P("comp", None, None),
        P(None, "tile", "face", None),
        P(),
    )
    return jax.shard_map(
        per_device,
        mesh=mesh,
        in_specs=placed,
        out_specs=P("comp", "tile", "face", None),
        check_vma=False,
    )
```

time: 208 us -> 70.3 us (0.34)
  the two profiles are of different devices: /device:TPU:30 before, /device:TPU:6 now
where the time goes in v1:
time: 70.3 us; the launch traced here: 69.9 us
  Pallas kernels  41.6 us (59%)
  starting transfers between devices  11.8 us (17%)
  waiting for transfers between devices  9.2 us (13%)
  local copies, waits for them, and re-layouts  6.91 us (10%)
    pallas_call x1, Pallas kernels, per_device(): pl.pallas_call(kernel_window, in_specs=[SMEM] + [VMEM] * 15, out_specs=VM...  25.8 us
    pallas_call x1, Pallas kernels, per_device(): pl.pallas_call(kernel_cross, in_specs=[SMEM, SMEM, VMEM, VMEM], out_specs...  11.5 us
    ppermute x1, waiting for transfers between devices, per_device(): south = lax.ppermute(grid_x[:BR], 'tile', down_ring)  7.73 us
    unnamed x29, local copies, waits for them, and re-layouts  5.73 us
    ppermute x1, starting transfers between devices, per_device(): north = lax.ppermute(grid_x[-BR:], 'tile', up_ring)  5.7 us
    pallas_call x1, Pallas kernels, per_device(): pl.pallas_call(kernel_own, grid=(2,), in_specs=[block, pl.BlockSpec((3, D...  2.7 us
    ppermute x1, starting transfers between devices, per_device(): lax.ppermute(tall[:, :BR], 'face', west_ring).reshape((NB + 2) * SIDE, D)  2.56 us
    ppermute x1, starting transfers between devices, per_device(): south = lax.ppermute(grid_x[:BR], 'tile', down_ring)  1.92 us
  transfers between devices with their start and end apart: 5, of which 2 were waited for; matrix products, arithmetic and copies ran while one was open for 2% of the time, Pallas kernels for 20%

profile of v1, /device:TPU:6, one launch (start us, length us, event | category | flops | bytes accessed | tf_op | source)
XLA Modules:
  0.0 69.9 jit_solution(15929994401804975813)
XLA Ops:
  0.0 0.0 copy-start
  0.0 1.2 %copy-done = bf16[1,64,16,512]{3,2,1,0:T(8,128)(2,1)S(1)} copy-done((bf16[1,64,16,512]{3,2,1,0:T(8,128)(2,1)S(1)}, bf16[1,64,16,512]{3,2,1,0:T(8,128)(2,1)}, u32[]{:S(2)}) %copy-start) | copy-done | bytes 1048600
  1.2 0.0 copy-start.2
  1.2 1.2 %copy-done.2 = bf16[1,512,1024]{2,1,0:T(8,128)(2,1)S(1)} copy-done((bf16[1,512,1024]{2,1,0:T(8,128)(2,1)S(1)}, bf16[1,512,1024]{2,1,0:T(8,128)(2,1)}, u32[]{:S(2)}) %copy-start.2) | copy-done | bytes 1048600
  2.5 0.0 copy-start.3
  2.5 0.7 copy-done.3
  3.1 1.6 %cross_kv.1 = bf16[1024,1024]{1,0:T(8,128)(2,1)S(1)} custom-call(bf16[1024,512]{1,0:T(8,128)(2,1)S(1)} %bitcast.19, bf16[3,512]{1,0:T(4,128)(2,1)S(1)} %bitcast.26, bf16[512,1024]{1,0:T(8,128)(2,1)S(1)} %bitcast.23), custom_call_target="tpu_custom_call" | custom-call | flops 1073741824 | bytes 4194304 | tf_op jit(solution)/shard_map/cross_kv/pallas_call | solution.py:300
  4.8 0.1 collective-permute-start.4
  4.9 5.7 %collective-permute-start = (bf16[8,16,512]{2,1,0:T(8,128)(2,1)S(1)}, bf16[8,16,512]{2,1,0:T(8,128)(2,1)S(1)}, u32[]{:S(2)}, u32[]{:S(2)}) collective-permute-start(bf16[8,16,512]{2,1,0:T(8,128)(2,1)S(1)} %get-tuple-element.16), channel_id=1, source_target_pairs={{0,1},{1,2},{2,3},{3,4},{4,5},{5,6},{6,7},{8,9},{9,10},{10,11},{11... | collective-permute-start | bytes 393224 | tf_op jit(solution)/shard_map/ppermute | solution.py:296
  10.6 1.9 %collective-permute-start.1 = (bf16[8,16,512]{2,1,0:T(8,128)(2,1)S(1)}, bf16[8,16,512]{2,1,0:T(8,128)(2,1)S(1)}, u32[]{:S(2)}, u32[]{:S(2)}) collective-permute-start(bf16[8,16,512]{2,1,0:T(8,128)(2,1)S(1)} %get-tuple-element.15), channel_id=1, source_target_pairs={{1,0},{2,1},{3,2},{4,3},{5,4},{6,5},{7,6},{9,8},{10,9},{11,10},{12... | collective-permute-start | bytes 393224 | tf_op jit(solution)/shard_map/ppermute | solution.py:297
  12.5 1.5 %collective-permute-done = bf16[8,16,512]{2,1,0:T(8,128)(2,1)S(1)} collective-permute-done((bf16[8,16,512]{2,1,0:T(8,128)(2,1)S(1)}, bf16[8,16,512]{2,1,0:T(8,128)(2,1)S(1)}, u32[]{:S(2)}, u32[]{:S(2)}) %collective-permute-start) | collective-permute-done | bytes 131104 | tf_op jit(solution)/shard_map/ppermute | solution.py:296
  14.0 7.7 %collective-permute-done.1 = bf16[8,16,512]{2,1,0:T(8,128)(2,1)S(1)} collective-permute-done((bf16[8,16,512]{2,1,0:T(8,128)(2,1)S(1)}, bf16[8,16,512]{2,1,0:T(8,128)(2,1)S(1)}, u32[]{:S(2)}, u32[]{:S(2)}) %collective-permute-start.1) | collective-permute-done | bytes 131104 | tf_op jit(solution)/shard_map/ppermute | solution.py:297
  21.7 0.2 pad_maximum_fusion
  21.9 0.0 copy-start.13
  21.9 0.0 copy-start.1
  21.9 0.0 copy-start.4
  21.9 1.2 %fusion = (bf16[80,8,512]{2,1,0:T(8,128)(2,1)}, bf16[80,8,512]{2,1,0:T(8,128)(2,1)}) fusion(bf16[80,16,512]{2,1,0:T(8,128)(2,1)S(1)} %pad_maximum_fusion), kind=kLoop, calls=%fused_computation.3 | loop fusion | bytes 2621440 | tf_op jit(solution)/shard_map/slice | solution.py:318
  23.1 1.6 %collective-permute-start.2 = (bf16[80,8,512]{2,1,0:T(8,128)(2,1)}, bf16[80,8,512]{2,1,0:T(8,128)(2,1)}, u32[]{:S(2)}, u32[]{:S(2)}) collective-permute-start(bf16[80,8,512]{2,1,0:T(8,128)(2,1)} %get-tuple-element.14), channel_id=1, source_target_pairs={{0,8},{8,16},{16,24},{24,32},{32,40},{40,48},{48,56},{56,0},{1,9},... | collective-permute-start | bytes 1966088 | tf_op jit(solution)/shard_map/ppermute | solution.py:317
  24.7 2.6 %collective-permute-start.3 = (bf16[80,8,512]{2,1,0:T(8,128)(2,1)}, bf16[80,8,512]{2,1,0:T(8,128)(2,1)}, u32[]{:S(2)}, u32[]{:S(2)}) collective-permute-start(bf16[80,8,512]{2,1,0:T(8,128)(2,1)} %get-tuple-element.13), channel_id=1, source_target_pairs={{8,0},{16,8},{24,16},{32,24},{40,32},{48,40},{56,48},{0,56},{9,1},... | collective-permute-start | bytes 1966088 | tf_op jit(solution)/shard_map/ppermute | solution.py:318
  27.2 0.0 copy-done.13
  27.2 0.1 copy.12.links_ref
  27.3 0.0 copy-done.1
  27.3 0.0 copy-done.4
  27.3 0.0 copy-start.7
  27.3 1.4 %copy-done.7 = bf16[1,512,1536]{2,1,0:T(8,128)(2,1)S(1)} copy-done((bf16[1,512,1536]{2,1,0:T(8,128)(2,1)S(1)}, bf16[1,512,1536]{2,1,0:T(8,128)(2,1)}, u32[]{:S(2)}) %copy-start.7) | copy-done | bytes 1572888
  28.7 0.0 copy-start.9
  28.7 1.0 %copy-done.9 = bf16[1,512,512]{2,1,0:T(8,128)(2,1)S(1)} copy-done((bf16[1,512,512]{2,1,0:T(8,128)(2,1)S(1)}, bf16[1,512,512]{2,1,0:T(8,128)(2,1)}, u32[]{:S(2)}) %copy-start.9) | copy-done | bytes 524312
  29.8 0.0 copy-start.12
  29.8 2.7 %own.1 = (bf16[1024,512]{1,0:T(8,128)(2,1)S(1)}, bf16[1024,512]{1,0:T(8,128)(2,1)S(1)}, bf16[1024,512]{1,0:T(8,128)(2,1)S(1)}, bf16[1024,512]{1,0:T(8,128)(2,1)S(1)}) custom-call(bf16[1024,512]{1,0:T(8,128)(2,1)S(1)} %bitcast.21, bf16[3,512]{1,0:T(4,128)(2,1)S(1)} %bitcast.27, bf16[512,1536]{1,0:T(8,128)(2,1)S(1)} %bitcast.31, bf16[512,512]{1,0:T(8,128)(2,1)S(1)} %bitcast.33), custom_call_target="tpu_custom_call" | custom-call | flops 2147483648 | bytes 7340032 | tf_op jit(solution)/shard_map/own/pallas_call | solution.py:321
  32.5 0.0 collective-permute-done.4.kv_ref
  32.5 0.0 copy-done.12
  32.5 0.0 copy-start.5
  32.5 0.0 copy-start.6
  32.5 0.0 copy-start.8
  32.5 0.0 copy-start.10
  32.5 0.0 copy-start.11
  32.5 11.5 %cross.1.cross_ref = bf16[1024,512]{1,0:T(8,128)(2,1)S(1)} custom-call(s32[2,8,1,4]{3,2,1,0:T(1,128)S(1)} %copy.12.links_ref, s32[8,8]{1,0:T(8,128)S(1)} %copy-done.12, bf16[1024,512]{1,0:T(8,128)(2,1)S(1)} %get-tuple-element.12.q_ref, bf16[1024,1024]{1,0:T(8,128)(2,1)} %collective-permute-done.4.kv_ref), custom_call_target="tpu_custom_call" | custom-call | flops 4294967296 | bytes 4194304 | tf_op jit(solution)/shard_map/cross/pallas_call | solution.py:337
  44.1 0.0 collective-permute-done.2
  44.1 0.0 collective-permute-done.3
  44.1 0.0 copy-done.5
  44.1 0.0 copy-done.6
  44.1 0.0 copy-done.8
  44.1 0.0 copy-done.10
  44.1 0.0 copy-done.11
  44.1 25.8 %window.1 = bf16[1024,512]{1,0:T(8,128)(2,1)} custom-call(s32[8,8]{1,0:T(8,128)S(1)} %copy-done.12, bf16[1024,512]{1,0:T(8,128)(2,1)S(1)} %bitcast.22, bf16[128,512]{1,0:T(8,128)(2,1)S(1)} %bitcast.24, bf16[128,512]{1,0:T(8,128)(2,1)S(1)} %bitcast.25, bf16[640,512]{1,0:T(8,128)(2,1)} %bitcast.6.west_ref, bf16[640,512]{1,0:T(8,128)(2,1)} %bitcast.7.east_ref, ...), custom_call_target="tpu_custom_call" | custom-call | flops 12884901888 | bytes 12582912 | tf_op jit(solution)/shard_map/window/pallas_call | solution.py:349
  (1 shorter events, 0.0 us)
Async XLA Ops:
  0.0 1.2 %copy-start = (bf16[1,64,16,512]{3,2,1,0:T(8,128)(2,1)S(1)}, bf16[1,64,16,512]{3,2,1,0:T(8,128)(2,1)}, u32[]{:S(2)}) copy-start(bf16[1,64,16,512]{3,2,1,0:T(8,128)(2,1)} %param.11) | copy-start | bytes 3145732
  1.2 1.2 %copy-start.2 = (bf16[1,512,1024]{2,1,0:T(8,128)(2,1)S(1)}, bf16[1,512,1024]{2,1,0:T(8,128)(2,1)}, u32[]{:S(2)}) copy-start(bf16[1,512,1024]{2,1,0:T(8,128)(2,1)} %param.16) | copy-start | bytes 3145732
  2.5 0.7 copy-start.3
  4.8 27.7 %collective-permute-start.4 = (bf16[1024,1024]{1,0:T(8,128)(2,1)S(1)}, bf16[1024,1024]{1,0:T(8,128)(2,1)}, u32[]{:S(2)}, u32[]{:S(2)}) collective-permute-start(bf16[1024,1024]{1,0:T(8,128)(2,1)S(1)} %cross_kv.1), channel_id=1, source_target_pairs={{0,64},{64,0},{1,65},{65,1},{2,66},{66,2},{3,67},{67,3},{4,68},{68... | collective-permute-start | bytes 6291464 | tf_op jit(solution)/shard_map/ppermute | solution.py:314
  4.9 9.1 %collective-permute-start = (bf16[8,16,512]{2,1,0:T(8,128)(2,1)S(1)}, bf16[8,16,512]{2,1,0:T(8,128)(2,1)S(1)}, u32[]{:S(2)}, u32[]{:S(2)}) collective-permute-start(bf16[8,16,512]{2,1,0:T(8,128)(2,1)S(1)} %get-tuple-element.16), channel_id=1, source_target_pairs={{0,1},{1,2},{2,3},{3,4},{4,5},{5,6},{6,7},{8,9},{9,10},{10,11},{11... | collective-permute-start | bytes 393224 | tf_op jit(solution)/shard_map/ppermute | solution.py:296
  10.6 11.1 %collective-permute-start.1 = (bf16[8,16,512]{2,1,0:T(8,128)(2,1)S(1)}, bf16[8,16,512]{2,1,0:T(8,128)(2,1)S(1)}, u32[]{:S(2)}, u32[]{:S(2)}) collective-permute-start(bf16[8,16,512]{2,1,0:T(8,128)(2,1)S(1)} %get-tuple-element.15), channel_id=1, source_target_pairs={{1,0},{2,1},{3,2},{4,3},{5,4},{6,5},{7,6},{9,8},{10,9},{11,10},{12... | collective-permute-start | bytes 393224 | tf_op jit(solution)/shard_map/ppermute | solution.py:297
  21.9 5.3 %copy-start.13 = (s32[2,8,1,4]{1,3,2,0:T(4,128)S(1)}, s32[2,8,1,4]{1,3,2,0:T(4,128)}, u32[]{:S(2)}) copy-start(s32[2,8,1,4]{1,3,2,0:T(4,128)} %param.20) | copy-start | bytes 772
  21.9 5.4 %copy-start.1 = (bf16[1,64,16,512]{3,2,1,0:T(8,128)(2,1)S(1)}, bf16[1,64,16,512]{3,2,1,0:T(8,128)(2,1)}, u32[]{:S(2)}) copy-start(bf16[1,64,16,512]{3,2,1,0:T(8,128)(2,1)} %param.11) | copy-start | bytes 3145732
  21.9 5.4 %copy-start.4 = (bf16[1,3,512]{2,1,0:T(4,128)(2,1)S(1)}, bf16[1,3,512]{2,1,0:T(4,128)(2,1)}, u32[]{:S(2)}) copy-start(bf16[1,3,512]{2,1,0:T(4,128)(2,1)} %param.12) | copy-start | bytes 9220
  23.1 21.0 %collective-permute-start.2 = (bf16[80,8,512]{2,1,0:T(8,128)(2,1)}, bf16[80,8,512]{2,1,0:T(8,128)(2,1)}, u32[]{:S(2)}, u32[]{:S(2)}) collective-permute-start(bf16[80,8,512]{2,1,0:T(8,128)(2,1)} %get-tuple-element.14), channel_id=1, source_target_pairs={{0,8},{8,16},{16,24},{24,32},{32,40},{40,48},{48,56},{56,0},{1,9},... | collective-permute-start | bytes 1966088 | tf_op jit(solution)/shard_map/ppermute | solution.py:317
  24.7 19.4 %collective-permute-start.3 = (bf16[80,8,512]{2,1,0:T(8,128)(2,1)}, bf16[80,8,512]{2,1,0:T(8,128)(2,1)}, u32[]{:S(2)}, u32[]{:S(2)}) collective-permute-start(bf16[80,8,512]{2,1,0:T(8,128)(2,1)} %get-tuple-element.13), channel_id=1, source_target_pairs={{8,0},{16,8},{24,16},{32,24},{40,32},{48,40},{56,48},{0,56},{9,1},... | collective-permute-start | bytes 1966088 | tf_op jit(solution)/shard_map/ppermute | solution.py:318
  27.3 1.4 %copy-start.7 = (bf16[1,512,1536]{2,1,0:T(8,128)(2,1)S(1)}, bf16[1,512,1536]{2,1,0:T(8,128)(2,1)}, u32[]{:S(2)}) copy-start(bf16[1,512,1536]{2,1,0:T(8,128)(2,1)} %param.13) | copy-start | bytes 4718596
  28.7 1.0 %copy-start.9 = (bf16[1,512,512]{2,1,0:T(8,128)(2,1)S(1)}, bf16[1,512,512]{2,1,0:T(8,128)(2,1)}, u32[]{:S(2)}) copy-start(bf16[1,512,512]{2,1,0:T(8,128)(2,1)} %param.15) | copy-start | bytes 1572868
  29.8 2.7 %copy-start.12 = (s32[8,8]{1,0:T(8,128)S(1)}, s32[8,8]{1,0:T(8,128)}, u32[]{:S(2)}) copy-start(s32[8,8]{1,0:T(8,128)} %land_ref.3) | copy-start | bytes 772
  32.5 11.6 %copy-start.5 = (bf16[1,512,2048]{2,1,0:T(8,128)(2,1)S(1)}, bf16[1,512,2048]{2,1,0:T(8,128)(2,1)}, u32[]{:S(2)}) copy-start(bf16[1,512,2048]{2,1,0:T(8,128)(2,1)} %param.18) | copy-start | bytes 6291460
  32.5 11.6 %copy-start.6 = (bf16[1,2048,512]{2,1,0:T(8,128)(2,1)S(1)}, bf16[1,2048,512]{2,1,0:T(8,128)(2,1)}, u32[]{:S(2)}) copy-start(bf16[1,2048,512]{2,1,0:T(8,128)(2,1)} %param.19) | copy-start | bytes 6291460
  32.5 11.6 %copy-start.8 = (bf16[1,512,1536]{2,1,0:T(8,128)(2,1)S(1)}, bf16[1,512,1536]{2,1,0:T(8,128)(2,1)}, u32[]{:S(2)}) copy-start(bf16[1,512,1536]{2,1,0:T(8,128)(2,1)} %param.13) | copy-start | bytes 4718596
  32.5 11.6 %copy-start.10 = (bf16[1,512,512]{2,1,0:T(8,128)(2,1)S(1)}, bf16[1,512,512]{2,1,0:T(8,128)(2,1)}, u32[]{:S(2)}) copy-start(bf16[1,512,512]{2,1,0:T(8,128)(2,1)} %param.14) | copy-start | bytes 1572868
  32.5 11.6 %copy-start.11 = (bf16[1,512,512]{2,1,0:T(8,128)(2,1)S(1)}, bf16[1,512,512]{2,1,0:T(8,128)(2,1)}, u32[]{:S(2)}) copy-start(bf16[1,512,512]{2,1,0:T(8,128)(2,1)} %param.17) | copy-start | bytes 1572868

commit v2 on v1

--- a/solution.py
+++ b/solution.py
@@ -293,8 +293,9 @@
     east_ring = [(i, (i + 1) % 8) for i in range(8)]
     west_ring = [((i + 1) % 8, i) for i in range(8)]
 
-    north = lax.ppermute(grid_x[-BR:], "tile", up_ring)
-    south = lax.ppermute(grid_x[:BR], "tile", down_ring)
+    top, bottom, x = lax.optimization_barrier((grid_x[:BR], grid_x[-BR:], x))
+    north = lax.ppermute(bottom, "tile", up_ring)
+    south = lax.ppermute(top, "tile", down_ring)
 
     half = ROWS // 2
     pair_out = pl.pallas_call(
@@ -311,11 +312,13 @@
         compiler_params=pltpu.CompilerParams(vmem_limit_bytes=24 * MIB),
         name="cross_kv",
     )(x, gains, cross_kv[0])
+    tall = jnp.concatenate([north, grid_x, south], axis=0)
+    west_edge, east_edge, pair_out = lax.optimization_barrier(
+        (tall[:, :BR], tall[:, RX - BR :], pair_out)
+    )
+    west = lax.ppermute(east_edge, "face", east_ring).reshape((NB + 2) * SIDE, D)
+    east = lax.ppermute(west_edge, "face", west_ring).reshape((NB + 2) * SIDE, D)
     partner = lax.ppermute(pair_out, "comp", [(0, 1), (1, 0)])
-
-    tall = jnp.concatenate([north, grid_x, south], axis=0)
-    west = lax.ppermute(tall[:, RX - BR :], "face", east_ring).reshape((NB + 2) * SIDE, D)
-    east = lax.ppermute(tall[:, :BR], "face", west_ring).reshape((NB + 2) * SIDE, D)
 
     block = pl.BlockSpec((half, D), lambda i: (i, 0))
     q, k, v, cross_q = pl.pallas_call(

time: 70.3 us -> 65.9 us (0.937)
  the two profiles are of different devices: /device:TPU:6 before, /device:TPU:7 now
where the time goes in v2:
time: 65.9 us; the launch traced here: 65.6 us
  Pallas kernels  41.7 us (63%)
  starting transfers between devices  13 us (20%)
  local copies, waits for them, and re-layouts  7.87 us (12%)
  waiting for transfers between devices  2.64 us (4%)
    pallas_call x1, Pallas kernels, per_device(): pl.pallas_call(kernel_window, in_specs=[SMEM] + [VMEM] * 15, out_specs=VM...  25.8 us
    pallas_call x1, Pallas kernels, per_device(): pl.pallas_call(kernel_cross, in_specs=[SMEM, SMEM, VMEM, VMEM], out_specs...  11.6 us
    unnamed x29, local copies, waits for them, and re-layouts  5.72 us
    ppermute x1, starting transfers between devices, per_device(): north = lax.ppermute(bottom, 'tile', up_ring)  5.42 us
    pallas_call x1, Pallas kernels, per_device(): pl.pallas_call(kernel_own, grid=(2,), in_specs=[block, pl.BlockSpec((3, D...  2.7 us
    ppermute x1, waiting for transfers between devices, per_device(): south = lax.ppermute(top, 'tile', down_ring)  2.63 us
    ppermute x1, starting transfers between devices, per_device(): lax.ppermute(west_edge, 'face', west_ring).reshape((NB + 2) * SIDE, D)  2.28 us
    ppermute x1, starting transfers between devices, per_device(): partner = lax.ppermute(pair_out, 'comp', [(0, 1), (1, 0)])  2.1 us
  transfers between devices with their start and end apart: 5, of which 1 were waited for; matrix products, arithmetic and copies ran while one was open for 0% of the time, Pallas kernels for 24%

profile of v2, /device:TPU:7, one launch (start us, length us, event | category | flops | bytes accessed | tf_op | source)
XLA Modules:
  0.0 65.6 jit_solution(14471908590970952742)
XLA Ops:
  0.0 1.0 %slice_bitcast_fusion = (bf16[8,16,512]{2,1,0:T(8,128)(2,1)S(1)}, bf16[8,16,512]{2,1,0:T(8,128)(2,1)S(1)}) fusion(bf16[1,64,16,512]{3,2,1,0:T(8,128)(2,1)} %param.11), kind=kLoop, calls=%fused_computation.1 | loop fusion | bytes 524288 | tf_op jit(solution)/shard_map/slice | solution.py:296
  1.0 5.4 %collective-permute-start = (bf16[8,16,512]{2,1,0:T(8,128)(2,1)S(1)}, bf16[8,16,512]{2,1,0:T(8,128)(2,1)S(1)}, u32[]{:S(2)}, u32[]{:S(2)}) collective-permute-start(bf16[8,16,512]{2,1,0:T(8,128)(2,1)S(1)} %get-tuple-element.16), channel_id=1, source_target_pairs={{0,1},{1,2},{2,3},{3,4},{4,5},{5,6},{6,7},{8,9},{9,10},{10,11},{11... | collective-permute-start | bytes 393224 | tf_op jit(solution)/shard_map/ppermute | solution.py:297
  6.4 1.9 %collective-permute-start.1 = (bf16[8,16,512]{2,1,0:T(8,128)(2,1)S(1)}, bf16[8,16,512]{2,1,0:T(8,128)(2,1)S(1)}, u32[]{:S(2)}, u32[]{:S(2)}) collective-permute-start(bf16[8,16,512]{2,1,0:T(8,128)(2,1)S(1)} %get-tuple-element.17), channel_id=1, source_target_pairs={{1,0},{2,1},{3,2},{4,3},{5,4},{6,5},{7,6},{9,8},{10,9},{11,10},{12... | collective-permute-start | bytes 393224 | tf_op jit(solution)/shard_map/ppermute | solution.py:298
  8.3 0.0 copy-start
  8.4 1.2 %copy-done = bf16[1,64,16,512]{3,2,1,0:T(8,128)(2,1)S(1)} copy-done((bf16[1,64,16,512]{3,2,1,0:T(8,128)(2,1)S(1)}, bf16[1,64,16,512]{3,2,1,0:T(8,128)(2,1)}, u32[]{:S(2)}) %copy-start) | copy-done | bytes 1048600
  9.6 0.0 copy-start.2
  9.6 1.2 %copy-done.2 = bf16[1,512,1024]{2,1,0:T(8,128)(2,1)S(1)} copy-done((bf16[1,512,1024]{2,1,0:T(8,128)(2,1)S(1)}, bf16[1,512,1024]{2,1,0:T(8,128)(2,1)}, u32[]{:S(2)}) %copy-start.2) | copy-done | bytes 1048600
  10.8 0.0 copy-start.3
  10.8 0.7 %copy-done.3 = bf16[1,3,512]{2,1,0:T(4,128)(2,1)S(1)} copy-done((bf16[1,3,512]{2,1,0:T(4,128)(2,1)S(1)}, bf16[1,3,512]{2,1,0:T(4,128)(2,1)}, u32[]{:S(2)}) %copy-start.3) | copy-done | bytes 3096
  11.5 1.6 %cross_kv.1 = bf16[1024,1024]{1,0:T(8,128)(2,1)S(1)} custom-call(bf16[1024,512]{1,0:T(8,128)(2,1)S(1)} %bitcast.19, bf16[3,512]{1,0:T(4,128)(2,1)S(1)} %bitcast.26, bf16[512,1024]{1,0:T(8,128)(2,1)S(1)} %bitcast.23), custom_call_target="tpu_custom_call" | custom-call | flops 1073741824 | bytes 4194304 | tf_op jit(solution)/shard_map/cross_kv/pallas_call | solution.py:301
  13.1 0.0 collective-permute-done
  13.1 2.6 %collective-permute-done.1 = bf16[8,16,512]{2,1,0:T(8,128)(2,1)S(1)} collective-permute-done((bf16[8,16,512]{2,1,0:T(8,128)(2,1)S(1)}, bf16[8,16,512]{2,1,0:T(8,128)(2,1)S(1)}, u32[]{:S(2)}, u32[]{:S(2)}) %collective-permute-start.1) | collective-permute-done | bytes 131104 | tf_op jit(solution)/shard_map/ppermute | solution.py:298
  15.7 0.2 pad_maximum_fusion
  15.9 0.0 copy-start.13
  15.9 0.0 copy-start.1
  15.9 0.0 copy-start.4
  15.9 1.2 %fusion = (bf16[80,8,512]{2,1,0:T(8,128)(2,1)}, bf16[80,8,512]{2,1,0:T(8,128)(2,1)}) fusion(bf16[80,16,512]{2,1,0:T(8,128)(2,1)S(1)} %pad_maximum_fusion), kind=kLoop, calls=%fused_computation.3 | loop fusion | bytes 2621440 | tf_op jit(solution)/shard_map/slice | solution.py:317
  17.1 2.1 %collective-permute-start.4 = (bf16[1024,1024]{1,0:T(8,128)(2,1)S(1)}, bf16[1024,1024]{1,0:T(8,128)(2,1)}, u32[]{:S(2)}, u32[]{:S(2)}) collective-permute-start(bf16[1024,1024]{1,0:T(8,128)(2,1)S(1)} %cross_kv.1), channel_id=1, source_target_pairs={{0,64},{64,0},{1,65},{65,1},{2,66},{66,2},{3,67},{67,3},{4,68},{68... | collective-permute-start | bytes 6291464 | tf_op jit(solution)/shard_map/ppermute | solution.py:321
  19.2 1.3 %collective-permute-start.2 = (bf16[80,8,512]{2,1,0:T(8,128)(2,1)}, bf16[80,8,512]{2,1,0:T(8,128)(2,1)}, u32[]{:S(2)}, u32[]{:S(2)}) collective-permute-start(bf16[80,8,512]{2,1,0:T(8,128)(2,1)} %get-tuple-element.18), channel_id=1, source_target_pairs={{0,8},{8,16},{16,24},{24,32},{32,40},{40,48},{48,56},{56,0},{1,9},... | collective-permute-start | bytes 1966088 | tf_op jit(solution)/shard_map/ppermute | solution.py:319
  20.5 2.3 %collective-permute-start.3 = (bf16[80,8,512]{2,1,0:T(8,128)(2,1)}, bf16[80,8,512]{2,1,0:T(8,128)(2,1)}, u32[]{:S(2)}, u32[]{:S(2)}) collective-permute-start(bf16[80,8,512]{2,1,0:T(8,128)(2,1)} %get-tuple-element.19), channel_id=1, source_target_pairs={{8,0},{16,8},{24,16},{32,24},{40,32},{48,40},{56,48},{0,56},{9,1},... | collective-permute-start | bytes 1966088 | tf_op jit(solution)/shard_map/ppermute | solution.py:320
  22.8 0.0 copy-done.13
  22.8 0.1 copy.12.links_ref
  22.9 0.0 copy-done.1
  22.9 0.0 copy-done.4
  22.9 0.0 copy-start.7
  22.9 1.4 %copy-done.7 = bf16[1,512,1536]{2,1,0:T(8,128)(2,1)S(1)} copy-done((bf16[1,512,1536]{2,1,0:T(8,128)(2,1)S(1)}, bf16[1,512,1536]{2,1,0:T(8,128)(2,1)}, u32[]{:S(2)}) %copy-start.7) | copy-done | bytes 1572888
  24.3 0.0 copy-start.9
  24.3 1.0 %copy-done.9 = bf16[1,512,512]{2,1,0:T(8,128)(2,1)S(1)} copy-done((bf16[1,512,512]{2,1,0:T(8,128)(2,1)S(1)}, bf16[1,512,512]{2,1,0:T(8,128)(2,1)}, u32[]{:S(2)}) %copy-start.9) | copy-done | bytes 524312
  25.3 0.0 copy-start.12
  25.3 2.7 %own.1 = (bf16[1024,512]{1,0:T(8,128)(2,1)S(1)}, bf16[1024,512]{1,0:T(8,128)(2,1)S(1)}, bf16[1024,512]{1,0:T(8,128)(2,1)S(1)}, bf16[1024,512]{1,0:T(8,128)(2,1)S(1)}) custom-call(bf16[1024,512]{1,0:T(8,128)(2,1)S(1)} %bitcast.21, bf16[3,512]{1,0:T(4,128)(2,1)S(1)} %bitcast.27, bf16[512,1536]{1,0:T(8,128)(2,1)S(1)} %bitcast.31, bf16[512,512]{1,0:T(8,128)(2,1)S(1)} %bitcast.33), custom_call_target="tpu_custom_call" | custom-call | flops 2147483648 | bytes 7340032 | tf_op jit(solution)/shard_map/own/pallas_call | solution.py:324
  28.0 0.0 collective-permute-done.4.kv_ref
  28.1 0.0 copy-done.12
  28.1 0.0 copy-start.5
  28.1 0.0 copy-start.6
  28.1 0.0 copy-start.8
  28.1 0.0 copy-start.10
  28.1 0.0 copy-start.11
  28.1 11.6 %cross.1.cross_ref = bf16[1024,512]{1,0:T(8,128)(2,1)S(1)} custom-call(s32[2,8,1,4]{3,2,1,0:T(1,128)S(1)} %copy.12.links_ref, s32[8,8]{1,0:T(8,128)S(1)} %copy-done.12, bf16[1024,512]{1,0:T(8,128)(2,1)S(1)} %get-tuple-element.23.q_ref, bf16[1024,1024]{1,0:T(8,128)(2,1)} %collective-permute-done.4.kv_ref), custom_call_target="tpu_custom_call" | custom-call | flops 4294967296 | bytes 4194304 | tf_op jit(solution)/shard_map/cross/pallas_call | solution.py:340
  39.7 0.0 collective-permute-done.2
  39.7 0.0 collective-permute-done.3
  39.7 0.0 copy-done.5
  39.7 0.0 copy-done.6
  39.7 0.0 copy-done.8
  39.7 0.0 copy-done.10
  39.8 0.0 copy-done.11
  39.8 25.8 %window.1 = bf16[1024,512]{1,0:T(8,128)(2,1)} custom-call(s32[8,8]{1,0:T(8,128)S(1)} %copy-done.12, bf16[1024,512]{1,0:T(8,128)(2,1)S(1)} %bitcast.22, bf16[128,512]{1,0:T(8,128)(2,1)S(1)} %bitcast.24, bf16[128,512]{1,0:T(8,128)(2,1)S(1)} %bitcast.25, bf16[640,512]{1,0:T(8,128)(2,1)} %bitcast.8.west_ref, bf16[640,512]{1,0:T(8,128)(2,1)} %bitcast.9.east_ref, ...), custom_call_target="tpu_custom_call" | custom-call | flops 12884901888 | bytes 12582912 | tf_op jit(solution)/shard_map/window/pallas_call | solution.py:352
Async XLA Ops:
  1.0 12.1 %collective-permute-start = (bf16[8,16,512]{2,1,0:T(8,128)(2,1)S(1)}, bf16[8,16,512]{2,1,0:T(8,128)(2,1)S(1)}, u32[]{:S(2)}, u32[]{:S(2)}) collective-permute-start(bf16[8,16,512]{2,1,0:T(8,128)(2,1)S(1)} %get-tuple-element.16), channel_id=1, source_target_pairs={{0,1},{1,2},{2,3},{3,4},{4,5},{5,6},{6,7},{8,9},{9,10},{10,11},{11... | collective-permute-start | bytes 393224 | tf_op jit(solution)/shard_map/ppermute | solution.py:297
  6.4 9.3 %collective-permute-start.1 = (bf16[8,16,512]{2,1,0:T(8,128)(2,1)S(1)}, bf16[8,16,512]{2,1,0:T(8,128)(2,1)S(1)}, u32[]{:S(2)}, u32[]{:S(2)}) collective-permute-start(bf16[8,16,512]{2,1,0:T(8,128)(2,1)S(1)} %get-tuple-element.17), channel_id=1, source_target_pairs={{1,0},{2,1},{3,2},{4,3},{5,4},{6,5},{7,6},{9,8},{10,9},{11,10},{12... | collective-permute-start | bytes 393224 | tf_op jit(solution)/shard_map/ppermute | solution.py:298
  8.3 1.2 %copy-start = (bf16[1,64,16,512]{3,2,1,0:T(8,128)(2,1)S(1)}, bf16[1,64,16,512]{3,2,1,0:T(8,128)(2,1)}, u32[]{:S(2)}) copy-start(bf16[1,64,16,512]{3,2,1,0:T(8,128)(2,1)} %param.11) | copy-start | bytes 3145732
  9.6 1.2 %copy-start.2 = (bf16[1,512,1024]{2,1,0:T(8,128)(2,1)S(1)}, bf16[1,512,1024]{2,1,0:T(8,128)(2,1)}, u32[]{:S(2)}) copy-start(bf16[1,512,1024]{2,1,0:T(8,128)(2,1)} %param.16) | copy-start | bytes 3145732
  10.8 0.7 %copy-start.3 = (bf16[1,3,512]{2,1,0:T(4,128)(2,1)S(1)}, bf16[1,3,512]{2,1,0:T(4,128)(2,1)}, u32[]{:S(2)}) copy-start(bf16[1,3,512]{2,1,0:T(4,128)(2,1)} %param.12) | copy-start | bytes 9220
  15.9 6.9 %copy-start.13 = (s32[2,8,1,4]{1,3,2,0:T(4,128)S(1)}, s32[2,8,1,4]{1,3,2,0:T(4,128)}, u32[]{:S(2)}) copy-start(s32[2,8,1,4]{1,3,2,0:T(4,128)} %param.20) | copy-start | bytes 772
  15.9 7.0 %copy-start.1 = (bf16[1,64,16,512]{3,2,1,0:T(8,128)(2,1)S(1)}, bf16[1,64,16,512]{3,2,1,0:T(8,128)(2,1)}, u32[]{:S(2)}) copy-start(bf16[1,64,16,512]{3,2,1,0:T(8,128)(2,1)} %param.11) | copy-start | bytes 3145732
  15.9 7.0 %copy-start.4 = (bf16[1,3,512]{2,1,0:T(4,128)(2,1)S(1)}, bf16[1,3,512]{2,1,0:T(4,128)(2,1)}, u32[]{:S(2)}) copy-start(bf16[1,3,512]{2,1,0:T(4,128)(2,1)} %param.12) | copy-start | bytes 9220
  17.1 10.9 %collective-permute-start.4 = (bf16[1024,1024]{1,0:T(8,128)(2,1)S(1)}, bf16[1024,1024]{1,0:T(8,128)(2,1)}, u32[]{:S(2)}, u32[]{:S(2)}) collective-permute-start(bf16[1024,1024]{1,0:T(8,128)(2,1)S(1)} %cross_kv.1), channel_id=1, source_target_pairs={{0,64},{64,0},{1,65},{65,1},{2,66},{66,2},{3,67},{67,3},{4,68},{68... | collective-permute-start | bytes 6291464 | tf_op jit(solution)/shard_map/ppermute | solution.py:321
  19.2 20.5 %collective-permute-start.2 = (bf16[80,8,512]{2,1,0:T(8,128)(2,1)}, bf16[80,8,512]{2,1,0:T(8,128)(2,1)}, u32[]{:S(2)}, u32[]{:S(2)}) collective-permute-start(bf16[80,8,512]{2,1,0:T(8,128)(2,1)} %get-tuple-element.18), channel_id=1, source_target_pairs={{0,8},{8,16},{16,24},{24,32},{32,40},{40,48},{48,56},{56,0},{1,9},... | collective-permute-start | bytes 1966088 | tf_op jit(solution)/shard_map/ppermute | solution.py:319
  20.5 19.2 %collective-permute-start.3 = (bf16[80,8,512]{2,1,0:T(8,128)(2,1)}, bf16[80,8,512]{2,1,0:T(8,128)(2,1)}, u32[]{:S(2)}, u32[]{:S(2)}) collective-permute-start(bf16[80,8,512]{2,1,0:T(8,128)(2,1)} %get-tuple-element.19), channel_id=1, source_target_pairs={{8,0},{16,8},{24,16},{32,24},{40,32},{48,40},{56,48},{0,56},{9,1},... | collective-permute-start | bytes 1966088 | tf_op jit(solution)/shard_map/ppermute | solution.py:320
  22.9 1.4 %copy-start.7 = (bf16[1,512,1536]{2,1,0:T(8,128)(2,1)S(1)}, bf16[1,512,1536]{2,1,0:T(8,128)(2,1)}, u32[]{:S(2)}) copy-start(bf16[1,512,1536]{2,1,0:T(8,128)(2,1)} %param.13) | copy-start | bytes 4718596
  24.3 1.0 %copy-start.9 = (bf16[1,512,512]{2,1,0:T(8,128)(2,1)S(1)}, bf16[1,512,512]{2,1,0:T(8,128)(2,1)}, u32[]{:S(2)}) copy-start(bf16[1,512,512]{2,1,0:T(8,128)(2,1)} %param.15) | copy-start | bytes 1572868
  25.3 2.7 %copy-start.12 = (s32[8,8]{1,0:T(8,128)S(1)}, s32[8,8]{1,0:T(8,128)}, u32[]{:S(2)}) copy-start(s32[8,8]{1,0:T(8,128)} %land_ref.3) | copy-start | bytes 772
  28.1 11.7 %copy-start.5 = (bf16[1,512,2048]{2,1,0:T(8,128)(2,1)S(1)}, bf16[1,512,2048]{2,1,0:T(8,128)(2,1)}, u32[]{:S(2)}) copy-start(bf16[1,512,2048]{2,1,0:T(8,128)(2,1)} %param.18) | copy-start | bytes 6291460
  28.1 11.7 %copy-start.6 = (bf16[1,2048,512]{2,1,0:T(8,128)(2,1)S(1)}, bf16[1,2048,512]{2,1,0:T(8,128)(2,1)}, u32[]{:S(2)}) copy-start(bf16[1,2048,512]{2,1,0:T(8,128)(2,1)} %param.19) | copy-start | bytes 6291460
  28.1 11.6 %copy-start.8 = (bf16[1,512,1536]{2,1,0:T(8,128)(2,1)S(1)}, bf16[1,512,1536]{2,1,0:T(8,128)(2,1)}, u32[]{:S(2)}) copy-start(bf16[1,512,1536]{2,1,0:T(8,128)(2,1)} %param.13) | copy-start | bytes 4718596
  28.1 11.6 %copy-start.10 = (bf16[1,512,512]{2,1,0:T(8,128)(2,1)S(1)}, bf16[1,512,512]{2,1,0:T(8,128)(2,1)}, u32[]{:S(2)}) copy-start(bf16[1,512,512]{2,1,0:T(8,128)(2,1)} %param.14) | copy-start | bytes 1572868
  28.1 11.6 %copy-start.11 = (bf16[1,512,512]{2,1,0:T(8,128)(2,1)S(1)}, bf16[1,512,512]{2,1,0:T(8,128)(2,1)}, u32[]{:S(2)}) copy-start(bf16[1,512,512]{2,1,0:T(8,128)(2,1)} %param.17) | copy-start | bytes 1572868

commit v3 on v2

v3 whole, which is shorter than its diff:
```python
import jax
import jax.numpy as jnp
from jax import lax
from jax.experimental import pallas as pl
from jax.experimental.pallas import tpu as pltpu
from jax.sharding import PartitionSpec as P

D = 512
FF = 2048
HEADS = 8
PAIRS = HEADS // 2
LANES = 128
RX = 16
BR = 8
NB = 8
KC = 4
CELLS = BR * RX
ROWS = NB * CELLS
SIDE = BR * BR
GROUP = CELLS + 2 * SIDE
WINDOW = 3 * GROUP
EXTRA = 16
VROWS = LANES + EXTRA

EPSILON = 1e-05
Q_SCALE = 1.4426950408889634 / 8.0
LIMIT = 2.0**100
BF = jnp.bfloat16
F32 = jnp.float32
MIB = 1 << 20


def norm_round(values, gain):
    mean_square = jnp.mean(values * values, axis=-1, keepdims=True)
    return (values * lax.rsqrt(mean_square + EPSILON) * gain.astype(F32)).astype(BF)


def mm(a, b):
    return jnp.dot(a, b, preferred_element_type=F32)


def mm_nt(a, b):
    return lax.dot_general(a, b, (((1,), (1,)), ((), ())), preferred_element_type=F32)


def mm_tn(a, b):
    return lax.dot_general(a, b, (((0,), (0,)), ((), ())), preferred_element_type=F32)


def mm_tt(a, b):
    return lax.dot_general(a, b, (((0,), (1,)), ((), ())), preferred_element_type=F32)


def augment(values_t, flag, out_ref, lane):
    keep = flag.astype(F32).astype(BF)
    for p in range(PAIRS):
        rows = values_t[p * LANES : (p + 1) * LANES]
        out_ref[pl.ds(p * VROWS, LANES), pl.ds(lane, CELLS)] = rows * keep
        out_ref[pl.ds(p * VROWS + LANES, EXTRA), pl.ds(lane, CELLS)] = (
            jnp.ones((EXTRA, CELLS), BF) * keep
        )


def score(pair, keys):
    low = lax.broadcasted_iota(jnp.int32, pair.shape, 1) < LANES // 2
    zero = jnp.zeros_like(pair)
    stacked = jnp.concatenate([jnp.where(low, pair, zero), jnp.where(low, zero, pair)], axis=0)
    return mm_nt(keys, stacked)


def blend(values_t, terms, extra):
    both = mm(values_t, terms)
    sums = both[LANES : LANES + 8]
    share = 1.0 / (sums + extra)
    half = LANES // 2
    result = jnp.concatenate(
        [both[:half, :CELLS] * share[:1, :CELLS], both[half:LANES, CELLS:] * share[:1, CELLS:]],
        axis=0,
    )
    return result.astype(BF), sums


def attention(queries, keys, values, penalties, out_ref, bad_ref):
    bad_ref[...] = jnp.zeros_like(bad_ref)

    def terms_of(i, p):
        return jnp.exp2(score(queries(i, p), keys(i, p))).astype(BF)

    steps = [(i, p) for i in range(NB) for p in range(PAIRS)]
    following = terms_of(*steps[0])
    for n, (i, p) in enumerate(steps):
        terms = following
        if n + 1 < len(steps):
            following = terms_of(*steps[n + 1])
        result, sums = blend(values(i, p), terms, 1.0)
        out_ref[pl.ds(p * LANES, LANES), pl.ds(i * CELLS, CELLS)] = result
        bad_ref[...] += jnp.where(sums < LIMIT, 0.0, 1.0)

    @pl.when(jnp.sum(bad_ref[...]) > 0.0)
    def _():
        def band(i, carry):
            lane = pl.multiple_of(i * CELLS, CELLS)
            for p in range(PAIRS):
                scores = score(queries(i, p), keys(i, p))
                at = 0
                pieces = []
                for rows, penalty in penalties(i):
                    pieces.append(scores[at : at + rows] + penalty)
                    at += rows
                scores = jnp.concatenate(pieces, axis=0)
                highest = jnp.maximum(jnp.max(scores, axis=0, keepdims=True), 0.0)
                terms = jnp.exp2(scores - highest).astype(BF)
                result, _ = blend(values(i, p), terms, jnp.exp2(-highest))
                out_ref[pl.ds(p * LANES, LANES), pl.ds(lane, CELLS)] = result
            return carry

        lax.fori_loop(0, NB, band, 0)


def aligned(i, size):
    return i * size if isinstance(i, int) else pl.multiple_of(i * size, size)


def kernel_cross_kv(x_ref, gain_ref, weight_ref, out_ref):
    cross_input = norm_round(x_ref[...].astype(F32), gain_ref[1:2, :])
    out_ref[:, :D] = mm(cross_input, weight_ref[:, :D]).astype(BF)
    out_ref[:, D:] = mm_tt(weight_ref[:, D:], cross_input).astype(BF)


def kernel_own(x_ref, gain_ref, qkv_ref, cq_ref, q_ref, k_ref, v_ref, c_ref):
    values = x_ref[...].astype(F32)
    mean_square = jnp.mean(values * values, axis=-1, keepdims=True)
    unit = values * lax.rsqrt(mean_square + EPSILON)
    attn_input = (unit * gain_ref[0:1, :].astype(F32)).astype(BF)
    cross_input = (unit * gain_ref[1:2, :].astype(F32)).astype(BF)
    q_ref[...] = (mm(attn_input, qkv_ref[:, :D]) * Q_SCALE).astype(BF)
    k_ref[...] = mm(attn_input, qkv_ref[:, D : 2 * D]).astype(BF)
    v_ref[...] = mm_tt(qkv_ref[:, 2 * D :], attn_input).astype(BF)
    c_ref[...] = (mm(cross_input, cq_ref[...]) * Q_SCALE).astype(BF)


def kernel_cross(links_ref, land_ref, q_ref, kv_ref, out_ref, va_ref, bad_ref):
    component = lax.axis_index("comp")
    own_land = land_ref[lax.axis_index("tile"), lax.axis_index("face")]
    floor = jnp.where(component == 1, 0, own_land)

    for j in range(NB):
        row, lane = (j // 4) * D, D + (j % 4) * CELLS
        augment(kv_ref[row : row + D, lane : lane + CELLS], j >= floor, va_ref, j * CELLS)

    def picks(i):
        return [links_ref[component, i, 0, k] for k in range(KC)]

    def queries(i, p):
        return q_ref[pl.ds(aligned(i, CELLS), CELLS), pl.ds(p * LANES, LANES)]

    def keys(i, p):
        return jnp.concatenate(
            [kv_ref[pl.ds(aligned(j, CELLS), CELLS), pl.ds(p * LANES, LANES)] for j in picks(i)],
            axis=0,
        )

    def values(i, p):
        return jnp.concatenate(
            [va_ref[pl.ds(p * VROWS, VROWS), pl.ds(aligned(j, CELLS), CELLS)] for j in picks(i)],
            axis=1,
        )

    def penalties(i):
        return [(CELLS, jnp.where(j >= floor, 0.0, -1e30)) for j in picks(i)]

    attention(queries, keys, values, penalties, out_ref, bad_ref)


def kernel_window(
    land_ref,
    x_ref,
    north_ref,
    south_ref,
    west_ref,
    east_ref,
    gain_ref,
    qkv_ref,
    q_ref,
    k_ref,
    v_ref,
    cross_ref,
    out_w_ref,
    cross_w_ref,
    up_ref,
    down_ref,
    out_ref,
    keys_ref,
    va_ref,
    win_ref,
    bad_ref,
):
    is_air = lax.axis_index("comp") == 0
    tile_row = lax.axis_index("tile")
    tile_col = lax.axis_index("face")
    columns = (tile_col, (tile_col + 7) % 8, (tile_col + 1) % 8)

    def flags(r):
        inside_row = jnp.where(r == 0, tile_row - 1, jnp.where(r == NB + 1, tile_row + 1, tile_row))
        lat_ok = (inside_row >= 0) & (inside_row < 8)
        safe_row = jnp.clip(inside_row, 0, 7)
        index = jnp.where(r == 0, NB - 1, jnp.where(r == NB + 1, 0, r - 1))
        return [lat_ok & (is_air | (index >= land_ref[safe_row, c])) for c in columns]

    def project(rows_x):
        normed = norm_round(rows_x.astype(F32), gain_ref[0:1, :])
        keys = mm(normed, qkv_ref[:, D : 2 * D]).astype(BF)
        return keys, mm_tt(qkv_ref[:, 2 * D :], normed).astype(BF)

    def put(r, offset, keys, values_t, flag):
        keys_ref[pl.ds(r * GROUP + offset, CELLS), :] = keys
        augment(values_t, flag, va_ref, r * GROUP + offset)

    west_lane = lax.broadcasted_iota(jnp.int32, (1, CELLS), 1) < SIDE
    bands = NB + 2
    blocks = 2
    for b in range(blocks):
        members = range(b * bands // blocks, (b + 1) * bands // blocks)
        rows_x = []
        for r in members:
            rows_x += [west_ref[r * SIDE : (r + 1) * SIDE, :], east_ref[r * SIDE : (r + 1) * SIDE, :]]
        keys, values_t = project(jnp.concatenate(rows_x, axis=0))
        for n, r in enumerate(members):
            _, west_ok, east_ok = flags(r)
            at = slice(n * CELLS, (n + 1) * CELLS)
            flag = jnp.where(west_lane, west_ok.astype(F32), east_ok.astype(F32))
            put(r, CELLS, keys[at], values_t[:, at], flag)
    keys, values_t = project(jnp.concatenate([north_ref[...], south_ref[...]], axis=0))
    put(0, 0, keys[:CELLS], values_t[:, :CELLS], flags(0)[0])
    put(NB + 1, 0, keys[CELLS:], values_t[:, CELLS:], flags(NB + 1)[0])
    for i in range(NB):
        at = slice(i * CELLS, (i + 1) * CELLS)
        put(i + 1, 0, k_ref[at, :], v_ref[:, at], flags(i + 1)[0])

    def queries(i, p):
        return q_ref[pl.ds(aligned(i, CELLS), CELLS), pl.ds(p * LANES, LANES)]

    def keys_of(i, p):
        return keys_ref[pl.ds(aligned(i, GROUP), WINDOW), pl.ds(p * LANES, LANES)]

    def values_of(i, p):
        return va_ref[pl.ds(p * VROWS, VROWS), pl.ds(aligned(i, GROUP), WINDOW)]

    def penalties(i):
        pieces = []
        for b in range(3):
            for rows, flag in zip((CELLS, SIDE, SIDE), flags(i + b)):
                pieces.append((rows, jnp.where(flag, 0.0, -1e30)))
        return pieces

    attention(queries, keys_of, values_of, penalties, win_ref, bad_ref)

    chunk = 512
    own_land = land_ref[tile_row, tile_col]
    for c in range(ROWS // chunk):
        at = slice(c * chunk, (c + 1) * chunk)
        index = (c * chunk + lax.broadcasted_iota(jnp.int32, (chunk, 1), 0)) // CELLS
        live = jnp.where(is_air | (index >= own_land), 1.0, 0.0)
        update = mm_tn(win_ref[:, at], out_w_ref[...]) + mm_tn(cross_ref[:, at], cross_w_ref[...])
        middle = x_ref[at, :].astype(F32) + live * update
        mlp_input = norm_round(middle, gain_ref[2:3, :])
        half = 0.5 * mm(mlp_input, up_ref[...])
        hidden = (half + half * jnp.tanh(half)).astype(BF)
        out_ref[at, :] = (middle + live * mm(hidden, down_ref[...])).astype(BF)


VMEM = pl.BlockSpec(memory_space=pltpu.VMEM)
SMEM = pl.BlockSpec(memory_space=pltpu.SMEM)


def array(*shape, dtype=BF):
    return jax.ShapeDtypeStruct(shape, dtype)


def cost(macs, size, exps=0):
    return pl.CostEstimate(flops=2 * macs, bytes_accessed=size, transcendentals=exps)


def per_device(
    tokens,
    norm_gains,
    qkv_weight,
    out_weight,
    cross_query,
    cross_kv,
    cross_out,
    up_weight,
    down_weight,
    intersection_list,
    land_bands,
):
    grid_x = tokens[0]
    x = grid_x.reshape(ROWS, D)
    gains = norm_gains[0]
    up_ring = [(i, i + 1) for i in range(7)]
    down_ring = [(i + 1, i) for i in range(7)]
    east_ring = [(i, (i + 1) % 8) for i in range(8)]
    west_ring = [((i + 1) % 8, i) for i in range(8)]

    top, bottom, x = lax.optimization_barrier((grid_x[:BR], grid_x[-BR:], x))
    north = lax.ppermute(bottom, "tile", up_ring)
    south = lax.ppermute(top, "tile", down_ring)

    half = ROWS // 2
    pair_out = pl.pallas_call(
        kernel_cross_kv,
        grid=(2,),
        in_specs=[
            pl.BlockSpec((half, D), lambda i: (i, 0)),
            pl.BlockSpec((3, D), lambda i: (0, 0)),
            pl.BlockSpec((D, 2 * D), lambda i: (0, 0)),
        ],
        out_specs=pl.BlockSpec((half, 2 * D), lambda i: (i, 0)),
        out_shape=array(ROWS, 2 * D),
        cost_estimate=cost(ROWS * D * 2 * D, 4 * MIB),
        compiler_params=pltpu.CompilerParams(vmem_limit_bytes=24 * MIB),
        name="cross_kv",
    )(x, gains, cross_kv[0])
    tall = jnp.concatenate([north, grid_x, south], axis=0)
    west_edge, east_edge, pair_out = lax.optimization_barrier(
        (tall[:, :BR], tall[:, RX - BR :], pair_out)
    )
    west = lax.ppermute(east_edge, "face", east_ring).reshape((NB + 2) * SIDE, D)
    east = lax.ppermute(west_edge, "face", west_ring).reshape((NB + 2) * SIDE, D)
    partner = lax.ppermute(pair_out, "comp", [(0, 1), (1, 0)])

    block = pl.BlockSpec((half, D), lambda i: (i, 0))
    q, k, v, cross_q = pl.pallas_call(
        kernel_own,
        grid=(2,),
        in_specs=[
            block,
            pl.BlockSpec((3, D), lambda i: (0, 0)),
            pl.BlockSpec((D, 3 * D), lambda i: (0, 0)),
            pl.BlockSpec((D, D), lambda i: (0, 0)),
        ],
        out_specs=[block, block, pl.BlockSpec((D, half), lambda i: (0, i)), block],
        out_shape=[array(ROWS, D), array(ROWS, D), array(D, ROWS), array(ROWS, D)],
        cost_estimate=cost(ROWS * D * 4 * D, 7 * MIB),
        compiler_params=pltpu.CompilerParams(vmem_limit_bytes=24 * MIB),
        name="own",
    )(x, gains, qkv_weight[0], cross_query[0])

    cross = pl.pallas_call(
        kernel_cross,
        in_specs=[SMEM, SMEM, VMEM, VMEM],
        out_specs=VMEM,
        out_shape=array(D, ROWS),
        scratch_shapes=[pltpu.VMEM((PAIRS * VROWS, ROWS), BF), pltpu.VMEM((8, 2 * CELLS), F32)],
        cost_estimate=cost(8 * ROWS * 512 * D, 4 * MIB, ROWS * HEADS * 512),
        compiler_params=pltpu.CompilerParams(vmem_limit_bytes=24 * MIB),
        name="cross",
    )(intersection_list, land_bands, cross_q, partner)

    padded_rows = (NB + 2) * GROUP
    result = pl.pallas_call(
        kernel_window,
        in_specs=[SMEM] + [VMEM] * 15,
        out_specs=VMEM,
        out_shape=array(ROWS, D),
        scratch_shapes=[
            pltpu.VMEM((padded_rows, D), BF),
            pltpu.VMEM((PAIRS * VROWS, padded_rows), BF),
            pltpu.VMEM((D, ROWS), BF),
            pltpu.VMEM((8, 2 * CELLS), F32),
        ],
        cost_estimate=cost(6 << 30, 12 * MIB, ROWS * HEADS * WINDOW),
        compiler_params=pltpu.CompilerParams(vmem_limit_bytes=40 * MIB),
        name="window",
    )(
        land_bands,
        x,
        north.reshape(CELLS, D),
        south.reshape(CELLS, D),
        west,
        east,
        gains,
        qkv_weight[0],
        q,
        k,
        v,
        cross,
        out_weight[0],
        cross_out[0],
        up_weight[0],
        down_weight[0],
    )
    return result.reshape(1, NB * BR, RX, D)


def solution(mesh):
    placed = (
        P("comp", "tile", "face", None),
        P("comp", None, None),
        P("comp", None, None),
        P("comp", None, None),
        P("comp", None, None),
        P("comp", None, None),
        P("comp", None, None),
        P("comp", None, None),
        P("comp", None, None),
        P(None, "tile", "face", None),
        P(),
    )
    return jax.shard_map(
        per_device,
        mesh=mesh,
        in_specs=placed,
        out_specs=P("comp", "tile", "face", None),
        check_vma=False,
    )
```

time: 65.9 us -> 56.2 us (0.85)
  the two profiles are of different devices: /device:TPU:7 before, /device:TPU:30 now
where the time goes in v3:
time: 56.2 us; the launch traced here: 55.8 us
  Pallas kernels  29 us (52%)
  starting transfers between devices  9.65 us (17%)
  waiting for transfers between devices  8.96 us (16%)
  local copies, waits for them, and re-layouts  7.87 us (14%)
    pallas_call x1, Pallas kernels, per_device(): pl.pallas_call(kernel_window, in_specs=[SMEM] + [VMEM] * 15, out_specs=VM...  17.3 us
    pallas_call x1, Pallas kernels, per_device(): pl.pallas_call(kernel_cross, in_specs=[SMEM, SMEM, VMEM, VMEM], out_specs...  7.37 us
    unnamed x29, local copies, waits for them, and re-layouts  5.72 us
    ppermute x1, starting transfers between devices, per_device(): north = lax.ppermute(bottom, 'tile', up_ring)  5.7 us
    ppermute x1, waiting for transfers between devices, per_device(): south = lax.ppermute(top, 'tile', down_ring)  3.79 us
    pallas_call x1, Pallas kernels, per_device(): pl.pallas_call(kernel_own, grid=(2,), in_specs=[block, pl.BlockSpec((3, D...  2.75 us
    ppermute x1, waiting for transfers between devices, per_device(): lax.ppermute(east_edge, 'face', east_ring).reshape((NB + 2) * SIDE, D)  2.66 us
    ppermute x1, waiting for transfers between devices, per_device(): lax.ppermute(west_edge, 'face', west_ring).reshape((NB + 2) * SIDE, D)  2.51 us
  transfers between devices with their start and end apart: 5, of which 3 were waited for; matrix products, arithmetic and copies ran while one was open for 0% of the time, Pallas kernels for 21%

profile of v3, /device:TPU:30, one launch (start us, length us, event | category | flops | bytes accessed | tf_op | source)
XLA Modules:
  0.0 55.8 jit_solution(17216978092450012415)
XLA Ops:
  0.0 1.0 %slice_bitcast_fusion = (bf16[8,16,512]{2,1,0:T(8,128)(2,1)S(1)}, bf16[8,16,512]{2,1,0:T(8,128)(2,1)S(1)}) fusion(bf16[1,64,16,512]{3,2,1,0:T(8,128)(2,1)} %param.11), kind=kLoop, calls=%fused_computation.1 | loop fusion | bytes 524288 | tf_op jit(solution)/shard_map/slice | solution.py:305
  1.0 5.7 %collective-permute-start = (bf16[8,16,512]{2,1,0:T(8,128)(2,1)S(1)}, bf16[8,16,512]{2,1,0:T(8,128)(2,1)S(1)}, u32[]{:S(2)}, u32[]{:S(2)}) collective-permute-start(bf16[8,16,512]{2,1,0:T(8,128)(2,1)S(1)} %get-tuple-element.16), channel_id=1, source_target_pairs={{0,1},{1,2},{2,3},{3,4},{4,5},{5,6},{6,7},{8,9},{9,10},{10,11},{11... | collective-permute-start | bytes 393224 | tf_op jit(solution)/shard_map/ppermute | solution.py:306
  6.7 1.9 %collective-permute-start.1 = (bf16[8,16,512]{2,1,0:T(8,128)(2,1)S(1)}, bf16[8,16,512]{2,1,0:T(8,128)(2,1)S(1)}, u32[]{:S(2)}, u32[]{:S(2)}) collective-permute-start(bf16[8,16,512]{2,1,0:T(8,128)(2,1)S(1)} %get-tuple-element.17), channel_id=1, source_target_pairs={{1,0},{2,1},{3,2},{4,3},{5,4},{6,5},{7,6},{9,8},{10,9},{11,10},{12... | collective-permute-start | bytes 393224 | tf_op jit(solution)/shard_map/ppermute | solution.py:307
  8.6 0.0 copy-start
  8.6 1.2 %copy-done = bf16[1,64,16,512]{3,2,1,0:T(8,128)(2,1)S(1)} copy-done((bf16[1,64,16,512]{3,2,1,0:T(8,128)(2,1)S(1)}, bf16[1,64,16,512]{3,2,1,0:T(8,128)(2,1)}, u32[]{:S(2)}) %copy-start) | copy-done | bytes 1048600
  9.9 0.0 copy-start.2
  9.9 1.2 %copy-done.2 = bf16[1,512,1024]{2,1,0:T(8,128)(2,1)S(1)} copy-done((bf16[1,512,1024]{2,1,0:T(8,128)(2,1)S(1)}, bf16[1,512,1024]{2,1,0:T(8,128)(2,1)}, u32[]{:S(2)}) %copy-start.2) | copy-done | bytes 1048600
  11.1 0.0 copy-start.3
  11.1 0.7 %copy-done.3 = bf16[1,3,512]{2,1,0:T(4,128)(2,1)S(1)} copy-done((bf16[1,3,512]{2,1,0:T(4,128)(2,1)S(1)}, bf16[1,3,512]{2,1,0:T(4,128)(2,1)}, u32[]{:S(2)}) %copy-start.3) | copy-done | bytes 3096
  11.8 1.6 %cross_kv.1 = bf16[1024,1024]{1,0:T(8,128)(2,1)S(1)} custom-call(bf16[1024,512]{1,0:T(8,128)(2,1)S(1)} %bitcast.19, bf16[3,512]{1,0:T(4,128)(2,1)S(1)} %bitcast.26, bf16[512,1024]{1,0:T(8,128)(2,1)S(1)} %bitcast.23), custom_call_target="tpu_custom_call" | custom-call | flops 1073741824 | bytes 4194304 | tf_op jit(solution)/shard_map/cross_kv/pallas_call | solution.py:310
  13.4 0.0 collective-permute-done
  13.4 3.8 %collective-permute-done.1 = bf16[8,16,512]{2,1,0:T(8,128)(2,1)S(1)} collective-permute-done((bf16[8,16,512]{2,1,0:T(8,128)(2,1)S(1)}, bf16[8,16,512]{2,1,0:T(8,128)(2,1)S(1)}, u32[]{:S(2)}, u32[]{:S(2)}) %collective-permute-start.1) | collective-permute-done | bytes 131104 | tf_op jit(solution)/shard_map/ppermute | solution.py:307
  17.2 0.2 pad_maximum_fusion
  17.3 0.0 copy-start.13
  17.4 0.0 copy-start.1
  17.4 0.0 copy-start.4
  17.4 1.2 %fusion = (bf16[80,8,512]{2,1,0:T(8,128)(2,1)}, bf16[80,8,512]{2,1,0:T(8,128)(2,1)}) fusion(bf16[80,16,512]{2,1,0:T(8,128)(2,1)S(1)} %pad_maximum_fusion), kind=kLoop, calls=%fused_computation.3 | loop fusion | bytes 2621440 | tf_op jit(solution)/shard_map/slice | solution.py:326
  18.5 0.0 collective-permute-start.4
  18.5 0.7 %collective-permute-start.2 = (bf16[80,8,512]{2,1,0:T(8,128)(2,1)}, bf16[80,8,512]{2,1,0:T(8,128)(2,1)}, u32[]{:S(2)}, u32[]{:S(2)}) collective-permute-start(bf16[80,8,512]{2,1,0:T(8,128)(2,1)} %get-tuple-element.18), channel_id=1, source_target_pairs={{0,8},{8,16},{16,24},{24,32},{32,40},{40,48},{48,56},{56,0},{1,9},... | collective-permute-start | bytes 1966088 | tf_op jit(solution)/shard_map/ppermute | solution.py:328
  19.2 1.3 %collective-permute-start.3 = (bf16[80,8,512]{2,1,0:T(8,128)(2,1)}, bf16[80,8,512]{2,1,0:T(8,128)(2,1)}, u32[]{:S(2)}, u32[]{:S(2)}) collective-permute-start(bf16[80,8,512]{2,1,0:T(8,128)(2,1)} %get-tuple-element.19), channel_id=1, source_target_pairs={{8,0},{16,8},{24,16},{32,24},{40,32},{48,40},{56,48},{0,56},{9,1},... | collective-permute-start | bytes 1966088 | tf_op jit(solution)/shard_map/ppermute | solution.py:329
  20.6 0.0 copy-done.13
  20.6 0.1 copy.12.links_ref
  20.7 0.0 copy-done.1
  20.7 0.0 copy-done.4
  20.7 0.0 copy-start.7
  20.7 1.4 %copy-done.7 = bf16[1,512,1536]{2,1,0:T(8,128)(2,1)S(1)} copy-done((bf16[1,512,1536]{2,1,0:T(8,128)(2,1)S(1)}, bf16[1,512,1536]{2,1,0:T(8,128)(2,1)}, u32[]{:S(2)}) %copy-start.7) | copy-done | bytes 1572888
  22.1 0.0 copy-start.9
  22.1 1.0 %copy-done.9 = bf16[1,512,512]{2,1,0:T(8,128)(2,1)S(1)} copy-done((bf16[1,512,512]{2,1,0:T(8,128)(2,1)S(1)}, bf16[1,512,512]{2,1,0:T(8,128)(2,1)}, u32[]{:S(2)}) %copy-start.9) | copy-done | bytes 524312
  23.1 0.0 copy-start.12
  23.1 2.7 %own.1 = (bf16[1024,512]{1,0:T(8,128)(2,1)S(1)}, bf16[1024,512]{1,0:T(8,128)(2,1)S(1)}, bf16[512,1024]{1,0:T(8,128)(2,1)S(1)}, bf16[1024,512]{1,0:T(8,128)(2,1)S(1)}) custom-call(bf16[1024,512]{1,0:T(8,128)(2,1)S(1)} %bitcast.21, bf16[3,512]{1,0:T(4,128)(2,1)S(1)} %bitcast.27, bf16[512,1536]{1,0:T(8,128)(2,1)S(1)} %bitcast.31, bf16[512,512]{1,0:T(8,128)(2,1)S(1)} %bitcast.33), custom_call_target="tpu_custom_call" | custom-call | flops 2147483648 | bytes 7340032 | tf_op jit(solution)/shard_map/own/pallas_call | solution.py:333
  25.9 0.0 collective-permute-done.4.kv_ref
  25.9 0.0 copy-done.12
  25.9 0.0 copy-start.5
  25.9 0.0 copy-start.6
  25.9 0.0 copy-start.8
  25.9 0.0 copy-start.10
  25.9 0.0 copy-start.11
  26.0 7.4 %cross.1.cross_ref = bf16[512,1024]{1,0:T(8,128)(2,1)S(1)} custom-call(s32[2,8,1,4]{3,2,1,0:T(1,128)S(1)} %copy.12.links_ref, s32[8,8]{1,0:T(8,128)S(1)} %copy-done.12, bf16[1024,512]{1,0:T(8,128)(2,1)S(1)} %get-tuple-element.23.q_ref, bf16[1024,1024]{1,0:T(8,128)(2,1)} %collective-permute-done.4.kv_ref), custom_call_target="tpu_custom_call" | custom-call | flops 4294967296 | bytes 4194304 | tf_op jit(solution)/shard_map/cross/pallas_call | solution.py:349
  33.3 2.7 %collective-permute-done.2 = bf16[80,8,512]{2,1,0:T(8,128)(2,1)} collective-permute-done((bf16[80,8,512]{2,1,0:T(8,128)(2,1)}, bf16[80,8,512]{2,1,0:T(8,128)(2,1)}, u32[]{:S(2)}, u32[]{:S(2)}) %collective-permute-start.2) | collective-permute-done | bytes 655392 | tf_op jit(solution)/shard_map/ppermute | solution.py:328
  36.0 2.5 %collective-permute-done.3 = bf16[80,8,512]{2,1,0:T(8,128)(2,1)} collective-permute-done((bf16[80,8,512]{2,1,0:T(8,128)(2,1)}, bf16[80,8,512]{2,1,0:T(8,128)(2,1)}, u32[]{:S(2)}, u32[]{:S(2)}) %collective-permute-start.3) | collective-permute-done | bytes 655392 | tf_op jit(solution)/shard_map/ppermute | solution.py:329
  38.5 0.0 copy-done.5
  38.5 0.0 copy-done.6
  38.5 0.0 copy-done.8
  38.5 0.0 copy-done.10
  38.5 0.0 copy-done.11
  38.5 17.3 %window.1 = bf16[1024,512]{1,0:T(8,128)(2,1)} custom-call(s32[8,8]{1,0:T(8,128)S(1)} %copy-done.12, bf16[1024,512]{1,0:T(8,128)(2,1)S(1)} %bitcast.22, bf16[128,512]{1,0:T(8,128)(2,1)S(1)} %bitcast.24, bf16[128,512]{1,0:T(8,128)(2,1)S(1)} %bitcast.25, bf16[640,512]{1,0:T(8,128)(2,1)} %bitcast.8.west_ref, bf16[640,512]{1,0:T(8,128)(2,1)} %bitcast.9.east_ref, ...), custom_call_target="tpu_custom_call" | custom-call | flops 12884901888 | bytes 12582912 | tf_op jit(solution)/shard_map/window/pallas_call | solution.py:361
Async XLA Ops:
  1.0 12.4 %collective-permute-start = (bf16[8,16,512]{2,1,0:T(8,128)(2,1)S(1)}, bf16[8,16,512]{2,1,0:T(8,128)(2,1)S(1)}, u32[]{:S(2)}, u32[]{:S(2)}) collective-permute-start(bf16[8,16,512]{2,1,0:T(8,128)(2,1)S(1)} %get-tuple-element.16), channel_id=1, source_target_pairs={{0,1},{1,2},{2,3},{3,4},{4,5},{5,6},{6,7},{8,9},{9,10},{10,11},{11... | collective-permute-start | bytes 393224 | tf_op jit(solution)/shard_map/ppermute | solution.py:306
  6.7 10.5 %collective-permute-start.1 = (bf16[8,16,512]{2,1,0:T(8,128)(2,1)S(1)}, bf16[8,16,512]{2,1,0:T(8,128)(2,1)S(1)}, u32[]{:S(2)}, u32[]{:S(2)}) collective-permute-start(bf16[8,16,512]{2,1,0:T(8,128)(2,1)S(1)} %get-tuple-element.17), channel_id=1, source_target_pairs={{1,0},{2,1},{3,2},{4,3},{5,4},{6,5},{7,6},{9,8},{10,9},{11,10},{12... | collective-permute-start | bytes 393224 | tf_op jit(solution)/shard_map/ppermute | solution.py:307
  8.6 1.2 %copy-start = (bf16[1,64,16,512]{3,2,1,0:T(8,128)(2,1)S(1)}, bf16[1,64,16,512]{3,2,1,0:T(8,128)(2,1)}, u32[]{:S(2)}) copy-start(bf16[1,64,16,512]{3,2,1,0:T(8,128)(2,1)} %param.11) | copy-start | bytes 3145732
  9.9 1.2 %copy-start.2 = (bf16[1,512,1024]{2,1,0:T(8,128)(2,1)S(1)}, bf16[1,512,1024]{2,1,0:T(8,128)(2,1)}, u32[]{:S(2)}) copy-start(bf16[1,512,1024]{2,1,0:T(8,128)(2,1)} %param.16) | copy-start | bytes 3145732
  11.1 0.7 %copy-start.3 = (bf16[1,3,512]{2,1,0:T(4,128)(2,1)S(1)}, bf16[1,3,512]{2,1,0:T(4,128)(2,1)}, u32[]{:S(2)}) copy-start(bf16[1,3,512]{2,1,0:T(4,128)(2,1)} %param.12) | copy-start | bytes 9220
  17.3 3.2 %copy-start.13 = (s32[2,8,1,4]{1,3,2,0:T(4,128)S(1)}, s32[2,8,1,4]{1,3,2,0:T(4,128)}, u32[]{:S(2)}) copy-start(s32[2,8,1,4]{1,3,2,0:T(4,128)} %param.20) | copy-start | bytes 772
  17.4 3.3 %copy-start.1 = (bf16[1,64,16,512]{3,2,1,0:T(8,128)(2,1)S(1)}, bf16[1,64,16,512]{3,2,1,0:T(8,128)(2,1)}, u32[]{:S(2)}) copy-start(bf16[1,64,16,512]{3,2,1,0:T(8,128)(2,1)} %param.11) | copy-start | bytes 3145732
  17.4 3.3 %copy-start.4 = (bf16[1,3,512]{2,1,0:T(4,128)(2,1)S(1)}, bf16[1,3,512]{2,1,0:T(4,128)(2,1)}, u32[]{:S(2)}) copy-start(bf16[1,3,512]{2,1,0:T(4,128)(2,1)} %param.12) | copy-start | bytes 9220
  18.5 7.3 %collective-permute-start.4 = (bf16[1024,1024]{1,0:T(8,128)(2,1)S(1)}, bf16[1024,1024]{1,0:T(8,128)(2,1)}, u32[]{:S(2)}, u32[]{:S(2)}) collective-permute-start(bf16[1024,1024]{1,0:T(8,128)(2,1)S(1)} %cross_kv.1), channel_id=1, source_target_pairs={{0,64},{64,0},{1,65},{65,1},{2,66},{66,2},{3,67},{67,3},{4,68},{68... | collective-permute-start | bytes 6291464 | tf_op jit(solution)/shard_map/ppermute | solution.py:330
  18.5 17.5 %collective-permute-start.2 = (bf16[80,8,512]{2,1,0:T(8,128)(2,1)}, bf16[80,8,512]{2,1,0:T(8,128)(2,1)}, u32[]{:S(2)}, u32[]{:S(2)}) collective-permute-start(bf16[80,8,512]{2,1,0:T(8,128)(2,1)} %get-tuple-element.18), channel_id=1, source_target_pairs={{0,8},{8,16},{16,24},{24,32},{32,40},{40,48},{48,56},{56,0},{1,9},... | collective-permute-start | bytes 1966088 | tf_op jit(solution)/shard_map/ppermute | solution.py:328
  19.2 19.3 %collective-permute-start.3 = (bf16[80,8,512]{2,1,0:T(8,128)(2,1)}, bf16[80,8,512]{2,1,0:T(8,128)(2,1)}, u32[]{:S(2)}, u32[]{:S(2)}) collective-permute-start(bf16[80,8,512]{2,1,0:T(8,128)(2,1)} %get-tuple-element.19), channel_id=1, source_target_pairs={{8,0},{16,8},{24,16},{32,24},{40,32},{48,40},{56,48},{0,56},{9,1},... | collective-permute-start | bytes 1966088 | tf_op jit(solution)/shard_map/ppermute | solution.py:329
  20.7 1.4 %copy-start.7 = (bf16[1,512,1536]{2,1,0:T(8,128)(2,1)S(1)}, bf16[1,512,1536]{2,1,0:T(8,128)(2,1)}, u32[]{:S(2)}) copy-start(bf16[1,512,1536]{2,1,0:T(8,128)(2,1)} %param.13) | copy-start | bytes 4718596
  22.1 1.0 %copy-start.9 = (bf16[1,512,512]{2,1,0:T(8,128)(2,1)S(1)}, bf16[1,512,512]{2,1,0:T(8,128)(2,1)}, u32[]{:S(2)}) copy-start(bf16[1,512,512]{2,1,0:T(8,128)(2,1)} %param.15) | copy-start | bytes 1572868
  23.1 2.8 %copy-start.12 = (s32[8,8]{1,0:T(8,128)S(1)}, s32[8,8]{1,0:T(8,128)}, u32[]{:S(2)}) copy-start(s32[8,8]{1,0:T(8,128)} %land_ref.3) | copy-start | bytes 772
  25.9 12.6 %copy-start.5 = (bf16[1,512,2048]{2,1,0:T(8,128)(2,1)S(1)}, bf16[1,512,2048]{2,1,0:T(8,128)(2,1)}, u32[]{:S(2)}) copy-start(bf16[1,512,2048]{2,1,0:T(8,128)(2,1)} %param.18) | copy-start | bytes 6291460
  25.9 12.6 %copy-start.6 = (bf16[1,2048,512]{2,1,0:T(8,128)(2,1)S(1)}, bf16[1,2048,512]{2,1,0:T(8,128)(2,1)}, u32[]{:S(2)}) copy-start(bf16[1,2048,512]{2,1,0:T(8,128)(2,1)} %param.19) | copy-start | bytes 6291460
  25.9 12.6 %copy-start.8 = (bf16[1,512,1536]{2,1,0:T(8,128)(2,1)S(1)}, bf16[1,512,1536]{2,1,0:T(8,128)(2,1)}, u32[]{:S(2)}) copy-start(bf16[1,512,1536]{2,1,0:T(8,128)(2,1)} %param.13) | copy-start | bytes 4718596
  25.9 12.6 %copy-start.10 = (bf16[1,512,512]{2,1,0:T(8,128)(2,1)S(1)}, bf16[1,512,512]{2,1,0:T(8,128)(2,1)}, u32[]{:S(2)}) copy-start(bf16[1,512,512]{2,1,0:T(8,128)(2,1)} %param.14) | copy-start | bytes 1572868
  25.9 12.6 %copy-start.11 = (bf16[1,512,512]{2,1,0:T(8,128)(2,1)S(1)}, bf16[1,512,512]{2,1,0:T(8,128)(2,1)}, u32[]{:S(2)}) copy-start(bf16[1,512,512]{2,1,0:T(8,128)(2,1)} %param.17) | copy-start | bytes 1572868

commit v4 on v3

--- a/solution.py
+++ b/solution.py
@@ -139,7 +139,23 @@
     c_ref[...] = (mm(cross_input, cq_ref[...]) * Q_SCALE).astype(BF)
 
 
-def kernel_cross(links_ref, land_ref, q_ref, kv_ref, out_ref, va_ref, bad_ref):
+def kernel_cross(
+    links_ref,
+    land_ref,
+    q_ref,
+    kv_ref,
+    win_ref,
+    x_ref,
+    gain_ref,
+    out_w_ref,
+    cross_w_ref,
+    up_ref,
+    down_ref,
+    out_ref,
+    cross_ref,
+    va_ref,
+    bad_ref,
+):
     component = lax.axis_index("comp")
     own_land = land_ref[lax.axis_index("tile"), lax.axis_index("face")]
     floor = jnp.where(component == 1, 0, own_land)
@@ -169,30 +185,38 @@
     def penalties(i):
         return [(CELLS, jnp.where(j >= floor, 0.0, -1e30)) for j in picks(i)]
 
-    attention(queries, keys, values, penalties, out_ref, bad_ref)
+    attention(queries, keys, values, penalties, cross_ref, bad_ref)
+
+    chunk = 512
+    is_air = component == 0
+    for c in range(ROWS // chunk):
+        at = slice(c * chunk, (c + 1) * chunk)
+        index = (c * chunk + lax.broadcasted_iota(jnp.int32, (chunk, 1), 0)) // CELLS
+        live = jnp.where(is_air | (index >= own_land), 1.0, 0.0)
+        update = mm_tn(win_ref[:, at], out_w_ref[...]) + mm_tn(cross_ref[:, at], cross_w_ref[...])
+        middle = x_ref[at, :].astype(F32) + live * update
+        mlp_input = norm_round(middle, gain_ref[2:3, :])
+        half = 0.5 * mm(mlp_input, up_ref[...])
+        hidden = (half + half * jnp.tanh(half)).astype(BF)
+        out_ref[at, :] = (middle + live * mm(hidden, down_ref[...])).astype(BF)
 
 
 def kernel_window(
     land_ref,
-    x_ref,
     north_ref,
     south_ref,
     west_ref,
     east_ref,
+    corner_west_ref,
+    corner_east_ref,
     gain_ref,
     qkv_ref,
     q_ref,
     k_ref,
     v_ref,
-    cross_ref,
-    out_w_ref,
-    cross_w_ref,
-    up_ref,
-    down_ref,
-    out_ref,
+    win_ref,
     keys_ref,
     va_ref,
-    win_ref,
     bad_ref,
 ):
     is_air = lax.axis_index("comp") == 0
@@ -223,7 +247,11 @@
         members = range(b * bands // blocks, (b + 1) * bands // blocks)
         rows_x = []
         for r in members:
-            rows_x += [west_ref[r * SIDE : (r + 1) * SIDE, :], east_ref[r * SIDE : (r + 1) * SIDE, :]]
+            for side_ref, corner_ref in ((west_ref, corner_west_ref), (east_ref, corner_east_ref)):
+                if 1 <= r <= NB:
+                    rows_x.append(side_ref[(r - 1) * SIDE : r * SIDE, :])
+                else:
+                    rows_x.append(corner_ref[min(r, 1) * SIDE : (min(r, 1) + 1) * SIDE, :])
         keys, values_t = project(jnp.concatenate(rows_x, axis=0))
         for n, r in enumerate(members):
             _, west_ok, east_ok = flags(r)
@@ -254,19 +282,6 @@
         return pieces
 
     attention(queries, keys_of, values_of, penalties, win_ref, bad_ref)
-
-    chunk = 512
-    own_land = land_ref[tile_row, tile_col]
-    for c in range(ROWS // chunk):
-        at = slice(c * chunk, (c + 1) * chunk)
-        index = (c * chunk + lax.broadcasted_iota(jnp.int32, (chunk, 1), 0)) // CELLS
-        live = jnp.where(is_air | (index >= own_land), 1.0, 0.0)
-        update = mm_tn(win_ref[:, at], out_w_ref[...]) + mm_tn(cross_ref[:, at], cross_w_ref[...])
-        middle = x_ref[at, :].astype(F32) + live * update
-        mlp_input = norm_round(middle, gain_ref[2:3, :])
-        half = 0.5 * mm(mlp_input, up_ref[...])
-        hidden = (half + half * jnp.tanh(half)).astype(BF)
-        out_ref[at, :] = (middle + live * mm(hidden, down_ref[...])).astype(BF)
 
 
 VMEM = pl.BlockSpec(memory_space=pltpu.VMEM)
@@ -302,89 +317,114 @@
     east_ring = [(i, (i + 1) % 8) for i in range(8)]
     west_ring = [((i + 1) % 8, i) for i in range(8)]
 
-    top, bottom, x = lax.optimization_barrier((grid_x[:BR], grid_x[-BR:], x))
+    top, bottom, west_edge, east_edge, x_first = lax.optimization_barrier(
+        (grid_x[:BR], grid_x[-BR:], grid_x[:, :BR], grid_x[:, -BR:], x)
+    )
+    west = lax.ppermute(east_edge, "face", east_ring)
+    east = lax.ppermute(west_edge, "face", west_ring)
     north = lax.ppermute(bottom, "tile", up_ring)
     south = lax.ppermute(top, "tile", down_ring)
 
-    half = ROWS // 2
-    pair_out = pl.pallas_call(
-        kernel_cross_kv,
-        grid=(2,),
-        in_specs=[
-            pl.BlockSpec((half, D), lambda i: (i, 0)),
-            pl.BlockSpec((3, D), lambda i: (0, 0)),
-            pl.BlockSpec((D, 2 * D), lambda i: (0, 0)),
-        ],
-        out_specs=pl.BlockSpec((half, 2 * D), lambda i: (i, 0)),
-        out_shape=array(ROWS, 2 * D),
-        cost_estimate=cost(ROWS * D * 2 * D, 4 * MIB),
-        compiler_params=pltpu.CompilerParams(vmem_limit_bytes=24 * MIB),
-        name="cross_kv",
-    )(x, gains, cross_kv[0])
-    tall = jnp.concatenate([north, grid_x, south], axis=0)
-    west_edge, east_edge, pair_out = lax.optimization_barrier(
-        (tall[:, :BR], tall[:, RX - BR :], pair_out)
-    )
-    west = lax.ppermute(east_edge, "face", east_ring).reshape((NB + 2) * SIDE, D)
-    east = lax.ppermute(west_edge, "face", west_ring).reshape((NB + 2) * SIDE, D)
-    partner = lax.ppermute(pair_out, "comp", [(0, 1), (1, 0)])
-
-    block = pl.BlockSpec((half, D), lambda i: (i, 0))
+    steps = 4
+    part = ROWS // steps
+    block = pl.BlockSpec((part, D), lambda i: (i, 0))
+    streamed = pltpu.CompilerParams(vmem_limit_bytes=56 * MIB)
     q, k, v, cross_q = pl.pallas_call(
         kernel_own,
-        grid=(2,),
+        grid=(steps,),
         in_specs=[
             block,
             pl.BlockSpec((3, D), lambda i: (0, 0)),
             pl.BlockSpec((D, 3 * D), lambda i: (0, 0)),
             pl.BlockSpec((D, D), lambda i: (0, 0)),
         ],
-        out_specs=[block, block, pl.BlockSpec((D, half), lambda i: (0, i)), block],
+        out_specs=[block, block, pl.BlockSpec((D, part), lambda i: (0, i)), block],
         out_shape=[array(ROWS, D), array(ROWS, D), array(D, ROWS), array(ROWS, D)],
         cost_estimate=cost(ROWS * D * 4 * D, 7 * MIB),
-        compiler_params=pltpu.CompilerParams(vmem_limit_bytes=24 * MIB),
+        compiler_params=streamed,
         name="own",
-    )(x, gains, qkv_weight[0], cross_query[0])
-
-    cross = pl.pallas_call(
-        kernel_cross,
-        in_specs=[SMEM, SMEM, VMEM, VMEM],
+    )(x_first, gains, qkv_weight[0], cross_query[0])
+
+    west_corner, east_corner = [
+        jnp.concatenate([north[:, cut], south[:, cut]], axis=0)
+        for cut in (slice(0, BR), slice(RX - BR, RX))
+    ]
+    west_corner, east_corner, q, x_second = lax.optimization_barrier(
+        (west_corner, east_corner, q, x)
+    )
+
+    pair_out = pl.pallas_call(
+        kernel_cross_kv,
+        grid=(2,),
+        in_specs=[
+            pl.BlockSpec((ROWS // 2, D), lambda i: (i, 0)),
+            pl.BlockSpec((3, D), lambda i: (0, 0)),
+            pl.BlockSpec((D, 2 * D), lambda i: (0, 0)),
+        ],
+        out_specs=pl.BlockSpec((ROWS // 2, 2 * D), lambda i: (i, 0)),
+        out_shape=array(ROWS, 2 * D),
+        cost_estimate=cost(ROWS * D * 2 * D, 4 * MIB),
+        compiler_params=streamed,
+        name="cross_kv",
+    )(x_second, gains, cross_kv[0])
+
+    corner_west = lax.ppermute(east_corner, "face", east_ring)
+    corner_east = lax.ppermute(west_corner, "face", west_ring)
+    west, east, corner_west, corner_east, pair_out = lax.optimization_barrier(
+        (west, east, corner_west, corner_east, pair_out)
+    )
+    partner = lax.ppermute(pair_out, "comp", [(0, 1), (1, 0)])
+
+    padded_rows = (NB + 2) * GROUP
+    window = pl.pallas_call(
+        kernel_window,
+        in_specs=[SMEM] + [VMEM] * 11,
         out_specs=VMEM,
         out_shape=array(D, ROWS),
-        scratch_shapes=[pltpu.VMEM((PAIRS * VROWS, ROWS), BF), pltpu.VMEM((8, 2 * CELLS), F32)],
-        cost_estimate=cost(8 * ROWS * 512 * D, 4 * MIB, ROWS * HEADS * 512),
-        compiler_params=pltpu.CompilerParams(vmem_limit_bytes=24 * MIB),
-        name="cross",
-    )(intersection_list, land_bands, cross_q, partner)
-
-    padded_rows = (NB + 2) * GROUP
-    result = pl.pallas_call(
-        kernel_window,
-        in_specs=[SMEM] + [VMEM] * 15,
-        out_specs=VMEM,
-        out_shape=array(ROWS, D),
         scratch_shapes=[
             pltpu.VMEM((padded_rows, D), BF),
             pltpu.VMEM((PAIRS * VROWS, padded_rows), BF),
-            pltpu.VMEM((D, ROWS), BF),
             pltpu.VMEM((8, 2 * CELLS), F32),
         ],
-        cost_estimate=cost(6 << 30, 12 * MIB, ROWS * HEADS * WINDOW),
-        compiler_params=pltpu.CompilerParams(vmem_limit_bytes=40 * MIB),
+        cost_estimate=cost(4 << 30, 7 * MIB, ROWS * HEADS * WINDOW),
+        compiler_params=pltpu.CompilerParams(vmem_limit_bytes=32 * MIB),
         name="window",
     )(
         land_bands,
-        x,
         north.reshape(CELLS, D),
         south.reshape(CELLS, D),
-        west,
-        east,
+        west.reshape(NB * SIDE, D),
+        east.reshape(NB * SIDE, D),
+        corner_west.reshape(2 * SIDE, D),
+        corner_east.reshape(2 * SIDE, D),
         gains,
         qkv_weight[0],
         q,
         k,
         v,
-        cross,
+    )
+
+    result = pl.pallas_call(
+        kernel_cross,
+        in_specs=[SMEM] * 2 + [VMEM] * 9,
+        out_specs=VMEM,
+        out_shape=array(ROWS, D),
+        scratch_shapes=[
+            pltpu.VMEM((D, ROWS), BF),
+            pltpu.VMEM((PAIRS * VROWS, ROWS), BF),
+            pltpu.VMEM((8, 2 * CELLS), F32),
+        ],
+        cost_estimate=cost(5 << 30, 11 * MIB, ROWS * HEADS * 512),
+        compiler_params=pltpu.CompilerParams(vmem_limit_bytes=40 * MIB),
+        name="cross",
+    )(
+        intersection_list,
+        land_bands,
+        cross_q,
+        partner,
+        window,
+        x,
+        gains,
         out_weight[0],
         cross_out[0],
         up_weight[0],

time: 56.2 us -> 62.5 us (1.11)
  the two profiles are of different devices: /device:TPU:30 before, /device:TPU:89 now
where the time goes in v4:
time: 62.5 us; the launch traced here: 62 us
  Pallas kernels  32.9 us (53%)
  starting transfers between devices  15.5 us (25%)
  local copies, waits for them, and re-layouts  9.73 us (16%)
  waiting for transfers between devices  3.71 us (6%)
    pallas_call x1, Pallas kernels, per_device(): pl.pallas_call(kernel_cross, in_specs=[SMEM] * 2 + [VMEM] * 9, out_specs=...  13.8 us
    pallas_call x1, Pallas kernels, per_device(): pl.pallas_call(kernel_window, in_specs=[SMEM] + [VMEM] * 11, out_specs=VM...  9.11 us
    unnamed x29, local copies, waits for them, and re-layouts  7.45 us
    pallas_call x1, Pallas kernels, per_device(): pl.pallas_call(kernel_own, grid=(steps,), in_specs=[block, pl.BlockSpec((...  5.97 us
    ppermute x1, starting transfers between devices, per_device(): south = lax.ppermute(top, 'tile', down_ring)  5.78 us
    pallas_call x1, Pallas kernels, per_device(): pl.pallas_call(kernel_cross_kv, grid=(2,), in_specs=[pl.BlockSpec((ROWS /...  3.99 us
    ppermute x1, waiting for transfers between devices, per_device(): corner_east = lax.ppermute(west_corner, 'face', west_ring)  3.4 us
    ppermute x1, starting transfers between devices, per_device(): corner_west = lax.ppermute(east_corner, 'face', east_ring)  3.19 us
  transfers between devices with their start and end apart: 7, of which 2 were waited for; matrix products, arithmetic and copies ran while one was open for 1% of the time, Pallas kernels for 31%

profile of v4, /device:TPU:89, one launch (start us, length us, event | category | flops | bytes accessed | tf_op | source)
XLA Modules:
  0.0 62.0 jit_solution(3918587985436619855)
XLA Ops:
  0.0 1.0 %slice_bitcast_fusion = (bf16[8,16,512]{2,1,0:T(8,128)(2,1)S(1)}, bf16[8,16,512]{2,1,0:T(8,128)(2,1)S(1)}) fusion(bf16[1,64,16,512]{3,2,1,0:T(8,128)(2,1)} %param.11), kind=kLoop, calls=%fused_computation.2 | loop fusion | bytes 524288 | tf_op jit(solution)/shard_map/slice | solution.py:321
  1.0 1.3 %fusion = (bf16[64,8,512]{2,1,0:T(8,128)(2,1)S(1)}, bf16[64,8,512]{2,1,0:T(8,128)(2,1)S(1)}) fusion(bf16[64,16,512]{2,1,0:T(8,128)(2,1)} %bitcast.21), kind=kLoop, calls=%fused_computation.4 | loop fusion | bytes 2097152 | tf_op jit(solution)/shard_map/slice | solution.py:321
  2.3 3.1 %collective-permute-start.2 = (bf16[8,16,512]{2,1,0:T(8,128)(2,1)S(1)}, bf16[8,16,512]{2,1,0:T(8,128)(2,1)S(1)}, u32[]{:S(2)}, u32[]{:S(2)}) collective-permute-start(bf16[8,16,512]{2,1,0:T(8,128)(2,1)S(1)} %get-tuple-element.27), channel_id=1, source_target_pairs={{0,1},{1,2},{2,3},{3,4},{4,5},{5,6},{6,7},{8,9},{9,10},{10,11},{11... | collective-permute-start | bytes 393224 | tf_op jit(solution)/shard_map/ppermute | solution.py:325
  5.4 5.8 %collective-permute-start.3 = (bf16[8,16,512]{2,1,0:T(8,128)(2,1)S(1)}, bf16[8,16,512]{2,1,0:T(8,128)(2,1)S(1)}, u32[]{:S(2)}, u32[]{:S(2)}) collective-permute-start(bf16[8,16,512]{2,1,0:T(8,128)(2,1)S(1)} %get-tuple-element.28), channel_id=1, source_target_pairs={{1,0},{2,1},{3,2},{4,3},{5,4},{6,5},{7,6},{9,8},{10,9},{11,10},{12... | collective-permute-start | bytes 393224 | tf_op jit(solution)/shard_map/ppermute | solution.py:326
  11.2 1.1 %collective-permute-start = (bf16[64,8,512]{2,1,0:T(8,128)(2,1)S(1)}, bf16[64,8,512]{2,1,0:T(8,128)(2,1)S(1)}, u32[]{:S(2)}, u32[]{:S(2)}) collective-permute-start(bf16[64,8,512]{2,1,0:T(8,128)(2,1)S(1)} %get-tuple-element.25), channel_id=1, source_target_pairs={{0,8},{8,16},{16,24},{24,32},{32,40},{40,48},{48,56},{56,0},{1,9},... | collective-permute-start | bytes 1572872 | tf_op jit(solution)/shard_map/ppermute | solution.py:323
  12.2 0.5 collective-permute-start.1
  12.7 6.0 %own.1 = (bf16[1024,512]{1,0:T(8,128)(2,1)}, bf16[1024,512]{1,0:T(8,128)(2,1)}, bf16[512,1024]{1,0:T(8,128)(2,1)}, bf16[1024,512]{1,0:T(8,128)(2,1)}) custom-call(bf16[1024,512]{1,0:T(8,128)(2,1)} %bitcast.22, bf16[3,512]{1,0:T(4,128)(2,1)} %bitcast.27, bf16[512,1536]{1,0:T(8,128)(2,1)} %bitcast.33, bf16[512,512]{1,0:T(8,128)(2,1)} %bitcast.42), custom_call_target="tpu_custom_call" | custom-call | flops 2147483648 | bytes 7340032 | tf_op jit(solution)/shard_map/own/pallas_call | solution.py:332
  18.7 0.0 collective-permute-done.2
  18.7 0.0 collective-permute-done.3
  18.8 3.2 %collective-permute-start.4 = (bf16[16,8,512]{2,1,0:T(8,128)(2,1)S(1)}, bf16[16,8,512]{2,1,0:T(8,128)(2,1)S(1)}, u32[]{:S(2)}, u32[]{:S(2)}) collective-permute-start(bf16[16,8,512]{2,1,0:T(8,128)(2,1)S(1)} %get-tuple-element.30), channel_id=1, source_target_pairs={{0,8},{8,16},{16,24},{24,32},{32,40},{40,48},{48,56},{56,0},{1,9},... | collective-permute-start | bytes 393224 | tf_op jit(solution)/shard_map/ppermute | solution.py:371
  21.9 0.0 collective-permute-start.5
  21.9 0.0 copy-start.1
  22.0 0.0 copy-start.9
  22.0 4.0 %cross_kv.1 = bf16[1024,1024]{1,0:T(8,128)(2,1)} custom-call(bf16[1024,512]{1,0:T(8,128)(2,1)} %bitcast.23, bf16[3,512]{1,0:T(4,128)(2,1)} %bitcast.28, bf16[512,1024]{1,0:T(8,128)(2,1)} %bitcast.41), custom_call_target="tpu_custom_call" | custom-call | flops 1073741824 | bytes 4194304 | tf_op jit(solution)/shard_map/cross_kv/pallas_call | solution.py:356
  25.9 0.3 collective-permute-done.4
  26.2 3.4 %collective-permute-done.5 = bf16[16,8,512]{2,1,0:T(8,128)(2,1)S(1)} collective-permute-done((bf16[16,8,512]{2,1,0:T(8,128)(2,1)S(1)}, bf16[16,8,512]{2,1,0:T(8,128)(2,1)S(1)}, u32[]{:S(2)}, u32[]{:S(2)}) %collective-permute-start.5) | collective-permute-done | bytes 131104 | tf_op jit(solution)/shard_map/ppermute | solution.py:372
  29.6 0.0 copy-start.7
  29.6 0.7 %copy-done.7 = bf16[16,8,512]{2,1,0:T(8,128)(2,1)} copy-done((bf16[16,8,512]{2,1,0:T(8,128)(2,1)}, bf16[16,8,512]{2,1,0:T(8,128)(2,1)S(1)}, u32[]{:S(2)}) %copy-start.7) | copy-done | bytes 131096
  30.3 0.0 collective-permute-done
  30.3 0.0 collective-permute-done.1
  30.3 1.9 %collective-permute-start.6 = (bf16[1024,1024]{1,0:T(8,128)(2,1)}, bf16[1024,1024]{1,0:T(8,128)(2,1)S(1)}, u32[]{:S(2)}, u32[]{:S(2)}) collective-permute-start(bf16[1024,1024]{1,0:T(8,128)(2,1)} %cross_kv.1), channel_id=1, source_target_pairs={{0,64},{64,0},{1,65},{65,1},{2,66},{66,2},{3,67},{67,3},{4,68},{68... | collective-permute-start | bytes 6291464 | tf_op jit(solution)/shard_map/ppermute | solution.py:376
  32.2 0.8 %copy.12.links_ref = s32[2,8,1,4]{3,2,1,0:T(1,128)S(1)} copy(s32[2,8,1,4]{1,3,2,0:T(4,128)} %param.20) | data formatting | bytes 512 | tf_op args[9]
  33.0 0.0 copy-done.1
  33.0 0.0 copy-done.9
  33.0 0.0 copy-start.4
  33.0 1.4 %copy-done.4 = bf16[1,512,1536]{2,1,0:T(8,128)(2,1)S(1)} copy-done((bf16[1,512,1536]{2,1,0:T(8,128)(2,1)S(1)}, bf16[1,512,1536]{2,1,0:T(8,128)(2,1)}, u32[]{:S(2)}) %copy-start.4) | copy-done | bytes 1572888
  34.4 0.0 copy-start.8
  34.4 0.9 %copy-done.8 = bf16[16,8,512]{2,1,0:T(8,128)(2,1)S(1)} copy-done((bf16[16,8,512]{2,1,0:T(8,128)(2,1)S(1)}, bf16[16,8,512]{2,1,0:T(8,128)(2,1)}, u32[]{:S(2)}) %copy-start.8) | copy-done | bytes 131096
  35.3 0.0 copy-start.11
  35.3 1.2 %copy-done.11 = bf16[1024,512]{1,0:T(8,128)(2,1)S(1)} copy-done((bf16[1024,512]{1,0:T(8,128)(2,1)S(1)}, bf16[1024,512]{1,0:T(8,128)(2,1)}, u32[]{:S(2)}) %copy-start.11) | copy-done | bytes 1048600
  36.5 0.0 copy-start.12
  36.5 1.2 %copy-done.12 = bf16[1024,512]{1,0:T(8,128)(2,1)S(1)} copy-done((bf16[1024,512]{1,0:T(8,128)(2,1)S(1)}, bf16[1024,512]{1,0:T(8,128)(2,1)}, u32[]{:S(2)}) %copy-start.12) | copy-done | bytes 1048600
  37.7 0.0 copy-start.13
  37.7 1.2 %copy-done.13 = bf16[512,1024]{1,0:T(8,128)(2,1)S(1)} copy-done((bf16[512,1024]{1,0:T(8,128)(2,1)S(1)}, bf16[512,1024]{1,0:T(8,128)(2,1)}, u32[]{:S(2)}) %copy-start.13) | copy-done | bytes 1048600
  38.9 0.0 copy-start
  38.9 0.0 copy-start.2
  39.0 0.0 copy-start.3
  39.0 0.0 copy-start.5
  39.0 0.0 copy-start.6
  39.0 0.0 copy-start.10
  39.0 9.1 %window.1.win_ref = bf16[512,1024]{1,0:T(8,128)(2,1)S(1)} custom-call(s32[8,8]{1,0:T(8,128)S(1)} %copy-done.9, bf16[128,512]{1,0:T(8,128)(2,1)S(1)} %bitcast.25, bf16[128,512]{1,0:T(8,128)(2,1)S(1)} %bitcast.26, bf16[512,512]{1,0:T(8,128)(2,1)S(1)} %bitcast.37, bf16[512,512]{1,0:T(8,128)(2,1)S(1)} %bitcast.38, bf16[128,512]{1,0:T(8,128)(2,1)S(1)} %bitcast.39, ...), custom_call_target="tpu_custom_call" | custom-call | flops 8589934592 | bytes 7340032 | tf_op jit(solution)/shard_map/window/pallas_call | solution.py:379
  48.1 0.0 collective-permute-done.6.kv_ref
  48.1 0.0 copy-done
  48.1 0.0 copy-done.2
  48.1 0.0 copy-done.3
  48.1 0.0 copy-done.5
  48.2 0.0 copy-done.6
  48.2 0.0 copy-done.10
  48.2 13.8 %cross.1 = bf16[1024,512]{1,0:T(8,128)(2,1)} custom-call(s32[2,8,1,4]{3,2,1,0:T(1,128)S(1)} %copy.12.links_ref, s32[8,8]{1,0:T(8,128)S(1)} %copy-done.9, bf16[1024,512]{1,0:T(8,128)(2,1)S(1)} %copy-done.10, bf16[1024,1024]{1,0:T(8,128)(2,1)S(1)} %collective-permute-done.6.kv_ref, bf16[512,1024]{1,0:T(8,128)(2,1)S(1)} %window.1.win_ref, ...), custom_call_target="tpu_custom_call" | custom-call | flops 10737418240 | bytes 11534336 | tf_op jit(solution)/shard_map/cross/pallas_call | solution.py:407
  (3 shorter events, 0.0 us)
Async XLA Ops:
  2.3 16.4 %collective-permute-start.2 = (bf16[8,16,512]{2,1,0:T(8,128)(2,1)S(1)}, bf16[8,16,512]{2,1,0:T(8,128)(2,1)S(1)}, u32[]{:S(2)}, u32[]{:S(2)}) collective-permute-start(bf16[8,16,512]{2,1,0:T(8,128)(2,1)S(1)} %get-tuple-element.27), channel_id=1, source_target_pairs={{0,1},{1,2},{2,3},{3,4},{4,5},{5,6},{6,7},{8,9},{9,10},{10,11},{11... | collective-permute-start | bytes 393224 | tf_op jit(solution)/shard_map/ppermute | solution.py:325
  5.4 13.3 %collective-permute-start.3 = (bf16[8,16,512]{2,1,0:T(8,128)(2,1)S(1)}, bf16[8,16,512]{2,1,0:T(8,128)(2,1)S(1)}, u32[]{:S(2)}, u32[]{:S(2)}) collective-permute-start(bf16[8,16,512]{2,1,0:T(8,128)(2,1)S(1)} %get-tuple-element.28), channel_id=1, source_target_pairs={{1,0},{2,1},{3,2},{4,3},{5,4},{6,5},{7,6},{9,8},{10,9},{11,10},{12... | collective-permute-start | bytes 393224 | tf_op jit(solution)/shard_map/ppermute | solution.py:326
  11.2 19.1 %collective-permute-start = (bf16[64,8,512]{2,1,0:T(8,128)(2,1)S(1)}, bf16[64,8,512]{2,1,0:T(8,128)(2,1)S(1)}, u32[]{:S(2)}, u32[]{:S(2)}) collective-permute-start(bf16[64,8,512]{2,1,0:T(8,128)(2,1)S(1)} %get-tuple-element.25), channel_id=1, source_target_pairs={{0,8},{8,16},{16,24},{24,32},{32,40},{40,48},{48,56},{56,0},{1,9},... | collective-permute-start | bytes 1572872 | tf_op jit(solution)/shard_map/ppermute | solution.py:323
  12.2 18.1 %collective-permute-start.1 = (bf16[64,8,512]{2,1,0:T(8,128)(2,1)S(1)}, bf16[64,8,512]{2,1,0:T(8,128)(2,1)S(1)}, u32[]{:S(2)}, u32[]{:S(2)}) collective-permute-start(bf16[64,8,512]{2,1,0:T(8,128)(2,1)S(1)} %get-tuple-element.26), channel_id=1, source_target_pairs={{8,0},{16,8},{24,16},{32,24},{40,32},{48,40},{56,48},{0,56},{9,1},... | collective-permute-start | bytes 1572872 | tf_op jit(solution)/shard_map/ppermute | solution.py:324
  18.8 7.5 %collective-permute-start.4 = (bf16[16,8,512]{2,1,0:T(8,128)(2,1)S(1)}, bf16[16,8,512]{2,1,0:T(8,128)(2,1)S(1)}, u32[]{:S(2)}, u32[]{:S(2)}) collective-permute-start(bf16[16,8,512]{2,1,0:T(8,128)(2,1)S(1)} %get-tuple-element.30), channel_id=1, source_target_pairs={{0,8},{8,16},{16,24},{24,32},{32,40},{40,48},{48,56},{56,0},{1,9},... | collective-permute-start | bytes 393224 | tf_op jit(solution)/shard_map/ppermute | solution.py:371
  21.9 7.7 %collective-permute-start.5 = (bf16[16,8,512]{2,1,0:T(8,128)(2,1)S(1)}, bf16[16,8,512]{2,1,0:T(8,128)(2,1)S(1)}, u32[]{:S(2)}, u32[]{:S(2)}) collective-permute-start(bf16[16,8,512]{2,1,0:T(8,128)(2,1)S(1)} %get-tuple-element.31), channel_id=1, source_target_pairs={{8,0},{16,8},{24,16},{32,24},{40,32},{48,40},{56,48},{0,56},{9,1},... | collective-permute-start | bytes 393224 | tf_op jit(solution)/shard_map/ppermute | solution.py:372
  21.9 11.0 %copy-start.1 = (bf16[1,3,512]{2,1,0:T(4,128)(2,1)S(1)}, bf16[1,3,512]{2,1,0:T(4,128)(2,1)}, u32[]{:S(2)}) copy-start(bf16[1,3,512]{2,1,0:T(4,128)(2,1)} %param.12) | copy-start | bytes 9220
  22.0 11.0 %copy-start.9 = (s32[8,8]{1,0:T(8,128)S(1)}, s32[8,8]{1,0:T(8,128)}, u32[]{:S(2)}) copy-start(s32[8,8]{1,0:T(8,128)} %land_ref.3) | copy-start | bytes 772
  29.6 0.7 %copy-start.7 = (bf16[16,8,512]{2,1,0:T(8,128)(2,1)}, bf16[16,8,512]{2,1,0:T(8,128)(2,1)S(1)}, u32[]{:S(2)}) copy-start(bf16[16,8,512]{2,1,0:T(8,128)(2,1)S(1)} %collective-permute-done.5) | copy-start | bytes 393220
  30.3 17.8 %collective-permute-start.6 = (bf16[1024,1024]{1,0:T(8,128)(2,1)}, bf16[1024,1024]{1,0:T(8,128)(2,1)S(1)}, u32[]{:S(2)}, u32[]{:S(2)}) collective-permute-start(bf16[1024,1024]{1,0:T(8,128)(2,1)} %cross_kv.1), channel_id=1, source_target_pairs={{0,64},{64,0},{1,65},{65,1},{2,66},{66,2},{3,67},{67,3},{4,68},{68... | collective-permute-start | bytes 6291464 | tf_op jit(solution)/shard_map/ppermute | solution.py:376
  33.0 1.4 %copy-start.4 = (bf16[1,512,1536]{2,1,0:T(8,128)(2,1)S(1)}, bf16[1,512,1536]{2,1,0:T(8,128)(2,1)}, u32[]{:S(2)}) copy-start(bf16[1,512,1536]{2,1,0:T(8,128)(2,1)} %param.13) | copy-start | bytes 4718596
  34.4 0.9 %copy-start.8 = (bf16[16,8,512]{2,1,0:T(8,128)(2,1)S(1)}, bf16[16,8,512]{2,1,0:T(8,128)(2,1)}, u32[]{:S(2)}) copy-start(bf16[16,8,512]{2,1,0:T(8,128)(2,1)} %copy-done.7) | copy-start | bytes 393220
  35.3 1.2 %copy-start.11 = (bf16[1024,512]{1,0:T(8,128)(2,1)S(1)}, bf16[1024,512]{1,0:T(8,128)(2,1)}, u32[]{:S(2)}) copy-start(bf16[1024,512]{1,0:T(8,128)(2,1)} %get-tuple-element.38.q_ref) | copy-start | bytes 3145732
  36.5 1.2 %copy-start.12 = (bf16[1024,512]{1,0:T(8,128)(2,1)S(1)}, bf16[1024,512]{1,0:T(8,128)(2,1)}, u32[]{:S(2)}) copy-start(bf16[1024,512]{1,0:T(8,128)(2,1)} %get-tuple-element.39.k_ref) | copy-start | bytes 3145732
  37.7 1.2 %copy-start.13 = (bf16[512,1024]{1,0:T(8,128)(2,1)S(1)}, bf16[512,1024]{1,0:T(8,128)(2,1)}, u32[]{:S(2)}) copy-start(bf16[512,1024]{1,0:T(8,128)(2,1)} %get-tuple-element.40.v_ref) | copy-start | bytes 3145732
  38.9 9.2 %copy-start = (bf16[1,64,16,512]{3,2,1,0:T(8,128)(2,1)S(1)}, bf16[1,64,16,512]{3,2,1,0:T(8,128)(2,1)}, u32[]{:S(2)}) copy-start(bf16[1,64,16,512]{3,2,1,0:T(8,128)(2,1)} %param.11) | copy-start | bytes 3145732
  38.9 9.2 %copy-start.2 = (bf16[1,512,2048]{2,1,0:T(8,128)(2,1)S(1)}, bf16[1,512,2048]{2,1,0:T(8,128)(2,1)}, u32[]{:S(2)}) copy-start(bf16[1,512,2048]{2,1,0:T(8,128)(2,1)} %param.18) | copy-start | bytes 6291460
  39.0 9.2 %copy-start.3 = (bf16[1,2048,512]{2,1,0:T(8,128)(2,1)S(1)}, bf16[1,2048,512]{2,1,0:T(8,128)(2,1)}, u32[]{:S(2)}) copy-start(bf16[1,2048,512]{2,1,0:T(8,128)(2,1)} %param.19) | copy-start | bytes 6291460
  39.0 9.2 %copy-start.5 = (bf16[1,512,512]{2,1,0:T(8,128)(2,1)S(1)}, bf16[1,512,512]{2,1,0:T(8,128)(2,1)}, u32[]{:S(2)}) copy-start(bf16[1,512,512]{2,1,0:T(8,128)(2,1)} %param.14) | copy-start | bytes 1572868
  39.0 9.2 %copy-start.6 = (bf16[1,512,512]{2,1,0:T(8,128)(2,1)S(1)}, bf16[1,512,512]{2,1,0:T(8,128)(2,1)}, u32[]{:S(2)}) copy-start(bf16[1,512,512]{2,1,0:T(8,128)(2,1)} %param.17) | copy-start | bytes 1572868
  39.0 9.2 %copy-start.10 = (bf16[1024,512]{1,0:T(8,128)(2,1)S(1)}, bf16[1024,512]{1,0:T(8,128)(2,1)}, u32[]{:S(2)}) copy-start(bf16[1024,512]{1,0:T(8,128)(2,1)} %get-tuple-element.24.q_ref) | copy-start | bytes 3145732

commit v5 on v4

v5 whole, which is shorter than its diff:
```python
import jax
import jax.numpy as jnp
from jax import lax
from jax.experimental import pallas as pl
from jax.experimental.pallas import tpu as pltpu
from jax.sharding import PartitionSpec as P

D = 512
FF = 2048
HEADS = 8
PAIRS = HEADS // 2
LANES = 128
RX = 16
BR = 8
NB = 8
KC = 4
CELLS = BR * RX
ROWS = NB * CELLS
SIDE = BR * BR
GROUP = CELLS + 2 * SIDE
WINDOW = 3 * GROUP
EXTRA = 16
VROWS = LANES + EXTRA

EPSILON = 1e-05
Q_SCALE = 1.4426950408889634 / 8.0
LIMIT = 2.0**100
BF = jnp.bfloat16
F32 = jnp.float32
MIB = 1 << 20


def norm_round(values, gain):
    mean_square = jnp.mean(values * values, axis=-1, keepdims=True)
    return (values * lax.rsqrt(mean_square + EPSILON) * gain.astype(F32)).astype(BF)


def mm(a, b):
    return jnp.dot(a, b, preferred_element_type=F32)


def mm_nt(a, b):
    return lax.dot_general(a, b, (((1,), (1,)), ((), ())), preferred_element_type=F32)


def mm_tn(a, b):
    return lax.dot_general(a, b, (((0,), (0,)), ((), ())), preferred_element_type=F32)


def mm_tt(a, b):
    return lax.dot_general(a, b, (((0,), (1,)), ((), ())), preferred_element_type=F32)


def augment(values_t, flag, out_ref, lane):
    keep = flag.astype(F32).astype(BF)
    for p in range(PAIRS):
        rows = values_t[p * LANES : (p + 1) * LANES]
        out_ref[pl.ds(p * VROWS, LANES), pl.ds(lane, CELLS)] = rows * keep
        out_ref[pl.ds(p * VROWS + LANES, EXTRA), pl.ds(lane, CELLS)] = (
            jnp.ones((EXTRA, CELLS), BF) * keep
        )


def score(pair, keys):
    low = lax.broadcasted_iota(jnp.int32, pair.shape, 1) < LANES // 2
    zero = jnp.zeros_like(pair)
    stacked = jnp.concatenate([jnp.where(low, pair, zero), jnp.where(low, zero, pair)], axis=0)
    return mm_nt(keys, stacked)


def blend(values_t, terms, extra):
    both = mm(values_t, terms)
    sums = both[LANES : LANES + 8]
    share = 1.0 / (sums + extra)
    half = LANES // 2
    result = jnp.concatenate(
        [both[:half, :CELLS] * share[:1, :CELLS], both[half:LANES, CELLS:] * share[:1, CELLS:]],
        axis=0,
    )
    return result.astype(BF), sums


def attention(queries, keys, values, penalties, out_ref, bad_ref):
    bad_ref[...] = jnp.zeros_like(bad_ref)

    def terms_of(i, p):
        return jnp.exp2(score(queries(i, p), keys(i, p))).astype(BF)

    steps = [(i, p) for i in range(NB) for p in range(PAIRS)]
    following = terms_of(*steps[0])
    for n, (i, p) in enumerate(steps):
        terms = following
        if n + 1 < len(steps):
            following = terms_of(*steps[n + 1])
        result, sums = blend(values(i, p), terms, 1.0)
        out_ref[pl.ds(p * LANES, LANES), pl.ds(i * CELLS, CELLS)] = result
        bad_ref[...] += jnp.where(sums < LIMIT, 0.0, 1.0)

    @pl.when(jnp.sum(bad_ref[...]) > 0.0)
    def _():
        def band(i, carry):
            lane = pl.multiple_of(i * CELLS, CELLS)
            for p in range(PAIRS):
                scores = score(queries(i, p), keys(i, p))
                at = 0
                pieces = []
                for rows, penalty in penalties(i):
                    pieces.append(scores[at : at + rows] + penalty)
                    at += rows
                scores = jnp.concatenate(pieces, axis=0)
                highest = jnp.maximum(jnp.max(scores, axis=0, keepdims=True), 0.0)
                terms = jnp.exp2(scores - highest).astype(BF)
                result, _ = blend(values(i, p), terms, jnp.exp2(-highest))
                out_ref[pl.ds(p * LANES, LANES), pl.ds(lane, CELLS)] = result
            return carry

        lax.fori_loop(0, NB, band, 0)


def aligned(i, size):
    return i * size if isinstance(i, int) else pl.multiple_of(i * size, size)


def start_all(sem, *moves):
    copies = [pltpu.make_async_copy(src, dst, sem.at[n]) for n, (src, dst) in enumerate(moves)]
    for copy in copies:
        copy.start()
    return copies


def wait_all(copies):
    for copy in copies:
        copy.wait()


def kernel_edges(x_hbm, west_hbm, east_hbm, north_hbm, south_hbm, sem):
    copies = start_all(
        sem,
        (x_hbm.at[:, pl.ds(0, BR)], west_hbm),
        (x_hbm.at[:, pl.ds(RX - BR, BR)], east_hbm),
        (x_hbm.at[pl.ds(0, BR)], north_hbm),
        (x_hbm.at[pl.ds(NB * BR - BR, BR)], south_hbm),
    )
    wait_all(copies)


def normed_rows(copies, x_ref, gain, out_ref):
    half = ROWS // 2
    for h in range(2):
        copies[h].wait()
        at = slice(h * half, (h + 1) * half)
        out_ref[at, :] = norm_round(x_ref[at, :].astype(F32), gain)


def halves(src, dst, size):
    return [(src.at[pl.ds(h * size, size)], dst.at[pl.ds(h * size, size)]) for h in range(2)]


def kernel_own(gain_ref, x_hbm, qkv_hbm, own_hbm, x_ref, qkv_ref, rows_ref, own_ref, sem, out_sem):
    half = ROWS // 2
    parts = [(qkv_hbm.at[:, pl.ds(n * D, D)], qkv_ref.at[:, pl.ds(n * D, D)]) for n in range(3)]
    copies = start_all(sem, *halves(x_hbm, x_ref, half), *parts)
    normed_rows(copies, x_ref, gain_ref[0:1, :], rows_ref)
    leaving = []

    def leave(n):
        at = pl.ds(n * ROWS, ROWS)
        copy = pltpu.make_async_copy(own_ref.at[at], own_hbm.at[at], out_sem.at[n])
        copy.start()
        leaving.append(copy)

    copies[2].wait()
    own_ref[:ROWS, :] = (mm(rows_ref[...], qkv_ref[:, :D]) * Q_SCALE).astype(BF)
    leave(0)
    copies[3].wait()
    own_ref[ROWS : 2 * ROWS, :] = mm(rows_ref[...], qkv_ref[:, D : 2 * D]).astype(BF)
    leave(1)
    copies[4].wait()
    for h in range(2):
        at = slice(2 * ROWS + h * half, 2 * ROWS + (h + 1) * half)
        rows = rows_ref[h * half : (h + 1) * half, :]
        own_ref[at, :] = mm_tt(qkv_ref[:, 2 * D :], rows).astype(BF)
    leave(2)
    wait_all(leaving)


def kernel_pair(gain_ref, x_hbm, ckv_hbm, cq_hbm, query_hbm, pair_hbm, x_ref, w_ref, rows_ref, own_ref, sem, out_sem):
    half = ROWS // 2
    parts = [(ckv_hbm.at[:, pl.ds(n * D, D)], w_ref.at[:, pl.ds(n * D, D)]) for n in range(2)]
    copies = start_all(
        sem, *halves(x_hbm, x_ref, half), *parts, (cq_hbm, w_ref.at[:, pl.ds(2 * D, D)])
    )
    normed_rows(copies, x_ref, gain_ref[1:2, :], rows_ref)
    leaving = []

    def leave(n, src, dst):
        copy = pltpu.make_async_copy(src, dst, out_sem.at[n])
        copy.start()
        leaving.append(copy)

    copies[2].wait()
    own_ref[:ROWS, :] = mm(rows_ref[...], w_ref[:, :D]).astype(BF)
    leave(0, own_ref.at[pl.ds(0, ROWS)], pair_hbm.at[pl.ds(0, ROWS)])
    copies[3].wait()
    for h in range(2):
        at = slice(ROWS + h * half, ROWS + (h + 1) * half)
        rows = rows_ref[h * half : (h + 1) * half, :]
        own_ref[at, :] = mm_tt(w_ref[:, D : 2 * D], rows).astype(BF)
    leave(1, own_ref.at[pl.ds(ROWS, ROWS)], pair_hbm.at[pl.ds(ROWS, ROWS)])
    copies[4].wait()
    own_ref[2 * ROWS :, :] = (mm(rows_ref[...], w_ref[:, 2 * D :]) * Q_SCALE).astype(BF)
    leave(2, own_ref.at[pl.ds(2 * ROWS, ROWS)], query_hbm)
    wait_all(leaving)


def kernel_window(
    land_ref,
    gain_ref,
    own_hbm,
    north_hbm,
    south_hbm,
    west_hbm,
    east_hbm,
    corner_west_hbm,
    corner_east_hbm,
    qkv_hbm,
    win_hbm,
    keys_ref,
    va_ref,
    win_ref,
    bad_ref,
    qkv_ref,
    sides_ref,
    polar_ref,
    q_ref,
    v_ref,
    sem,
    out_sem,
):
    bands = NB + 2
    left, right = pl.ds(0, SIDE), pl.ds(SIDE, SIDE)
    copies = start_all(
        sem,
        (west_hbm, sides_ref.at[pl.ds(1, NB), left]),
        (east_hbm, sides_ref.at[pl.ds(1, NB), right]),
        (corner_west_hbm.at[pl.ds(0, 1)], sides_ref.at[pl.ds(0, 1), left]),
        (corner_east_hbm.at[pl.ds(0, 1)], sides_ref.at[pl.ds(0, 1), right]),
        (corner_west_hbm.at[pl.ds(1, 1)], sides_ref.at[pl.ds(NB + 1, 1), left]),
        (corner_east_hbm.at[pl.ds(1, 1)], sides_ref.at[pl.ds(NB + 1, 1), right]),
        (qkv_hbm.at[:, pl.ds(D, 2 * D)], qkv_ref),
        (north_hbm, polar_ref.at[pl.ds(0, 1)]),
        (south_hbm, polar_ref.at[pl.ds(1, 1)]),
        (own_hbm.at[pl.ds(2 * NB, NB)], v_ref),
        (own_hbm.at[pl.ds(NB, NB)], keys_ref.at[pl.ds(1, NB), pl.ds(0, CELLS)]),
        (own_hbm.at[pl.ds(0, NB)], q_ref),
    )
    is_air = lax.axis_index("comp") == 0
    tile_row = lax.axis_index("tile")
    tile_col = lax.axis_index("face")
    columns = (tile_col, (tile_col + 7) % 8, (tile_col + 1) % 8)

    def flags(r):
        inside_row = jnp.where(r == 0, tile_row - 1, jnp.where(r == NB + 1, tile_row + 1, tile_row))
        lat_ok = (inside_row >= 0) & (inside_row < 8)
        safe_row = jnp.clip(inside_row, 0, 7)
        index = jnp.where(r == 0, NB - 1, jnp.where(r == NB + 1, 0, r - 1))
        return [lat_ok & (is_air | (index >= land_ref[safe_row, c])) for c in columns]

    def project(rows_x):
        normed = norm_round(rows_x.astype(F32), gain_ref[0:1, :])
        keys = mm(normed, qkv_ref[:, :D]).astype(BF)
        return keys, mm_tt(qkv_ref[:, D:], normed).astype(BF)

    west_lane = lax.broadcasted_iota(jnp.int32, (1, CELLS), 1) < SIDE
    wait_all(copies[:7])
    blocks = 2
    for b in range(blocks):
        members = range(b * bands // blocks, (b + 1) * bands // blocks)
        keys, values_t = project(sides_ref[members[0] : members[-1] + 1].reshape(-1, D))
        for n, r in enumerate(members):
            _, west_ok, east_ok = flags(r)
            at = slice(n * CELLS, (n + 1) * CELLS)
            keys_ref[r, CELLS:, :] = keys[at]
            flag = jnp.where(west_lane, west_ok.astype(F32), east_ok.astype(F32))
            augment(values_t[:, at], flag, va_ref, r * GROUP + CELLS)
    wait_all(copies[7:10])
    keys, values_t = project(polar_ref[...].reshape(2 * CELLS, D))
    for n, r in enumerate((0, bands - 1)):
        at = slice(n * CELLS, (n + 1) * CELLS)
        keys_ref[r, :CELLS, :] = keys[at]
        augment(values_t[:, at], flags(r)[0], va_ref, r * GROUP)
    for i in range(NB):
        rows = v_ref[i // 4 * 4 : i // 4 * 4 + 4, :, i % 4 * CELLS : (i % 4 + 1) * CELLS]
        augment(rows.reshape(D, CELLS), flags(i + 1)[0], va_ref, (i + 1) * GROUP)
    wait_all(copies[10:])

    def queries(i, p):
        return q_ref[i, :, pl.ds(p * LANES, LANES)]

    def keys_of(i, p):
        return keys_ref[pl.ds(i, 3), :, pl.ds(p * LANES, LANES)].reshape(WINDOW, LANES)

    def values_of(i, p):
        return va_ref[pl.ds(p * VROWS, VROWS), pl.ds(aligned(i, GROUP), WINDOW)]

    def penalties(i):
        pieces = []
        for b in range(3):
            for rows, flag in zip((CELLS, SIDE, SIDE), flags(i + b)):
                pieces.append((rows, jnp.where(flag, 0.0, -1e30)))
        return pieces

    attention(queries, keys_of, values_of, penalties, win_ref, bad_ref)
    copy = pltpu.make_async_copy(win_ref, win_hbm, out_sem)
    copy.start()
    copy.wait()


def kernel_cross(
    links_ref,
    land_ref,
    gain_ref,
    pair_hbm,
    q_hbm,
    win_hbm,
    x_hbm,
    out_w_hbm,
    cross_w_hbm,
    up_hbm,
    down_hbm,
    out_hbm,
    cross_ref,
    va_ref,
    bad_ref,
    pair_ref,
    q_ref,
    win_ref,
    x_ref,
    out_w_ref,
    cross_w_ref,
    up_ref,
    down_ref,
    out_ref,
    sem,
    out_sem,
):
    half = ROWS // 2
    copies = start_all(
        sem,
        (q_hbm, q_ref),
        *halves(pair_hbm, pair_ref, ROWS),
        (out_w_hbm, out_w_ref),
        (cross_w_hbm, cross_w_ref),
        (win_hbm, win_ref),
        (x_hbm, x_ref),
        (up_hbm, up_ref),
        (down_hbm, down_ref),
    )
    component = lax.axis_index("comp")
    own_land = land_ref[lax.axis_index("tile"), lax.axis_index("face")]
    floor = jnp.where(component == 1, 0, own_land)
    wait_all(copies[:3])
    for j in range(NB):
        row, lane = ROWS + (j // 4) * D, (j % 4) * CELLS
        augment(pair_ref[row : row + D, lane : lane + CELLS], j >= floor, va_ref, j * CELLS)

    def picks(i):
        return [links_ref[component, k, i] for k in range(KC)]

    def queries(i, p):
        return q_ref[pl.ds(aligned(i, CELLS), CELLS), pl.ds(p * LANES, LANES)]

    def keys(i, p):
        return jnp.concatenate(
            [pair_ref[pl.ds(aligned(j, CELLS), CELLS), pl.ds(p * LANES, LANES)] for j in picks(i)],
            axis=0,
        )

    def values(i, p):
        return jnp.concatenate(
            [va_ref[pl.ds(p * VROWS, VROWS), pl.ds(aligned(j, CELLS), CELLS)] for j in picks(i)],
            axis=1,
        )

    def penalties(i):
        return [(CELLS, jnp.where(j >= floor, 0.0, -1e30)) for j in picks(i)]

    attention(queries, keys, values, penalties, cross_ref, bad_ref)
    wait_all(copies[3:])
    leaving = []
    is_air = component == 0
    for c in range(2):
        at = slice(c * half, (c + 1) * half)
        index = (c * half + lax.broadcasted_iota(jnp.int32, (half, 1), 0)) // CELLS
        live = jnp.where(is_air | (index >= own_land), 1.0, 0.0)
        update = mm_tn(win_ref[:, at], out_w_ref[...]) + mm_tn(cross_ref[:, at], cross_w_ref[...])
        middle = x_ref[at, :].astype(F32) + live * update
        mlp_input = norm_round(middle, gain_ref[2:3, :])
        gate = 0.5 * mm(mlp_input, up_ref[...])
        hidden = (gate + gate * jnp.tanh(gate)).astype(BF)
        out_ref[at, :] = (middle + live * mm(hidden, down_ref[...])).astype(BF)
        rows = pl.ds(c * half, half)
        copy = pltpu.make_async_copy(out_ref.at[rows], out_hbm.at[rows], out_sem.at[c])
        copy.start()
        leaving.append(copy)
    wait_all(leaving)


VMEM = pl.BlockSpec(memory_space=pltpu.VMEM)
ANY = pl.BlockSpec(memory_space=pl.ANY)
HBM = pl.BlockSpec(memory_space=pltpu.HBM)
SMEM = pl.BlockSpec(memory_space=pltpu.SMEM)


def array(*shape):
    return jax.ShapeDtypeStruct(shape, BF)


def vmem(*shape):
    return pltpu.VMEM(shape, BF)


def cost(macs, size, exps=0):
    return pl.CostEstimate(flops=2 * macs, bytes_accessed=size, transcendentals=exps)


def per_device(
    tokens,
    norm_gains,
    qkv_weight,
    out_weight,
    cross_query,
    cross_kv,
    cross_out,
    up_weight,
    down_weight,
    intersection_list,
    land_bands,
):
    grid_x = tokens[0]
    x = grid_x.reshape(ROWS, D)
    gains = norm_gains[0]
    up_ring = [(i, i + 1) for i in range(7)]
    down_ring = [(i + 1, i) for i in range(7)]
    east_ring = [(i, (i + 1) % 8) for i in range(8)]
    west_ring = [((i + 1) % 8, i) for i in range(8)]

    params = pltpu.CompilerParams(vmem_limit_bytes=60 * MIB)
    dma = pltpu.SemaphoreType.DMA
    tall, wide = array(NB * BR, BR, D), array(BR, RX, D)
    edges = pl.pallas_call(
        kernel_edges,
        in_specs=[HBM],
        out_specs=[HBM] * 4,
        out_shape=[tall, tall, wide, wide],
        scratch_shapes=[dma((4,))],
        compiler_params=params,
        name="edges",
    )(grid_x)
    west_edge, east_edge, top, bottom, x_first = lax.optimization_barrier((*edges, x))
    west = lax.ppermute(east_edge, "face", east_ring)
    east = lax.ppermute(west_edge, "face", west_ring)
    north = lax.ppermute(bottom, "tile", up_ring)
    south = lax.ppermute(top, "tile", down_ring)

    own = pl.pallas_call(
        kernel_own,
        in_specs=[VMEM] + [HBM] * 2,
        out_specs=HBM,
        out_shape=array(3 * ROWS, D),
        scratch_shapes=[vmem(ROWS, D), vmem(D, 3 * D), vmem(ROWS, D), vmem(3 * ROWS, D), dma((5,)), dma((3,))],
        cost_estimate=cost(ROWS * D * 3 * D, 6 * MIB),
        compiler_params=params,
        name="own",
    )(gains, x_first, qkv_weight[0])

    west_corner, east_corner = [
        jnp.concatenate([north[:, cut], south[:, cut]], axis=0)
        for cut in (slice(0, BR), slice(RX - BR, RX))
    ]
    west_corner, east_corner, own, x_second = lax.optimization_barrier(
        (west_corner, east_corner, own, x)
    )
    corner_west = lax.ppermute(east_corner, "face", east_ring)
    corner_east = lax.ppermute(west_corner, "face", west_ring)

    cross_q, pair_out = pl.pallas_call(
        kernel_pair,
        in_specs=[VMEM] + [HBM] * 3,
        out_specs=[HBM] * 2,
        out_shape=[array(ROWS, D), array(2 * ROWS, D)],
        scratch_shapes=[vmem(ROWS, D), vmem(D, 3 * D), vmem(ROWS, D), vmem(3 * ROWS, D), dma((5,)), dma((3,))],
        cost_estimate=cost(ROWS * D * 3 * D, 6 * MIB),
        compiler_params=params,
        name="pair",
    )(gains, x_second, cross_kv[0], cross_query[0])

    west, east, corner_west, corner_east, pair_out = lax.optimization_barrier(
        (west, east, corner_west, corner_east, pair_out)
    )
    partner = lax.ppermute(pair_out, "comp", [(0, 1), (1, 0)])

    window = pl.pallas_call(
        kernel_window,
        in_specs=[SMEM] + [VMEM, HBM] + [ANY] * 6 + [HBM],
        out_specs=HBM,
        out_shape=array(D, ROWS),
        scratch_shapes=[
            vmem(NB + 2, GROUP, D),
            vmem(PAIRS * VROWS, (NB + 2) * GROUP),
            vmem(D, ROWS),
            pltpu.VMEM((8, 2 * CELLS), F32),
            vmem(D, 2 * D),
            vmem(NB + 2, 2 * SIDE, D),
            vmem(2, CELLS, D),
            vmem(NB, CELLS, D),
            vmem(NB, CELLS, D),
            dma((12,)),
            dma,
        ],
        cost_estimate=cost(4 << 30, 7 * MIB, ROWS * HEADS * WINDOW),
        compiler_params=params,
        name="window",
    )(
        land_bands,
        gains,
        own.reshape(3 * NB, CELLS, D),
        north.reshape(1, CELLS, D),
        south.reshape(1, CELLS, D),
        west.reshape(NB, SIDE, D),
        east.reshape(NB, SIDE, D),
        corner_west.reshape(2, SIDE, D),
        corner_east.reshape(2, SIDE, D),
        qkv_weight[0],
    )

    result = pl.pallas_call(
        kernel_cross,
        in_specs=[SMEM] * 2 + [VMEM, ANY] + [HBM] * 7,
        out_specs=HBM,
        out_shape=array(ROWS, D),
        scratch_shapes=[
            vmem(D, ROWS),
            vmem(PAIRS * VROWS, ROWS),
            pltpu.VMEM((8, 2 * CELLS), F32),
            vmem(2 * ROWS, D),
            vmem(ROWS, D),
            vmem(D, ROWS),
            vmem(ROWS, D),
            vmem(D, D),
            vmem(D, D),
            vmem(D, FF),
            vmem(FF, D),
            vmem(ROWS, D),
            dma((9,)),
            dma((2,)),
        ],
        cost_estimate=cost(5 << 30, 11 * MIB, ROWS * HEADS * 512),
        compiler_params=params,
        name="cross",
    )(
        intersection_list.transpose(0, 2, 3, 1).reshape(2, KC, NB),
        land_bands,
        gains,
        partner,
        cross_q,
        window,
        x,
        out_weight[0],
        cross_out[0],
        up_weight[0],
        down_weight[0],
    )
    return result.reshape(1, NB * BR, RX, D)


def solution(mesh):
    placed = (
        P("comp", "tile", "face", None),
        P("comp", None, None),
        P("comp", None, None),
        P("comp", None, None),
        P("comp", None, None),
        P("comp", None, None),
        P("comp", None, None),
        P("comp", None, None),
        P("comp", None, None),
        P(None, "tile", "face", None),
        P(),
    )
    return jax.shard_map(
        per_device,
        mesh=mesh,
        in_specs=placed,
        out_specs=P("comp", "tile", "face", None),
        check_vma=False,
    )
```

time: 62.5 us -> 101 us (1.62)
  the two profiles are of different devices: /device:TPU:89 before, /device:TPU:6 now
where the time goes in v5:
time: 101 us
  Pallas kernels  80 us (79%)
  starting transfers between devices  16.3 us (16%)
  local copies, waits for them, and re-layouts  2.07 us (2%)
  waiting for transfers between devices  1.96 us (2%)
    pallas_call x1, Pallas kernels, per_device(): pl.pallas_call(kernel_edges, in_specs=[HBM], out_specs=[HBM] * 4, out_sha...  40.8 us
    pallas_call x1, Pallas kernels, per_device(): pl.pallas_call(kernel_cross, in_specs=[SMEM] * 2 + [VMEM, ANY] + [HBM] *...  15.6 us
    pallas_call x1, Pallas kernels, per_device(): pl.pallas_call(kernel_window, in_specs=[SMEM] + [VMEM, HBM] + [ANY] * 6 +...  12.8 us
    ppermute x1, starting transfers between devices, per_device(): north = lax.ppermute(bottom, 'tile', up_ring)  5.7 us
    pallas_call x1, Pallas kernels, per_device(): pl.pallas_call(kernel_pair, in_specs=[VMEM] + [HBM] * 3, out_specs=[HBM]...  5.37 us
    pallas_call x1, Pallas kernels, per_device(): pl.pallas_call(kernel_own, in_specs=[VMEM] + [HBM] * 2, out_specs=HBM, ou...  5.34 us
    ppermute x1, starting transfers between devices, per_device(): corner_east = lax.ppermute(west_corner, 'face', west_ring)  4.12 us
    ppermute x1, starting transfers between devices, per_device(): east = lax.ppermute(west_edge, 'face', west_ring)  2.56 us
  transfers between devices with their start and end apart: 7, of which 1 were waited for; matrix products, arithmetic and copies ran while one was open for 0% of the time, Pallas kernels for 23%

profile of v5, /device:TPU:6, one launch (start us, length us, event | category | flops | bytes accessed | tf_op | source)
XLA Modules:
  0.0 100.7 jit_solution(4584261996722058868)
XLA Ops:
  0.0 40.8 %edges.1 = (bf16[64,8,512]{2,1,0:T(8,128)(2,1)}, bf16[64,8,512]{2,1,0:T(8,128)(2,1)}, bf16[8,16,512]{2,1,0:T(8,128)(2,1)}, bf16[8,16,512]{2,1,0:T(8,128)(2,1)}) custom-call(bf16[64,16,512]{2,1,0:T(8,128)(2,1)} %bitcast.21), custom_call_target="tpu_custom_call" | custom-call | tf_op jit(solution)/shard_map/edges/pallas_call | solution.py:451
  40.8 5.7 %collective-permute-start.2 = (bf16[8,16,512]{2,1,0:T(8,128)(2,1)}, bf16[8,16,512]{2,1,0:T(8,128)(2,1)S(1)}, u32[]{:S(2)}, u32[]{:S(2)}) collective-permute-start(bf16[8,16,512]{2,1,0:T(8,128)(2,1)} %get-tuple-element.31), channel_id=1, source_target_pairs={{0,1},{1,2},{2,3},{3,4},{4,5},{5,6},{6,7},{8,9},{9,10},{10,11},{11... | collective-permute-start | bytes 393224 | tf_op jit(solution)/shard_map/ppermute | solution.py:463
  46.6 1.9 %collective-permute-start.3 = (bf16[8,16,512]{2,1,0:T(8,128)(2,1)}, bf16[8,16,512]{2,1,0:T(8,128)(2,1)S(1)}, u32[]{:S(2)}, u32[]{:S(2)}) collective-permute-start(bf16[8,16,512]{2,1,0:T(8,128)(2,1)} %get-tuple-element.32), channel_id=1, source_target_pairs={{1,0},{2,1},{3,2},{4,3},{5,4},{6,5},{7,6},{9,8},{10,9},{11,10},{12... | collective-permute-start | bytes 393224 | tf_op jit(solution)/shard_map/ppermute | solution.py:464
  48.5 1.6 %collective-permute-start = (bf16[64,8,512]{2,1,0:T(8,128)(2,1)}, bf16[64,8,512]{2,1,0:T(8,128)(2,1)S(1)}, u32[]{:S(2)}, u32[]{:S(2)}) collective-permute-start(bf16[64,8,512]{2,1,0:T(8,128)(2,1)} %get-tuple-element.29), channel_id=1, source_target_pairs={{0,8},{8,16},{16,24},{24,32},{32,40},{40,48},{48,56},{56,0},{1,9},... | collective-permute-start | bytes 1572872 | tf_op jit(solution)/shard_map/ppermute | solution.py:461
  50.1 2.6 %collective-permute-start.1 = (bf16[64,8,512]{2,1,0:T(8,128)(2,1)}, bf16[64,8,512]{2,1,0:T(8,128)(2,1)S(1)}, u32[]{:S(2)}, u32[]{:S(2)}) collective-permute-start(bf16[64,8,512]{2,1,0:T(8,128)(2,1)} %get-tuple-element.30), channel_id=1, source_target_pairs={{8,0},{16,8},{24,16},{32,24},{40,32},{48,40},{56,48},{0,56},{9,1},... | collective-permute-start | bytes 1572872 | tf_op jit(solution)/shard_map/ppermute | solution.py:462
  52.7 5.3 %own.1 = bf16[3072,512]{1,0:T(8,128)(2,1)} custom-call(bf16[3,512]{1,0:T(4,128)(2,1)} %bitcast.40, bf16[1024,512]{1,0:T(8,128)(2,1)} %bitcast.22, bf16[512,1536]{1,0:T(8,128)(2,1)} %bitcast.29), custom_call_target="tpu_custom_call" | custom-call | flops 1610612736 | bytes 6291456 | tf_op jit(solution)/shard_map/own/pallas_call | solution.py:466
  58.0 0.0 collective-permute-done.2
  58.0 0.0 copy-start
  58.1 1.9 %collective-permute-done.3 = bf16[8,16,512]{2,1,0:T(8,128)(2,1)S(1)} collective-permute-done((bf16[8,16,512]{2,1,0:T(8,128)(2,1)}, bf16[8,16,512]{2,1,0:T(8,128)(2,1)S(1)}, u32[]{:S(2)}, u32[]{:S(2)}) %collective-permute-start.3) | collective-permute-done | bytes 131104 | tf_op jit(solution)/shard_map/ppermute | solution.py:464
  60.0 0.0 copy-start.1
  60.1 0.1 collective-permute-start.4
  60.1 4.1 %collective-permute-start.5 = (bf16[16,8,512]{2,1,0:T(8,128)(2,1)S(1)}, bf16[16,8,512]{2,1,0:T(8,128)(2,1)S(1)}, u32[]{:S(2)}, u32[]{:S(2)}) collective-permute-start(bf16[16,8,512]{2,1,0:T(8,128)(2,1)S(1)} %get-tuple-element.35), channel_id=1, source_target_pairs={{8,0},{16,8},{24,16},{32,24},{40,32},{48,40},{56,48},{0,56},{9,1},... | collective-permute-start | bytes 393224 | tf_op jit(solution)/shard_map/ppermute | solution.py:485
  64.3 5.4 %pair.1 = (bf16[1024,512]{1,0:T(8,128)(2,1)}, bf16[2048,512]{1,0:T(8,128)(2,1)}) custom-call(bf16[3,512]{1,0:T(4,128)(2,1)} %bitcast.41, bf16[1024,512]{1,0:T(8,128)(2,1)} %bitcast.23, bf16[512,1024]{1,0:T(8,128)(2,1)} %bitcast.31, bf16[512,512]{1,0:T(8,128)(2,1)} %bitcast.32), custom_call_target="tpu_custom_call" | custom-call | flops 1610612736 | bytes 6291456 | tf_op jit(solution)/shard_map/pair/pallas_call | solution.py:487
  69.6 0.0 copy-done
  69.7 0.0 copy-done.1
  69.7 0.0 collective-permute-done.4
  69.7 0.0 copy-start.5
  69.7 0.0 collective-permute-done.5
  69.7 0.0 copy-start.6
  69.7 0.0 collective-permute-done
  69.7 0.0 copy-start.3
  69.7 0.0 collective-permute-done.1
  69.7 0.0 copy-start.4
  69.7 0.3 collective-permute-start.6
  70.0 0.3 copy-done.5
  70.3 0.1 copy-done.6
  70.4 0.2 copy-done.3
  70.6 0.1 copy-done.4
  70.7 12.8 %window.1.win_hbm = bf16[512,1024]{1,0:T(8,128)(2,1)} custom-call(s32[8,8]{1,0:T(8,128)} %land_ref.3, bf16[3,512]{1,0:T(4,128)(2,1)} %bitcast.42, bf16[24,128,512]{2,1,0:T(8,128)(2,1)} %bitcast.44, bf16[1,128,512]{2,1,0:T(8,128)(2,1)} %bitcast.25, bf16[1,128,512]{2,1,0:T(8,128)(2,1)} %bitcast.26, bf16[8,64,512]{2,1,0:T(8,128)(2,1)} %bitcast.35, ...), custom_call_target="tpu_custom_call" | custom-call | flops 8589934592 | bytes 7340032 | tf_op jit(solution)/shard_map/window/pallas_call | solution.py:503
  83.5 0.0 collective-permute-done.6.pair_hbm
  83.6 0.0 copy-start.2
  83.6 1.3 %copy-done.2 = bf16[2048,512]{1,0:T(8,128)(2,1)} copy-done((bf16[2048,512]{1,0:T(8,128)(2,1)}, bf16[2048,512]{1,0:T(8,128)(2,1)S(1)}, u32[]{:S(2)}) %copy-start.2) | copy-done | bytes 2097176
  84.9 15.6 %cross.1 = bf16[1024,512]{1,0:T(8,128)(2,1)} custom-call(s32[2,4,8]{2,1,0:T(4,128)} %bitcast.39, s32[8,8]{1,0:T(8,128)} %land_ref.3, bf16[3,512]{1,0:T(4,128)(2,1)} %bitcast.43, bf16[2048,512]{1,0:T(8,128)(2,1)} %copy-done.2, bf16[1024,512]{1,0:T(8,128)(2,1)} %get-tuple-element.39.q_hbm, bf16[512,1024]{1,0:T(8,128)(2,1)} %window.1.win_hbm, ...), custom_call_target="tpu_custom_call" | custom-call | flops 10737418240 | bytes 11534336 | tf_op jit(solution)/shard_map/cross/pallas_call | solution.py:537
  (3 shorter events, 0.0 us)
Async XLA Ops:
  40.8 17.2 %collective-permute-start.2 = (bf16[8,16,512]{2,1,0:T(8,128)(2,1)}, bf16[8,16,512]{2,1,0:T(8,128)(2,1)S(1)}, u32[]{:S(2)}, u32[]{:S(2)}) collective-permute-start(bf16[8,16,512]{2,1,0:T(8,128)(2,1)} %get-tuple-element.31), channel_id=1, source_target_pairs={{0,1},{1,2},{2,3},{3,4},{4,5},{5,6},{6,7},{8,9},{9,10},{10,11},{11... | collective-permute-start | bytes 393224 | tf_op jit(solution)/shard_map/ppermute | solution.py:463
  46.6 13.5 %collective-permute-start.3 = (bf16[8,16,512]{2,1,0:T(8,128)(2,1)}, bf16[8,16,512]{2,1,0:T(8,128)(2,1)S(1)}, u32[]{:S(2)}, u32[]{:S(2)}) collective-permute-start(bf16[8,16,512]{2,1,0:T(8,128)(2,1)} %get-tuple-element.32), channel_id=1, source_target_pairs={{1,0},{2,1},{3,2},{4,3},{5,4},{6,5},{7,6},{9,8},{10,9},{11,10},{12... | collective-permute-start | bytes 393224 | tf_op jit(solution)/shard_map/ppermute | solution.py:464
  48.5 21.2 %collective-permute-start = (bf16[64,8,512]{2,1,0:T(8,128)(2,1)}, bf16[64,8,512]{2,1,0:T(8,128)(2,1)S(1)}, u32[]{:S(2)}, u32[]{:S(2)}) collective-permute-start(bf16[64,8,512]{2,1,0:T(8,128)(2,1)} %get-tuple-element.29), channel_id=1, source_target_pairs={{0,8},{8,16},{16,24},{24,32},{32,40},{40,48},{48,56},{56,0},{1,9},... | collective-permute-start | bytes 1572872 | tf_op jit(solution)/shard_map/ppermute | solution.py:461
  50.1 19.6 %collective-permute-start.1 = (bf16[64,8,512]{2,1,0:T(8,128)(2,1)}, bf16[64,8,512]{2,1,0:T(8,128)(2,1)S(1)}, u32[]{:S(2)}, u32[]{:S(2)}) collective-permute-start(bf16[64,8,512]{2,1,0:T(8,128)(2,1)} %get-tuple-element.30), channel_id=1, source_target_pairs={{8,0},{16,8},{24,16},{32,24},{40,32},{48,40},{56,48},{0,56},{9,1},... | collective-permute-start | bytes 1572872 | tf_op jit(solution)/shard_map/ppermute | solution.py:462
  58.0 11.6 %copy-start = (bf16[8,16,512]{2,1,0:T(8,128)(2,1)}, bf16[8,16,512]{2,1,0:T(8,128)(2,1)S(1)}, u32[]{:S(2)}) copy-start(bf16[8,16,512]{2,1,0:T(8,128)(2,1)S(1)} %collective-permute-done.2) | copy-start | bytes 393220
  60.0 9.6 %copy-start.1 = (bf16[8,16,512]{2,1,0:T(8,128)(2,1)}, bf16[8,16,512]{2,1,0:T(8,128)(2,1)S(1)}, u32[]{:S(2)}) copy-start(bf16[8,16,512]{2,1,0:T(8,128)(2,1)S(1)} %collective-permute-done.3) | copy-start | bytes 393220
  60.1 9.6 %collective-permute-start.4 = (bf16[16,8,512]{2,1,0:T(8,128)(2,1)S(1)}, bf16[16,8,512]{2,1,0:T(8,128)(2,1)S(1)}, u32[]{:S(2)}, u32[]{:S(2)}) collective-permute-start(bf16[16,8,512]{2,1,0:T(8,128)(2,1)S(1)} %get-tuple-element.34), channel_id=1, source_target_pairs={{0,8},{8,16},{16,24},{24,32},{32,40},{40,48},{48,56},{56,0},{1,9},... | collective-permute-start | bytes 393224 | tf_op jit(solution)/shard_map/ppermute | solution.py:484
  60.1 9.5 %collective-permute-start.5 = (bf16[16,8,512]{2,1,0:T(8,128)(2,1)S(1)}, bf16[16,8,512]{2,1,0:T(8,128)(2,1)S(1)}, u32[]{:S(2)}, u32[]{:S(2)}) collective-permute-start(bf16[16,8,512]{2,1,0:T(8,128)(2,1)S(1)} %get-tuple-element.35), channel_id=1, source_target_pairs={{8,0},{16,8},{24,16},{32,24},{40,32},{48,40},{56,48},{0,56},{9,1},... | collective-permute-start | bytes 393224 | tf_op jit(solution)/shard_map/ppermute | solution.py:485
  69.7 0.7 copy-start.5
  69.7 0.7 copy-start.6
  69.7 0.9 copy-start.3
  69.7 1.0 copy-start.4
  69.7 13.8 %collective-permute-start.6 = (bf16[2048,512]{1,0:T(8,128)(2,1)}, bf16[2048,512]{1,0:T(8,128)(2,1)S(1)}, u32[]{:S(2)}, u32[]{:S(2)}) collective-permute-start(bf16[2048,512]{1,0:T(8,128)(2,1)} %get-tuple-element.38), channel_id=1, source_target_pairs={{0,64},{64,0},{1,65},{65,1},{2,66},{66,2},{3,67},{67,3},{4,68},{68... | collective-permute-start | bytes 6291464 | tf_op jit(solution)/shard_map/ppermute | solution.py:501
  83.6 1.3 %copy-start.2 = (bf16[2048,512]{1,0:T(8,128)(2,1)}, bf16[2048,512]{1,0:T(8,128)(2,1)S(1)}, u32[]{:S(2)}) copy-start(bf16[2048,512]{1,0:T(8,128)(2,1)S(1)} %collective-permute-done.6.pair_hbm) | copy-start | bytes 6291460

commit v6 on v4

--- a/solution.py
+++ b/solution.py
@@ -125,18 +125,6 @@
     cross_input = norm_round(x_ref[...].astype(F32), gain_ref[1:2, :])
     out_ref[:, :D] = mm(cross_input, weight_ref[:, :D]).astype(BF)
     out_ref[:, D:] = mm_tt(weight_ref[:, D:], cross_input).astype(BF)
-
-
-def kernel_own(x_ref, gain_ref, qkv_ref, cq_ref, q_ref, k_ref, v_ref, c_ref):
-    values = x_ref[...].astype(F32)
-    mean_square = jnp.mean(values * values, axis=-1, keepdims=True)
-    unit = values * lax.rsqrt(mean_square + EPSILON)
-    attn_input = (unit * gain_ref[0:1, :].astype(F32)).astype(BF)
-    cross_input = (unit * gain_ref[1:2, :].astype(F32)).astype(BF)
-    q_ref[...] = (mm(attn_input, qkv_ref[:, :D]) * Q_SCALE).astype(BF)
-    k_ref[...] = mm(attn_input, qkv_ref[:, D : 2 * D]).astype(BF)
-    v_ref[...] = mm_tt(qkv_ref[:, 2 * D :], attn_input).astype(BF)
-    c_ref[...] = (mm(cross_input, cq_ref[...]) * Q_SCALE).astype(BF)
 
 
 def kernel_cross(
@@ -165,7 +153,7 @@
         augment(kv_ref[row : row + D, lane : lane + CELLS], j >= floor, va_ref, j * CELLS)
 
     def picks(i):
-        return [links_ref[component, i, 0, k] for k in range(KC)]
+        return [links_ref[component, k, i] for k in range(KC)]
 
     def queries(i, p):
         return q_ref[pl.ds(aligned(i, CELLS), CELLS), pl.ds(p * LANES, LANES)]
@@ -203,20 +191,21 @@
 
 def kernel_window(
     land_ref,
-    north_ref,
-    south_ref,
-    west_ref,
-    east_ref,
-    corner_west_ref,
-    corner_east_ref,
+    x_ref,
+    face_a_ref,
+    face_b_ref,
+    tile_a_ref,
+    tile_b_ref,
+    corner_a_ref,
+    corner_b_ref,
     gain_ref,
     qkv_ref,
-    q_ref,
-    k_ref,
-    v_ref,
+    cq_ref,
     win_ref,
+    query_ref,
     keys_ref,
     va_ref,
+    q_ref,
     bad_ref,
 ):
     is_air = lax.axis_index("comp") == 0
@@ -240,6 +229,27 @@
         keys_ref[pl.ds(r * GROUP + offset, CELLS), :] = keys
         augment(values_t, flag, va_ref, r * GROUP + offset)
 
+    values = x_ref[...].astype(F32)
+    mean_square = jnp.mean(values * values, axis=-1, keepdims=True)
+    unit = values * lax.rsqrt(mean_square + EPSILON)
+    attn_input = (unit * gain_ref[0:1, :].astype(F32)).astype(BF)
+    cross_input = (unit * gain_ref[1:2, :].astype(F32)).astype(BF)
+    q_ref[...] = (mm(attn_input, qkv_ref[:, :D]) * Q_SCALE).astype(BF)
+    keys = mm(attn_input, qkv_ref[:, D : 2 * D]).astype(BF)
+    values_t = mm_tt(qkv_ref[:, 2 * D :], attn_input).astype(BF)
+    for i in range(NB):
+        at = slice(i * CELLS, (i + 1) * CELLS)
+        put(i + 1, 0, keys[at], values_t[:, at], flags(i + 1)[0])
+    query_ref[...] = (mm(cross_input, cq_ref[...]) * Q_SCALE).astype(BF)
+
+    odd_row = tile_row % 2 == 1
+    odd_col = tile_col % 2 == 1
+
+    def sorted_pair(odd, a, b):
+        return jnp.where(odd, a, b), jnp.where(odd, b, a)
+
+    west, east = sorted_pair(odd_col, face_a_ref[...], face_b_ref[...])
+    corners = [sorted_pair(odd_row, c[:SIDE], c[SIDE:]) for c in sorted_pair(odd_col, corner_a_ref[...], corner_b_ref[...])]
     west_lane = lax.broadcasted_iota(jnp.int32, (1, CELLS), 1) < SIDE
     bands = NB + 2
     blocks = 2
@@ -247,23 +257,19 @@
         members = range(b * bands // blocks, (b + 1) * bands // blocks)
         rows_x = []
         for r in members:
-            for side_ref, corner_ref in ((west_ref, corner_west_ref), (east_ref, corner_east_ref)):
-                if 1 <= r <= NB:
-                    rows_x.append(side_ref[(r - 1) * SIDE : r * SIDE, :])
-                else:
-                    rows_x.append(corner_ref[min(r, 1) * SIDE : (min(r, 1) + 1) * SIDE, :])
+            for side, corner in zip((west, east), corners):
+                inside = side[(r - 1) * SIDE : r * SIDE]
+                rows_x.append(inside if 1 <= r <= NB else corner[min(r, 1)])
         keys, values_t = project(jnp.concatenate(rows_x, axis=0))
         for n, r in enumerate(members):
             _, west_ok, east_ok = flags(r)
             at = slice(n * CELLS, (n + 1) * CELLS)
             flag = jnp.where(west_lane, west_ok.astype(F32), east_ok.astype(F32))
             put(r, CELLS, keys[at], values_t[:, at], flag)
-    keys, values_t = project(jnp.concatenate([north_ref[...], south_ref[...]], axis=0))
+    polar = sorted_pair(odd_row, tile_a_ref[...], tile_b_ref[...])
+    keys, values_t = project(jnp.concatenate(polar, axis=0))
     put(0, 0, keys[:CELLS], values_t[:, :CELLS], flags(0)[0])
-    put(NB + 1, 0, keys[CELLS:], values_t[:, CELLS:], flags(NB + 1)[0])
-    for i in range(NB):
-        at = slice(i * CELLS, (i + 1) * CELLS)
-        put(i + 1, 0, k_ref[at, :], v_ref[:, at], flags(i + 1)[0])
+    put(bands - 1, 0, keys[CELLS:], values_t[:, CELLS:], flags(bands - 1)[0])
 
     def queries(i, p):
         return q_ref[pl.ds(aligned(i, CELLS), CELLS), pl.ds(p * LANES, LANES)]
@@ -312,96 +318,80 @@
     grid_x = tokens[0]
     x = grid_x.reshape(ROWS, D)
     gains = norm_gains[0]
-    up_ring = [(i, i + 1) for i in range(7)]
-    down_ring = [(i + 1, i) for i in range(7)]
-    east_ring = [(i, (i + 1) % 8) for i in range(8)]
-    west_ring = [((i + 1) % 8, i) for i in range(8)]
-
-    top, bottom, west_edge, east_edge, x_first = lax.optimization_barrier(
-        (grid_x[:BR], grid_x[-BR:], grid_x[:, :BR], grid_x[:, -BR:], x)
-    )
-    west = lax.ppermute(east_edge, "face", east_ring)
-    east = lax.ppermute(west_edge, "face", west_ring)
-    north = lax.ppermute(bottom, "tile", up_ring)
-    south = lax.ppermute(top, "tile", down_ring)
-
-    steps = 4
-    part = ROWS // steps
-    block = pl.BlockSpec((part, D), lambda i: (i, 0))
-    streamed = pltpu.CompilerParams(vmem_limit_bytes=56 * MIB)
-    q, k, v, cross_q = pl.pallas_call(
-        kernel_own,
-        grid=(steps,),
-        in_specs=[
-            block,
-            pl.BlockSpec((3, D), lambda i: (0, 0)),
-            pl.BlockSpec((D, 3 * D), lambda i: (0, 0)),
-            pl.BlockSpec((D, D), lambda i: (0, 0)),
-        ],
-        out_specs=[block, block, pl.BlockSpec((D, part), lambda i: (0, i)), block],
-        out_shape=[array(ROWS, D), array(ROWS, D), array(D, ROWS), array(ROWS, D)],
-        cost_estimate=cost(ROWS * D * 4 * D, 7 * MIB),
-        compiler_params=streamed,
-        name="own",
-    )(x_first, gains, qkv_weight[0], cross_query[0])
-
-    west_corner, east_corner = [
-        jnp.concatenate([north[:, cut], south[:, cut]], axis=0)
-        for cut in (slice(0, BR), slice(RX - BR, RX))
-    ]
-    west_corner, east_corner, q, x_second = lax.optimization_barrier(
-        (west_corner, east_corner, q, x)
-    )
-
+    swap_a = [(i, i ^ 1) for i in range(8)]
+    swap_b = [(i, (i + 1) % 8 if i % 2 else (i - 1) % 8) for i in range(8)]
+    odd_row = lax.axis_index("tile") % 2 == 1
+    odd_col = lax.axis_index("face") % 2 == 1
+
+    def columns(block):
+        low, high = block[:, :BR], block[:, RX - BR :]
+        return jnp.where(odd_col, low, high), jnp.where(odd_col, high, low)
+
+    top, bottom = grid_x[:BR], grid_x[NB * BR - BR :]
+    face_src_a, face_src_b = columns(grid_x)
+    tile_src_a, tile_src_b = jnp.where(odd_row, top, bottom), jnp.where(odd_row, bottom, top)
+    face_src_a, face_src_b, tile_src_a, tile_src_b, x_first = lax.optimization_barrier(
+        (face_src_a, face_src_b, tile_src_a, tile_src_b, x)
+    )
+    face_a = lax.ppermute(face_src_a, "face", swap_a)
+    face_b = lax.ppermute(face_src_b, "face", swap_b)
+    tile_a = lax.ppermute(tile_src_a, "tile", swap_a)
+    tile_b = lax.ppermute(tile_src_b, "tile", swap_b)
+
+    half = ROWS // 2
     pair_out = pl.pallas_call(
         kernel_cross_kv,
         grid=(2,),
         in_specs=[
-            pl.BlockSpec((ROWS // 2, D), lambda i: (i, 0)),
+            pl.BlockSpec((half, D), lambda i: (i, 0)),
             pl.BlockSpec((3, D), lambda i: (0, 0)),
             pl.BlockSpec((D, 2 * D), lambda i: (0, 0)),
         ],
-        out_specs=pl.BlockSpec((ROWS // 2, 2 * D), lambda i: (i, 0)),
+        out_specs=pl.BlockSpec((half, 2 * D), lambda i: (i, 0)),
         out_shape=array(ROWS, 2 * D),
         cost_estimate=cost(ROWS * D * 2 * D, 4 * MIB),
-        compiler_params=streamed,
+        compiler_params=pltpu.CompilerParams(vmem_limit_bytes=24 * MIB),
         name="cross_kv",
-    )(x_second, gains, cross_kv[0])
-
-    corner_west = lax.ppermute(east_corner, "face", east_ring)
-    corner_east = lax.ppermute(west_corner, "face", west_ring)
-    west, east, corner_west, corner_east, pair_out = lax.optimization_barrier(
-        (west, east, corner_west, corner_east, pair_out)
+    )(x_first, gains, cross_kv[0])
+
+    corner_src_a, corner_src_b = columns(jnp.concatenate([tile_a, tile_b], axis=0))
+    corner_src_a, corner_src_b, pair_out = lax.optimization_barrier(
+        (corner_src_a, corner_src_b, pair_out)
+    )
+    corner_a = lax.ppermute(corner_src_a, "face", swap_a)
+    corner_b = lax.ppermute(corner_src_b, "face", swap_b)
+    face_a, face_b, corner_a, corner_b, pair_out = lax.optimization_barrier(
+        (face_a, face_b, corner_a, corner_b, pair_out)
     )
     partner = lax.ppermute(pair_out, "comp", [(0, 1), (1, 0)])
 
     padded_rows = (NB + 2) * GROUP
-    window = pl.pallas_call(
+    window, cross_q = pl.pallas_call(
         kernel_window,
-        in_specs=[SMEM] + [VMEM] * 11,
-        out_specs=VMEM,
-        out_shape=array(D, ROWS),
+        in_specs=[SMEM] + [VMEM] * 10,
+        out_specs=[VMEM] * 2,
+        out_shape=[array(D, ROWS), array(ROWS, D)],
         scratch_shapes=[
             pltpu.VMEM((padded_rows, D), BF),
             pltpu.VMEM((PAIRS * VROWS, padded_rows), BF),
+            pltpu.VMEM((ROWS, D), BF),
             pltpu.VMEM((8, 2 * CELLS), F32),
         ],
         cost_estimate=cost(4 << 30, 7 * MIB, ROWS * HEADS * WINDOW),
-        compiler_params=pltpu.CompilerParams(vmem_limit_bytes=32 * MIB),
+        compiler_params=pltpu.CompilerParams(vmem_limit_bytes=28 * MIB),
         name="window",
     )(
         land_bands,
-        north.reshape(CELLS, D),
-        south.reshape(CELLS, D),
-        west.reshape(NB * SIDE, D),
-        east.reshape(NB * SIDE, D),
-        corner_west.reshape(2 * SIDE, D),
-        corner_east.reshape(2 * SIDE, D),
+        x,
+        face_a.reshape(NB * SIDE, D),
+        face_b.reshape(NB * SIDE, D),
+        tile_a.reshape(CELLS, D),
+        tile_b.reshape(CELLS, D),
+        corner_a.reshape(2 * SIDE, D),
+        corner_b.reshape(2 * SIDE, D),
         gains,
         qkv_weight[0],
-        q,
-        k,
-        v,
+        cross_query[0],
     )
 
     result = pl.pallas_call(
@@ -415,10 +405,10 @@
             pltpu.VMEM((8, 2 * CELLS), F32),
         ],
         cost_estimate=cost(5 << 30, 11 * MIB, ROWS * HEADS * 512),
-        compiler_params=pltpu.CompilerParams(vmem_limit_bytes=40 * MIB),
+        compiler_params=pltpu.CompilerParams(vmem_limit_bytes=24 * MIB),
         name="cross",
     )(
-        intersection_list,
+        intersection_list.transpose(0, 2, 3, 1).reshape(2, KC, NB),
         land_bands,
         cross_q,
         partner,

time: 62.5 us -> 55.6 us (0.89)
  the two profiles are of different devices: /device:TPU:89 before, /device:TPU:1 now
where the time goes in v6:
time: 55.6 us; the launch traced here: 55.4 us
  Pallas kernels  26.6 us (48%)
  starting transfers between devices  14.9 us (27%)
  waiting for transfers between devices  11.1 us (20%)
  other arithmetic  2.43 us (4%)
    pallas_call x1, Pallas kernels, per_device(): pl.pallas_call(kernel_cross, in_specs=[SMEM] * 2 + [VMEM] * 9, out_specs=...  13.6 us
    pallas_call x1, Pallas kernels, per_device(): pl.pallas_call(kernel_window, in_specs=[SMEM] + [VMEM] * 10, out_specs=[V...  11.5 us
    ppermute x1, waiting for transfers between devices, per_device(): corner_a = lax.ppermute(corner_src_a, 'face', swap_a)  8.01 us
    ppermute x1, starting transfers between devices, per_device(): tile_b = lax.ppermute(tile_src_b, 'tile', swap_b)  5.13 us
    ppermute x1, waiting for transfers between devices, per_device(): corner_b = lax.ppermute(corner_src_b, 'face', swap_b)  3.13 us
    ppermute x1, starting transfers between devices, per_device(): partner = lax.ppermute(pair_out, 'comp', [(0, 1), (1, 0)])  2.44 us
    ppermute x1, starting transfers between devices, per_device(): face_b = lax.ppermute(face_src_b, 'face', swap_b)  2.36 us
    ppermute x1, starting transfers between devices, per_device(): tile_a = lax.ppermute(tile_src_a, 'tile', swap_a)  2.12 us
  transfers between devices with their start and end apart: 7, of which 2 were waited for; matrix products, arithmetic and copies ran while one was open for 0% of the time, Pallas kernels for 24%

profile of v6, /device:TPU:1, one launch (start us, length us, event | category | flops | bytes accessed | tf_op | source)
XLA Modules:
  0.0 55.4 jit_solution(8492619052696165250)
XLA Ops:
  0.0 0.0 copy-start
  0.0 0.0 copy-start.2
  0.0 0.0 copy-start.1
  0.0 1.1 %select_bitcast_fusion = (bf16[8,16,512]{2,1,0:T(8,128)(2,1)S(1)}, bf16[8,16,512]{2,1,0:T(8,128)(2,1)S(1)}) fusion(pred[]{:T(512)S(6)} %eq.10, bf16[1,64,16,512]{3,2,1,0:T(8,128)(2,1)} %param.11), kind=kLoop, calls=%fused_computation.2 | loop fusion | flops 131072 | bytes 524289 | tf_op jit(solution)/shard_map/jit(_where)/select_n | solution.py:332
  1.2 1.3 %broadcast_select_fusion = (bf16[64,8,512]{2,1,0:T(8,128)(2,1)S(1)}, bf16[64,8,512]{2,1,0:T(8,128)(2,1)S(1)}) fusion(pred[]{:T(512)S(6)} %eq.9, bf16[64,16,512]{2,1,0:T(8,128)(2,1)} %bitcast.24), kind=kLoop, calls=%fused_computation | loop fusion | flops 524288 | bytes 2097153 | tf_op jit(solution)/shard_map/jit(_where)/select_n | solution.py:328
  2.4 2.1 %collective-permute-start.2 = (bf16[8,16,512]{2,1,0:T(8,128)(2,1)S(1)}, bf16[8,16,512]{2,1,0:T(8,128)(2,1)S(1)}, u32[]{:S(2)}, u32[]{:S(2)}) collective-permute-start(bf16[8,16,512]{2,1,0:T(8,128)(2,1)S(1)} %get-tuple-element.22), channel_id=1, source_target_pairs={{0,1},{1,0},{2,3},{3,2},{4,5},{5,4},{6,7},{7,6},{8,9},{9,8},{10,11... | collective-permute-start | bytes 393224 | tf_op jit(solution)/shard_map/ppermute | solution.py:338
  4.6 5.1 %collective-permute-start.3 = (bf16[8,16,512]{2,1,0:T(8,128)(2,1)S(1)}, bf16[8,16,512]{2,1,0:T(8,128)(2,1)S(1)}, u32[]{:S(2)}, u32[]{:S(2)}) collective-permute-start(bf16[8,16,512]{2,1,0:T(8,128)(2,1)S(1)} %get-tuple-element.23), channel_id=1, source_target_pairs={{0,7},{1,2},{2,1},{3,4},{4,3},{5,6},{6,5},{7,0},{8,15},{9,10},{10,... | collective-permute-start | bytes 393224 | tf_op jit(solution)/shard_map/ppermute | solution.py:339
  9.7 1.3 %collective-permute-start = (bf16[64,8,512]{2,1,0:T(8,128)(2,1)S(1)}, bf16[64,8,512]{2,1,0:T(8,128)(2,1)S(1)}, u32[]{:S(2)}, u32[]{:S(2)}) collective-permute-start(bf16[64,8,512]{2,1,0:T(8,128)(2,1)S(1)} %get-tuple-element.20), channel_id=1, source_target_pairs={{0,8},{8,0},{16,24},{24,16},{32,40},{40,32},{48,56},{56,48},{1,9},... | collective-permute-start | bytes 1572872 | tf_op jit(solution)/shard_map/ppermute | solution.py:336
  11.0 2.4 %collective-permute-start.1 = (bf16[64,8,512]{2,1,0:T(8,128)(2,1)S(1)}, bf16[64,8,512]{2,1,0:T(8,128)(2,1)S(1)}, u32[]{:S(2)}, u32[]{:S(2)}) collective-permute-start(bf16[64,8,512]{2,1,0:T(8,128)(2,1)S(1)} %get-tuple-element.21), channel_id=1, source_target_pairs={{0,56},{8,16},{16,8},{24,32},{32,24},{40,48},{48,40},{56,0},{1,57}... | collective-permute-start | bytes 1572872 | tf_op jit(solution)/shard_map/ppermute | solution.py:337
  13.3 0.0 copy-done
  13.4 0.0 copy-done.2
  13.4 0.0 copy-done.1
  13.4 0.0 copy-start.5
  13.4 0.0 copy-start.6
  13.4 0.0 copy-start.10
  13.4 1.6 %cross_kv.1 = bf16[1024,1024]{1,0:T(8,128)(2,1)S(1)} custom-call(bf16[1024,512]{1,0:T(8,128)(2,1)S(1)} %bitcast.25, bf16[3,512]{1,0:T(4,128)(2,1)S(1)} %bitcast.31, bf16[512,1024]{1,0:T(8,128)(2,1)S(1)} %bitcast.28), custom_call_target="tpu_custom_call" | custom-call | flops 1073741824 | bytes 4194304 | tf_op jit(solution)/shard_map/cross_kv/pallas_call | solution.py:342
  15.0 0.0 collective-permute-done.2
  15.0 0.0 collective-permute-done.3
  15.1 0.1 collective-permute-start.4
  15.2 1.5 %collective-permute-start.5 = (bf16[16,8,512]{2,1,0:T(8,128)(2,1)S(1)}, bf16[16,8,512]{2,1,0:T(8,128)(2,1)S(1)}, u32[]{:S(2)}, u32[]{:S(2)}) collective-permute-start(bf16[16,8,512]{2,1,0:T(8,128)(2,1)S(1)} %get-tuple-element.26), channel_id=1, source_target_pairs={{0,56},{8,16},{16,8},{24,32},{32,24},{40,48},{48,40},{56,0},{1,57}... | collective-permute-start | bytes 393224 | tf_op jit(solution)/shard_map/ppermute | solution.py:362
  16.7 8.0 %collective-permute-done.4 = bf16[16,8,512]{2,1,0:T(8,128)(2,1)S(1)} collective-permute-done((bf16[16,8,512]{2,1,0:T(8,128)(2,1)S(1)}, bf16[16,8,512]{2,1,0:T(8,128)(2,1)S(1)}, u32[]{:S(2)}, u32[]{:S(2)}) %collective-permute-start.4) | collective-permute-done | bytes 131104 | tf_op jit(solution)/shard_map/ppermute | solution.py:361
  24.7 3.1 %collective-permute-done.5 = bf16[16,8,512]{2,1,0:T(8,128)(2,1)S(1)} collective-permute-done((bf16[16,8,512]{2,1,0:T(8,128)(2,1)S(1)}, bf16[16,8,512]{2,1,0:T(8,128)(2,1)S(1)}, u32[]{:S(2)}, u32[]{:S(2)}) %collective-permute-start.5) | collective-permute-done | bytes 131104 | tf_op jit(solution)/shard_map/ppermute | solution.py:362
  27.8 0.0 collective-permute-done
  27.8 0.0 collective-permute-done.1
  27.8 2.4 %collective-permute-start.6 = (bf16[1024,1024]{1,0:T(8,128)(2,1)S(1)}, bf16[1024,1024]{1,0:T(8,128)(2,1)S(1)}, u32[]{:S(2)}, u32[]{:S(2)}) collective-permute-start(bf16[1024,1024]{1,0:T(8,128)(2,1)S(1)} %cross_kv.1), channel_id=1, source_target_pairs={{0,64},{64,0},{1,65},{65,1},{2,66},{66,2},{3,67},{67,3},{4,68},{68... | collective-permute-start | bytes 6291464 | tf_op jit(solution)/shard_map/ppermute | solution.py:366
  30.3 0.0 copy-done.5
  30.3 0.0 copy-done.6
  30.3 0.0 copy-done.10
  30.3 0.0 copy-start.3
  30.3 0.0 copy-start.4
  30.3 0.0 copy-start.7
  30.3 0.0 copy-start.8
  30.3 0.0 copy-start.9
  30.3 11.5 %window.1 = (bf16[512,1024]{1,0:T(8,128)(2,1)S(1)}, bf16[1024,512]{1,0:T(8,128)(2,1)S(1)}) custom-call(s32[8,8]{1,0:T(8,128)S(1)} %copy-done.10, bf16[1024,512]{1,0:T(8,128)(2,1)S(1)} %bitcast.26, bf16[512,512]{1,0:T(8,128)(2,1)S(1)} %bitcast.40, bf16[512,512]{1,0:T(8,128)(2,1)S(1)} %bitcast.41, bf16[128,512]{1,0:T(8,128)(2,1)S(1)} %bitcast.29, ...), custom_call_target="tpu_custom_call" | custom-call | flops 8589934592 | bytes 7340032 | tf_op jit(solution)/shard_map/window/pallas_call | solution.py:369
  41.8 0.0 collective-permute-done.6.kv_ref
  41.8 0.0 copy-done.3
  41.8 0.0 copy-done.4
  41.9 0.0 copy-done.7
  41.9 0.0 copy-done.8
  41.9 0.0 copy-done.9
  41.9 13.6 %cross.1 = bf16[1024,512]{1,0:T(8,128)(2,1)} custom-call(s32[2,4,8]{2,1,0:T(4,128)S(1)} %bitcast.44, s32[8,8]{1,0:T(8,128)S(1)} %copy-done.10, bf16[1024,512]{1,0:T(8,128)(2,1)S(1)} %get-tuple-element.32.q_ref, bf16[1024,1024]{1,0:T(8,128)(2,1)S(1)} %collective-permute-done.6.kv_ref, bf16[512,1024]{1,0:T(8,128)(2,1)S(1)} %get-tuple-element.34.win_ref, ...), custom_call_target="tpu_custom_call" | custom-call | flops 10737418240 | bytes 11534336 | tf_op jit(solution)/shard_map/cross/pallas_call | solution.py:397
  (3 shorter events, 0.0 us)
Async XLA Ops:
  0.0 13.4 %copy-start = (bf16[1,64,16,512]{3,2,1,0:T(8,128)(2,1)S(1)}, bf16[1,64,16,512]{3,2,1,0:T(8,128)(2,1)}, u32[]{:S(2)}) copy-start(bf16[1,64,16,512]{3,2,1,0:T(8,128)(2,1)} %param.11) | copy-start | bytes 3145732
  0.0 13.4 %copy-start.2 = (bf16[1,3,512]{2,1,0:T(4,128)(2,1)S(1)}, bf16[1,3,512]{2,1,0:T(4,128)(2,1)}, u32[]{:S(2)}) copy-start(bf16[1,3,512]{2,1,0:T(4,128)(2,1)} %param.12) | copy-start | bytes 9220
  0.0 13.4 %copy-start.1 = (bf16[1,512,1024]{2,1,0:T(8,128)(2,1)S(1)}, bf16[1,512,1024]{2,1,0:T(8,128)(2,1)}, u32[]{:S(2)}) copy-start(bf16[1,512,1024]{2,1,0:T(8,128)(2,1)} %param.16) | copy-start | bytes 3145732
  2.4 12.6 %collective-permute-start.2 = (bf16[8,16,512]{2,1,0:T(8,128)(2,1)S(1)}, bf16[8,16,512]{2,1,0:T(8,128)(2,1)S(1)}, u32[]{:S(2)}, u32[]{:S(2)}) collective-permute-start(bf16[8,16,512]{2,1,0:T(8,128)(2,1)S(1)} %get-tuple-element.22), channel_id=1, source_target_pairs={{0,1},{1,0},{2,3},{3,2},{4,5},{5,4},{6,7},{7,6},{8,9},{9,8},{10,11... | collective-permute-start | bytes 393224 | tf_op jit(solution)/shard_map/ppermute | solution.py:338
  4.6 10.5 %collective-permute-start.3 = (bf16[8,16,512]{2,1,0:T(8,128)(2,1)S(1)}, bf16[8,16,512]{2,1,0:T(8,128)(2,1)S(1)}, u32[]{:S(2)}, u32[]{:S(2)}) collective-permute-start(bf16[8,16,512]{2,1,0:T(8,128)(2,1)S(1)} %get-tuple-element.23), channel_id=1, source_target_pairs={{0,7},{1,2},{2,1},{3,4},{4,3},{5,6},{6,5},{7,0},{8,15},{9,10},{10,... | collective-permute-start | bytes 393224 | tf_op jit(solution)/shard_map/ppermute | solution.py:339
  9.7 18.1 %collective-permute-start = (bf16[64,8,512]{2,1,0:T(8,128)(2,1)S(1)}, bf16[64,8,512]{2,1,0:T(8,128)(2,1)S(1)}, u32[]{:S(2)}, u32[]{:S(2)}) collective-permute-start(bf16[64,8,512]{2,1,0:T(8,128)(2,1)S(1)} %get-tuple-element.20), channel_id=1, source_target_pairs={{0,8},{8,0},{16,24},{24,16},{32,40},{40,32},{48,56},{56,48},{1,9},... | collective-permute-start | bytes 1572872 | tf_op jit(solution)/shard_map/ppermute | solution.py:336
  11.0 16.8 %collective-permute-start.1 = (bf16[64,8,512]{2,1,0:T(8,128)(2,1)S(1)}, bf16[64,8,512]{2,1,0:T(8,128)(2,1)S(1)}, u32[]{:S(2)}, u32[]{:S(2)}) collective-permute-start(bf16[64,8,512]{2,1,0:T(8,128)(2,1)S(1)} %get-tuple-element.21), channel_id=1, source_target_pairs={{0,56},{8,16},{16,8},{24,32},{32,24},{40,48},{48,40},{56,0},{1,57}... | collective-permute-start | bytes 1572872 | tf_op jit(solution)/shard_map/ppermute | solution.py:337
  13.4 16.9 %copy-start.5 = (bf16[1,512,1536]{2,1,0:T(8,128)(2,1)S(1)}, bf16[1,512,1536]{2,1,0:T(8,128)(2,1)}, u32[]{:S(2)}) copy-start(bf16[1,512,1536]{2,1,0:T(8,128)(2,1)} %param.13) | copy-start | bytes 4718596
  13.4 16.9 %copy-start.6 = (bf16[1,512,512]{2,1,0:T(8,128)(2,1)S(1)}, bf16[1,512,512]{2,1,0:T(8,128)(2,1)}, u32[]{:S(2)}) copy-start(bf16[1,512,512]{2,1,0:T(8,128)(2,1)} %param.15) | copy-start | bytes 1572868
  13.4 16.9 %copy-start.10 = (s32[8,8]{1,0:T(8,128)S(1)}, s32[8,8]{1,0:T(8,128)}, u32[]{:S(2)}) copy-start(s32[8,8]{1,0:T(8,128)} %land_ref.3) | copy-start | bytes 772
  15.1 9.6 %collective-permute-start.4 = (bf16[16,8,512]{2,1,0:T(8,128)(2,1)S(1)}, bf16[16,8,512]{2,1,0:T(8,128)(2,1)S(1)}, u32[]{:S(2)}, u32[]{:S(2)}) collective-permute-start(bf16[16,8,512]{2,1,0:T(8,128)(2,1)S(1)} %get-tuple-element.25), channel_id=1, source_target_pairs={{0,8},{8,0},{16,24},{24,16},{32,40},{40,32},{48,56},{56,48},{1,9},... | collective-permute-start | bytes 393224 | tf_op jit(solution)/shard_map/ppermute | solution.py:361
  15.2 12.6 %collective-permute-start.5 = (bf16[16,8,512]{2,1,0:T(8,128)(2,1)S(1)}, bf16[16,8,512]{2,1,0:T(8,128)(2,1)S(1)}, u32[]{:S(2)}, u32[]{:S(2)}) collective-permute-start(bf16[16,8,512]{2,1,0:T(8,128)(2,1)S(1)} %get-tuple-element.26), channel_id=1, source_target_pairs={{0,56},{8,16},{16,8},{24,32},{32,24},{40,48},{48,40},{56,0},{1,57}... | collective-permute-start | bytes 393224 | tf_op jit(solution)/shard_map/ppermute | solution.py:362
  27.8 14.0 %collective-permute-start.6 = (bf16[1024,1024]{1,0:T(8,128)(2,1)S(1)}, bf16[1024,1024]{1,0:T(8,128)(2,1)S(1)}, u32[]{:S(2)}, u32[]{:S(2)}) collective-permute-start(bf16[1024,1024]{1,0:T(8,128)(2,1)S(1)} %cross_kv.1), channel_id=1, source_target_pairs={{0,64},{64,0},{1,65},{65,1},{2,66},{66,2},{3,67},{67,3},{4,68},{68... | collective-permute-start | bytes 6291464 | tf_op jit(solution)/shard_map/ppermute | solution.py:366
  30.3 11.6 %copy-start.3 = (bf16[1,512,2048]{2,1,0:T(8,128)(2,1)S(1)}, bf16[1,512,2048]{2,1,0:T(8,128)(2,1)}, u32[]{:S(2)}) copy-start(bf16[1,512,2048]{2,1,0:T(8,128)(2,1)} %param.18) | copy-start | bytes 6291460
  30.3 11.6 %copy-start.4 = (bf16[1,2048,512]{2,1,0:T(8,128)(2,1)S(1)}, bf16[1,2048,512]{2,1,0:T(8,128)(2,1)}, u32[]{:S(2)}) copy-start(bf16[1,2048,512]{2,1,0:T(8,128)(2,1)} %param.19) | copy-start | bytes 6291460
  30.3 11.6 %copy-start.7 = (bf16[1,512,512]{2,1,0:T(8,128)(2,1)S(1)}, bf16[1,512,512]{2,1,0:T(8,128)(2,1)}, u32[]{:S(2)}) copy-start(bf16[1,512,512]{2,1,0:T(8,128)(2,1)} %param.14) | copy-start | bytes 1572868
  30.3 11.6 %copy-start.8 = (bf16[1,512,512]{2,1,0:T(8,128)(2,1)S(1)}, bf16[1,512,512]{2,1,0:T(8,128)(2,1)}, u32[]{:S(2)}) copy-start(bf16[1,512,512]{2,1,0:T(8,128)(2,1)} %param.17) | copy-start | bytes 1572868
  30.3 11.6 %copy-start.9 = (s32[2,8,1,4]{1,3,2,0:T(4,128)S(1)}, s32[2,8,1,4]{1,3,2,0:T(4,128)}, u32[]{:S(2)}) copy-start(s32[2,8,1,4]{1,3,2,0:T(4,128)} %param.20) | copy-start | bytes 772

commit v7 on v3

v7 whole, which is shorter than its diff:
```python
import jax
import jax.numpy as jnp
from jax import lax
from jax.experimental import pallas as pl
from jax.experimental.pallas import tpu as pltpu
from jax.sharding import PartitionSpec as P

D = 512
FF = 2048
HEADS = 8
PAIRS = HEADS // 2
LANES = 128
RX = 16
BR = 8
NB = 8
KC = 4
CELLS = BR * RX
ROWS = NB * CELLS
SIDE = BR * BR
GROUP = CELLS + 2 * SIDE
WINDOW = 3 * GROUP
EXTRA = 16
VROWS = LANES + EXTRA

EPSILON = 1e-05
Q_SCALE = 1.4426950408889634 / 8.0
LIMIT = 2.0**100
BF = jnp.bfloat16
F32 = jnp.float32
MIB = 1 << 20


def norm_round(values, gain):
    mean_square = jnp.mean(values * values, axis=-1, keepdims=True)
    return (values * lax.rsqrt(mean_square + EPSILON) * gain.astype(F32)).astype(BF)


def mm(a, b):
    return jnp.dot(a, b, preferred_element_type=F32)


def mm_nt(a, b):
    return lax.dot_general(a, b, (((1,), (1,)), ((), ())), preferred_element_type=F32)


def mm_tn(a, b):
    return lax.dot_general(a, b, (((0,), (0,)), ((), ())), preferred_element_type=F32)


def mm_tt(a, b):
    return lax.dot_general(a, b, (((0,), (1,)), ((), ())), preferred_element_type=F32)


def augment(values_t, flag, out_ref, lane):
    keep = flag.astype(F32).astype(BF)
    for p in range(PAIRS):
        rows = values_t[p * LANES : (p + 1) * LANES]
        out_ref[pl.ds(p * VROWS, LANES), pl.ds(lane, CELLS)] = rows * keep
        out_ref[pl.ds(p * VROWS + LANES, EXTRA), pl.ds(lane, CELLS)] = (
            jnp.ones((EXTRA, CELLS), BF) * keep
        )


def score(pair, keys):
    low = lax.broadcasted_iota(jnp.int32, pair.shape, 1) < LANES // 2
    zero = jnp.zeros_like(pair)
    stacked = jnp.concatenate([jnp.where(low, pair, zero), jnp.where(low, zero, pair)], axis=0)
    return mm_nt(keys, stacked)


def blend(values_t, terms, extra):
    both = mm(values_t, terms)
    sums = both[LANES : LANES + 8]
    share = 1.0 / (sums + extra)
    half = LANES // 2
    result = jnp.concatenate(
        [both[:half, :CELLS] * share[:1, :CELLS], both[half:LANES, CELLS:] * share[:1, CELLS:]],
        axis=0,
    )
    return result.astype(BF), sums


def attention(count, queries, keys, values, penalties, lane, out_ref, bad_ref):
    bad_ref[...] = jnp.zeros_like(bad_ref)

    def terms_of(i, p):
        return jnp.exp2(score(queries(i, p), keys(i, p))).astype(BF)

    steps = [(i, p) for i in range(count) for p in range(PAIRS)]
    following = terms_of(*steps[0])
    for n, (i, p) in enumerate(steps):
        terms = following
        if n + 1 < len(steps):
            following = terms_of(*steps[n + 1])
        result, sums = blend(values(i, p), terms, 1.0)
        out_ref[pl.ds(p * LANES, LANES), pl.ds(lane(i), CELLS)] = result
        bad_ref[...] += jnp.where(sums < LIMIT, 0.0, 1.0)

    @pl.when(jnp.sum(bad_ref[...]) > 0.0)
    def _():
        def band(i, carry):
            for p in range(PAIRS):
                scores = score(queries(i, p), keys(i, p))
                at = 0
                pieces = []
                for rows, penalty in penalties(i):
                    pieces.append(scores[at : at + rows] + penalty)
                    at += rows
                scores = jnp.concatenate(pieces, axis=0)
                highest = jnp.maximum(jnp.max(scores, axis=0, keepdims=True), 0.0)
                terms = jnp.exp2(scores - highest).astype(BF)
                result, _ = blend(values(i, p), terms, jnp.exp2(-highest))
                out_ref[pl.ds(p * LANES, LANES), pl.ds(lane(i), CELLS)] = result
            return carry

        lax.fori_loop(0, count, band, 0)


def aligned(i, size):
    return i * size if isinstance(i, int) else pl.multiple_of(i * size, size)


def kernel_cross_kv(x_ref, gain_ref, weight_ref, out_ref):
    cross_input = norm_round(x_ref[...].astype(F32), gain_ref[1:2, :])
    out_ref[:, :D] = mm(cross_input, weight_ref[:, :D]).astype(BF)
    out_ref[:, D:] = mm_tt(weight_ref[:, D:], cross_input).astype(BF)


def kernel_own(x_ref, gain_ref, qkv_ref, cq_ref, q_ref, k_ref, v_ref, c_ref):
    values = x_ref[...].astype(F32)
    mean_square = jnp.mean(values * values, axis=-1, keepdims=True)
    unit = values * lax.rsqrt(mean_square + EPSILON)
    attn_input = (unit * gain_ref[0:1, :].astype(F32)).astype(BF)
    cross_input = (unit * gain_ref[1:2, :].astype(F32)).astype(BF)
    q_ref[...] = (mm(attn_input, qkv_ref[:, :D]) * Q_SCALE).astype(BF)
    k_ref[...] = mm(attn_input, qkv_ref[:, D : 2 * D]).astype(BF)
    v_ref[...] = mm_tt(qkv_ref[:, 2 * D :], attn_input).astype(BF)
    c_ref[...] = (mm(cross_input, cq_ref[...]) * Q_SCALE).astype(BF)


def kernel_cross(links_ref, land_ref, q_ref, kv_ref, out_ref, va_ref, bad_ref):
    component = lax.axis_index("comp")
    own_land = land_ref[lax.axis_index("tile"), lax.axis_index("face")]
    floor = jnp.where(component == 1, 0, own_land)

    for j in range(NB):
        row, lane = (j // 4) * D, D + (j % 4) * CELLS
        augment(kv_ref[row : row + D, lane : lane + CELLS], j >= floor, va_ref, j * CELLS)

    def picks(i):
        return [links_ref[component, k, i] for k in range(KC)]

    def queries(i, p):
        return q_ref[pl.ds(aligned(i, CELLS), CELLS), pl.ds(p * LANES, LANES)]

    def keys(i, p):
        return jnp.concatenate(
            [kv_ref[pl.ds(aligned(j, CELLS), CELLS), pl.ds(p * LANES, LANES)] for j in picks(i)],
            axis=0,
        )

    def values(i, p):
        return jnp.concatenate(
            [va_ref[pl.ds(p * VROWS, VROWS), pl.ds(aligned(j, CELLS), CELLS)] for j in picks(i)],
            axis=1,
        )

    def penalties(i):
        return [(CELLS, jnp.where(j >= floor, 0.0, -1e30)) for j in picks(i)]

    def lane(i):
        return aligned(i, CELLS)

    attention(NB, queries, keys, values, penalties, lane, out_ref, bad_ref)


def place(land_ref):
    is_air = lax.axis_index("comp") == 0
    tile_row = lax.axis_index("tile")
    tile_col = lax.axis_index("face")
    columns = (tile_col, (tile_col + 7) % 8, (tile_col + 1) % 8)

    def flags(r):
        inside_row = jnp.where(r == 0, tile_row - 1, jnp.where(r == NB + 1, tile_row + 1, tile_row))
        lat_ok = (inside_row >= 0) & (inside_row < 8)
        safe_row = jnp.clip(inside_row, 0, 7)
        index = jnp.where(r == 0, NB - 1, jnp.where(r == NB + 1, 0, r - 1))
        return [lat_ok & (is_air | (index >= land_ref[safe_row, c])) for c in columns]

    return is_air, tile_row % 2 == 1, tile_col % 2 == 1, flags


def sorted_pair(odd, a, b):
    return jnp.where(odd, a, b), jnp.where(odd, b, a)


def project(rows_x, gain_ref, qkv_ref):
    normed = norm_round(rows_x.astype(F32), gain_ref[0:1, :])
    keys = mm(normed, qkv_ref[:, D : 2 * D]).astype(BF)
    return keys, mm_tt(qkv_ref[:, 2 * D :], normed).astype(BF)


def side_flag(flags, r):
    _, west_ok, east_ok = flags(r)
    west_lane = lax.broadcasted_iota(jnp.int32, (1, CELLS), 1) < SIDE
    return jnp.where(west_lane, west_ok.astype(F32), east_ok.astype(F32))


def window_penalties(flags, i):
    pieces = []
    for b in range(3):
        for rows, flag in zip((CELLS, SIDE, SIDE), flags(i + b)):
            pieces.append((rows, jnp.where(flag, 0.0, -1e30)))
    return pieces


def kernel_window(
    land_ref,
    face_a_ref,
    face_b_ref,
    gain_ref,
    qkv_ref,
    q_ref,
    k_ref,
    v_ref,
    win_ref,
    edge_keys_ref,
    edge_va_ref,
    keys_ref,
    va_ref,
    bad_ref,
):
    _, _, odd_col, flags = place(land_ref)

    def put(r, offset, keys, values_t, flag):
        at = (r - 1) * GROUP + offset
        keys_ref[pl.ds(at, CELLS), :] = keys
        augment(values_t, flag, va_ref, at)

    west, east = sorted_pair(odd_col, face_a_ref[...], face_b_ref[...])
    blocks = 2
    for b in range(blocks):
        members = range(1 + b * NB // blocks, 1 + (b + 1) * NB // blocks)
        rows_x = []
        for r in members:
            rows_x += [side[(r - 1) * SIDE : r * SIDE] for side in (west, east)]
        keys, values_t = project(jnp.concatenate(rows_x, axis=0), gain_ref, qkv_ref)
        for n, r in enumerate(members):
            at = slice(n * CELLS, (n + 1) * CELLS)
            put(r, CELLS, keys[at], values_t[:, at], side_flag(flags, r))
    for i in range(NB):
        at = slice(i * CELLS, (i + 1) * CELLS)
        put(i + 1, 0, k_ref[at, :], v_ref[:, at], flags(i + 1)[0])
    for n, at in enumerate((0, (NB - 2) * GROUP)):
        to = slice(n * 2 * GROUP, (n + 1) * 2 * GROUP)
        edge_keys_ref[to, :] = keys_ref[at : at + 2 * GROUP, :]
        edge_va_ref[:, to] = va_ref[:, at : at + 2 * GROUP]

    def queries(n, p):
        return q_ref[pl.ds(aligned(n, CELLS) + CELLS, CELLS), pl.ds(p * LANES, LANES)]

    def keys_of(n, p):
        return keys_ref[pl.ds(aligned(n, GROUP), WINDOW), pl.ds(p * LANES, LANES)]

    def values_of(n, p):
        return va_ref[pl.ds(p * VROWS, VROWS), pl.ds(aligned(n, GROUP), WINDOW)]

    def penalties(n):
        return window_penalties(flags, n + 1)

    def lane(n):
        return aligned(n, CELLS) + CELLS

    attention(NB - 2, queries, keys_of, values_of, penalties, lane, win_ref, bad_ref)


def kernel_last(
    land_ref,
    tile_a_ref,
    tile_b_ref,
    edge_keys_ref,
    edge_va_ref,
    q_ref,
    win_ref,
    cross_ref,
    x_ref,
    gain_ref,
    qkv_ref,
    out_w_ref,
    cross_w_ref,
    up_ref,
    down_ref,
    out_ref,
    keys_ref,
    va_ref,
    full_ref,
    bad_ref,
):
    is_air, odd_row, odd_col, flags = place(land_ref)
    full_ref[:, CELLS : ROWS - CELLS] = win_ref[:, CELLS : ROWS - CELLS]
    rows_x = []
    for rows in sorted_pair(odd_row, tile_a_ref[...], tile_b_ref[...]):
        west, east = sorted_pair(odd_col, rows[CELLS : CELLS + SIDE], rows[CELLS + SIDE :])
        rows_x += [rows[:CELLS], west, east]
    new_keys, new_values = project(jnp.concatenate(rows_x, axis=0), gain_ref, qkv_ref)
    for n in range(2):
        new, held = n * WINDOW + n * 2 * GROUP, n * WINDOW + (1 - n) * GROUP
        src = slice(n * 2 * GROUP, (n + 1) * 2 * GROUP)
        keys_ref[new : new + GROUP, :] = new_keys[n * GROUP : (n + 1) * GROUP]
        keys_ref[held : held + 2 * GROUP, :] = edge_keys_ref[src, :]
        va_ref[:, held : held + 2 * GROUP] = edge_va_ref[:, src]
        r = n * (NB + 1)
        at = n * GROUP
        augment(new_values[:, at : at + CELLS], flags(r)[0], va_ref, new)
        augment(new_values[:, at + CELLS : at + GROUP], side_flag(flags, r), va_ref, new + CELLS)

    def queries(n, p):
        return q_ref[pl.ds(aligned(n, ROWS - CELLS), CELLS), pl.ds(p * LANES, LANES)]

    def keys_of(n, p):
        return keys_ref[pl.ds(aligned(n, WINDOW), WINDOW), pl.ds(p * LANES, LANES)]

    def values_of(n, p):
        return va_ref[pl.ds(p * VROWS, VROWS), pl.ds(aligned(n, WINDOW), WINDOW)]

    def penalties(n):
        return window_penalties(flags, n * (NB - 1))

    def lane(n):
        return aligned(n, ROWS - CELLS)

    attention(2, queries, keys_of, values_of, penalties, lane, full_ref, bad_ref)

    chunk = 512
    own_land = land_ref[lax.axis_index("tile"), lax.axis_index("face")]
    for c in range(ROWS // chunk):
        at = slice(c * chunk, (c + 1) * chunk)
        index = (c * chunk + lax.broadcasted_iota(jnp.int32, (chunk, 1), 0)) // CELLS
        live = jnp.where(is_air | (index >= own_land), 1.0, 0.0)
        update = mm_tn(full_ref[:, at], out_w_ref[...]) + mm_tn(cross_ref[:, at], cross_w_ref[...])
        middle = x_ref[at, :].astype(F32) + live * update
        mlp_input = norm_round(middle, gain_ref[2:3, :])
        gate = 0.5 * mm(mlp_input, up_ref[...])
        hidden = (gate + gate * jnp.tanh(gate)).astype(BF)
        out_ref[at, :] = (middle + live * mm(hidden, down_ref[...])).astype(BF)


VMEM = pl.BlockSpec(memory_space=pltpu.VMEM)
SMEM = pl.BlockSpec(memory_space=pltpu.SMEM)


def array(*shape, dtype=BF):
    return jax.ShapeDtypeStruct(shape, dtype)


def cost(macs, size, exps=0):
    return pl.CostEstimate(flops=2 * macs, bytes_accessed=size, transcendentals=exps)


def per_device(
    tokens,
    norm_gains,
    qkv_weight,
    out_weight,
    cross_query,
    cross_kv,
    cross_out,
    up_weight,
    down_weight,
    intersection_list,
    land_bands,
):
    grid_x = tokens[0]
    x = grid_x.reshape(ROWS, D)
    gains = norm_gains[0]
    swap_a = [(i, i ^ 1) for i in range(8)]
    swap_b = [(i, (i + 1) % 8 if i % 2 else (i - 1) % 8) for i in range(8)]
    odd_row = lax.axis_index("tile") % 2 == 1
    odd_col = lax.axis_index("face") % 2 == 1

    def columns(block):
        low, high = block[:, :BR], block[:, RX - BR :]
        return jnp.where(odd_col, low, high), jnp.where(odd_col, high, low)

    face_src_a, face_src_b, x_first = lax.optimization_barrier((*columns(grid_x), x))
    face_a = lax.ppermute(face_src_a, "face", swap_a).reshape(NB * SIDE, D)
    face_b = lax.ppermute(face_src_b, "face", swap_b).reshape(NB * SIDE, D)

    half = ROWS // 2
    block = pl.BlockSpec((half, D), lambda i: (i, 0))
    params = pltpu.CompilerParams(vmem_limit_bytes=24 * MIB)
    pair_out = pl.pallas_call(
        kernel_cross_kv,
        grid=(2,),
        in_specs=[
            block,
            pl.BlockSpec((3, D), lambda i: (0, 0)),
            pl.BlockSpec((D, 2 * D), lambda i: (0, 0)),
        ],
        out_specs=pl.BlockSpec((half, 2 * D), lambda i: (i, 0)),
        out_shape=array(ROWS, 2 * D),
        cost_estimate=cost(ROWS * D * 2 * D, 4 * MIB),
        compiler_params=params,
        name="cross_kv",
    )(x_first, gains, cross_kv[0])
    partner = lax.ppermute(pair_out, "comp", [(0, 1), (1, 0)])

    q, k, v, cross_q = pl.pallas_call(
        kernel_own,
        grid=(2,),
        in_specs=[
            block,
            pl.BlockSpec((3, D), lambda i: (0, 0)),
            pl.BlockSpec((D, 3 * D), lambda i: (0, 0)),
            pl.BlockSpec((D, D), lambda i: (0, 0)),
        ],
        out_specs=[block, block, pl.BlockSpec((D, half), lambda i: (0, i)), block],
        out_shape=[array(ROWS, D), array(ROWS, D), array(D, ROWS), array(ROWS, D)],
        cost_estimate=cost(ROWS * D * 4 * D, 7 * MIB),
        compiler_params=params,
        name="own",
    )(x_first, gains, qkv_weight[0], cross_query[0])

    bad = pltpu.VMEM((8, 2 * CELLS), F32)
    cross = pl.pallas_call(
        kernel_cross,
        in_specs=[SMEM] * 2 + [VMEM] * 2,
        out_specs=VMEM,
        out_shape=array(D, ROWS),
        scratch_shapes=[pltpu.VMEM((PAIRS * VROWS, ROWS), BF), bad],
        cost_estimate=cost(8 * ROWS * 512 * D, 4 * MIB, ROWS * HEADS * 512),
        compiler_params=params,
        name="cross",
    )(intersection_list.transpose(0, 2, 3, 1).reshape(2, KC, NB), land_bands, cross_q, partner)

    face_a, face_b, cross = lax.optimization_barrier((face_a, face_b, cross))
    top, bottom = [
        jnp.concatenate(
            [x[at * CELLS : (at + 1) * CELLS], *[f[at * SIDE : (at + 1) * SIDE] for f in (face_a, face_b)]],
            axis=0,
        )
        for at in (0, NB - 1)
    ]
    tile_a = lax.ppermute(jnp.where(odd_row, top, bottom), "tile", swap_a)
    tile_b = lax.ppermute(jnp.where(odd_row, bottom, top), "tile", swap_b)

    window, edge_keys, edge_va = pl.pallas_call(
        kernel_window,
        in_specs=[SMEM] + [VMEM] * 7,
        out_specs=[VMEM] * 3,
        out_shape=[array(D, ROWS), array(4 * GROUP, D), array(PAIRS * VROWS, 4 * GROUP)],
        scratch_shapes=[
            pltpu.VMEM((NB * GROUP, D), BF),
            pltpu.VMEM((PAIRS * VROWS, NB * GROUP), BF),
            bad,
        ],
        cost_estimate=cost(4 << 30, 7 * MIB, ROWS * HEADS * WINDOW),
        compiler_params=params,
        name="window",
    )(land_bands, face_a, face_b, gains, qkv_weight[0], q, k, v)

    result = pl.pallas_call(
        kernel_last,
        in_specs=[SMEM] + [VMEM] * 14,
        out_specs=VMEM,
        out_shape=array(ROWS, D),
        scratch_shapes=[
            pltpu.VMEM((2 * WINDOW, D), BF),
            pltpu.VMEM((PAIRS * VROWS, 2 * WINDOW), BF),
            pltpu.VMEM((D, ROWS), BF),
            bad,
        ],
        cost_estimate=cost(5 << 30, 11 * MIB, ROWS * HEADS * 512),
        compiler_params=pltpu.CompilerParams(vmem_limit_bytes=28 * MIB),
        name="last",
    )(
        land_bands,
        tile_a,
        tile_b,
        edge_keys,
        edge_va,
        q,
        window,
        cross,
        x,
        gains,
        qkv_weight[0],
        out_weight[0],
        cross_out[0],
        up_weight[0],
        down_weight[0],
    )
    return result.reshape(1, NB * BR, RX, D)


def solution(mesh):
    placed = (
        P("comp", "tile", "face", None),
        P("comp", None, None),
        P("comp", None, None),
        P("comp", None, None),
        P("comp", None, None),
        P("comp", None, None),
        P("comp", None, None),
        P("comp", None, None),
        P("comp", None, None),
        P(None, "tile", "face", None),
        P(),
    )
    return jax.shard_map(
        per_device,
        mesh=mesh,
        in_specs=placed,
        out_specs=P("comp", "tile", "face", None),
        check_vma=False,
    )
```

time: 56.2 us -> 49.2 us (0.88)
  the two profiles are of different devices: /device:TPU:30 before, /device:TPU:0 now
where the time goes in v7:
time: 49.2 us; the launch traced here: 49 us
  Pallas kernels  30.1 us (61%)
  starting transfers between devices  12.3 us (25%)
  local copies, waits for them, and re-layouts  3.46 us (7%)
  other arithmetic  2.48 us (5%)
    pallas_call x1, Pallas kernels, per_device(): pl.pallas_call(kernel_last, in_specs=[SMEM] + [VMEM] * 14, out_specs=VMEM...  10.9 us
    pallas_call x1, Pallas kernels, per_device(): pl.pallas_call(kernel_window, in_specs=[SMEM] + [VMEM] * 7, out_specs=[VM...  7.75 us
    pallas_call x1, Pallas kernels, per_device(): pl.pallas_call(kernel_cross, in_specs=[SMEM] * 2 + [VMEM] * 2, out_specs=...  7.16 us
    ppermute x1, starting transfers between devices, per_device(): tile_b = lax.ppermute(jnp.where(odd_row, bottom, top), 'tile', swap_b)  5.41 us
    ppermute x1, starting transfers between devices, per_device(): face_b = lax.ppermute(face_src_b, 'face', swap_b).reshape(NB * SIDE, D)  3.54 us
    pallas_call x1, Pallas kernels, per_device(): pl.pallas_call(kernel_own, grid=(2,), in_specs=[block, pl.BlockSpec((3, D...  2.75 us
    unnamed x24, local copies, waits for them, and re-layouts  2.49 us
    select_n x1, other arithmetic, columns(): return (jnp.where(odd_col, low, high), jnp.where(odd_col, high, low))  2.38 us
  transfers between devices with their start and end apart: 5, of which 1 were waited for; matrix products, arithmetic and copies ran while one was open for 0% of the time, Pallas kernels for 36%

profile of v7, /device:TPU:0, one launch (start us, length us, event | category | flops | bytes accessed | tf_op | source)
XLA Modules:
  0.0 49.0 jit_solution(1653804474098697927)
XLA Ops:
  0.0 0.0 copy-start
  0.0 0.0 copy-start.2
  0.0 0.0 copy-start.1
  0.0 2.4 %broadcast_select_fusion = (bf16[64,8,512]{2,1,0:T(8,128)(2,1)}, bf16[64,8,512]{2,1,0:T(8,128)(2,1)}) fusion(pred[]{:T(512)S(6)} %eq.10, bf16[64,16,512]{2,1,0:T(8,128)(2,1)} %bitcast.18), kind=kLoop, calls=%fused_computation | loop fusion | flops 524288 | bytes 2097153 | tf_op jit(solution)/shard_map/jit(_where)/select_n | solution.py:383
  2.4 0.0 copy-done
  2.4 0.0 copy-done.2
  2.4 0.0 copy-done.1
  2.4 1.6 %cross_kv.1 = bf16[1024,1024]{1,0:T(8,128)(2,1)S(1)} custom-call(bf16[1024,512]{1,0:T(8,128)(2,1)S(1)} %bitcast.19, bf16[3,512]{1,0:T(4,128)(2,1)S(1)} %bitcast.23, bf16[512,1024]{1,0:T(8,128)(2,1)S(1)} %bitcast.22), custom_call_target="tpu_custom_call" | custom-call | flops 1073741824 | bytes 4194304 | tf_op jit(solution)/shard_map/cross_kv/pallas_call | solution.py:392
  4.0 0.1 collective-permute-start.2
  4.1 1.7 %collective-permute-start = (bf16[64,8,512]{2,1,0:T(8,128)(2,1)}, bf16[64,8,512]{2,1,0:T(8,128)(2,1)}, u32[]{:S(2)}, u32[]{:S(2)}) collective-permute-start(bf16[64,8,512]{2,1,0:T(8,128)(2,1)} %get-tuple-element.18), channel_id=1, source_target_pairs={{0,8},{8,0},{16,24},{24,16},{32,40},{40,32},{48,56},{56,48},{1,9},... | collective-permute-start | bytes 1572872 | tf_op jit(solution)/shard_map/ppermute | solution.py:386
  5.8 3.5 %collective-permute-start.1 = (bf16[64,8,512]{2,1,0:T(8,128)(2,1)}, bf16[64,8,512]{2,1,0:T(8,128)(2,1)}, u32[]{:S(2)}, u32[]{:S(2)}) collective-permute-start(bf16[64,8,512]{2,1,0:T(8,128)(2,1)} %get-tuple-element.19), channel_id=1, source_target_pairs={{0,56},{8,16},{16,8},{24,32},{32,24},{40,48},{48,40},{56,0},{1,57}... | collective-permute-start | bytes 1572872 | tf_op jit(solution)/shard_map/ppermute | solution.py:387
  9.4 0.0 copy-start.5
  9.4 1.4 %copy-done.5 = bf16[1,512,1536]{2,1,0:T(8,128)(2,1)S(1)} copy-done((bf16[1,512,1536]{2,1,0:T(8,128)(2,1)S(1)}, bf16[1,512,1536]{2,1,0:T(8,128)(2,1)}, u32[]{:S(2)}) %copy-start.5) | copy-done | bytes 1572888
  10.8 0.0 copy-start.7
  10.8 1.0 %copy-done.7 = bf16[1,512,512]{2,1,0:T(8,128)(2,1)S(1)} copy-done((bf16[1,512,512]{2,1,0:T(8,128)(2,1)S(1)}, bf16[1,512,512]{2,1,0:T(8,128)(2,1)}, u32[]{:S(2)}) %copy-start.7) | copy-done | bytes 524312
  11.9 0.0 copy-start.10
  11.9 0.0 copy-start.11
  11.9 2.7 %own.1 = (bf16[1024,512]{1,0:T(8,128)(2,1)S(1)}, bf16[1024,512]{1,0:T(8,128)(2,1)S(1)}, bf16[512,1024]{1,0:T(8,128)(2,1)S(1)}, bf16[1024,512]{1,0:T(8,128)(2,1)S(1)}) custom-call(bf16[1024,512]{1,0:T(8,128)(2,1)S(1)} %bitcast.20, bf16[3,512]{1,0:T(4,128)(2,1)S(1)} %bitcast.24, bf16[512,1536]{1,0:T(8,128)(2,1)S(1)} %bitcast.29, bf16[512,512]{1,0:T(8,128)(2,1)S(1)} %bitcast.32), custom_call_target="tpu_custom_call" | custom-call | flops 2147483648 | bytes 7340032 | tf_op jit(solution)/shard_map/own/pallas_call | solution.py:408
  14.6 0.0 collective-permute-done.2.kv_ref
  14.6 0.0 copy-done.10
  14.6 0.0 copy-done.11
  14.6 0.0 copy-start.6
  14.7 7.2 %cross.1.cross_ref = bf16[512,1024]{1,0:T(8,128)(2,1)S(1)} custom-call(s32[2,4,8]{2,1,0:T(4,128)S(1)} %bitcast.35, s32[8,8]{1,0:T(8,128)S(1)} %copy-done.11, bf16[1024,512]{1,0:T(8,128)(2,1)S(1)} %get-tuple-element.21.q_ref, bf16[1024,1024]{1,0:T(8,128)(2,1)} %collective-permute-done.2.kv_ref), custom_call_target="tpu_custom_call" | custom-call | flops 4294967296 | bytes 4194304 | tf_op jit(solution)/shard_map/cross/pallas_call | solution.py:425
  21.8 0.0 collective-permute-done
  21.8 0.4 collective-permute-done.1
  22.2 1.0 %fusion.1 = (bf16[64,512]{1,0:T(8,128)(2,1)S(1)}, bf16[64,512]{1,0:T(8,128)(2,1)S(1)}, bf16[64,512]{1,0:T(8,128)(2,1)S(1)}, bf16[64,512]{1,0:T(8,128)(2,1)S(1)}) fusion(bf16[512,512]{1,0:T(8,128)(2,1)} %bitcast.3.face_a_ref, bf16[512,512]{1,0:T(8,128)(2,1)} %bitcast.4.face_b_ref), kind=kLoop, calls=%fused_computation.7 | loop fusion | bytes 524288 | tf_op jit(solution)/shard_map/slice | solution.py:439
  23.2 0.1 broadcast_select_fusion.2
  23.3 1.6 %collective-permute-start.3 = (bf16[256,512]{1,0:T(8,128)(2,1)S(1)}, bf16[256,512]{1,0:T(8,128)(2,1)S(1)}, u32[]{:S(2)}, u32[]{:S(2)}) collective-permute-start(bf16[256,512]{1,0:T(8,128)(2,1)S(1)} %get-tuple-element.36), channel_id=1, source_target_pairs={{0,1},{1,0},{2,3},{3,2},{4,5},{5,4},{6,7},{7,6},{8,9},{9,8},{10,11... | collective-permute-start | bytes 786440 | tf_op jit(solution)/shard_map/ppermute | solution.py:444
  24.9 5.4 %collective-permute-start.4 = (bf16[256,512]{1,0:T(8,128)(2,1)S(1)}, bf16[256,512]{1,0:T(8,128)(2,1)S(1)}, u32[]{:S(2)}, u32[]{:S(2)}) collective-permute-start(bf16[256,512]{1,0:T(8,128)(2,1)S(1)} %get-tuple-element.35), channel_id=1, source_target_pairs={{0,7},{1,2},{2,1},{3,4},{4,3},{5,6},{6,5},{7,0},{8,15},{9,10},{10,... | collective-permute-start | bytes 786440 | tf_op jit(solution)/shard_map/ppermute | solution.py:445
  30.3 0.0 copy-done.6
  30.3 0.0 copy-start.3
  30.3 0.0 copy-start.4
  30.3 0.0 copy-start.8
  30.3 0.0 copy-start.9
  30.3 7.8 %window.1 = (bf16[512,1024]{1,0:T(8,128)(2,1)S(1)}, bf16[1024,512]{1,0:T(8,128)(2,1)S(1)}, bf16[576,1024]{1,0:T(8,128)(2,1)S(1)}) custom-call(s32[8,8]{1,0:T(8,128)S(1)} %copy-done.11, bf16[512,512]{1,0:T(8,128)(2,1)} %bitcast.3.face_a_ref, bf16[512,512]{1,0:T(8,128)(2,1)} %bitcast.4.face_b_ref, bf16[3,512]{1,0:T(4,128)(2,1)S(1)} %bitcast.25, ...), custom_call_target="tpu_custom_call" | custom-call | flops 8589934592 | bytes 7340032 | tf_op jit(solution)/shard_map/window/pallas_call | solution.py:447
  38.1 0.0 collective-permute-done.3.tile_a_ref
  38.1 0.0 collective-permute-done.4.tile_b_ref
  38.1 0.0 copy-done.3
  38.1 0.0 copy-done.4
  38.1 0.0 copy-done.8
  38.1 0.0 copy-done.9
  38.1 10.9 %last.1 = bf16[1024,512]{1,0:T(8,128)(2,1)} custom-call(s32[8,8]{1,0:T(8,128)S(1)} %copy-done.11, bf16[256,512]{1,0:T(8,128)(2,1)S(1)} %collective-permute-done.3.tile_a_ref, bf16[256,512]{1,0:T(8,128)(2,1)S(1)} %collective-permute-done.4.tile_b_ref, bf16[1024,512]{1,0:T(8,128)(2,1)S(1)} %get-tuple-element.27.edge_keys_ref, ...), custom_call_target="tpu_custom_call" | custom-call | flops 10737418240 | bytes 11534336 | tf_op jit(solution)/shard_map/last/pallas_call | solution.py:462
  (1 shorter events, 0.0 us)
Async XLA Ops:
  0.0 2.4 %copy-start = (bf16[1,64,16,512]{3,2,1,0:T(8,128)(2,1)S(1)}, bf16[1,64,16,512]{3,2,1,0:T(8,128)(2,1)}, u32[]{:S(2)}) copy-start(bf16[1,64,16,512]{3,2,1,0:T(8,128)(2,1)} %param.11) | copy-start | bytes 3145732
  0.0 2.4 %copy-start.2 = (bf16[1,3,512]{2,1,0:T(4,128)(2,1)S(1)}, bf16[1,3,512]{2,1,0:T(4,128)(2,1)}, u32[]{:S(2)}) copy-start(bf16[1,3,512]{2,1,0:T(4,128)(2,1)} %param.12) | copy-start | bytes 9220
  0.0 2.4 %copy-start.1 = (bf16[1,512,1024]{2,1,0:T(8,128)(2,1)S(1)}, bf16[1,512,1024]{2,1,0:T(8,128)(2,1)}, u32[]{:S(2)}) copy-start(bf16[1,512,1024]{2,1,0:T(8,128)(2,1)} %param.16) | copy-start | bytes 3145732
  4.0 10.6 %collective-permute-start.2 = (bf16[1024,1024]{1,0:T(8,128)(2,1)S(1)}, bf16[1024,1024]{1,0:T(8,128)(2,1)}, u32[]{:S(2)}, u32[]{:S(2)}) collective-permute-start(bf16[1024,1024]{1,0:T(8,128)(2,1)S(1)} %cross_kv.1), channel_id=1, source_target_pairs={{0,64},{64,0},{1,65},{65,1},{2,66},{66,2},{3,67},{67,3},{4,68},{68... | collective-permute-start | bytes 6291464 | tf_op jit(solution)/shard_map/ppermute | solution.py:406
  4.1 17.7 %collective-permute-start = (bf16[64,8,512]{2,1,0:T(8,128)(2,1)}, bf16[64,8,512]{2,1,0:T(8,128)(2,1)}, u32[]{:S(2)}, u32[]{:S(2)}) collective-permute-start(bf16[64,8,512]{2,1,0:T(8,128)(2,1)} %get-tuple-element.18), channel_id=1, source_target_pairs={{0,8},{8,0},{16,24},{24,16},{32,40},{40,32},{48,56},{56,48},{1,9},... | collective-permute-start | bytes 1572872 | tf_op jit(solution)/shard_map/ppermute | solution.py:386
  5.8 16.4 %collective-permute-start.1 = (bf16[64,8,512]{2,1,0:T(8,128)(2,1)}, bf16[64,8,512]{2,1,0:T(8,128)(2,1)}, u32[]{:S(2)}, u32[]{:S(2)}) collective-permute-start(bf16[64,8,512]{2,1,0:T(8,128)(2,1)} %get-tuple-element.19), channel_id=1, source_target_pairs={{0,56},{8,16},{16,8},{24,32},{32,24},{40,48},{48,40},{56,0},{1,57}... | collective-permute-start | bytes 1572872 | tf_op jit(solution)/shard_map/ppermute | solution.py:387
  9.4 1.4 %copy-start.5 = (bf16[1,512,1536]{2,1,0:T(8,128)(2,1)S(1)}, bf16[1,512,1536]{2,1,0:T(8,128)(2,1)}, u32[]{:S(2)}) copy-start(bf16[1,512,1536]{2,1,0:T(8,128)(2,1)} %param.13) | copy-start | bytes 4718596
  10.8 1.0 %copy-start.7 = (bf16[1,512,512]{2,1,0:T(8,128)(2,1)S(1)}, bf16[1,512,512]{2,1,0:T(8,128)(2,1)}, u32[]{:S(2)}) copy-start(bf16[1,512,512]{2,1,0:T(8,128)(2,1)} %param.15) | copy-start | bytes 1572868
  11.9 2.8 %copy-start.10 = (s32[2,8,1,4]{1,3,2,0:T(4,128)S(1)}, s32[2,8,1,4]{1,3,2,0:T(4,128)}, u32[]{:S(2)}) copy-start(s32[2,8,1,4]{1,3,2,0:T(4,128)} %param.20) | copy-start | bytes 772
  11.9 2.8 %copy-start.11 = (s32[8,8]{1,0:T(8,128)S(1)}, s32[8,8]{1,0:T(8,128)}, u32[]{:S(2)}) copy-start(s32[8,8]{1,0:T(8,128)} %land_ref.5) | copy-start | bytes 772
  14.6 15.6 %copy-start.6 = (bf16[1,512,1536]{2,1,0:T(8,128)(2,1)S(1)}, bf16[1,512,1536]{2,1,0:T(8,128)(2,1)}, u32[]{:S(2)}) copy-start(bf16[1,512,1536]{2,1,0:T(8,128)(2,1)} %param.13) | copy-start | bytes 4718596
  23.3 14.8 %collective-permute-start.3 = (bf16[256,512]{1,0:T(8,128)(2,1)S(1)}, bf16[256,512]{1,0:T(8,128)(2,1)S(1)}, u32[]{:S(2)}, u32[]{:S(2)}) collective-permute-start(bf16[256,512]{1,0:T(8,128)(2,1)S(1)} %get-tuple-element.36), channel_id=1, source_target_pairs={{0,1},{1,0},{2,3},{3,2},{4,5},{5,4},{6,7},{7,6},{8,9},{9,8},{10,11... | collective-permute-start | bytes 786440 | tf_op jit(solution)/shard_map/ppermute | solution.py:444
  24.9 13.2 %collective-permute-start.4 = (bf16[256,512]{1,0:T(8,128)(2,1)S(1)}, bf16[256,512]{1,0:T(8,128)(2,1)S(1)}, u32[]{:S(2)}, u32[]{:S(2)}) collective-permute-start(bf16[256,512]{1,0:T(8,128)(2,1)S(1)} %get-tuple-element.35), channel_id=1, source_target_pairs={{0,7},{1,2},{2,1},{3,4},{4,3},{5,6},{6,5},{7,0},{8,15},{9,10},{10,... | collective-permute-start | bytes 786440 | tf_op jit(solution)/shard_map/ppermute | solution.py:445
  30.3 7.8 %copy-start.3 = (bf16[1,512,2048]{2,1,0:T(8,128)(2,1)S(1)}, bf16[1,512,2048]{2,1,0:T(8,128)(2,1)}, u32[]{:S(2)}) copy-start(bf16[1,512,2048]{2,1,0:T(8,128)(2,1)} %param.18) | copy-start | bytes 6291460
  30.3 7.8 %copy-start.4 = (bf16[1,2048,512]{2,1,0:T(8,128)(2,1)S(1)}, bf16[1,2048,512]{2,1,0:T(8,128)(2,1)}, u32[]{:S(2)}) copy-start(bf16[1,2048,512]{2,1,0:T(8,128)(2,1)} %param.19) | copy-start | bytes 6291460
  30.3 7.8 %copy-start.8 = (bf16[1,512,512]{2,1,0:T(8,128)(2,1)S(1)}, bf16[1,512,512]{2,1,0:T(8,128)(2,1)}, u32[]{:S(2)}) copy-start(bf16[1,512,512]{2,1,0:T(8,128)(2,1)} %param.14) | copy-start | bytes 1572868
  30.3 7.8 %copy-start.9 = (bf16[1,512,512]{2,1,0:T(8,128)(2,1)S(1)}, bf16[1,512,512]{2,1,0:T(8,128)(2,1)}, u32[]{:S(2)}) copy-start(bf16[1,512,512]{2,1,0:T(8,128)(2,1)} %param.17) | copy-start | bytes 1572868

commit v8 on v7

--- a/solution.py
+++ b/solution.py
@@ -187,11 +187,7 @@
         index = jnp.where(r == 0, NB - 1, jnp.where(r == NB + 1, 0, r - 1))
         return [lat_ok & (is_air | (index >= land_ref[safe_row, c])) for c in columns]
 
-    return is_air, tile_row % 2 == 1, tile_col % 2 == 1, flags
-
-
-def sorted_pair(odd, a, b):
-    return jnp.where(odd, a, b), jnp.where(odd, b, a)
+    return is_air, flags
 
 
 def project(rows_x, gain_ref, qkv_ref):
@@ -216,8 +212,8 @@
 
 def kernel_window(
     land_ref,
-    face_a_ref,
-    face_b_ref,
+    west_ref,
+    east_ref,
     gain_ref,
     qkv_ref,
     q_ref,
@@ -230,20 +226,19 @@
     va_ref,
     bad_ref,
 ):
-    _, _, odd_col, flags = place(land_ref)
+    _, flags = place(land_ref)
 
     def put(r, offset, keys, values_t, flag):
         at = (r - 1) * GROUP + offset
         keys_ref[pl.ds(at, CELLS), :] = keys
         augment(values_t, flag, va_ref, at)
 
-    west, east = sorted_pair(odd_col, face_a_ref[...], face_b_ref[...])
     blocks = 2
     for b in range(blocks):
         members = range(1 + b * NB // blocks, 1 + (b + 1) * NB // blocks)
         rows_x = []
         for r in members:
-            rows_x += [side[(r - 1) * SIDE : r * SIDE] for side in (west, east)]
+            rows_x += [ref[(r - 1) * SIDE : r * SIDE, :] for ref in (west_ref, east_ref)]
         keys, values_t = project(jnp.concatenate(rows_x, axis=0), gain_ref, qkv_ref)
         for n, r in enumerate(members):
             at = slice(n * CELLS, (n + 1) * CELLS)
@@ -276,8 +271,8 @@
 
 def kernel_last(
     land_ref,
-    tile_a_ref,
-    tile_b_ref,
+    north_ref,
+    south_ref,
     edge_keys_ref,
     edge_va_ref,
     q_ref,
@@ -296,13 +291,10 @@
     full_ref,
     bad_ref,
 ):
-    is_air, odd_row, odd_col, flags = place(land_ref)
+    is_air, flags = place(land_ref)
     full_ref[:, CELLS : ROWS - CELLS] = win_ref[:, CELLS : ROWS - CELLS]
-    rows_x = []
-    for rows in sorted_pair(odd_row, tile_a_ref[...], tile_b_ref[...]):
-        west, east = sorted_pair(odd_col, rows[CELLS : CELLS + SIDE], rows[CELLS + SIDE :])
-        rows_x += [rows[:CELLS], west, east]
-    new_keys, new_values = project(jnp.concatenate(rows_x, axis=0), gain_ref, qkv_ref)
+    rows_x = jnp.concatenate([north_ref[...], south_ref[...]], axis=0)
+    new_keys, new_values = project(rows_x, gain_ref, qkv_ref)
     for n in range(2):
         new, held = n * WINDOW + n * 2 * GROUP, n * WINDOW + (1 - n) * GROUP
         src = slice(n * 2 * GROUP, (n + 1) * 2 * GROUP)
@@ -373,18 +365,13 @@
     grid_x = tokens[0]
     x = grid_x.reshape(ROWS, D)
     gains = norm_gains[0]
-    swap_a = [(i, i ^ 1) for i in range(8)]
-    swap_b = [(i, (i + 1) % 8 if i % 2 else (i - 1) % 8) for i in range(8)]
-    odd_row = lax.axis_index("tile") % 2 == 1
-    odd_col = lax.axis_index("face") % 2 == 1
-
-    def columns(block):
-        low, high = block[:, :BR], block[:, RX - BR :]
-        return jnp.where(odd_col, low, high), jnp.where(odd_col, high, low)
-
-    face_src_a, face_src_b, x_first = lax.optimization_barrier((*columns(grid_x), x))
-    face_a = lax.ppermute(face_src_a, "face", swap_a).reshape(NB * SIDE, D)
-    face_b = lax.ppermute(face_src_b, "face", swap_b).reshape(NB * SIDE, D)
+    forward = [(i, (i + 1) % 8) for i in range(8)]
+    backward = [((i + 1) % 8, i) for i in range(8)]
+    east_edge, west_edge, x_first = lax.optimization_barrier(
+        (grid_x[:, RX - BR :], grid_x[:, :BR], x)
+    )
+    west = lax.ppermute(east_edge, "face", forward).reshape(NB * SIDE, D)
+    east = lax.ppermute(west_edge, "face", backward).reshape(NB * SIDE, D)
 
     half = ROWS // 2
     block = pl.BlockSpec((half, D), lambda i: (i, 0))
@@ -433,16 +420,16 @@
         name="cross",
     )(intersection_list.transpose(0, 2, 3, 1).reshape(2, KC, NB), land_bands, cross_q, partner)
 
-    face_a, face_b, cross = lax.optimization_barrier((face_a, face_b, cross))
+    west, east, cross = lax.optimization_barrier((west, east, cross))
     top, bottom = [
         jnp.concatenate(
-            [x[at * CELLS : (at + 1) * CELLS], *[f[at * SIDE : (at + 1) * SIDE] for f in (face_a, face_b)]],
+            [x[at * CELLS : (at + 1) * CELLS], *[side[at * SIDE : (at + 1) * SIDE] for side in (west, east)]],
             axis=0,
         )
         for at in (0, NB - 1)
     ]
-    tile_a = lax.ppermute(jnp.where(odd_row, top, bottom), "tile", swap_a)
-    tile_b = lax.ppermute(jnp.where(odd_row, bottom, top), "tile", swap_b)
+    north = lax.ppermute(bottom, "tile", forward)
+    south = lax.ppermute(top, "tile", backward)
 
     window, edge_keys, edge_va = pl.pallas_call(
         kernel_window,
@@ -457,7 +444,7 @@
         cost_estimate=cost(4 << 30, 7 * MIB, ROWS * HEADS * WINDOW),
         compiler_params=params,
         name="window",
-    )(land_bands, face_a, face_b, gains, qkv_weight[0], q, k, v)
+    )(land_bands, west, east, gains, qkv_weight[0], q, k, v)
 
     result = pl.pallas_call(
         kernel_last,
@@ -475,8 +462,8 @@
         name="last",
     )(
         land_bands,
-        tile_a,
-        tile_b,
+        north,
+        south,
         edge_keys,
         edge_va,
         q,

time: 49.2 us -> 47.1 us (0.957)
  the two profiles are of different devices: /device:TPU:0 before, /device:TPU:30 now
where the time goes in v8:
time: 47.1 us; the launch traced here: 47 us
  Pallas kernels  28.4 us (60%)
  waiting for transfers between devices  10.5 us (22%)
  starting transfers between devices  6 us (13%)
  local copies, waits for them, and re-layouts  1.93 us (4%)
    pallas_call x1, Pallas kernels, per_device(): pl.pallas_call(kernel_last, in_specs=[SMEM] + [VMEM] * 14, out_specs=VMEM...  10.9 us
    pallas_call x1, Pallas kernels, per_device(): pl.pallas_call(kernel_window, in_specs=[SMEM] + [VMEM] * 7, out_specs=[VM...  6.99 us
    pallas_call x1, Pallas kernels, per_device(): pl.pallas_call(kernel_cross, in_specs=[SMEM] * 2 + [VMEM] * 2, out_specs=...  6.09 us
    ppermute x1, waiting for transfers between devices, per_device(): south = lax.ppermute(top, 'tile', backward)  3.8 us
    ppermute x1, starting transfers between devices, per_device(): north = lax.ppermute(bottom, 'tile', forward)  3.57 us
    ppermute x1, waiting for transfers between devices, per_device(): east = lax.ppermute(west_edge, 'face', backward).reshape(NB * SIDE, D)  3.41 us
    ppermute x1, waiting for transfers between devices, per_device(): west = lax.ppermute(east_edge, 'face', forward).reshape(NB * SIDE, D)  3.23 us
    pallas_call x1, Pallas kernels, per_device(): pl.pallas_call(kernel_own, grid=(2,), in_specs=[block, pl.BlockSpec((3, D...  2.82 us
  transfers between devices with their start and end apart: 5, of which 3 were waited for; matrix products, arithmetic and copies ran while one was open for 0% of the time, Pallas kernels for 34%

profile of v8, /device:TPU:30, one launch (start us, length us, event | category | flops | bytes accessed | tf_op | source)
XLA Modules:
  0.0 47.0 jit_solution(917638638406715450)
XLA Ops:
  0.0 0.0 copy-start
  0.0 0.0 copy-start.1
  0.0 0.0 copy-start.2
  0.0 1.4 %fusion.1 = (bf16[64,8,512]{2,1,0:T(8,128)(2,1)S(1)}, bf16[64,8,512]{2,1,0:T(8,128)(2,1)S(1)}) fusion(bf16[64,16,512]{2,1,0:T(8,128)(2,1)} %bitcast.18), kind=kLoop, calls=%fused_computation.3 | loop fusion | bytes 2097152 | tf_op jit(solution)/shard_map/slice | solution.py:371
  1.4 0.1 copy-done
  1.5 0.3 copy-done.1
  1.9 0.0 copy-done.2
  1.9 0.0 copy-start.5
  1.9 0.0 copy-start.6
  1.9 1.6 %cross_kv.1 = bf16[1024,1024]{1,0:T(8,128)(2,1)S(1)} custom-call(bf16[1024,512]{1,0:T(8,128)(2,1)S(1)} %bitcast.19, bf16[3,512]{1,0:T(4,128)(2,1)S(1)} %bitcast.27, bf16[512,1024]{1,0:T(8,128)(2,1)S(1)} %bitcast.22), custom_call_target="tpu_custom_call" | custom-call | flops 1073741824 | bytes 4194304 | tf_op jit(solution)/shard_map/cross_kv/pallas_call | solution.py:379
  3.5 0.1 collective-permute-start.2
  3.6 1.7 %collective-permute-start = (bf16[64,8,512]{2,1,0:T(8,128)(2,1)S(1)}, bf16[64,8,512]{2,1,0:T(8,128)(2,1)S(1)}, u32[]{:S(2)}, u32[]{:S(2)}) collective-permute-start(bf16[64,8,512]{2,1,0:T(8,128)(2,1)S(1)} %get-tuple-element.18), channel_id=1, source_target_pairs={{0,8},{8,16},{16,24},{24,32},{32,40},{40,48},{48,56},{56,0},{1,9},... | collective-permute-start | bytes 1572872 | tf_op jit(solution)/shard_map/ppermute | solution.py:373
  5.2 0.4 collective-permute-start.1
  5.7 0.0 copy-done.5
  5.7 0.0 copy-done.6
  5.7 0.0 copy-start.9
  5.7 0.0 copy-start.10
  5.7 2.8 %own.1 = (bf16[1024,512]{1,0:T(8,128)(2,1)S(1)}, bf16[1024,512]{1,0:T(8,128)(2,1)S(1)}, bf16[512,1024]{1,0:T(8,128)(2,1)S(1)}, bf16[1024,512]{1,0:T(8,128)(2,1)S(1)}) custom-call(bf16[1024,512]{1,0:T(8,128)(2,1)S(1)} %bitcast.20, bf16[3,512]{1,0:T(4,128)(2,1)S(1)} %bitcast.28, bf16[512,1536]{1,0:T(8,128)(2,1)S(1)} %bitcast.33, bf16[512,512]{1,0:T(8,128)(2,1)S(1)} %bitcast.36), custom_call_target="tpu_custom_call" | custom-call | flops 2147483648 | bytes 7340032 | tf_op jit(solution)/shard_map/own/pallas_call | solution.py:395
  8.6 0.0 collective-permute-done.2.kv_ref
  8.6 0.0 copy-done.9
  8.6 0.0 copy-done.10
  8.6 6.1 %cross.1.cross_ref = bf16[512,1024]{1,0:T(8,128)(2,1)S(1)} custom-call(s32[2,4,8]{2,1,0:T(4,128)S(1)} %bitcast.39, s32[8,8]{1,0:T(8,128)S(1)} %copy-done.10, bf16[1024,512]{1,0:T(8,128)(2,1)S(1)} %get-tuple-element.21.q_ref, bf16[1024,1024]{1,0:T(8,128)(2,1)S(1)} %collective-permute-done.2.kv_ref), custom_call_target="tpu_custom_call" | custom-call | flops 4294967296 | bytes 4194304 | tf_op jit(solution)/shard_map/cross/pallas_call | solution.py:412
  14.7 3.2 %collective-permute-done = bf16[64,8,512]{2,1,0:T(8,128)(2,1)S(1)} collective-permute-done((bf16[64,8,512]{2,1,0:T(8,128)(2,1)S(1)}, bf16[64,8,512]{2,1,0:T(8,128)(2,1)S(1)}, u32[]{:S(2)}, u32[]{:S(2)}) %collective-permute-start) | collective-permute-done | bytes 524320 | tf_op jit(solution)/shard_map/ppermute | solution.py:373
  17.9 3.4 %collective-permute-done.1 = bf16[64,8,512]{2,1,0:T(8,128)(2,1)S(1)} collective-permute-done((bf16[64,8,512]{2,1,0:T(8,128)(2,1)S(1)}, bf16[64,8,512]{2,1,0:T(8,128)(2,1)S(1)}, u32[]{:S(2)}, u32[]{:S(2)}) %collective-permute-start.1) | collective-permute-done | bytes 524320 | tf_op jit(solution)/shard_map/ppermute | solution.py:374
  21.4 3.6 %collective-permute-start.3 = (bf16[256,512]{1,0:T(8,128)(2,1)S(1)}, bf16[256,512]{1,0:T(8,128)(2,1)S(1)}, u32[]{:S(2)}, u32[]{:S(2)}) collective-permute-start(bf16[256,512]{1,0:T(8,128)(2,1)S(1)} %pad_maximum_fusion), channel_id=1, source_target_pairs={{0,1},{1,2},{2,3},{3,4},{4,5},{5,6},{6,7},{7,0},{8,9},{9,10},{10,1... | collective-permute-start | bytes 786440 | tf_op jit(solution)/shard_map/ppermute | solution.py:431
  25.0 0.3 collective-permute-start.4
  25.2 0.0 copy-start.3
  25.2 0.0 copy-start.4
  25.3 0.0 copy-start.7
  25.3 0.0 copy-start.8
  25.3 7.0 %window.1 = (bf16[512,1024]{1,0:T(8,128)(2,1)S(1)}, bf16[1024,512]{1,0:T(8,128)(2,1)S(1)}, bf16[576,1024]{1,0:T(8,128)(2,1)S(1)}) custom-call(s32[8,8]{1,0:T(8,128)S(1)} %copy-done.10, bf16[512,512]{1,0:T(8,128)(2,1)S(1)} %bitcast.24, bf16[512,512]{1,0:T(8,128)(2,1)S(1)} %bitcast.26, bf16[3,512]{1,0:T(4,128)(2,1)S(1)} %bitcast.29, ...), custom_call_target="tpu_custom_call" | custom-call | flops 8589934592 | bytes 7340032 | tf_op jit(solution)/shard_map/window/pallas_call | solution.py:434
  32.3 0.0 collective-permute-done.3.north_ref
  32.3 3.8 %collective-permute-done.4.south_ref = bf16[256,512]{1,0:T(8,128)(2,1)S(1)} collective-permute-done((bf16[256,512]{1,0:T(8,128)(2,1)S(1)}, bf16[256,512]{1,0:T(8,128)(2,1)S(1)}, u32[]{:S(2)}, u32[]{:S(2)}) %collective-permute-start.4) | collective-permute-done | bytes 262176 | tf_op jit(solution)/shard_map/ppermute | solution.py:432
  36.1 0.0 copy-done.3
  36.1 0.0 copy-done.4
  36.1 0.0 copy-done.7
  36.1 0.0 copy-done.8
  36.1 10.9 %last.1 = bf16[1024,512]{1,0:T(8,128)(2,1)} custom-call(s32[8,8]{1,0:T(8,128)S(1)} %copy-done.10, bf16[256,512]{1,0:T(8,128)(2,1)S(1)} %collective-permute-done.3.north_ref, bf16[256,512]{1,0:T(8,128)(2,1)S(1)} %collective-permute-done.4.south_ref, bf16[1024,512]{1,0:T(8,128)(2,1)S(1)} %get-tuple-element.27.edge_keys_ref, ...), custom_call_target="tpu_custom_call" | custom-call | flops 10737418240 | bytes 11534336 | tf_op jit(solution)/shard_map/last/pallas_call | solution.py:449
  (4 shorter events, 0.1 us)
Async XLA Ops:
  0.0 1.5 %copy-start = (bf16[1,64,16,512]{3,2,1,0:T(8,128)(2,1)S(1)}, bf16[1,64,16,512]{3,2,1,0:T(8,128)(2,1)}, u32[]{:S(2)}) copy-start(bf16[1,64,16,512]{3,2,1,0:T(8,128)(2,1)} %param.11) | copy-start | bytes 3145732
  0.0 1.9 %copy-start.1 = (bf16[1,512,1024]{2,1,0:T(8,128)(2,1)S(1)}, bf16[1,512,1024]{2,1,0:T(8,128)(2,1)}, u32[]{:S(2)}) copy-start(bf16[1,512,1024]{2,1,0:T(8,128)(2,1)} %param.16) | copy-start | bytes 3145732
  0.0 1.9 %copy-start.2 = (bf16[1,3,512]{2,1,0:T(4,128)(2,1)S(1)}, bf16[1,3,512]{2,1,0:T(4,128)(2,1)}, u32[]{:S(2)}) copy-start(bf16[1,3,512]{2,1,0:T(4,128)(2,1)} %param.12) | copy-start | bytes 9220
  1.9 3.8 %copy-start.5 = (bf16[1,512,1536]{2,1,0:T(8,128)(2,1)S(1)}, bf16[1,512,1536]{2,1,0:T(8,128)(2,1)}, u32[]{:S(2)}) copy-start(bf16[1,512,1536]{2,1,0:T(8,128)(2,1)} %param.13) | copy-start | bytes 4718596
  1.9 3.8 %copy-start.6 = (bf16[1,512,512]{2,1,0:T(8,128)(2,1)S(1)}, bf16[1,512,512]{2,1,0:T(8,128)(2,1)}, u32[]{:S(2)}) copy-start(bf16[1,512,512]{2,1,0:T(8,128)(2,1)} %param.15) | copy-start | bytes 1572868
  3.5 5.1 %collective-permute-start.2 = (bf16[1024,1024]{1,0:T(8,128)(2,1)S(1)}, bf16[1024,1024]{1,0:T(8,128)(2,1)S(1)}, u32[]{:S(2)}, u32[]{:S(2)}) collective-permute-start(bf16[1024,1024]{1,0:T(8,128)(2,1)S(1)} %cross_kv.1), channel_id=1, source_target_pairs={{0,64},{64,0},{1,65},{65,1},{2,66},{66,2},{3,67},{67,3},{4,68},{68... | collective-permute-start | bytes 6291464 | tf_op jit(solution)/shard_map/ppermute | solution.py:393
  3.6 14.3 %collective-permute-start = (bf16[64,8,512]{2,1,0:T(8,128)(2,1)S(1)}, bf16[64,8,512]{2,1,0:T(8,128)(2,1)S(1)}, u32[]{:S(2)}, u32[]{:S(2)}) collective-permute-start(bf16[64,8,512]{2,1,0:T(8,128)(2,1)S(1)} %get-tuple-element.18), channel_id=1, source_target_pairs={{0,8},{8,16},{16,24},{24,32},{32,40},{40,48},{48,56},{56,0},{1,9},... | collective-permute-start | bytes 1572872 | tf_op jit(solution)/shard_map/ppermute | solution.py:373
  5.2 16.1 %collective-permute-start.1 = (bf16[64,8,512]{2,1,0:T(8,128)(2,1)S(1)}, bf16[64,8,512]{2,1,0:T(8,128)(2,1)S(1)}, u32[]{:S(2)}, u32[]{:S(2)}) collective-permute-start(bf16[64,8,512]{2,1,0:T(8,128)(2,1)S(1)} %get-tuple-element.19), channel_id=1, source_target_pairs={{8,0},{16,8},{24,16},{32,24},{40,32},{48,40},{56,48},{0,56},{9,1},... | collective-permute-start | bytes 1572872 | tf_op jit(solution)/shard_map/ppermute | solution.py:374
  5.7 2.9 %copy-start.9 = (s32[2,8,1,4]{1,3,2,0:T(4,128)S(1)}, s32[2,8,1,4]{1,3,2,0:T(4,128)}, u32[]{:S(2)}) copy-start(s32[2,8,1,4]{1,3,2,0:T(4,128)} %param.20) | copy-start | bytes 772
  5.7 2.9 %copy-start.10 = (s32[8,8]{1,0:T(8,128)S(1)}, s32[8,8]{1,0:T(8,128)}, u32[]{:S(2)}) copy-start(s32[8,8]{1,0:T(8,128)} %land_ref.5) | copy-start | bytes 772
  21.4 10.9 %collective-permute-start.3 = (bf16[256,512]{1,0:T(8,128)(2,1)S(1)}, bf16[256,512]{1,0:T(8,128)(2,1)S(1)}, u32[]{:S(2)}, u32[]{:S(2)}) collective-permute-start(bf16[256,512]{1,0:T(8,128)(2,1)S(1)} %pad_maximum_fusion), channel_id=1, source_target_pairs={{0,1},{1,2},{2,3},{3,4},{4,5},{5,6},{6,7},{7,0},{8,9},{9,10},{10,1... | collective-permute-start | bytes 786440 | tf_op jit(solution)/shard_map/ppermute | solution.py:431
  25.0 11.1 %collective-permute-start.4 = (bf16[256,512]{1,0:T(8,128)(2,1)S(1)}, bf16[256,512]{1,0:T(8,128)(2,1)S(1)}, u32[]{:S(2)}, u32[]{:S(2)}) collective-permute-start(bf16[256,512]{1,0:T(8,128)(2,1)S(1)} %pad_maximum_fusion.1), channel_id=1, source_target_pairs={{1,0},{2,1},{3,2},{4,3},{5,4},{6,5},{7,6},{0,7},{9,8},{10,9},{11,1... | collective-permute-start | bytes 786440 | tf_op jit(solution)/shard_map/ppermute | solution.py:432
  25.2 10.9 %copy-start.3 = (bf16[1,512,2048]{2,1,0:T(8,128)(2,1)S(1)}, bf16[1,512,2048]{2,1,0:T(8,128)(2,1)}, u32[]{:S(2)}) copy-start(bf16[1,512,2048]{2,1,0:T(8,128)(2,1)} %param.18) | copy-start | bytes 6291460
  25.2 10.9 %copy-start.4 = (bf16[1,2048,512]{2,1,0:T(8,128)(2,1)S(1)}, bf16[1,2048,512]{2,1,0:T(8,128)(2,1)}, u32[]{:S(2)}) copy-start(bf16[1,2048,512]{2,1,0:T(8,128)(2,1)} %param.19) | copy-start | bytes 6291460
  25.3 10.8 %copy-start.7 = (bf16[1,512,512]{2,1,0:T(8,128)(2,1)S(1)}, bf16[1,512,512]{2,1,0:T(8,128)(2,1)}, u32[]{:S(2)}) copy-start(bf16[1,512,512]{2,1,0:T(8,128)(2,1)} %param.14) | copy-start | bytes 1572868
  25.3 10.8 %copy-start.8 = (bf16[1,512,512]{2,1,0:T(8,128)(2,1)S(1)}, bf16[1,512,512]{2,1,0:T(8,128)(2,1)}, u32[]{:S(2)}) copy-start(bf16[1,512,512]{2,1,0:T(8,128)(2,1)} %param.17) | copy-start | bytes 1572868

commit v9 on v8

--- a/solution.py
+++ b/solution.py
@@ -138,7 +138,7 @@
     c_ref[...] = (mm(cross_input, cq_ref[...]) * Q_SCALE).astype(BF)
 
 
-def kernel_cross(links_ref, land_ref, q_ref, kv_ref, out_ref, va_ref, bad_ref):
+def kernel_cross(links_ref, land_ref, q_ref, kv_ref, cross_w_ref, out_ref, va_ref, cross_ref, bad_ref):
     component = lax.axis_index("comp")
     own_land = land_ref[lax.axis_index("tile"), lax.axis_index("face")]
     floor = jnp.where(component == 1, 0, own_land)
@@ -171,7 +171,8 @@
     def lane(i):
         return aligned(i, CELLS)
 
-    attention(NB, queries, keys, values, penalties, lane, out_ref, bad_ref)
+    attention(NB, queries, keys, values, penalties, lane, cross_ref, bad_ref)
+    out_ref[...] = mm_tn(cross_ref[...], cross_w_ref[...])
 
 
 def place(land_ref):
@@ -208,6 +209,15 @@
         for rows, flag in zip((CELLS, SIDE, SIDE), flags(i + b)):
             pieces.append((rows, jnp.where(flag, 0.0, -1e30)))
     return pieces
+
+
+def finish(index, own_land, is_air, win_t, update, x_rows, gain_ref, out_w_ref, up_ref, down_ref):
+    live = jnp.where(is_air | (index >= own_land), 1.0, 0.0)
+    middle = x_rows.astype(F32) + live * (mm_tn(win_t, out_w_ref[...]) + update)
+    mlp_input = norm_round(middle, gain_ref[2:3, :])
+    gate = 0.5 * mm(mlp_input, up_ref[...])
+    hidden = (gate + gate * jnp.tanh(gate)).astype(BF)
+    return (middle + live * mm(hidden, down_ref[...])).astype(BF)
 
 
 def kernel_window(
@@ -219,14 +229,20 @@
     q_ref,
     k_ref,
     v_ref,
-    win_ref,
+    update_ref,
+    x_ref,
+    out_w_ref,
+    up_ref,
+    down_ref,
+    out_ref,
     edge_keys_ref,
     edge_va_ref,
     keys_ref,
     va_ref,
+    win_ref,
     bad_ref,
 ):
-    _, flags = place(land_ref)
+    is_air, flags = place(land_ref)
 
     def put(r, offset, keys, values_t, flag):
         at = (r - 1) * GROUP + offset
@@ -268,6 +284,25 @@
 
     attention(NB - 2, queries, keys_of, values_of, penalties, lane, win_ref, bad_ref)
 
+    own_land = land_ref[lax.axis_index("tile"), lax.axis_index("face")]
+    chunk = (NB - 2) * CELLS // 2
+    for c in range(2):
+        start = CELLS + c * chunk
+        at = slice(start, start + chunk)
+        index = (start + lax.broadcasted_iota(jnp.int32, (chunk, 1), 0)) // CELLS
+        out_ref[at, :] = finish(
+            index,
+            own_land,
+            is_air,
+            win_ref[:, at],
+            update_ref[at, :],
+            x_ref[at, :],
+            gain_ref,
+            out_w_ref,
+            up_ref,
+            down_ref,
+        )
+
 
 def kernel_last(
     land_ref,
@@ -276,23 +311,24 @@
     edge_keys_ref,
     edge_va_ref,
     q_ref,
-    win_ref,
-    cross_ref,
+    update_ref,
     x_ref,
     gain_ref,
     qkv_ref,
     out_w_ref,
-    cross_w_ref,
     up_ref,
     down_ref,
-    out_ref,
+    held_hbm,
+    out_hbm,
     keys_ref,
     va_ref,
-    full_ref,
+    win_ref,
+    rows_ref,
     bad_ref,
+    sem,
 ):
+    del held_hbm
     is_air, flags = place(land_ref)
-    full_ref[:, CELLS : ROWS - CELLS] = win_ref[:, CELLS : ROWS - CELLS]
     rows_x = jnp.concatenate([north_ref[...], south_ref[...]], axis=0)
     new_keys, new_values = project(rows_x, gain_ref, qkv_ref)
     for n in range(2):
@@ -319,25 +355,42 @@
         return window_penalties(flags, n * (NB - 1))
 
     def lane(n):
-        return aligned(n, ROWS - CELLS)
-
-    attention(2, queries, keys_of, values_of, penalties, lane, full_ref, bad_ref)
-
-    chunk = 512
+        return aligned(n, CELLS)
+
+    attention(2, queries, keys_of, values_of, penalties, lane, win_ref, bad_ref)
+
+    def edge_rows(ref):
+        return jnp.concatenate([ref[:CELLS, :], ref[ROWS - CELLS :, :]], axis=0)
+
     own_land = land_ref[lax.axis_index("tile"), lax.axis_index("face")]
-    for c in range(ROWS // chunk):
-        at = slice(c * chunk, (c + 1) * chunk)
-        index = (c * chunk + lax.broadcasted_iota(jnp.int32, (chunk, 1), 0)) // CELLS
-        live = jnp.where(is_air | (index >= own_land), 1.0, 0.0)
-        update = mm_tn(full_ref[:, at], out_w_ref[...]) + mm_tn(cross_ref[:, at], cross_w_ref[...])
-        middle = x_ref[at, :].astype(F32) + live * update
-        mlp_input = norm_round(middle, gain_ref[2:3, :])
-        gate = 0.5 * mm(mlp_input, up_ref[...])
-        hidden = (gate + gate * jnp.tanh(gate)).astype(BF)
-        out_ref[at, :] = (middle + live * mm(hidden, down_ref[...])).astype(BF)
+    index = lax.broadcasted_iota(jnp.int32, (2 * CELLS, 1), 0) // CELLS * (NB - 1)
+    rows_ref[...] = finish(
+        index,
+        own_land,
+        is_air,
+        win_ref[...],
+        edge_rows(update_ref),
+        edge_rows(x_ref),
+        gain_ref,
+        out_w_ref,
+        up_ref,
+        down_ref,
+    )
+    copies = []
+    for n in range(2):
+        copy = pltpu.make_async_copy(
+            rows_ref.at[pl.ds(n * CELLS, CELLS)],
+            out_hbm.at[pl.ds(n * (ROWS - CELLS), CELLS)],
+            sem.at[n],
+        )
+        copy.start()
+        copies.append(copy)
+    for copy in copies:
+        copy.wait()
 
 
 VMEM = pl.BlockSpec(memory_space=pltpu.VMEM)
+ANY = pl.BlockSpec(memory_space=pl.ANY)
 SMEM = pl.BlockSpec(memory_space=pltpu.SMEM)
 
 
@@ -409,18 +462,24 @@
     )(x_first, gains, qkv_weight[0], cross_query[0])
 
     bad = pltpu.VMEM((8, 2 * CELLS), F32)
-    cross = pl.pallas_call(
+    update = pl.pallas_call(
         kernel_cross,
-        in_specs=[SMEM] * 2 + [VMEM] * 2,
+        in_specs=[SMEM] * 2 + [VMEM] * 3,
         out_specs=VMEM,
-        out_shape=array(D, ROWS),
-        scratch_shapes=[pltpu.VMEM((PAIRS * VROWS, ROWS), BF), bad],
+        out_shape=jax.ShapeDtypeStruct((ROWS, D), F32),
+        scratch_shapes=[pltpu.VMEM((PAIRS * VROWS, ROWS), BF), pltpu.VMEM((D, ROWS), BF), bad],
         cost_estimate=cost(8 * ROWS * 512 * D, 4 * MIB, ROWS * HEADS * 512),
         compiler_params=params,
         name="cross",
-    )(intersection_list.transpose(0, 2, 3, 1).reshape(2, KC, NB), land_bands, cross_q, partner)
-
-    west, east, cross = lax.optimization_barrier((west, east, cross))
+    )(
+        intersection_list.transpose(0, 2, 3, 1).reshape(2, KC, NB),
+        land_bands,
+        cross_q,
+        partner,
+        cross_out[0],
+    )
+
+    west, east, update = lax.optimization_barrier((west, east, update))
     top, bottom = [
         jnp.concatenate(
             [x[at * CELLS : (at + 1) * CELLS], *[side[at * SIDE : (at + 1) * SIDE] for side in (west, east)]],
@@ -431,34 +490,52 @@
     north = lax.ppermute(bottom, "tile", forward)
     south = lax.ppermute(top, "tile", backward)
 
-    window, edge_keys, edge_va = pl.pallas_call(
+    inner, edge_keys, edge_va = pl.pallas_call(
         kernel_window,
-        in_specs=[SMEM] + [VMEM] * 7,
+        in_specs=[SMEM] + [VMEM] * 12,
         out_specs=[VMEM] * 3,
-        out_shape=[array(D, ROWS), array(4 * GROUP, D), array(PAIRS * VROWS, 4 * GROUP)],
+        out_shape=[array(ROWS, D), array(4 * GROUP, D), array(PAIRS * VROWS, 4 * GROUP)],
         scratch_shapes=[
             pltpu.VMEM((NB * GROUP, D), BF),
             pltpu.VMEM((PAIRS * VROWS, NB * GROUP), BF),
+            pltpu.VMEM((D, ROWS), BF),
             bad,
         ],
-        cost_estimate=cost(4 << 30, 7 * MIB, ROWS * HEADS * WINDOW),
-        compiler_params=params,
+        cost_estimate=cost(6 << 30, 12 * MIB, ROWS * HEADS * WINDOW),
+        compiler_params=pltpu.CompilerParams(vmem_limit_bytes=28 * MIB),
         name="window",
-    )(land_bands, west, east, gains, qkv_weight[0], q, k, v)
+    )(
+        land_bands,
+        west,
+        east,
+        gains,
+        qkv_weight[0],
+        q,
+        k,
+        v,
+        update,
+        x,
+        out_weight[0],
+        up_weight[0],
+        down_weight[0],
+    )
 
     result = pl.pallas_call(
         kernel_last,
-        in_specs=[SMEM] + [VMEM] * 14,
-        out_specs=VMEM,
+        in_specs=[SMEM] + [VMEM] * 12 + [ANY],
+        out_specs=ANY,
         out_shape=array(ROWS, D),
+        input_output_aliases={13: 0},
         scratch_shapes=[
             pltpu.VMEM((2 * WINDOW, D), BF),
             pltpu.VMEM((PAIRS * VROWS, 2 * WINDOW), BF),
-            pltpu.VMEM((D, ROWS), BF),
+            pltpu.VMEM((D, 2 * CELLS), BF),
+            pltpu.VMEM((2 * CELLS, D), BF),
             bad,
+            pltpu.SemaphoreType.DMA((2,)),
         ],
-        cost_estimate=cost(5 << 30, 11 * MIB, ROWS * HEADS * 512),
-        compiler_params=pltpu.CompilerParams(vmem_limit_bytes=28 * MIB),
+        cost_estimate=cost(2 << 30, 8 * MIB, ROWS * HEADS * 256),
+        compiler_params=params,
         name="last",
     )(
         land_bands,
@@ -467,15 +544,14 @@
         edge_keys,
         edge_va,
         q,
-        window,
-        cross,
+        update,
         x,
         gains,
         qkv_weight[0],
         out_weight[0],
-        cross_out[0],
         up_weight[0],
         down_weight[0],
+        inner,
     )
     return result.reshape(1, NB * BR, RX, D)
 

time: 47.1 us -> 46.3 us (0.983)
  waiting for transfers between devices: 10.5 us -> 5.81 us
  starting transfers between devices: 6 us -> 8.14 us
  Pallas kernels: 28.4 us -> 29.7 us
    ppermute x1, waiting for transfers between devices: 3.8 us -> 0.01 us  [per_device(): south = lax.ppermute(top, 'tile', backward)]
    ppermute x1, starting transfers between devices: 3.57 us -> 5.04 us  [per_device(): north = lax.ppermute(bottom, 'tile', forward)]
    pallas_call x3, Pallas kernels: 24 us -> 25.3 us  [the longest x1 12.9 us: per_device(): pl.pallas_call(kernel_window, in_specs=[SMEM] + [VMEM] * 12, out_specs=[V...]
    ppermute x1, waiting for transfers between devices: 3.23 us -> 2.4 us  [per_device(): west = lax.ppermute(east_edge, 'face', forward).reshape(NB * SIDE, D)]
    ppermute x1, starting transfers between devices: 0.26 us -> 0.92 us  [per_device(): south = lax.ppermute(top, 'tile', backward)]
  transfers between devices with their start and end apart: 5 -> 5, of which waited for: 3 -> 2; matrix products, arithmetic and copies ran while one was open for 0% -> 0% of each run, Pallas kernels for 34% -> 49%
where the time goes in v9:
time: 46.3 us; the launch traced here: 46 us
  Pallas kernels  29.7 us (64%)
  starting transfers between devices  8.14 us (18%)
  waiting for transfers between devices  5.81 us (13%)
  local copies, waits for them, and re-layouts  1.94 us (4%)
    pallas_call x1, Pallas kernels, per_device(): pl.pallas_call(kernel_window, in_specs=[SMEM] + [VMEM] * 12, out_specs=[V...  12.9 us
    pallas_call x1, Pallas kernels, per_device(): pl.pallas_call(kernel_cross, in_specs=[SMEM] * 2 + [VMEM] * 3, out_specs=...  6.85 us
    pallas_call x1, Pallas kernels, per_device(): pl.pallas_call(kernel_last, in_specs=[SMEM] + [VMEM] * 12 + [ANY], out_sp...  5.58 us
    ppermute x1, starting transfers between devices, per_device(): north = lax.ppermute(bottom, 'tile', forward)  5.04 us
    ppermute x1, waiting for transfers between devices, per_device(): east = lax.ppermute(west_edge, 'face', backward).reshape(NB * SIDE, D)  3.4 us
    pallas_call x1, Pallas kernels, per_device(): pl.pallas_call(kernel_own, grid=(2,), in_specs=[block, pl.BlockSpec((3, D...  2.82 us
    ppermute x1, waiting for transfers between devices, per_device(): west = lax.ppermute(east_edge, 'face', forward).reshape(NB * SIDE, D)  2.4 us
    ppermute x1, starting transfers between devices, per_device(): west = lax.ppermute(east_edge, 'face', forward).reshape(NB * SIDE, D)  1.64 us
  transfers between devices with their start and end apart: 5, of which 2 were waited for; matrix products, arithmetic and copies ran while one was open for 0% of the time, Pallas kernels for 49%

profile of v9, /device:TPU:30, one launch (start us, length us, event | category | flops | bytes accessed | tf_op | source)
XLA Modules:
  0.0 46.0 jit_solution(13650534936169546745)
XLA Ops:
  0.0 0.0 copy-start
  0.0 0.0 copy-start.2
  0.0 0.0 copy-start.1
  0.0 1.4 %fusion.1 = (bf16[64,8,512]{2,1,0:T(8,128)(2,1)S(1)}, bf16[64,8,512]{2,1,0:T(8,128)(2,1)S(1)}) fusion(bf16[64,16,512]{2,1,0:T(8,128)(2,1)} %bitcast.18), kind=kLoop, calls=%fused_computation.3 | loop fusion | bytes 2097152 | tf_op jit(solution)/shard_map/slice | solution.py:424
  1.4 0.1 copy-done
  1.5 0.0 copy-done.2
  1.5 0.3 copy-done.1
  1.9 0.0 copy-start.5
  1.9 0.0 copy-start.6
  1.9 1.6 %cross_kv.1 = bf16[1024,1024]{1,0:T(8,128)(2,1)S(1)} custom-call(bf16[1024,512]{1,0:T(8,128)(2,1)S(1)} %bitcast.19, bf16[3,512]{1,0:T(4,128)(2,1)S(1)} %bitcast.28, bf16[512,1024]{1,0:T(8,128)(2,1)S(1)} %bitcast.23), custom_call_target="tpu_custom_call" | custom-call | flops 1073741824 | bytes 4194304 | tf_op jit(solution)/shard_map/cross_kv/pallas_call | solution.py:432
  3.5 0.1 collective-permute-start.2
  3.6 1.6 %collective-permute-start = (bf16[64,8,512]{2,1,0:T(8,128)(2,1)S(1)}, bf16[64,8,512]{2,1,0:T(8,128)(2,1)S(1)}, u32[]{:S(2)}, u32[]{:S(2)}) collective-permute-start(bf16[64,8,512]{2,1,0:T(8,128)(2,1)S(1)} %get-tuple-element.18), channel_id=1, source_target_pairs={{0,8},{8,16},{16,24},{24,32},{32,40},{40,48},{48,56},{56,0},{1,9},... | collective-permute-start | bytes 1572872 | tf_op jit(solution)/shard_map/ppermute | solution.py:426
  5.2 0.5 collective-permute-start.1
  5.7 0.0 copy-done.5
  5.7 0.0 copy-done.6
  5.7 0.0 copy-start.7
  5.7 0.0 copy-start.9
  5.7 0.0 copy-start.10
  5.7 2.8 %own.1 = (bf16[1024,512]{1,0:T(8,128)(2,1)S(1)}, bf16[1024,512]{1,0:T(8,128)(2,1)S(1)}, bf16[512,1024]{1,0:T(8,128)(2,1)S(1)}, bf16[1024,512]{1,0:T(8,128)(2,1)S(1)}) custom-call(bf16[1024,512]{1,0:T(8,128)(2,1)S(1)} %bitcast.20, bf16[3,512]{1,0:T(4,128)(2,1)S(1)} %bitcast.29, bf16[512,1536]{1,0:T(8,128)(2,1)S(1)} %bitcast.36, bf16[512,512]{1,0:T(8,128)(2,1)S(1)} %bitcast.39), custom_call_target="tpu_custom_call" | custom-call | flops 2147483648 | bytes 7340032 | tf_op jit(solution)/shard_map/own/pallas_call | solution.py:448
  8.6 0.0 collective-permute-done.2.kv_ref
  8.6 0.0 copy-done.7
  8.6 0.0 copy-done.9
  8.6 0.0 copy-done.10
  8.6 0.0 copy-start.3
  8.6 0.0 copy-start.4
  8.6 0.0 copy-start.8
  8.7 6.9 %cross.1.update_ref = f32[1024,512]{1,0:T(8,128)S(1)} custom-call(s32[2,4,8]{2,1,0:T(4,128)S(1)} %bitcast.43, s32[8,8]{1,0:T(8,128)S(1)} %copy-done.10, bf16[1024,512]{1,0:T(8,128)(2,1)S(1)} %get-tuple-element.21.q_ref, bf16[1024,1024]{1,0:T(8,128)(2,1)S(1)} %collective-permute-done.2.kv_ref, bf16[512,512]{1,0:T(8,128)(2,1)S(1)} %bitcast.40), custom_call_target="tpu_custom_call" | custom-call | flops 4294967296 | bytes 4194304 | tf_op jit(solution)/shard_map/cross/pallas_call | solution.py:465
  15.5 2.4 %collective-permute-done = bf16[64,8,512]{2,1,0:T(8,128)(2,1)S(1)} collective-permute-done((bf16[64,8,512]{2,1,0:T(8,128)(2,1)S(1)}, bf16[64,8,512]{2,1,0:T(8,128)(2,1)S(1)}, u32[]{:S(2)}, u32[]{:S(2)}) %collective-permute-start) | collective-permute-done | bytes 524320 | tf_op jit(solution)/shard_map/ppermute | solution.py:426
  17.9 3.4 %collective-permute-done.1 = bf16[64,8,512]{2,1,0:T(8,128)(2,1)S(1)} collective-permute-done((bf16[64,8,512]{2,1,0:T(8,128)(2,1)S(1)}, bf16[64,8,512]{2,1,0:T(8,128)(2,1)S(1)}, u32[]{:S(2)}, u32[]{:S(2)}) %collective-permute-start.1) | collective-permute-done | bytes 524320 | tf_op jit(solution)/shard_map/ppermute | solution.py:427
  21.4 0.9 %collective-permute-start.4 = (bf16[256,512]{1,0:T(8,128)(2,1)S(1)}, bf16[256,512]{1,0:T(8,128)(2,1)S(1)}, u32[]{:S(2)}, u32[]{:S(2)}) collective-permute-start(bf16[256,512]{1,0:T(8,128)(2,1)S(1)} %pad_maximum_fusion.1), channel_id=1, source_target_pairs={{1,0},{2,1},{3,2},{4,3},{5,4},{6,5},{7,6},{0,7},{9,8},{10,9},{11,1... | collective-permute-start | bytes 786440 | tf_op jit(solution)/shard_map/ppermute | solution.py:491
  22.3 5.0 %collective-permute-start.3 = (bf16[256,512]{1,0:T(8,128)(2,1)S(1)}, bf16[256,512]{1,0:T(8,128)(2,1)S(1)}, u32[]{:S(2)}, u32[]{:S(2)}) collective-permute-start(bf16[256,512]{1,0:T(8,128)(2,1)S(1)} %pad_maximum_fusion), channel_id=1, source_target_pairs={{0,1},{1,2},{2,3},{3,4},{4,5},{5,6},{6,7},{7,0},{8,9},{9,10},{10,1... | collective-permute-start | bytes 786440 | tf_op jit(solution)/shard_map/ppermute | solution.py:490
  27.3 0.0 copy-done.3
  27.3 0.0 copy-done.4
  27.4 0.0 copy-done.8
  27.4 12.9 %window.1 = (bf16[1024,512]{1,0:T(8,128)(2,1)}, bf16[1024,512]{1,0:T(8,128)(2,1)S(1)}, bf16[576,1024]{1,0:T(8,128)(2,1)S(1)}) custom-call(s32[8,8]{1,0:T(8,128)S(1)} %copy-done.10, bf16[512,512]{1,0:T(8,128)(2,1)S(1)} %bitcast.25, bf16[512,512]{1,0:T(8,128)(2,1)S(1)} %bitcast.27, bf16[3,512]{1,0:T(4,128)(2,1)S(1)} %bitcast.30, ...), custom_call_target="tpu_custom_call" | custom-call | flops 12884901888 | bytes 12582912 | tf_op jit(solution)/shard_map/window/pallas_call | solution.py:493
  40.2 0.0 collective-permute-done.4.south_ref
  40.2 0.0 collective-permute-done.3.north_ref
  40.2 5.6 %last.1 = bf16[1024,512]{1,0:T(8,128)(2,1)} custom-call(s32[8,8]{1,0:T(8,128)S(1)} %copy-done.10, bf16[256,512]{1,0:T(8,128)(2,1)S(1)} %collective-permute-done.3.north_ref, bf16[256,512]{1,0:T(8,128)(2,1)S(1)} %collective-permute-done.4.south_ref, bf16[1024,512]{1,0:T(8,128)(2,1)S(1)} %get-tuple-element.28.edge_keys_ref, ...), custom_call_target="tpu_custom_call", output_to_operand_aliasing={{}: (13, {})} | custom-call | flops 4294967296 | bytes 8388608 | tf_op jit(solution)/shard_map/last/pallas_call | solution.py:523
  (4 shorter events, 0.1 us)
Async XLA Ops:
  0.0 1.5 %copy-start = (bf16[1,64,16,512]{3,2,1,0:T(8,128)(2,1)S(1)}, bf16[1,64,16,512]{3,2,1,0:T(8,128)(2,1)}, u32[]{:S(2)}) copy-start(bf16[1,64,16,512]{3,2,1,0:T(8,128)(2,1)} %param.11) | copy-start | bytes 3145732
  0.0 1.5 %copy-start.2 = (bf16[1,3,512]{2,1,0:T(4,128)(2,1)S(1)}, bf16[1,3,512]{2,1,0:T(4,128)(2,1)}, u32[]{:S(2)}) copy-start(bf16[1,3,512]{2,1,0:T(4,128)(2,1)} %param.12) | copy-start | bytes 9220
  0.0 1.9 %copy-start.1 = (bf16[1,512,1024]{2,1,0:T(8,128)(2,1)S(1)}, bf16[1,512,1024]{2,1,0:T(8,128)(2,1)}, u32[]{:S(2)}) copy-start(bf16[1,512,1024]{2,1,0:T(8,128)(2,1)} %param.16) | copy-start | bytes 3145732
  1.9 3.8 %copy-start.5 = (bf16[1,512,1536]{2,1,0:T(8,128)(2,1)S(1)}, bf16[1,512,1536]{2,1,0:T(8,128)(2,1)}, u32[]{:S(2)}) copy-start(bf16[1,512,1536]{2,1,0:T(8,128)(2,1)} %param.13) | copy-start | bytes 4718596
  1.9 3.8 %copy-start.6 = (bf16[1,512,512]{2,1,0:T(8,128)(2,1)S(1)}, bf16[1,512,512]{2,1,0:T(8,128)(2,1)}, u32[]{:S(2)}) copy-start(bf16[1,512,512]{2,1,0:T(8,128)(2,1)} %param.15) | copy-start | bytes 1572868
  3.5 5.1 %collective-permute-start.2 = (bf16[1024,1024]{1,0:T(8,128)(2,1)S(1)}, bf16[1024,1024]{1,0:T(8,128)(2,1)S(1)}, u32[]{:S(2)}, u32[]{:S(2)}) collective-permute-start(bf16[1024,1024]{1,0:T(8,128)(2,1)S(1)} %cross_kv.1), channel_id=1, source_target_pairs={{0,64},{64,0},{1,65},{65,1},{2,66},{66,2},{3,67},{67,3},{4,68},{68... | collective-permute-start | bytes 6291464 | tf_op jit(solution)/shard_map/ppermute | solution.py:446
  3.6 14.3 %collective-permute-start = (bf16[64,8,512]{2,1,0:T(8,128)(2,1)S(1)}, bf16[64,8,512]{2,1,0:T(8,128)(2,1)S(1)}, u32[]{:S(2)}, u32[]{:S(2)}) collective-permute-start(bf16[64,8,512]{2,1,0:T(8,128)(2,1)S(1)} %get-tuple-element.18), channel_id=1, source_target_pairs={{0,8},{8,16},{16,24},{24,32},{32,40},{40,48},{48,56},{56,0},{1,9},... | collective-permute-start | bytes 1572872 | tf_op jit(solution)/shard_map/ppermute | solution.py:426
  5.2 16.1 %collective-permute-start.1 = (bf16[64,8,512]{2,1,0:T(8,128)(2,1)S(1)}, bf16[64,8,512]{2,1,0:T(8,128)(2,1)S(1)}, u32[]{:S(2)}, u32[]{:S(2)}) collective-permute-start(bf16[64,8,512]{2,1,0:T(8,128)(2,1)S(1)} %get-tuple-element.19), channel_id=1, source_target_pairs={{8,0},{16,8},{24,16},{32,24},{40,32},{48,40},{56,48},{0,56},{9,1},... | collective-permute-start | bytes 1572872 | tf_op jit(solution)/shard_map/ppermute | solution.py:427
  5.7 2.9 %copy-start.7 = (bf16[1,512,512]{2,1,0:T(8,128)(2,1)S(1)}, bf16[1,512,512]{2,1,0:T(8,128)(2,1)}, u32[]{:S(2)}) copy-start(bf16[1,512,512]{2,1,0:T(8,128)(2,1)} %param.17) | copy-start | bytes 1572868
  5.7 2.9 %copy-start.9 = (s32[2,8,1,4]{1,3,2,0:T(4,128)S(1)}, s32[2,8,1,4]{1,3,2,0:T(4,128)}, u32[]{:S(2)}) copy-start(s32[2,8,1,4]{1,3,2,0:T(4,128)} %param.20) | copy-start | bytes 772
  5.7 2.9 %copy-start.10 = (s32[8,8]{1,0:T(8,128)S(1)}, s32[8,8]{1,0:T(8,128)}, u32[]{:S(2)}) copy-start(s32[8,8]{1,0:T(8,128)} %land_ref.5) | copy-start | bytes 772
  8.6 18.7 %copy-start.3 = (bf16[1,512,2048]{2,1,0:T(8,128)(2,1)S(1)}, bf16[1,512,2048]{2,1,0:T(8,128)(2,1)}, u32[]{:S(2)}) copy-start(bf16[1,512,2048]{2,1,0:T(8,128)(2,1)} %param.18) | copy-start | bytes 6291460
  8.6 18.7 %copy-start.4 = (bf16[1,2048,512]{2,1,0:T(8,128)(2,1)S(1)}, bf16[1,2048,512]{2,1,0:T(8,128)(2,1)}, u32[]{:S(2)}) copy-start(bf16[1,2048,512]{2,1,0:T(8,128)(2,1)} %param.19) | copy-start | bytes 6291460
  8.6 18.7 %copy-start.8 = (bf16[1,512,512]{2,1,0:T(8,128)(2,1)S(1)}, bf16[1,512,512]{2,1,0:T(8,128)(2,1)}, u32[]{:S(2)}) copy-start(bf16[1,512,512]{2,1,0:T(8,128)(2,1)} %param.14) | copy-start | bytes 1572868
  21.4 18.9 %collective-permute-start.4 = (bf16[256,512]{1,0:T(8,128)(2,1)S(1)}, bf16[256,512]{1,0:T(8,128)(2,1)S(1)}, u32[]{:S(2)}, u32[]{:S(2)}) collective-permute-start(bf16[256,512]{1,0:T(8,128)(2,1)S(1)} %pad_maximum_fusion.1), channel_id=1, source_target_pairs={{1,0},{2,1},{3,2},{4,3},{5,4},{6,5},{7,6},{0,7},{9,8},{10,9},{11,1... | collective-permute-start | bytes 786440 | tf_op jit(solution)/shard_map/ppermute | solution.py:491
  22.3 17.9 %collective-permute-start.3 = (bf16[256,512]{1,0:T(8,128)(2,1)S(1)}, bf16[256,512]{1,0:T(8,128)(2,1)S(1)}, u32[]{:S(2)}, u32[]{:S(2)}) collective-permute-start(bf16[256,512]{1,0:T(8,128)(2,1)S(1)} %pad_maximum_fusion), channel_id=1, source_target_pairs={{0,1},{1,2},{2,3},{3,4},{4,5},{5,6},{6,7},{7,0},{8,9},{9,10},{10,1... | collective-permute-start | bytes 786440 | tf_op jit(solution)/shard_map/ppermute | solution.py:490

commit v10 on v9

--- a/solution.py
+++ b/solution.py
@@ -69,7 +69,10 @@
 
 
 def blend(values_t, terms, extra):
-    both = mm(values_t, terms)
+    return share_out(mm(values_t, terms), extra)
+
+
+def share_out(both, extra):
     sums = both[LANES : LANES + 8]
     share = 1.0 / (sums + extra)
     half = LANES // 2
@@ -80,9 +83,7 @@
     return result.astype(BF), sums
 
 
-def attention(count, queries, keys, values, penalties, lane, out_ref, bad_ref):
-    bad_ref[...] = jnp.zeros_like(bad_ref)
-
+def products(count, queries, keys, values):
     def terms_of(i, p):
         return jnp.exp2(score(queries(i, p), keys(i, p))).astype(BF)
 
@@ -92,7 +93,15 @@
         terms = following
         if n + 1 < len(steps):
             following = terms_of(*steps[n + 1])
-        result, sums = blend(values(i, p), terms, 1.0)
+        yield i, p, mm(values(i, p), terms)
+
+
+def attention(count, queries, keys, values, penalties, lane, out_ref, bad_ref, sides=None):
+    bad_ref[...] = jnp.zeros_like(bad_ref)
+
+    some_keys, some_values, held = sides or (keys, values, lambda i, p: 0.0)
+    for i, p, both in products(count, queries, some_keys, some_values):
+        result, sums = share_out(both + held(i, p), 1.0)
         out_ref[pl.ds(p * LANES, LANES), pl.ds(lane(i), CELLS)] = result
         bad_ref[...] += jnp.where(sums < LIMIT, 0.0, 1.0)
 
@@ -220,6 +229,25 @@
     return (middle + live * mm(hidden, down_ref[...])).astype(BF)
 
 
+def kernel_near(land_ref, q_ref, k_ref, v_ref, part_ref, va_ref):
+    _, flags = place(land_ref)
+    for i in range(NB):
+        at = slice(i * CELLS, (i + 1) * CELLS)
+        augment(v_ref[:, at], flags(i + 1)[0], va_ref, i * CELLS)
+
+    def queries(n, p):
+        return q_ref[(n + 1) * CELLS : (n + 2) * CELLS, p * LANES : (p + 1) * LANES]
+
+    def keys(n, p):
+        return k_ref[n * CELLS : (n + 3) * CELLS, p * LANES : (p + 1) * LANES]
+
+    def values(n, p):
+        return va_ref[p * VROWS : (p + 1) * VROWS, n * CELLS : (n + 3) * CELLS]
+
+    for n, p, both in products(NB - 2, queries, keys, values):
+        part_ref[n * PAIRS + p] = both
+
+
 def kernel_window(
     land_ref,
     west_ref,
@@ -229,6 +257,7 @@
     q_ref,
     k_ref,
     v_ref,
+    part_ref,
     update_ref,
     x_ref,
     out_w_ref,
@@ -282,7 +311,23 @@
     def lane(n):
         return aligned(n, CELLS) + CELLS
 
-    attention(NB - 2, queries, keys_of, values_of, penalties, lane, win_ref, bad_ref)
+    def side_keys(n, p):
+        at = [(n + b) * GROUP + CELLS for b in range(3)]
+        return jnp.concatenate(
+            [keys_ref[a : a + CELLS, p * LANES : (p + 1) * LANES] for a in at], axis=0
+        )
+
+    def side_values(n, p):
+        at = [(n + b) * GROUP + CELLS for b in range(3)]
+        return jnp.concatenate(
+            [va_ref[p * VROWS : (p + 1) * VROWS, a : a + CELLS] for a in at], axis=1
+        )
+
+    def held(n, p):
+        return part_ref[n * PAIRS + p]
+
+    sides = (side_keys, side_values, held)
+    attention(NB - 2, queries, keys_of, values_of, penalties, lane, win_ref, bad_ref, sides)
 
     own_land = land_ref[lax.axis_index("tile"), lax.axis_index("face")]
     chunk = (NB - 2) * CELLS // 2
@@ -479,7 +524,18 @@
         cross_out[0],
     )
 
-    west, east, update = lax.optimization_barrier((west, east, update))
+    part = pl.pallas_call(
+        kernel_near,
+        in_specs=[SMEM] + [VMEM] * 3,
+        out_specs=VMEM,
+        out_shape=jax.ShapeDtypeStruct(((NB - 2) * PAIRS, VROWS, 2 * CELLS), F32),
+        scratch_shapes=[pltpu.VMEM((PAIRS * VROWS, ROWS), BF)],
+        cost_estimate=cost(6 * ROWS * 384 * D, 7 * MIB, ROWS * HEADS * 384),
+        compiler_params=params,
+        name="near",
+    )(land_bands, q, k, v)
+
+    west, east, update, part = lax.optimization_barrier((west, east, update, part))
     top, bottom = [
         jnp.concatenate(
             [x[at * CELLS : (at + 1) * CELLS], *[side[at * SIDE : (at + 1) * SIDE] for side in (west, east)]],
@@ -492,7 +548,7 @@
 
     inner, edge_keys, edge_va = pl.pallas_call(
         kernel_window,
-        in_specs=[SMEM] + [VMEM] * 12,
+        in_specs=[SMEM] + [VMEM] * 13,
         out_specs=[VMEM] * 3,
         out_shape=[array(ROWS, D), array(4 * GROUP, D), array(PAIRS * VROWS, 4 * GROUP)],
         scratch_shapes=[
@@ -513,6 +569,7 @@
         q,
         k,
         v,
+        part,
         update,
         x,
         out_weight[0],

time: 46.3 us -> 46.4 us (level)
  the two profiles are of different devices: /device:TPU:30 before, /device:TPU:1 now
where the time goes in v10:
time: 46.4 us; the launch traced here: 46.3 us
  Pallas kernels  32.6 us (70%)
  starting transfers between devices  11.4 us (25%)
  local copies, waits for them, and re-layouts  1.95 us (4%)
    pallas_call x1, Pallas kernels, per_device(): pl.pallas_call(kernel_window, in_specs=[SMEM] + [VMEM] * 13, out_specs=[V...  11.6 us
    pallas_call x1, Pallas kernels, per_device(): pl.pallas_call(kernel_cross, in_specs=[SMEM] * 2 + [VMEM] * 3, out_specs=...  7.05 us
    ppermute x1, starting transfers between devices, per_device(): south = lax.ppermute(top, 'tile', backward)  5.59 us
    pallas_call x1, Pallas kernels, per_device(): pl.pallas_call(kernel_last, in_specs=[SMEM] + [VMEM] * 12 + [ANY], out_sp...  5.57 us
    pallas_call x1, Pallas kernels, per_device(): pl.pallas_call(kernel_near, in_specs=[SMEM] + [VMEM] * 3, out_specs=VMEM,...  4.01 us
    ppermute x1, starting transfers between devices, per_device(): east = lax.ppermute(west_edge, 'face', backward).reshape(NB * SIDE, D)  2.78 us
    pallas_call x1, Pallas kernels, per_device(): pl.pallas_call(kernel_own, grid=(2,), in_specs=[block, pl.BlockSpec((3, D...  2.75 us
    pallas_call x1, Pallas kernels, per_device(): pl.pallas_call(kernel_cross_kv, grid=(2,), in_specs=[block, pl.BlockSpec(...  1.59 us
  transfers between devices with their start and end apart: 5, of which 0 were waited for; matrix products, arithmetic and copies ran while one was open for 0% of the time, Pallas kernels for 55%

profile of v10, /device:TPU:1, one launch (start us, length us, event | category | flops | bytes accessed | tf_op | source)
XLA Modules:
  0.0 46.3 jit_solution(371411114890504272)
XLA Ops:
  0.0 0.0 copy-start
  0.0 0.0 copy-start.2
  0.0 0.0 copy-start.1
  0.0 1.4 %fusion.1 = (bf16[64,8,512]{2,1,0:T(8,128)(2,1)S(1)}, bf16[64,8,512]{2,1,0:T(8,128)(2,1)S(1)}) fusion(bf16[64,16,512]{2,1,0:T(8,128)(2,1)} %bitcast.18), kind=kLoop, calls=%fused_computation.3 | loop fusion | bytes 2097152 | tf_op jit(solution)/shard_map/slice | solution.py:469
  1.4 0.1 copy-done
  1.5 0.0 copy-done.2
  1.5 0.3 copy-done.1
  1.9 0.0 copy-start.5
  1.9 0.0 copy-start.6
  1.9 1.6 %cross_kv.1 = bf16[1024,1024]{1,0:T(8,128)(2,1)S(1)} custom-call(bf16[1024,512]{1,0:T(8,128)(2,1)S(1)} %bitcast.19, bf16[3,512]{1,0:T(4,128)(2,1)S(1)} %bitcast.28, bf16[512,1024]{1,0:T(8,128)(2,1)S(1)} %bitcast.23), custom_call_target="tpu_custom_call" | custom-call | flops 1073741824 | bytes 4194304 | tf_op jit(solution)/shard_map/cross_kv/pallas_call | solution.py:477
  3.5 1.5 %collective-permute-start.2 = (bf16[1024,1024]{1,0:T(8,128)(2,1)S(1)}, bf16[1024,1024]{1,0:T(8,128)(2,1)S(1)}, u32[]{:S(2)}, u32[]{:S(2)}) collective-permute-start(bf16[1024,1024]{1,0:T(8,128)(2,1)S(1)} %cross_kv.1), channel_id=1, source_target_pairs={{0,64},{64,0},{1,65},{65,1},{2,66},{66,2},{3,67},{67,3},{4,68},{68... | collective-permute-start | bytes 6291464 | tf_op jit(solution)/shard_map/ppermute | solution.py:491
  5.0 1.4 %collective-permute-start = (bf16[64,8,512]{2,1,0:T(8,128)(2,1)S(1)}, bf16[64,8,512]{2,1,0:T(8,128)(2,1)S(1)}, u32[]{:S(2)}, u32[]{:S(2)}) collective-permute-start(bf16[64,8,512]{2,1,0:T(8,128)(2,1)S(1)} %get-tuple-element.19), channel_id=1, source_target_pairs={{0,8},{8,16},{16,24},{24,32},{32,40},{40,48},{48,56},{56,0},{1,9},... | collective-permute-start | bytes 1572872 | tf_op jit(solution)/shard_map/ppermute | solution.py:471
  6.4 2.8 %collective-permute-start.1 = (bf16[64,8,512]{2,1,0:T(8,128)(2,1)S(1)}, bf16[64,8,512]{2,1,0:T(8,128)(2,1)S(1)}, u32[]{:S(2)}, u32[]{:S(2)}) collective-permute-start(bf16[64,8,512]{2,1,0:T(8,128)(2,1)S(1)} %get-tuple-element.20), channel_id=1, source_target_pairs={{8,0},{16,8},{24,16},{32,24},{40,32},{48,40},{56,48},{0,56},{9,1},... | collective-permute-start | bytes 1572872 | tf_op jit(solution)/shard_map/ppermute | solution.py:472
  9.2 0.0 copy-done.5
  9.2 0.0 copy-done.6
  9.2 0.0 copy-start.10
  9.2 2.8 %own.1 = (bf16[1024,512]{1,0:T(8,128)(2,1)S(1)}, bf16[1024,512]{1,0:T(8,128)(2,1)S(1)}, bf16[512,1024]{1,0:T(8,128)(2,1)S(1)}, bf16[1024,512]{1,0:T(8,128)(2,1)S(1)}) custom-call(bf16[1024,512]{1,0:T(8,128)(2,1)S(1)} %bitcast.20, bf16[3,512]{1,0:T(4,128)(2,1)S(1)} %bitcast.29, bf16[512,1536]{1,0:T(8,128)(2,1)S(1)} %bitcast.36, bf16[512,512]{1,0:T(8,128)(2,1)S(1)} %bitcast.39), custom_call_target="tpu_custom_call" | custom-call | flops 2147483648 | bytes 7340032 | tf_op jit(solution)/shard_map/own/pallas_call | solution.py:493
  12.0 0.0 copy-done.10
  12.0 0.0 copy-start.7
  12.0 0.0 copy-start.9
  12.0 4.0 %near.1.part_ref = f32[24,144,256]{2,1,0:T(8,128)S(1)} custom-call(s32[8,8]{1,0:T(8,128)S(1)} %copy-done.10, bf16[1024,512]{1,0:T(8,128)(2,1)S(1)} %get-tuple-element.23.q_ref, bf16[1024,512]{1,0:T(8,128)(2,1)S(1)} %get-tuple-element.24.k_ref, bf16[512,1024]{1,0:T(8,128)(2,1)S(1)} %get-tuple-element.25.v_ref), custom_call_target="tpu_custom_call" | custom-call | flops 2415919104 | bytes 7340032 | tf_op jit(solution)/shard_map/near/pallas_call | solution.py:527
  16.0 0.0 collective-permute-done.2.kv_ref
  16.0 0.0 copy-done.7
  16.0 0.0 copy-done.9
  16.1 0.0 copy-start.3
  16.1 0.0 copy-start.4
  16.1 0.0 copy-start.8
  16.1 7.1 %cross.1.update_ref = f32[1024,512]{1,0:T(8,128)S(1)} custom-call(s32[2,4,8]{2,1,0:T(4,128)S(1)} %bitcast.43, s32[8,8]{1,0:T(8,128)S(1)} %copy-done.10, bf16[1024,512]{1,0:T(8,128)(2,1)S(1)} %get-tuple-element.22.q_ref, bf16[1024,1024]{1,0:T(8,128)(2,1)S(1)} %collective-permute-done.2.kv_ref, bf16[512,512]{1,0:T(8,128)(2,1)S(1)} %bitcast.40), custom_call_target="tpu_custom_call" | custom-call | flops 4294967296 | bytes 4194304 | tf_op jit(solution)/shard_map/cross/pallas_call | solution.py:510
  23.1 0.0 collective-permute-done
  23.2 0.0 collective-permute-done.1
  23.2 5.6 %collective-permute-start.4 = (bf16[256,512]{1,0:T(8,128)(2,1)S(1)}, bf16[256,512]{1,0:T(8,128)(2,1)S(1)}, u32[]{:S(2)}, u32[]{:S(2)}) collective-permute-start(bf16[256,512]{1,0:T(8,128)(2,1)S(1)} %pad_maximum_fusion.1), channel_id=1, source_target_pairs={{1,0},{2,1},{3,2},{4,3},{5,4},{6,5},{7,6},{0,7},{9,8},{10,9},{11,1... | collective-permute-start | bytes 786440 | tf_op jit(solution)/shard_map/ppermute | solution.py:547
  28.8 0.1 collective-permute-start.3
  28.9 0.0 copy-done.3
  28.9 0.0 copy-done.4
  28.9 0.0 copy-done.8
  28.9 11.6 %window.1 = (bf16[1024,512]{1,0:T(8,128)(2,1)}, bf16[1024,512]{1,0:T(8,128)(2,1)S(1)}, bf16[576,1024]{1,0:T(8,128)(2,1)S(1)}) custom-call(s32[8,8]{1,0:T(8,128)S(1)} %copy-done.10, bf16[512,512]{1,0:T(8,128)(2,1)S(1)} %bitcast.25, bf16[512,512]{1,0:T(8,128)(2,1)S(1)} %bitcast.27, bf16[3,512]{1,0:T(4,128)(2,1)S(1)} %bitcast.30, ...), custom_call_target="tpu_custom_call" | custom-call | flops 12884901888 | bytes 12582912 | tf_op jit(solution)/shard_map/window/pallas_call | solution.py:549
  40.5 0.0 collective-permute-done.4.south_ref
  40.5 0.0 collective-permute-done.3.north_ref
  40.5 5.6 %last.1 = bf16[1024,512]{1,0:T(8,128)(2,1)} custom-call(s32[8,8]{1,0:T(8,128)S(1)} %copy-done.10, bf16[256,512]{1,0:T(8,128)(2,1)S(1)} %collective-permute-done.3.north_ref, bf16[256,512]{1,0:T(8,128)(2,1)S(1)} %collective-permute-done.4.south_ref, bf16[1024,512]{1,0:T(8,128)(2,1)S(1)} %get-tuple-element.30.edge_keys_ref, ...), custom_call_target="tpu_custom_call", output_to_operand_aliasing={{}: (13, {})} | custom-call | flops 4294967296 | bytes 8388608 | tf_op jit(solution)/shard_map/last/pallas_call | solution.py:580
  (4 shorter events, 0.1 us)
Async XLA Ops:
  0.0 1.5 %copy-start = (bf16[1,64,16,512]{3,2,1,0:T(8,128)(2,1)S(1)}, bf16[1,64,16,512]{3,2,1,0:T(8,128)(2,1)}, u32[]{:S(2)}) copy-start(bf16[1,64,16,512]{3,2,1,0:T(8,128)(2,1)} %param.11) | copy-start | bytes 3145732
  0.0 1.5 %copy-start.2 = (bf16[1,3,512]{2,1,0:T(4,128)(2,1)S(1)}, bf16[1,3,512]{2,1,0:T(4,128)(2,1)}, u32[]{:S(2)}) copy-start(bf16[1,3,512]{2,1,0:T(4,128)(2,1)} %param.12) | copy-start | bytes 9220
  0.0 1.9 %copy-start.1 = (bf16[1,512,1024]{2,1,0:T(8,128)(2,1)S(1)}, bf16[1,512,1024]{2,1,0:T(8,128)(2,1)}, u32[]{:S(2)}) copy-start(bf16[1,512,1024]{2,1,0:T(8,128)(2,1)} %param.16) | copy-start | bytes 3145732
  1.9 7.3 %copy-start.5 = (bf16[1,512,1536]{2,1,0:T(8,128)(2,1)S(1)}, bf16[1,512,1536]{2,1,0:T(8,128)(2,1)}, u32[]{:S(2)}) copy-start(bf16[1,512,1536]{2,1,0:T(8,128)(2,1)} %param.13) | copy-start | bytes 4718596
  1.9 7.3 %copy-start.6 = (bf16[1,512,512]{2,1,0:T(8,128)(2,1)S(1)}, bf16[1,512,512]{2,1,0:T(8,128)(2,1)}, u32[]{:S(2)}) copy-start(bf16[1,512,512]{2,1,0:T(8,128)(2,1)} %param.15) | copy-start | bytes 1572868
  3.5 12.5 %collective-permute-start.2 = (bf16[1024,1024]{1,0:T(8,128)(2,1)S(1)}, bf16[1024,1024]{1,0:T(8,128)(2,1)S(1)}, u32[]{:S(2)}, u32[]{:S(2)}) collective-permute-start(bf16[1024,1024]{1,0:T(8,128)(2,1)S(1)} %cross_kv.1), channel_id=1, source_target_pairs={{0,64},{64,0},{1,65},{65,1},{2,66},{66,2},{3,67},{67,3},{4,68},{68... | collective-permute-start | bytes 6291464 | tf_op jit(solution)/shard_map/ppermute | solution.py:491
  5.0 18.1 %collective-permute-start = (bf16[64,8,512]{2,1,0:T(8,128)(2,1)S(1)}, bf16[64,8,512]{2,1,0:T(8,128)(2,1)S(1)}, u32[]{:S(2)}, u32[]{:S(2)}) collective-permute-start(bf16[64,8,512]{2,1,0:T(8,128)(2,1)S(1)} %get-tuple-element.19), channel_id=1, source_target_pairs={{0,8},{8,16},{16,24},{24,32},{32,40},{40,48},{48,56},{56,0},{1,9},... | collective-permute-start | bytes 1572872 | tf_op jit(solution)/shard_map/ppermute | solution.py:471
  6.4 16.8 %collective-permute-start.1 = (bf16[64,8,512]{2,1,0:T(8,128)(2,1)S(1)}, bf16[64,8,512]{2,1,0:T(8,128)(2,1)S(1)}, u32[]{:S(2)}, u32[]{:S(2)}) collective-permute-start(bf16[64,8,512]{2,1,0:T(8,128)(2,1)S(1)} %get-tuple-element.20), channel_id=1, source_target_pairs={{8,0},{16,8},{24,16},{32,24},{40,32},{48,40},{56,48},{0,56},{9,1},... | collective-permute-start | bytes 1572872 | tf_op jit(solution)/shard_map/ppermute | solution.py:472
  9.2 2.8 %copy-start.10 = (s32[8,8]{1,0:T(8,128)S(1)}, s32[8,8]{1,0:T(8,128)}, u32[]{:S(2)}) copy-start(s32[8,8]{1,0:T(8,128)} %land_ref.7) | copy-start | bytes 772
  12.0 4.1 %copy-start.7 = (bf16[1,512,512]{2,1,0:T(8,128)(2,1)S(1)}, bf16[1,512,512]{2,1,0:T(8,128)(2,1)}, u32[]{:S(2)}) copy-start(bf16[1,512,512]{2,1,0:T(8,128)(2,1)} %param.17) | copy-start | bytes 1572868
  12.0 4.1 %copy-start.9 = (s32[2,8,1,4]{1,3,2,0:T(4,128)S(1)}, s32[2,8,1,4]{1,3,2,0:T(4,128)}, u32[]{:S(2)}) copy-start(s32[2,8,1,4]{1,3,2,0:T(4,128)} %param.20) | copy-start | bytes 772
  16.1 12.9 %copy-start.3 = (bf16[1,512,2048]{2,1,0:T(8,128)(2,1)S(1)}, bf16[1,512,2048]{2,1,0:T(8,128)(2,1)}, u32[]{:S(2)}) copy-start(bf16[1,512,2048]{2,1,0:T(8,128)(2,1)} %param.18) | copy-start | bytes 6291460
  16.1 12.9 %copy-start.4 = (bf16[1,2048,512]{2,1,0:T(8,128)(2,1)S(1)}, bf16[1,2048,512]{2,1,0:T(8,128)(2,1)}, u32[]{:S(2)}) copy-start(bf16[1,2048,512]{2,1,0:T(8,128)(2,1)} %param.19) | copy-start | bytes 6291460
  16.1 12.9 %copy-start.8 = (bf16[1,512,512]{2,1,0:T(8,128)(2,1)S(1)}, bf16[1,512,512]{2,1,0:T(8,128)(2,1)}, u32[]{:S(2)}) copy-start(bf16[1,512,512]{2,1,0:T(8,128)(2,1)} %param.14) | copy-start | bytes 1572868
  23.2 17.3 %collective-permute-start.4 = (bf16[256,512]{1,0:T(8,128)(2,1)S(1)}, bf16[256,512]{1,0:T(8,128)(2,1)S(1)}, u32[]{:S(2)}, u32[]{:S(2)}) collective-permute-start(bf16[256,512]{1,0:T(8,128)(2,1)S(1)} %pad_maximum_fusion.1), channel_id=1, source_target_pairs={{1,0},{2,1},{3,2},{4,3},{5,4},{6,5},{7,6},{0,7},{9,8},{10,9},{11,1... | collective-permute-start | bytes 786440 | tf_op jit(solution)/shard_map/ppermute | solution.py:547
  28.8 11.7 %collective-permute-start.3 = (bf16[256,512]{1,0:T(8,128)(2,1)S(1)}, bf16[256,512]{1,0:T(8,128)(2,1)S(1)}, u32[]{:S(2)}, u32[]{:S(2)}) collective-permute-start(bf16[256,512]{1,0:T(8,128)(2,1)S(1)} %pad_maximum_fusion), channel_id=1, source_target_pairs={{0,1},{1,2},{2,3},{3,4},{4,5},{5,6},{6,7},{7,0},{8,9},{9,10},{10,1... | collective-permute-start | bytes 786440 | tf_op jit(solution)/shard_map/ppermute | solution.py:546

commit v11 on v9

--- a/solution.py
+++ b/solution.py
@@ -211,13 +211,18 @@
     return pieces
 
 
-def finish(index, own_land, is_air, win_t, update, x_rows, gain_ref, out_w_ref, up_ref, down_ref):
-    live = jnp.where(is_air | (index >= own_land), 1.0, 0.0)
-    middle = x_rows.astype(F32) + live * (mm_tn(win_t, out_w_ref[...]) + update)
-    mlp_input = norm_round(middle, gain_ref[2:3, :])
-    gate = 0.5 * mm(mlp_input, up_ref[...])
-    hidden = (gate + gate * jnp.tanh(gate)).astype(BF)
-    return (middle + live * mm(hidden, down_ref[...])).astype(BF)
+def finish(pieces, own_land, is_air, gain_ref, out_w_ref, up_ref, down_ref):
+    front = []
+    for index, win_t, update, x_rows in pieces:
+        live = jnp.where(is_air | (index >= own_land), 1.0, 0.0)
+        middle = x_rows.astype(F32) + live * (mm_tn(win_t, out_w_ref[...]) + update)
+        front.append((live, middle, norm_round(middle, gain_ref[2:3, :])))
+    gates = [0.5 * mm(mlp_input, up_ref[...]) for _, _, mlp_input in front]
+    results = []
+    for (live, middle, _), gate in zip(front, gates):
+        hidden = (gate + gate * jnp.tanh(gate)).astype(BF)
+        results.append((middle + live * mm(hidden, down_ref[...])).astype(BF))
+    return results
 
 
 def kernel_window(
@@ -286,22 +291,14 @@
 
     own_land = land_ref[lax.axis_index("tile"), lax.axis_index("face")]
     chunk = (NB - 2) * CELLS // 2
-    for c in range(2):
-        start = CELLS + c * chunk
-        at = slice(start, start + chunk)
-        index = (start + lax.broadcasted_iota(jnp.int32, (chunk, 1), 0)) // CELLS
-        out_ref[at, :] = finish(
-            index,
-            own_land,
-            is_air,
-            win_ref[:, at],
-            update_ref[at, :],
-            x_ref[at, :],
-            gain_ref,
-            out_w_ref,
-            up_ref,
-            down_ref,
-        )
+    spans = [slice(CELLS + c * chunk, CELLS + (c + 1) * chunk) for c in range(2)]
+    pieces = []
+    for at in spans:
+        index = (at.start + lax.broadcasted_iota(jnp.int32, (chunk, 1), 0)) // CELLS
+        pieces.append((index, win_ref[:, at], update_ref[at, :], x_ref[at, :]))
+    results = finish(pieces, own_land, is_air, gain_ref, out_w_ref, up_ref, down_ref)
+    for at, rows in zip(spans, results):
+        out_ref[at, :] = rows
 
 
 def kernel_last(
@@ -364,18 +361,8 @@
 
     own_land = land_ref[lax.axis_index("tile"), lax.axis_index("face")]
     index = lax.broadcasted_iota(jnp.int32, (2 * CELLS, 1), 0) // CELLS * (NB - 1)
-    rows_ref[...] = finish(
-        index,
-        own_land,
-        is_air,
-        win_ref[...],
-        edge_rows(update_ref),
-        edge_rows(x_ref),
-        gain_ref,
-        out_w_ref,
-        up_ref,
-        down_ref,
-    )
+    piece = (index, win_ref[...], edge_rows(update_ref), edge_rows(x_ref))
+    [rows_ref[...]] = finish([piece], own_land, is_air, gain_ref, out_w_ref, up_ref, down_ref)
     copies = []
     for n in range(2):
         copy = pltpu.make_async_copy(

time: 46.3 us -> 46 us (level)
  no operation moved by 1% of the time
where the time goes in v11:
time: 46 us; the launch traced here: 45.7 us
  Pallas kernels  29.4 us (64%)
  starting transfers between devices  8.14 us (18%)
  waiting for transfers between devices  5.82 us (13%)
  local copies, waits for them, and re-layouts  1.94 us (4%)
    pallas_call x1, Pallas kernels, per_device(): pl.pallas_call(kernel_window, in_specs=[SMEM] + [VMEM] * 12, out_specs=[V...  12.5 us
    pallas_call x1, Pallas kernels, per_device(): pl.pallas_call(kernel_cross, in_specs=[SMEM] * 2 + [VMEM] * 3, out_specs=...  6.85 us
    pallas_call x1, Pallas kernels, per_device(): pl.pallas_call(kernel_last, in_specs=[SMEM] + [VMEM] * 12 + [ANY], out_sp...  5.58 us
    ppermute x1, starting transfers between devices, per_device(): north = lax.ppermute(bottom, 'tile', forward)  5.04 us
    ppermute x1, waiting for transfers between devices, per_device(): east = lax.ppermute(west_edge, 'face', backward).reshape(NB * SIDE, D)  3.4 us
    pallas_call x1, Pallas kernels, per_device(): pl.pallas_call(kernel_own, grid=(2,), in_specs=[block, pl.BlockSpec((3, D...  2.82 us
    ppermute x1, waiting for transfers between devices, per_device(): west = lax.ppermute(east_edge, 'face', forward).reshape(NB * SIDE, D)  2.41 us
    ppermute x1, starting transfers between devices, per_device(): west = lax.ppermute(east_edge, 'face', forward).reshape(NB * SIDE, D)  1.64 us
  transfers between devices with their start and end apart: 5, of which 2 were waited for; matrix products, arithmetic and copies ran while one was open for 0% of the time, Pallas kernels for 49%

profile of v11, /device:TPU:30, one launch (start us, length us, event | category | flops | bytes accessed | tf_op | source)
XLA Modules:
  0.0 45.7 jit_solution(11705477899105895194)
XLA Ops:
  0.0 0.0 copy-start
  0.0 0.0 copy-start.2
  0.0 0.0 copy-start.1
  0.0 1.4 %fusion.1 = (bf16[64,8,512]{2,1,0:T(8,128)(2,1)S(1)}, bf16[64,8,512]{2,1,0:T(8,128)(2,1)S(1)}) fusion(bf16[64,16,512]{2,1,0:T(8,128)(2,1)} %bitcast.18), kind=kLoop, calls=%fused_computation.3 | loop fusion | bytes 2097152 | tf_op jit(solution)/shard_map/slice | solution.py:411
  1.4 0.1 copy-done
  1.5 0.0 copy-done.2
  1.5 0.3 copy-done.1
  1.9 0.0 copy-start.5
  1.9 0.0 copy-start.6
  1.9 1.6 %cross_kv.1 = bf16[1024,1024]{1,0:T(8,128)(2,1)S(1)} custom-call(bf16[1024,512]{1,0:T(8,128)(2,1)S(1)} %bitcast.19, bf16[3,512]{1,0:T(4,128)(2,1)S(1)} %bitcast.28, bf16[512,1024]{1,0:T(8,128)(2,1)S(1)} %bitcast.23), custom_call_target="tpu_custom_call" | custom-call | flops 1073741824 | bytes 4194304 | tf_op jit(solution)/shard_map/cross_kv/pallas_call | solution.py:419
  3.5 0.1 collective-permute-start.2
  3.6 1.6 %collective-permute-start = (bf16[64,8,512]{2,1,0:T(8,128)(2,1)S(1)}, bf16[64,8,512]{2,1,0:T(8,128)(2,1)S(1)}, u32[]{:S(2)}, u32[]{:S(2)}) collective-permute-start(bf16[64,8,512]{2,1,0:T(8,128)(2,1)S(1)} %get-tuple-element.18), channel_id=1, source_target_pairs={{0,8},{8,16},{16,24},{24,32},{32,40},{40,48},{48,56},{56,0},{1,9},... | collective-permute-start | bytes 1572872 | tf_op jit(solution)/shard_map/ppermute | solution.py:413
  5.2 0.5 collective-permute-start.1
  5.7 0.0 copy-done.5
  5.7 0.0 copy-done.6
  5.7 0.0 copy-start.7
  5.7 0.0 copy-start.9
  5.7 0.0 copy-start.10
  5.7 2.8 %own.1 = (bf16[1024,512]{1,0:T(8,128)(2,1)S(1)}, bf16[1024,512]{1,0:T(8,128)(2,1)S(1)}, bf16[512,1024]{1,0:T(8,128)(2,1)S(1)}, bf16[1024,512]{1,0:T(8,128)(2,1)S(1)}) custom-call(bf16[1024,512]{1,0:T(8,128)(2,1)S(1)} %bitcast.20, bf16[3,512]{1,0:T(4,128)(2,1)S(1)} %bitcast.29, bf16[512,1536]{1,0:T(8,128)(2,1)S(1)} %bitcast.36, bf16[512,512]{1,0:T(8,128)(2,1)S(1)} %bitcast.39), custom_call_target="tpu_custom_call" | custom-call | flops 2147483648 | bytes 7340032 | tf_op jit(solution)/shard_map/own/pallas_call | solution.py:435
  8.6 0.0 collective-permute-done.2.kv_ref
  8.6 0.0 copy-done.7
  8.6 0.0 copy-done.9
  8.6 0.0 copy-done.10
  8.6 0.0 copy-start.3
  8.6 0.0 copy-start.4
  8.6 0.0 copy-start.8
  8.7 6.8 %cross.1.update_ref = f32[1024,512]{1,0:T(8,128)S(1)} custom-call(s32[2,4,8]{2,1,0:T(4,128)S(1)} %bitcast.43, s32[8,8]{1,0:T(8,128)S(1)} %copy-done.10, bf16[1024,512]{1,0:T(8,128)(2,1)S(1)} %get-tuple-element.21.q_ref, bf16[1024,1024]{1,0:T(8,128)(2,1)S(1)} %collective-permute-done.2.kv_ref, bf16[512,512]{1,0:T(8,128)(2,1)S(1)} %bitcast.40), custom_call_target="tpu_custom_call" | custom-call | flops 4294967296 | bytes 4194304 | tf_op jit(solution)/shard_map/cross/pallas_call | solution.py:452
  15.5 2.4 %collective-permute-done = bf16[64,8,512]{2,1,0:T(8,128)(2,1)S(1)} collective-permute-done((bf16[64,8,512]{2,1,0:T(8,128)(2,1)S(1)}, bf16[64,8,512]{2,1,0:T(8,128)(2,1)S(1)}, u32[]{:S(2)}, u32[]{:S(2)}) %collective-permute-start) | collective-permute-done | bytes 524320 | tf_op jit(solution)/shard_map/ppermute | solution.py:413
  17.9 3.4 %collective-permute-done.1 = bf16[64,8,512]{2,1,0:T(8,128)(2,1)S(1)} collective-permute-done((bf16[64,8,512]{2,1,0:T(8,128)(2,1)S(1)}, bf16[64,8,512]{2,1,0:T(8,128)(2,1)S(1)}, u32[]{:S(2)}, u32[]{:S(2)}) %collective-permute-start.1) | collective-permute-done | bytes 524320 | tf_op jit(solution)/shard_map/ppermute | solution.py:414
  21.4 0.9 %collective-permute-start.4 = (bf16[256,512]{1,0:T(8,128)(2,1)S(1)}, bf16[256,512]{1,0:T(8,128)(2,1)S(1)}, u32[]{:S(2)}, u32[]{:S(2)}) collective-permute-start(bf16[256,512]{1,0:T(8,128)(2,1)S(1)} %pad_maximum_fusion.1), channel_id=1, source_target_pairs={{1,0},{2,1},{3,2},{4,3},{5,4},{6,5},{7,6},{0,7},{9,8},{10,9},{11,1... | collective-permute-start | bytes 786440 | tf_op jit(solution)/shard_map/ppermute | solution.py:478
  22.3 5.0 %collective-permute-start.3 = (bf16[256,512]{1,0:T(8,128)(2,1)S(1)}, bf16[256,512]{1,0:T(8,128)(2,1)S(1)}, u32[]{:S(2)}, u32[]{:S(2)}) collective-permute-start(bf16[256,512]{1,0:T(8,128)(2,1)S(1)} %pad_maximum_fusion), channel_id=1, source_target_pairs={{0,1},{1,2},{2,3},{3,4},{4,5},{5,6},{6,7},{7,0},{8,9},{9,10},{10,1... | collective-permute-start | bytes 786440 | tf_op jit(solution)/shard_map/ppermute | solution.py:477
  27.3 0.0 copy-done.3
  27.3 0.0 copy-done.4
  27.4 0.0 copy-done.8
  27.4 12.5 %window.1 = (bf16[1024,512]{1,0:T(8,128)(2,1)}, bf16[1024,512]{1,0:T(8,128)(2,1)S(1)}, bf16[576,1024]{1,0:T(8,128)(2,1)S(1)}) custom-call(s32[8,8]{1,0:T(8,128)S(1)} %copy-done.10, bf16[512,512]{1,0:T(8,128)(2,1)S(1)} %bitcast.25, bf16[512,512]{1,0:T(8,128)(2,1)S(1)} %bitcast.27, bf16[3,512]{1,0:T(4,128)(2,1)S(1)} %bitcast.30, ...), custom_call_target="tpu_custom_call" | custom-call | flops 12884901888 | bytes 12582912 | tf_op jit(solution)/shard_map/window/pallas_call | solution.py:480
  39.9 0.0 collective-permute-done.4.south_ref
  39.9 0.0 collective-permute-done.3.north_ref
  39.9 5.6 %last.1 = bf16[1024,512]{1,0:T(8,128)(2,1)} custom-call(s32[8,8]{1,0:T(8,128)S(1)} %copy-done.10, bf16[256,512]{1,0:T(8,128)(2,1)S(1)} %collective-permute-done.3.north_ref, bf16[256,512]{1,0:T(8,128)(2,1)S(1)} %collective-permute-done.4.south_ref, bf16[1024,512]{1,0:T(8,128)(2,1)S(1)} %get-tuple-element.28.edge_keys_ref, ...), custom_call_target="tpu_custom_call", output_to_operand_aliasing={{}: (13, {})} | custom-call | flops 4294967296 | bytes 8388608 | tf_op jit(solution)/shard_map/last/pallas_call | solution.py:510
  (4 shorter events, 0.1 us)
Async XLA Ops:
  0.0 1.5 %copy-start = (bf16[1,64,16,512]{3,2,1,0:T(8,128)(2,1)S(1)}, bf16[1,64,16,512]{3,2,1,0:T(8,128)(2,1)}, u32[]{:S(2)}) copy-start(bf16[1,64,16,512]{3,2,1,0:T(8,128)(2,1)} %param.11) | copy-start | bytes 3145732
  0.0 1.5 %copy-start.2 = (bf16[1,3,512]{2,1,0:T(4,128)(2,1)S(1)}, bf16[1,3,512]{2,1,0:T(4,128)(2,1)}, u32[]{:S(2)}) copy-start(bf16[1,3,512]{2,1,0:T(4,128)(2,1)} %param.12) | copy-start | bytes 9220
  0.0 1.9 %copy-start.1 = (bf16[1,512,1024]{2,1,0:T(8,128)(2,1)S(1)}, bf16[1,512,1024]{2,1,0:T(8,128)(2,1)}, u32[]{:S(2)}) copy-start(bf16[1,512,1024]{2,1,0:T(8,128)(2,1)} %param.16) | copy-start | bytes 3145732
  1.9 3.8 %copy-start.5 = (bf16[1,512,1536]{2,1,0:T(8,128)(2,1)S(1)}, bf16[1,512,1536]{2,1,0:T(8,128)(2,1)}, u32[]{:S(2)}) copy-start(bf16[1,512,1536]{2,1,0:T(8,128)(2,1)} %param.13) | copy-start | bytes 4718596
  1.9 3.8 %copy-start.6 = (bf16[1,512,512]{2,1,0:T(8,128)(2,1)S(1)}, bf16[1,512,512]{2,1,0:T(8,128)(2,1)}, u32[]{:S(2)}) copy-start(bf16[1,512,512]{2,1,0:T(8,128)(2,1)} %param.15) | copy-start | bytes 1572868
  3.5 5.1 %collective-permute-start.2 = (bf16[1024,1024]{1,0:T(8,128)(2,1)S(1)}, bf16[1024,1024]{1,0:T(8,128)(2,1)S(1)}, u32[]{:S(2)}, u32[]{:S(2)}) collective-permute-start(bf16[1024,1024]{1,0:T(8,128)(2,1)S(1)} %cross_kv.1), channel_id=1, source_target_pairs={{0,64},{64,0},{1,65},{65,1},{2,66},{66,2},{3,67},{67,3},{4,68},{68... | collective-permute-start | bytes 6291464 | tf_op jit(solution)/shard_map/ppermute | solution.py:433
  3.6 14.3 %collective-permute-start = (bf16[64,8,512]{2,1,0:T(8,128)(2,1)S(1)}, bf16[64,8,512]{2,1,0:T(8,128)(2,1)S(1)}, u32[]{:S(2)}, u32[]{:S(2)}) collective-permute-start(bf16[64,8,512]{2,1,0:T(8,128)(2,1)S(1)} %get-tuple-element.18), channel_id=1, source_target_pairs={{0,8},{8,16},{16,24},{24,32},{32,40},{40,48},{48,56},{56,0},{1,9},... | collective-permute-start | bytes 1572872 | tf_op jit(solution)/shard_map/ppermute | solution.py:413
  5.2 16.1 %collective-permute-start.1 = (bf16[64,8,512]{2,1,0:T(8,128)(2,1)S(1)}, bf16[64,8,512]{2,1,0:T(8,128)(2,1)S(1)}, u32[]{:S(2)}, u32[]{:S(2)}) collective-permute-start(bf16[64,8,512]{2,1,0:T(8,128)(2,1)S(1)} %get-tuple-element.19), channel_id=1, source_target_pairs={{8,0},{16,8},{24,16},{32,24},{40,32},{48,40},{56,48},{0,56},{9,1},... | collective-permute-start | bytes 1572872 | tf_op jit(solution)/shard_map/ppermute | solution.py:414
  5.7 2.9 %copy-start.7 = (bf16[1,512,512]{2,1,0:T(8,128)(2,1)S(1)}, bf16[1,512,512]{2,1,0:T(8,128)(2,1)}, u32[]{:S(2)}) copy-start(bf16[1,512,512]{2,1,0:T(8,128)(2,1)} %param.17) | copy-start | bytes 1572868
  5.7 2.9 %copy-start.9 = (s32[2,8,1,4]{1,3,2,0:T(4,128)S(1)}, s32[2,8,1,4]{1,3,2,0:T(4,128)}, u32[]{:S(2)}) copy-start(s32[2,8,1,4]{1,3,2,0:T(4,128)} %param.20) | copy-start | bytes 772
  5.7 2.9 %copy-start.10 = (s32[8,8]{1,0:T(8,128)S(1)}, s32[8,8]{1,0:T(8,128)}, u32[]{:S(2)}) copy-start(s32[8,8]{1,0:T(8,128)} %land_ref.5) | copy-start | bytes 772
  8.6 18.7 %copy-start.3 = (bf16[1,512,2048]{2,1,0:T(8,128)(2,1)S(1)}, bf16[1,512,2048]{2,1,0:T(8,128)(2,1)}, u32[]{:S(2)}) copy-start(bf16[1,512,2048]{2,1,0:T(8,128)(2,1)} %param.18) | copy-start | bytes 6291460
  8.6 18.7 %copy-start.4 = (bf16[1,2048,512]{2,1,0:T(8,128)(2,1)S(1)}, bf16[1,2048,512]{2,1,0:T(8,128)(2,1)}, u32[]{:S(2)}) copy-start(bf16[1,2048,512]{2,1,0:T(8,128)(2,1)} %param.19) | copy-start | bytes 6291460
  8.6 18.7 %copy-start.8 = (bf16[1,512,512]{2,1,0:T(8,128)(2,1)S(1)}, bf16[1,512,512]{2,1,0:T(8,128)(2,1)}, u32[]{:S(2)}) copy-start(bf16[1,512,512]{2,1,0:T(8,128)(2,1)} %param.14) | copy-start | bytes 1572868
  21.4 18.5 %collective-permute-start.4 = (bf16[256,512]{1,0:T(8,128)(2,1)S(1)}, bf16[256,512]{1,0:T(8,128)(2,1)S(1)}, u32[]{:S(2)}, u32[]{:S(2)}) collective-permute-start(bf16[256,512]{1,0:T(8,128)(2,1)S(1)} %pad_maximum_fusion.1), channel_id=1, source_target_pairs={{1,0},{2,1},{3,2},{4,3},{5,4},{6,5},{7,6},{0,7},{9,8},{10,9},{11,1... | collective-permute-start | bytes 786440 | tf_op jit(solution)/shard_map/ppermute | solution.py:478
  22.3 17.6 %collective-permute-start.3 = (bf16[256,512]{1,0:T(8,128)(2,1)S(1)}, bf16[256,512]{1,0:T(8,128)(2,1)S(1)}, u32[]{:S(2)}, u32[]{:S(2)}) collective-permute-start(bf16[256,512]{1,0:T(8,128)(2,1)S(1)} %pad_maximum_fusion), channel_id=1, source_target_pairs={{0,1},{1,2},{2,3},{3,4},{4,5},{5,6},{6,7},{7,0},{8,9},{9,10},{10,1... | collective-permute-start | bytes 786440 | tf_op jit(solution)/shard_map/ppermute | solution.py:477

commit v12 on v11

--- a/solution.py
+++ b/solution.py
@@ -80,7 +80,7 @@
     return result.astype(BF), sums
 
 
-def attention(count, queries, keys, values, penalties, lane, out_ref, bad_ref):
+def attention(count, queries, keys, values, penalties, lane, out_ref, bad_ref, prepare=None):
     bad_ref[...] = jnp.zeros_like(bad_ref)
 
     def terms_of(i, p):
@@ -88,6 +88,8 @@
 
     steps = [(i, p) for i in range(count) for p in range(PAIRS)]
     following = terms_of(*steps[0])
+    if prepare:
+        prepare()
     for n, (i, p) in enumerate(steps):
         terms = following
         if n + 1 < len(steps):
@@ -143,9 +145,10 @@
     own_land = land_ref[lax.axis_index("tile"), lax.axis_index("face")]
     floor = jnp.where(component == 1, 0, own_land)
 
-    for j in range(NB):
-        row, lane = (j // 4) * D, D + (j % 4) * CELLS
-        augment(kv_ref[row : row + D, lane : lane + CELLS], j >= floor, va_ref, j * CELLS)
+    def prepare():
+        for j in range(NB):
+            row, lane = (j // 4) * D, D + (j % 4) * CELLS
+            augment(kv_ref[row : row + D, lane : lane + CELLS], j >= floor, va_ref, j * CELLS)
 
     def picks(i):
         return [links_ref[component, k, i] for k in range(KC)]
@@ -171,7 +174,7 @@
     def lane(i):
         return aligned(i, CELLS)
 
-    attention(NB, queries, keys, values, penalties, lane, cross_ref, bad_ref)
+    attention(NB, queries, keys, values, penalties, lane, cross_ref, bad_ref, prepare)
     out_ref[...] = mm_tn(cross_ref[...], cross_w_ref[...])
 
 
@@ -254,40 +257,54 @@
         keys_ref[pl.ds(at, CELLS), :] = keys
         augment(values_t, flag, va_ref, at)
 
-    blocks = 2
-    for b in range(blocks):
-        members = range(1 + b * NB // blocks, 1 + (b + 1) * NB // blocks)
+    def normed_block(members):
         rows_x = []
         for r in members:
             rows_x += [ref[(r - 1) * SIDE : r * SIDE, :] for ref in (west_ref, east_ref)]
-        keys, values_t = project(jnp.concatenate(rows_x, axis=0), gain_ref, qkv_ref)
+        return norm_round(jnp.concatenate(rows_x, axis=0).astype(F32), gain_ref[0:1, :])
+
+    def put_own(own):
+        for i in own:
+            at = slice(i * CELLS, (i + 1) * CELLS)
+            put(i + 1, 0, k_ref[at, :], v_ref[:, at], flags(i + 1)[0])
+
+    def put_sides(members, keys, values_t):
         for n, r in enumerate(members):
             at = slice(n * CELLS, (n + 1) * CELLS)
             put(r, CELLS, keys[at], values_t[:, at], side_flag(flags, r))
-    for i in range(NB):
-        at = slice(i * CELLS, (i + 1) * CELLS)
-        put(i + 1, 0, k_ref[at, :], v_ref[:, at], flags(i + 1)[0])
+
+    near, far = range(1, 1 + NB // 2), range(1 + NB // 2, 1 + NB)
+    near_rows = normed_block(near)
+    near_keys = mm(near_rows, qkv_ref[:, D : 2 * D]).astype(BF)
+    far_rows = normed_block(far)
+    near_values = mm_tt(qkv_ref[:, 2 * D :], near_rows).astype(BF)
+    put_own(range(NB // 2))
+    far_keys = mm(far_rows, qkv_ref[:, D : 2 * D]).astype(BF)
+    put_sides(near, near_keys, near_values)
+    far_values = mm_tt(qkv_ref[:, 2 * D :], far_rows).astype(BF)
+    put_own(range(NB // 2, NB))
+    put_sides(far, far_keys, far_values)
+
+    def queries(n, p):
+        return q_ref[pl.ds(aligned(n, CELLS) + CELLS, CELLS), pl.ds(p * LANES, LANES)]
+
+    def keys_of(n, p):
+        return keys_ref[pl.ds(aligned(n, GROUP), WINDOW), pl.ds(p * LANES, LANES)]
+
+    def values_of(n, p):
+        return va_ref[pl.ds(p * VROWS, VROWS), pl.ds(aligned(n, GROUP), WINDOW)]
+
+    def penalties(n):
+        return window_penalties(flags, n + 1)
+
+    def lane(n):
+        return aligned(n, CELLS) + CELLS
+
+    attention(NB - 2, queries, keys_of, values_of, penalties, lane, win_ref, bad_ref)
     for n, at in enumerate((0, (NB - 2) * GROUP)):
         to = slice(n * 2 * GROUP, (n + 1) * 2 * GROUP)
         edge_keys_ref[to, :] = keys_ref[at : at + 2 * GROUP, :]
         edge_va_ref[:, to] = va_ref[:, at : at + 2 * GROUP]
-
-    def queries(n, p):
-        return q_ref[pl.ds(aligned(n, CELLS) + CELLS, CELLS), pl.ds(p * LANES, LANES)]
-
-    def keys_of(n, p):
-        return keys_ref[pl.ds(aligned(n, GROUP), WINDOW), pl.ds(p * LANES, LANES)]
-
-    def values_of(n, p):
-        return va_ref[pl.ds(p * VROWS, VROWS), pl.ds(aligned(n, GROUP), WINDOW)]
-
-    def penalties(n):
-        return window_penalties(flags, n + 1)
-
-    def lane(n):
-        return aligned(n, CELLS) + CELLS
-
-    attention(NB - 2, queries, keys_of, values_of, penalties, lane, win_ref, bad_ref)
 
     own_land = land_ref[lax.axis_index("tile"), lax.axis_index("face")]
     chunk = (NB - 2) * CELLS // 2

time: 46 us -> 45.9 us (level)
  no operation moved by 1% of the time
where the time goes in v12:
time: 45.9 us; the launch traced here: 45.6 us
  Pallas kernels  29.4 us (64%)
  starting transfers between devices  8.14 us (18%)
  waiting for transfers between devices  5.8 us (13%)
  local copies, waits for them, and re-layouts  1.94 us (4%)
    pallas_call x1, Pallas kernels, per_device(): pl.pallas_call(kernel_window, in_specs=[SMEM] + [VMEM] * 12, out_specs=[V...  12.5 us
    pallas_call x1, Pallas kernels, per_device(): pl.pallas_call(kernel_cross, in_specs=[SMEM] * 2 + [VMEM] * 3, out_specs=...  6.86 us
    pallas_call x1, Pallas kernels, per_device(): pl.pallas_call(kernel_last, in_specs=[SMEM] + [VMEM] * 12 + [ANY], out_sp...  5.59 us
    ppermute x1, starting transfers between devices, per_device(): north = lax.ppermute(bottom, 'tile', forward)  5.04 us
    ppermute x1, waiting for transfers between devices, per_device(): east = lax.ppermute(west_edge, 'face', backward).reshape(NB * SIDE, D)  3.4 us
    pallas_call x1, Pallas kernels, per_device(): pl.pallas_call(kernel_own, grid=(2,), in_specs=[block, pl.BlockSpec((3, D...  2.82 us
    ppermute x1, waiting for transfers between devices, per_device(): west = lax.ppermute(east_edge, 'face', forward).reshape(NB * SIDE, D)  2.39 us
    ppermute x1, starting transfers between devices, per_device(): west = lax.ppermute(east_edge, 'face', forward).reshape(NB * SIDE, D)  1.64 us
  transfers between devices with their start and end apart: 5, of which 2 were waited for; matrix products, arithmetic and copies ran while one was open for 0% of the time, Pallas kernels for 49%

profile of v12, /device:TPU:30, one launch (start us, length us, event | category | flops | bytes accessed | tf_op | source)
XLA Modules:
  0.0 45.6 jit_solution(4843119464823670962)
XLA Ops:
  0.0 0.0 copy-start
  0.0 0.0 copy-start.2
  0.0 0.0 copy-start.1
  0.0 1.4 %fusion.1 = (bf16[64,8,512]{2,1,0:T(8,128)(2,1)S(1)}, bf16[64,8,512]{2,1,0:T(8,128)(2,1)S(1)}) fusion(bf16[64,16,512]{2,1,0:T(8,128)(2,1)} %bitcast.18), kind=kLoop, calls=%fused_computation.3 | loop fusion | bytes 2097152 | tf_op jit(solution)/shard_map/slice | solution.py:428
  1.4 0.1 copy-done
  1.5 0.0 copy-done.2
  1.5 0.3 copy-done.1
  1.9 0.0 copy-start.5
  1.9 0.0 copy-start.6
  1.9 1.6 %cross_kv.1 = bf16[1024,1024]{1,0:T(8,128)(2,1)S(1)} custom-call(bf16[1024,512]{1,0:T(8,128)(2,1)S(1)} %bitcast.19, bf16[3,512]{1,0:T(4,128)(2,1)S(1)} %bitcast.28, bf16[512,1024]{1,0:T(8,128)(2,1)S(1)} %bitcast.23), custom_call_target="tpu_custom_call" | custom-call | flops 1073741824 | bytes 4194304 | tf_op jit(solution)/shard_map/cross_kv/pallas_call | solution.py:436
  3.5 0.1 collective-permute-start.2
  3.6 1.6 %collective-permute-start = (bf16[64,8,512]{2,1,0:T(8,128)(2,1)S(1)}, bf16[64,8,512]{2,1,0:T(8,128)(2,1)S(1)}, u32[]{:S(2)}, u32[]{:S(2)}) collective-permute-start(bf16[64,8,512]{2,1,0:T(8,128)(2,1)S(1)} %get-tuple-element.18), channel_id=1, source_target_pairs={{0,8},{8,16},{16,24},{24,32},{32,40},{40,48},{48,56},{56,0},{1,9},... | collective-permute-start | bytes 1572872 | tf_op jit(solution)/shard_map/ppermute | solution.py:430
  5.2 0.5 collective-permute-start.1
  5.7 0.0 copy-done.5
  5.7 0.0 copy-done.6
  5.7 0.0 copy-start.7
  5.7 0.0 copy-start.9
  5.7 0.0 copy-start.10
  5.7 2.8 %own.1 = (bf16[1024,512]{1,0:T(8,128)(2,1)S(1)}, bf16[1024,512]{1,0:T(8,128)(2,1)S(1)}, bf16[512,1024]{1,0:T(8,128)(2,1)S(1)}, bf16[1024,512]{1,0:T(8,128)(2,1)S(1)}) custom-call(bf16[1024,512]{1,0:T(8,128)(2,1)S(1)} %bitcast.20, bf16[3,512]{1,0:T(4,128)(2,1)S(1)} %bitcast.29, bf16[512,1536]{1,0:T(8,128)(2,1)S(1)} %bitcast.36, bf16[512,512]{1,0:T(8,128)(2,1)S(1)} %bitcast.39), custom_call_target="tpu_custom_call" | custom-call | flops 2147483648 | bytes 7340032 | tf_op jit(solution)/shard_map/own/pallas_call | solution.py:452
  8.6 0.0 collective-permute-done.2.kv_ref
  8.6 0.0 copy-done.7
  8.6 0.0 copy-done.9
  8.6 0.0 copy-done.10
  8.6 0.0 copy-start.3
  8.6 0.0 copy-start.4
  8.6 0.0 copy-start.8
  8.7 6.9 %cross.1.update_ref = f32[1024,512]{1,0:T(8,128)S(1)} custom-call(s32[2,4,8]{2,1,0:T(4,128)S(1)} %bitcast.43, s32[8,8]{1,0:T(8,128)S(1)} %copy-done.10, bf16[1024,512]{1,0:T(8,128)(2,1)S(1)} %get-tuple-element.21.q_ref, bf16[1024,1024]{1,0:T(8,128)(2,1)S(1)} %collective-permute-done.2.kv_ref, bf16[512,512]{1,0:T(8,128)(2,1)S(1)} %bitcast.40), custom_call_target="tpu_custom_call" | custom-call | flops 4294967296 | bytes 4194304 | tf_op jit(solution)/shard_map/cross/pallas_call | solution.py:469
  15.5 2.4 %collective-permute-done = bf16[64,8,512]{2,1,0:T(8,128)(2,1)S(1)} collective-permute-done((bf16[64,8,512]{2,1,0:T(8,128)(2,1)S(1)}, bf16[64,8,512]{2,1,0:T(8,128)(2,1)S(1)}, u32[]{:S(2)}, u32[]{:S(2)}) %collective-permute-start) | collective-permute-done | bytes 524320 | tf_op jit(solution)/shard_map/ppermute | solution.py:430
  17.9 3.4 %collective-permute-done.1 = bf16[64,8,512]{2,1,0:T(8,128)(2,1)S(1)} collective-permute-done((bf16[64,8,512]{2,1,0:T(8,128)(2,1)S(1)}, bf16[64,8,512]{2,1,0:T(8,128)(2,1)S(1)}, u32[]{:S(2)}, u32[]{:S(2)}) %collective-permute-start.1) | collective-permute-done | bytes 524320 | tf_op jit(solution)/shard_map/ppermute | solution.py:431
  21.4 0.9 %collective-permute-start.4 = (bf16[256,512]{1,0:T(8,128)(2,1)S(1)}, bf16[256,512]{1,0:T(8,128)(2,1)S(1)}, u32[]{:S(2)}, u32[]{:S(2)}) collective-permute-start(bf16[256,512]{1,0:T(8,128)(2,1)S(1)} %pad_maximum_fusion.1), channel_id=1, source_target_pairs={{1,0},{2,1},{3,2},{4,3},{5,4},{6,5},{7,6},{0,7},{9,8},{10,9},{11,1... | collective-permute-start | bytes 786440 | tf_op jit(solution)/shard_map/ppermute | solution.py:495
  22.3 5.0 %collective-permute-start.3 = (bf16[256,512]{1,0:T(8,128)(2,1)S(1)}, bf16[256,512]{1,0:T(8,128)(2,1)S(1)}, u32[]{:S(2)}, u32[]{:S(2)}) collective-permute-start(bf16[256,512]{1,0:T(8,128)(2,1)S(1)} %pad_maximum_fusion), channel_id=1, source_target_pairs={{0,1},{1,2},{2,3},{3,4},{4,5},{5,6},{6,7},{7,0},{8,9},{9,10},{10,1... | collective-permute-start | bytes 786440 | tf_op jit(solution)/shard_map/ppermute | solution.py:494
  27.3 0.0 copy-done.3
  27.3 0.0 copy-done.4
  27.4 0.0 copy-done.8
  27.4 12.5 %window.1 = (bf16[1024,512]{1,0:T(8,128)(2,1)}, bf16[1024,512]{1,0:T(8,128)(2,1)S(1)}, bf16[576,1024]{1,0:T(8,128)(2,1)S(1)}) custom-call(s32[8,8]{1,0:T(8,128)S(1)} %copy-done.10, bf16[512,512]{1,0:T(8,128)(2,1)S(1)} %bitcast.25, bf16[512,512]{1,0:T(8,128)(2,1)S(1)} %bitcast.27, bf16[3,512]{1,0:T(4,128)(2,1)S(1)} %bitcast.30, ...), custom_call_target="tpu_custom_call" | custom-call | flops 12884901888 | bytes 12582912 | tf_op jit(solution)/shard_map/window/pallas_call | solution.py:497
  39.9 0.0 collective-permute-done.4.south_ref
  39.9 0.0 collective-permute-done.3.north_ref
  39.9 5.6 %last.1 = bf16[1024,512]{1,0:T(8,128)(2,1)} custom-call(s32[8,8]{1,0:T(8,128)S(1)} %copy-done.10, bf16[256,512]{1,0:T(8,128)(2,1)S(1)} %collective-permute-done.3.north_ref, bf16[256,512]{1,0:T(8,128)(2,1)S(1)} %collective-permute-done.4.south_ref, bf16[1024,512]{1,0:T(8,128)(2,1)S(1)} %get-tuple-element.28.edge_keys_ref, ...), custom_call_target="tpu_custom_call", output_to_operand_aliasing={{}: (13, {})} | custom-call | flops 4294967296 | bytes 8388608 | tf_op jit(solution)/shard_map/last/pallas_call | solution.py:527
  (4 shorter events, 0.1 us)
Async XLA Ops:
  0.0 1.5 %copy-start = (bf16[1,64,16,512]{3,2,1,0:T(8,128)(2,1)S(1)}, bf16[1,64,16,512]{3,2,1,0:T(8,128)(2,1)}, u32[]{:S(2)}) copy-start(bf16[1,64,16,512]{3,2,1,0:T(8,128)(2,1)} %param.11) | copy-start | bytes 3145732
  0.0 1.5 %copy-start.2 = (bf16[1,3,512]{2,1,0:T(4,128)(2,1)S(1)}, bf16[1,3,512]{2,1,0:T(4,128)(2,1)}, u32[]{:S(2)}) copy-start(bf16[1,3,512]{2,1,0:T(4,128)(2,1)} %param.12) | copy-start | bytes 9220
  0.0 1.9 %copy-start.1 = (bf16[1,512,1024]{2,1,0:T(8,128)(2,1)S(1)}, bf16[1,512,1024]{2,1,0:T(8,128)(2,1)}, u32[]{:S(2)}) copy-start(bf16[1,512,1024]{2,1,0:T(8,128)(2,1)} %param.16) | copy-start | bytes 3145732
  1.9 3.8 %copy-start.5 = (bf16[1,512,1536]{2,1,0:T(8,128)(2,1)S(1)}, bf16[1,512,1536]{2,1,0:T(8,128)(2,1)}, u32[]{:S(2)}) copy-start(bf16[1,512,1536]{2,1,0:T(8,128)(2,1)} %param.13) | copy-start | bytes 4718596
  1.9 3.8 %copy-start.6 = (bf16[1,512,512]{2,1,0:T(8,128)(2,1)S(1)}, bf16[1,512,512]{2,1,0:T(8,128)(2,1)}, u32[]{:S(2)}) copy-start(bf16[1,512,512]{2,1,0:T(8,128)(2,1)} %param.15) | copy-start | bytes 1572868
  3.5 5.1 %collective-permute-start.2 = (bf16[1024,1024]{1,0:T(8,128)(2,1)S(1)}, bf16[1024,1024]{1,0:T(8,128)(2,1)S(1)}, u32[]{:S(2)}, u32[]{:S(2)}) collective-permute-start(bf16[1024,1024]{1,0:T(8,128)(2,1)S(1)} %cross_kv.1), channel_id=1, source_target_pairs={{0,64},{64,0},{1,65},{65,1},{2,66},{66,2},{3,67},{67,3},{4,68},{68... | collective-permute-start | bytes 6291464 | tf_op jit(solution)/shard_map/ppermute | solution.py:450
  3.6 14.3 %collective-permute-start = (bf16[64,8,512]{2,1,0:T(8,128)(2,1)S(1)}, bf16[64,8,512]{2,1,0:T(8,128)(2,1)S(1)}, u32[]{:S(2)}, u32[]{:S(2)}) collective-permute-start(bf16[64,8,512]{2,1,0:T(8,128)(2,1)S(1)} %get-tuple-element.18), channel_id=1, source_target_pairs={{0,8},{8,16},{16,24},{24,32},{32,40},{40,48},{48,56},{56,0},{1,9},... | collective-permute-start | bytes 1572872 | tf_op jit(solution)/shard_map/ppermute | solution.py:430
  5.2 16.1 %collective-permute-start.1 = (bf16[64,8,512]{2,1,0:T(8,128)(2,1)S(1)}, bf16[64,8,512]{2,1,0:T(8,128)(2,1)S(1)}, u32[]{:S(2)}, u32[]{:S(2)}) collective-permute-start(bf16[64,8,512]{2,1,0:T(8,128)(2,1)S(1)} %get-tuple-element.19), channel_id=1, source_target_pairs={{8,0},{16,8},{24,16},{32,24},{40,32},{48,40},{56,48},{0,56},{9,1},... | collective-permute-start | bytes 1572872 | tf_op jit(solution)/shard_map/ppermute | solution.py:431
  5.7 2.9 %copy-start.7 = (bf16[1,512,512]{2,1,0:T(8,128)(2,1)S(1)}, bf16[1,512,512]{2,1,0:T(8,128)(2,1)}, u32[]{:S(2)}) copy-start(bf16[1,512,512]{2,1,0:T(8,128)(2,1)} %param.17) | copy-start | bytes 1572868
  5.7 2.9 %copy-start.9 = (s32[2,8,1,4]{1,3,2,0:T(4,128)S(1)}, s32[2,8,1,4]{1,3,2,0:T(4,128)}, u32[]{:S(2)}) copy-start(s32[2,8,1,4]{1,3,2,0:T(4,128)} %param.20) | copy-start | bytes 772
  5.7 2.9 %copy-start.10 = (s32[8,8]{1,0:T(8,128)S(1)}, s32[8,8]{1,0:T(8,128)}, u32[]{:S(2)}) copy-start(s32[8,8]{1,0:T(8,128)} %land_ref.5) | copy-start | bytes 772
  8.6 18.7 %copy-start.3 = (bf16[1,512,2048]{2,1,0:T(8,128)(2,1)S(1)}, bf16[1,512,2048]{2,1,0:T(8,128)(2,1)}, u32[]{:S(2)}) copy-start(bf16[1,512,2048]{2,1,0:T(8,128)(2,1)} %param.18) | copy-start | bytes 6291460
  8.6 18.7 %copy-start.4 = (bf16[1,2048,512]{2,1,0:T(8,128)(2,1)S(1)}, bf16[1,2048,512]{2,1,0:T(8,128)(2,1)}, u32[]{:S(2)}) copy-start(bf16[1,2048,512]{2,1,0:T(8,128)(2,1)} %param.19) | copy-start | bytes 6291460
  8.6 18.7 %copy-start.8 = (bf16[1,512,512]{2,1,0:T(8,128)(2,1)S(1)}, bf16[1,512,512]{2,1,0:T(8,128)(2,1)}, u32[]{:S(2)}) copy-start(bf16[1,512,512]{2,1,0:T(8,128)(2,1)} %param.14) | copy-start | bytes 1572868
  21.4 18.5 %collective-permute-start.4 = (bf16[256,512]{1,0:T(8,128)(2,1)S(1)}, bf16[256,512]{1,0:T(8,128)(2,1)S(1)}, u32[]{:S(2)}, u32[]{:S(2)}) collective-permute-start(bf16[256,512]{1,0:T(8,128)(2,1)S(1)} %pad_maximum_fusion.1), channel_id=1, source_target_pairs={{1,0},{2,1},{3,2},{4,3},{5,4},{6,5},{7,6},{0,7},{9,8},{10,9},{11,1... | collective-permute-start | bytes 786440 | tf_op jit(solution)/shard_map/ppermute | solution.py:495
  22.3 17.6 %collective-permute-start.3 = (bf16[256,512]{1,0:T(8,128)(2,1)S(1)}, bf16[256,512]{1,0:T(8,128)(2,1)S(1)}, u32[]{:S(2)}, u32[]{:S(2)}) collective-permute-start(bf16[256,512]{1,0:T(8,128)(2,1)S(1)} %pad_maximum_fusion), channel_id=1, source_target_pairs={{0,1},{1,2},{2,3},{3,4},{4,5},{5,6},{6,7},{7,0},{8,9},{9,10},{10,1... | collective-permute-start | bytes 786440 | tf_op jit(solution)/shard_map/ppermute | solution.py:494

commit v13 on v12

--- a/solution.py
+++ b/solution.py
@@ -307,8 +307,8 @@
         edge_va_ref[:, to] = va_ref[:, at : at + 2 * GROUP]
 
     own_land = land_ref[lax.axis_index("tile"), lax.axis_index("face")]
-    chunk = (NB - 2) * CELLS // 2
-    spans = [slice(CELLS + c * chunk, CELLS + (c + 1) * chunk) for c in range(2)]
+    chunk = (NB - 2) * CELLS
+    spans = [slice(CELLS, CELLS + chunk)]
     pieces = []
     for at in spans:
         index = (at.start + lax.broadcasted_iota(jnp.int32, (chunk, 1), 0)) // CELLS
@@ -344,13 +344,17 @@
     del held_hbm
     is_air, flags = place(land_ref)
     rows_x = jnp.concatenate([north_ref[...], south_ref[...]], axis=0)
-    new_keys, new_values = project(rows_x, gain_ref, qkv_ref)
+    normed = norm_round(rows_x.astype(F32), gain_ref[0:1, :])
+    new_keys = mm(normed, qkv_ref[:, D : 2 * D]).astype(BF)
     for n in range(2):
-        new, held = n * WINDOW + n * 2 * GROUP, n * WINDOW + (1 - n) * GROUP
+        held = n * WINDOW + (1 - n) * GROUP
         src = slice(n * 2 * GROUP, (n + 1) * 2 * GROUP)
-        keys_ref[new : new + GROUP, :] = new_keys[n * GROUP : (n + 1) * GROUP]
         keys_ref[held : held + 2 * GROUP, :] = edge_keys_ref[src, :]
         va_ref[:, held : held + 2 * GROUP] = edge_va_ref[:, src]
+    new_values = mm_tt(qkv_ref[:, 2 * D :], normed).astype(BF)
+    for n in range(2):
+        new = n * WINDOW + n * 2 * GROUP
+        keys_ref[new : new + GROUP, :] = new_keys[n * GROUP : (n + 1) * GROUP]
         r = n * (NB + 1)
         at = n * GROUP
         augment(new_values[:, at : at + CELLS], flags(r)[0], va_ref, new)

time: 45.9 us -> 46 us (level)
  no operation moved by 1% of the time
where the time goes in v13:
time: 46 us; the launch traced here: 45.7 us
  Pallas kernels  29.4 us (64%)
  starting transfers between devices  8.14 us (18%)
  waiting for transfers between devices  5.81 us (13%)
  local copies, waits for them, and re-layouts  1.94 us (4%)
    pallas_call x1, Pallas kernels, per_device(): pl.pallas_call(kernel_window, in_specs=[SMEM] + [VMEM] * 12, out_specs=[V...  12.5 us
    pallas_call x1, Pallas kernels, per_device(): pl.pallas_call(kernel_cross, in_specs=[SMEM] * 2 + [VMEM] * 3, out_specs=...  6.85 us
    pallas_call x1, Pallas kernels, per_device(): pl.pallas_call(kernel_last, in_specs=[SMEM] + [VMEM] * 12 + [ANY], out_sp...  5.58 us
    ppermute x1, starting transfers between devices, per_device(): north = lax.ppermute(bottom, 'tile', forward)  5.04 us
    ppermute x1, waiting for transfers between devices, per_device(): east = lax.ppermute(west_edge, 'face', backward).reshape(NB * SIDE, D)  3.4 us
    pallas_call x1, Pallas kernels, per_device(): pl.pallas_call(kernel_own, grid=(2,), in_specs=[block, pl.BlockSpec((3, D...  2.82 us
    ppermute x1, waiting for transfers between devices, per_device(): west = lax.ppermute(east_edge, 'face', forward).reshape(NB * SIDE, D)  2.4 us
    ppermute x1, starting transfers between devices, per_device(): west = lax.ppermute(east_edge, 'face', forward).reshape(NB * SIDE, D)  1.64 us
  transfers between devices with their start and end apart: 5, of which 2 were waited for; matrix products, arithmetic and copies ran while one was open for 0% of the time, Pallas kernels for 49%

profile of v13, /device:TPU:30, one launch (start us, length us, event | category | flops | bytes accessed | tf_op | source)
XLA Modules:
  0.0 45.7 jit_solution(15754809106407778808)
XLA Ops:
  0.0 0.0 copy-start
  0.0 0.0 copy-start.2
  0.0 0.0 copy-start.1
  0.0 1.4 %fusion.1 = (bf16[64,8,512]{2,1,0:T(8,128)(2,1)S(1)}, bf16[64,8,512]{2,1,0:T(8,128)(2,1)S(1)}) fusion(bf16[64,16,512]{2,1,0:T(8,128)(2,1)} %bitcast.18), kind=kLoop, calls=%fused_computation.3 | loop fusion | bytes 2097152 | tf_op jit(solution)/shard_map/slice | solution.py:432
  1.4 0.1 copy-done
  1.5 0.0 copy-done.2
  1.5 0.3 copy-done.1
  1.9 0.0 copy-start.5
  1.9 0.0 copy-start.6
  1.9 1.6 %cross_kv.1 = bf16[1024,1024]{1,0:T(8,128)(2,1)S(1)} custom-call(bf16[1024,512]{1,0:T(8,128)(2,1)S(1)} %bitcast.19, bf16[3,512]{1,0:T(4,128)(2,1)S(1)} %bitcast.28, bf16[512,1024]{1,0:T(8,128)(2,1)S(1)} %bitcast.23), custom_call_target="tpu_custom_call" | custom-call | flops 1073741824 | bytes 4194304 | tf_op jit(solution)/shard_map/cross_kv/pallas_call | solution.py:440
  3.5 0.1 collective-permute-start.2
  3.6 1.6 %collective-permute-start = (bf16[64,8,512]{2,1,0:T(8,128)(2,1)S(1)}, bf16[64,8,512]{2,1,0:T(8,128)(2,1)S(1)}, u32[]{:S(2)}, u32[]{:S(2)}) collective-permute-start(bf16[64,8,512]{2,1,0:T(8,128)(2,1)S(1)} %get-tuple-element.18), channel_id=1, source_target_pairs={{0,8},{8,16},{16,24},{24,32},{32,40},{40,48},{48,56},{56,0},{1,9},... | collective-permute-start | bytes 1572872 | tf_op jit(solution)/shard_map/ppermute | solution.py:434
  5.2 0.5 collective-permute-start.1
  5.7 0.0 copy-done.5
  5.7 0.0 copy-done.6
  5.7 0.0 copy-start.7
  5.7 0.0 copy-start.9
  5.7 0.0 copy-start.10
  5.7 2.8 %own.1 = (bf16[1024,512]{1,0:T(8,128)(2,1)S(1)}, bf16[1024,512]{1,0:T(8,128)(2,1)S(1)}, bf16[512,1024]{1,0:T(8,128)(2,1)S(1)}, bf16[1024,512]{1,0:T(8,128)(2,1)S(1)}) custom-call(bf16[1024,512]{1,0:T(8,128)(2,1)S(1)} %bitcast.20, bf16[3,512]{1,0:T(4,128)(2,1)S(1)} %bitcast.29, bf16[512,1536]{1,0:T(8,128)(2,1)S(1)} %bitcast.36, bf16[512,512]{1,0:T(8,128)(2,1)S(1)} %bitcast.39), custom_call_target="tpu_custom_call" | custom-call | flops 2147483648 | bytes 7340032 | tf_op jit(solution)/shard_map/own/pallas_call | solution.py:456
  8.6 0.0 collective-permute-done.2.kv_ref
  8.6 0.0 copy-done.7
  8.6 0.0 copy-done.9
  8.6 0.0 copy-done.10
  8.6 0.0 copy-start.3
  8.6 0.0 copy-start.4
  8.6 0.0 copy-start.8
  8.7 6.9 %cross.1.update_ref = f32[1024,512]{1,0:T(8,128)S(1)} custom-call(s32[2,4,8]{2,1,0:T(4,128)S(1)} %bitcast.43, s32[8,8]{1,0:T(8,128)S(1)} %copy-done.10, bf16[1024,512]{1,0:T(8,128)(2,1)S(1)} %get-tuple-element.21.q_ref, bf16[1024,1024]{1,0:T(8,128)(2,1)S(1)} %collective-permute-done.2.kv_ref, bf16[512,512]{1,0:T(8,128)(2,1)S(1)} %bitcast.40), custom_call_target="tpu_custom_call" | custom-call | flops 4294967296 | bytes 4194304 | tf_op jit(solution)/shard_map/cross/pallas_call | solution.py:473
  15.5 2.4 %collective-permute-done = bf16[64,8,512]{2,1,0:T(8,128)(2,1)S(1)} collective-permute-done((bf16[64,8,512]{2,1,0:T(8,128)(2,1)S(1)}, bf16[64,8,512]{2,1,0:T(8,128)(2,1)S(1)}, u32[]{:S(2)}, u32[]{:S(2)}) %collective-permute-start) | collective-permute-done | bytes 524320 | tf_op jit(solution)/shard_map/ppermute | solution.py:434
  17.9 3.4 %collective-permute-done.1 = bf16[64,8,512]{2,1,0:T(8,128)(2,1)S(1)} collective-permute-done((bf16[64,8,512]{2,1,0:T(8,128)(2,1)S(1)}, bf16[64,8,512]{2,1,0:T(8,128)(2,1)S(1)}, u32[]{:S(2)}, u32[]{:S(2)}) %collective-permute-start.1) | collective-permute-done | bytes 524320 | tf_op jit(solution)/shard_map/ppermute | solution.py:435
  21.4 0.9 %collective-permute-start.4 = (bf16[256,512]{1,0:T(8,128)(2,1)S(1)}, bf16[256,512]{1,0:T(8,128)(2,1)S(1)}, u32[]{:S(2)}, u32[]{:S(2)}) collective-permute-start(bf16[256,512]{1,0:T(8,128)(2,1)S(1)} %pad_maximum_fusion.1), channel_id=1, source_target_pairs={{1,0},{2,1},{3,2},{4,3},{5,4},{6,5},{7,6},{0,7},{9,8},{10,9},{11,1... | collective-permute-start | bytes 786440 | tf_op jit(solution)/shard_map/ppermute | solution.py:499
  22.3 5.0 %collective-permute-start.3 = (bf16[256,512]{1,0:T(8,128)(2,1)S(1)}, bf16[256,512]{1,0:T(8,128)(2,1)S(1)}, u32[]{:S(2)}, u32[]{:S(2)}) collective-permute-start(bf16[256,512]{1,0:T(8,128)(2,1)S(1)} %pad_maximum_fusion), channel_id=1, source_target_pairs={{0,1},{1,2},{2,3},{3,4},{4,5},{5,6},{6,7},{7,0},{8,9},{9,10},{10,1... | collective-permute-start | bytes 786440 | tf_op jit(solution)/shard_map/ppermute | solution.py:498
  27.3 0.0 copy-done.3
  27.3 0.0 copy-done.4
  27.4 0.0 copy-done.8
  27.4 12.5 %window.1 = (bf16[1024,512]{1,0:T(8,128)(2,1)}, bf16[1024,512]{1,0:T(8,128)(2,1)S(1)}, bf16[576,1024]{1,0:T(8,128)(2,1)S(1)}) custom-call(s32[8,8]{1,0:T(8,128)S(1)} %copy-done.10, bf16[512,512]{1,0:T(8,128)(2,1)S(1)} %bitcast.25, bf16[512,512]{1,0:T(8,128)(2,1)S(1)} %bitcast.27, bf16[3,512]{1,0:T(4,128)(2,1)S(1)} %bitcast.30, ...), custom_call_target="tpu_custom_call" | custom-call | flops 12884901888 | bytes 12582912 | tf_op jit(solution)/shard_map/window/pallas_call | solution.py:501
  39.9 0.0 collective-permute-done.4.south_ref
  39.9 0.0 collective-permute-done.3.north_ref
  39.9 5.6 %last.1 = bf16[1024,512]{1,0:T(8,128)(2,1)} custom-call(s32[8,8]{1,0:T(8,128)S(1)} %copy-done.10, bf16[256,512]{1,0:T(8,128)(2,1)S(1)} %collective-permute-done.3.north_ref, bf16[256,512]{1,0:T(8,128)(2,1)S(1)} %collective-permute-done.4.south_ref, bf16[1024,512]{1,0:T(8,128)(2,1)S(1)} %get-tuple-element.28.edge_keys_ref, ...), custom_call_target="tpu_custom_call", output_to_operand_aliasing={{}: (13, {})} | custom-call | flops 4294967296 | bytes 8388608 | tf_op jit(solution)/shard_map/last/pallas_call | solution.py:531
  (4 shorter events, 0.1 us)
Async XLA Ops:
  0.0 1.5 %copy-start = (bf16[1,64,16,512]{3,2,1,0:T(8,128)(2,1)S(1)}, bf16[1,64,16,512]{3,2,1,0:T(8,128)(2,1)}, u32[]{:S(2)}) copy-start(bf16[1,64,16,512]{3,2,1,0:T(8,128)(2,1)} %param.11) | copy-start | bytes 3145732
  0.0 1.5 %copy-start.2 = (bf16[1,3,512]{2,1,0:T(4,128)(2,1)S(1)}, bf16[1,3,512]{2,1,0:T(4,128)(2,1)}, u32[]{:S(2)}) copy-start(bf16[1,3,512]{2,1,0:T(4,128)(2,1)} %param.12) | copy-start | bytes 9220
  0.0 1.9 %copy-start.1 = (bf16[1,512,1024]{2,1,0:T(8,128)(2,1)S(1)}, bf16[1,512,1024]{2,1,0:T(8,128)(2,1)}, u32[]{:S(2)}) copy-start(bf16[1,512,1024]{2,1,0:T(8,128)(2,1)} %param.16) | copy-start | bytes 3145732
  1.9 3.8 %copy-start.5 = (bf16[1,512,1536]{2,1,0:T(8,128)(2,1)S(1)}, bf16[1,512,1536]{2,1,0:T(8,128)(2,1)}, u32[]{:S(2)}) copy-start(bf16[1,512,1536]{2,1,0:T(8,128)(2,1)} %param.13) | copy-start | bytes 4718596
  1.9 3.8 %copy-start.6 = (bf16[1,512,512]{2,1,0:T(8,128)(2,1)S(1)}, bf16[1,512,512]{2,1,0:T(8,128)(2,1)}, u32[]{:S(2)}) copy-start(bf16[1,512,512]{2,1,0:T(8,128)(2,1)} %param.15) | copy-start | bytes 1572868
  3.5 5.1 %collective-permute-start.2 = (bf16[1024,1024]{1,0:T(8,128)(2,1)S(1)}, bf16[1024,1024]{1,0:T(8,128)(2,1)S(1)}, u32[]{:S(2)}, u32[]{:S(2)}) collective-permute-start(bf16[1024,1024]{1,0:T(8,128)(2,1)S(1)} %cross_kv.1), channel_id=1, source_target_pairs={{0,64},{64,0},{1,65},{65,1},{2,66},{66,2},{3,67},{67,3},{4,68},{68... | collective-permute-start | bytes 6291464 | tf_op jit(solution)/shard_map/ppermute | solution.py:454
  3.6 14.3 %collective-permute-start = (bf16[64,8,512]{2,1,0:T(8,128)(2,1)S(1)}, bf16[64,8,512]{2,1,0:T(8,128)(2,1)S(1)}, u32[]{:S(2)}, u32[]{:S(2)}) collective-permute-start(bf16[64,8,512]{2,1,0:T(8,128)(2,1)S(1)} %get-tuple-element.18), channel_id=1, source_target_pairs={{0,8},{8,16},{16,24},{24,32},{32,40},{40,48},{48,56},{56,0},{1,9},... | collective-permute-start | bytes 1572872 | tf_op jit(solution)/shard_map/ppermute | solution.py:434
  5.2 16.1 %collective-permute-start.1 = (bf16[64,8,512]{2,1,0:T(8,128)(2,1)S(1)}, bf16[64,8,512]{2,1,0:T(8,128)(2,1)S(1)}, u32[]{:S(2)}, u32[]{:S(2)}) collective-permute-start(bf16[64,8,512]{2,1,0:T(8,128)(2,1)S(1)} %get-tuple-element.19), channel_id=1, source_target_pairs={{8,0},{16,8},{24,16},{32,24},{40,32},{48,40},{56,48},{0,56},{9,1},... | collective-permute-start | bytes 1572872 | tf_op jit(solution)/shard_map/ppermute | solution.py:435
  5.7 2.9 %copy-start.7 = (bf16[1,512,512]{2,1,0:T(8,128)(2,1)S(1)}, bf16[1,512,512]{2,1,0:T(8,128)(2,1)}, u32[]{:S(2)}) copy-start(bf16[1,512,512]{2,1,0:T(8,128)(2,1)} %param.17) | copy-start | bytes 1572868
  5.7 2.9 %copy-start.9 = (s32[2,8,1,4]{1,3,2,0:T(4,128)S(1)}, s32[2,8,1,4]{1,3,2,0:T(4,128)}, u32[]{:S(2)}) copy-start(s32[2,8,1,4]{1,3,2,0:T(4,128)} %param.20) | copy-start | bytes 772
  5.7 2.9 %copy-start.10 = (s32[8,8]{1,0:T(8,128)S(1)}, s32[8,8]{1,0:T(8,128)}, u32[]{:S(2)}) copy-start(s32[8,8]{1,0:T(8,128)} %land_ref.5) | copy-start | bytes 772
  8.6 18.7 %copy-start.3 = (bf16[1,512,2048]{2,1,0:T(8,128)(2,1)S(1)}, bf16[1,512,2048]{2,1,0:T(8,128)(2,1)}, u32[]{:S(2)}) copy-start(bf16[1,512,2048]{2,1,0:T(8,128)(2,1)} %param.18) | copy-start | bytes 6291460
  8.6 18.7 %copy-start.4 = (bf16[1,2048,512]{2,1,0:T(8,128)(2,1)S(1)}, bf16[1,2048,512]{2,1,0:T(8,128)(2,1)}, u32[]{:S(2)}) copy-start(bf16[1,2048,512]{2,1,0:T(8,128)(2,1)} %param.19) | copy-start | bytes 6291460
  8.6 18.7 %copy-start.8 = (bf16[1,512,512]{2,1,0:T(8,128)(2,1)S(1)}, bf16[1,512,512]{2,1,0:T(8,128)(2,1)}, u32[]{:S(2)}) copy-start(bf16[1,512,512]{2,1,0:T(8,128)(2,1)} %param.14) | copy-start | bytes 1572868
  21.4 18.5 %collective-permute-start.4 = (bf16[256,512]{1,0:T(8,128)(2,1)S(1)}, bf16[256,512]{1,0:T(8,128)(2,1)S(1)}, u32[]{:S(2)}, u32[]{:S(2)}) collective-permute-start(bf16[256,512]{1,0:T(8,128)(2,1)S(1)} %pad_maximum_fusion.1), channel_id=1, source_target_pairs={{1,0},{2,1},{3,2},{4,3},{5,4},{6,5},{7,6},{0,7},{9,8},{10,9},{11,1... | collective-permute-start | bytes 786440 | tf_op jit(solution)/shard_map/ppermute | solution.py:499
  22.3 17.6 %collective-permute-start.3 = (bf16[256,512]{1,0:T(8,128)(2,1)S(1)}, bf16[256,512]{1,0:T(8,128)(2,1)S(1)}, u32[]{:S(2)}, u32[]{:S(2)}) collective-permute-start(bf16[256,512]{1,0:T(8,128)(2,1)S(1)} %pad_maximum_fusion), channel_id=1, source_target_pairs={{0,1},{1,2},{2,3},{3,4},{4,5},{5,6},{6,7},{7,0},{8,9},{9,10},{10,1... | collective-permute-start | bytes 786440 | tf_op jit(solution)/shard_map/ppermute | solution.py:498
